TPU v7x, 32 devices: a whole 2x2x4 slice. The times are simulated.
32 devices in a mesh: seq: 8 (over z, y), mlp: 4 (over x, core).
Axes of the slice: x: 2, y: 2, z: 4, core: 2. Of those that a mesh axis runs over, the one named last changes fastest.
Arguments:
- residual: bfloat16 [8, 512, 3072], P('seq', None, 'mlp'), may hold values from -24 to 24
- spatial_qkv: bfloat16 [8, 512, 3, 1536], P('seq', None, None, 'mlp'), may hold values from -12 to 12
- spatial_out: bfloat16 [1536, 3072], P('mlp'), may hold values from -0.21875 to 0.21875
- temporal_qkv: bfloat16 [3072, 3, 1536], P(None, None, 'mlp'), may hold values from -0.5 to 0.5
- temporal_norm_shift: float32 [3072], replicated, may hold values from -3 to 3
- norm_scale: float32 [3072], replicated, may hold values from -3 to 3
- branch_gate: float32 [3072], replicated, may hold values from 0.5 to 1.5
Outputs:
- updated: bfloat16 [8, 512, 3072], P('seq', None, 'mlp')
- temporal_mix: bfloat16 [8, 512, 1536], P('seq', None, 'mlp')
All inputs are finite; a program needn't handle non-finite values.
Results may differ from a plain program's by a relative error of at most 0.02.
Values may be sent and summed in bfloat16 or wider, within the bound.
No kernel may reach another device: no remote copies, remote signals or barrier semaphores. Data moves between devices by JAX's collectives and lax.ppermute only.
A program may use at most 64 MiB of HBM per device.

v0:
```python
import math

import jax
import jax.numpy as jnp
from jax import lax
from jax.sharding import PartitionSpec as P

D = 3072
HEAD_DIM = 128


epsilon = 1e-06


def softmax_weights(attention_logits):
    row_top = jnp.max(attention_logits, axis=-1, keepdims=True)
    exponent = jnp.exp(attention_logits - row_top)
    return (exponent / jnp.sum(exponent, axis=-1, keepdims=True)).astype(jnp.bfloat16)


def spatial_attend(query_rows, key_matrix_rows, value_matrix_rows):
    attention_logits = jnp.einsum(
        "bnhd,bmhd->bhnm", query_rows, key_matrix_rows, preferred_element_type=jnp.float32
    ) / math.sqrt(query_rows.shape[-1])
    attention_probs = softmax_weights(attention_logits)
    return jnp.einsum(
        "bhnm,bmhd->bnhd", attention_probs, value_matrix_rows, preferred_element_type=jnp.float32
    ).astype(jnp.bfloat16)


def temporal_attend(stacked):
    attention_logits = jnp.einsum(
        "fphd,gphd->phfg", stacked[:, :, 0], stacked[:, :, 1], preferred_element_type=jnp.float32
    ) / math.sqrt(stacked.shape[-1])
    attention_probs = softmax_weights(attention_logits)
    return jnp.einsum(
        "phfg,gphd->fphd", attention_probs, stacked[:, :, 2], preferred_element_type=jnp.float32
    ).astype(jnp.bfloat16)


def rotation_rates(head_size):
    return 10000.0 ** (-2.0 * jnp.arange(head_size // 2, dtype=jnp.float32) / head_size)


def rotary(stacked, angles):
    half_size = stacked.shape[-1] // 2
    first_half = stacked[..., :half_size]
    second_half = stacked[..., half_size:]
    cosine = jnp.cos(angles)
    sine_part = jnp.sin(angles)
    return jnp.concatenate(
        [
            first_half * cosine - second_half * sine_part,
            second_half * cosine + first_half * sine_part,
        ],
        axis=-1,
    )


def rotate_parts(projected, places):
    angles = places[:, None, None, None, None] * rotation_rates(projected.shape[-1])
    turned = rotary(projected[:, :, :2], angles)
    return jnp.concatenate([turned, projected[:, :, 2:]], axis=2).astype(jnp.bfloat16)


def modulate(row_data, temporal_norm_shift, norm_scale):
    values = row_data.astype(jnp.float32)
    row_mean = jnp.mean(values, axis=-1, keepdims=True)
    spread = jnp.mean(values * values, axis=-1, keepdims=True) - row_mean * row_mean
    return (
        (values - row_mean) * lax.rsqrt(spread + epsilon) * (1.0 + norm_scale) + temporal_norm_shift
    ).astype(jnp.bfloat16)


def on_device(
    residual, spatial_qkv, spatial_out, temporal_qkv, temporal_norm_shift, norm_scale, branch_gate
):
    frames, patches, share_cols = residual.shape
    local_width = spatial_qkv.shape[-1]
    heads_here = local_width // HEAD_DIM
    tokens = frames * patches
    blocks = spatial_qkv.reshape(frames, patches, 3, heads_here, HEAD_DIM)
    spatial = spatial_attend(blocks[:, :, 0], blocks[:, :, 1], blocks[:, :, 2]).reshape(
        tokens, local_width
    )
    head_terms = jnp.dot(spatial, spatial_out, preferred_element_type=jnp.float32) * branch_gate
    column = lax.axis_index("mlp") * share_cols
    wide_rows = lax.all_gather(residual, "mlp", axis=2, tiled=True).reshape(tokens, D)
    branch = lax.psum(head_terms.astype(jnp.bfloat16), "mlp").astype(jnp.float32)
    updated_full = (wide_rows.astype(jnp.float32) + branch).astype(jnp.bfloat16)
    normed_full = modulate(updated_full, temporal_norm_shift, norm_scale)
    updated = lax.dynamic_slice_in_dim(updated_full, column, share_cols, 1)
    projected = jnp.einsum(
        "td,dch->tch", normed_full, temporal_qkv, preferred_element_type=jnp.float32
    )
    shaped = projected.reshape(frames, patches, 3, heads_here, HEAD_DIM)
    places = (lax.axis_index("seq") * frames + jnp.arange(frames)).astype(jnp.float32)
    turned = rotate_parts(shaped, places)
    blended_head_output = temporal_attend(
        lax.all_to_all(turned, "seq", split_axis=1, concat_axis=0, tiled=True)
    )
    result = lax.all_to_all(blended_head_output, "seq", split_axis=0, concat_axis=1, tiled=True)
    return (
        updated.reshape(frames, patches, share_cols),
        result.reshape(frames, patches, local_width),
    )


def solution(mesh):
    return jax.shard_map(
        on_device,
        mesh=mesh,
        in_specs=(
            P("seq", None, "mlp"),
            P("seq", None, None, "mlp"),
            P("mlp", None),
            P(None, None, "mlp"),
            P(),
            P(),
            P(),
        ),
        out_specs=(P("seq", None, "mlp"), P("seq", None, "mlp")),
        check_vma=False,
    )
```

profile of v0, /device:TPU:0, one launch (start us, length us, event | category | flops | bytes accessed | tf_op | source)
XLA Modules:
  0.0 211.7 jit_solution(8836818418365332189)
XLA Ops:
  7.2 0.0 copy-start
  7.2 0.0 all-reduce.2.cloned.1.call-start
  7.2 1.7 copy.55
  9.0 0.6 fusion.24
  9.6 0.0 copy-start.2
  9.6 1.7 copy-done.2
  11.2 1.5 fusion.39
  12.7 0.0 copy-start.4
  12.7 4.8 %fusion.22 = bf16[3,512,128]{1,2,0:T(8,128)(2,1)} fusion(f32[3,512]{1,0:T(4,128)} %fusion.39, bf16[1,512,3,3,128]{1,4,3,2,0:T(8,128)(2,1)S(1)} %bitcast.55, f32[3,512,512]{1,2,0:T(8,128)} %copy-done.2), kind=kOutput, calls=%fused_computation.28 | convolution fusion | flops 205457408 | bytes 7086080 | tf_op jit(solution)/shard_map/bhnm,bmhd->bnhd/dot_general | solution.py:26
  17.5 0.0 copy-done
  17.5 0.0 copy-done.4
  17.5 4.5 %multiply_convert_fusion = bf16[512,3072]{1,0:T(8,128)(2,1)} fusion(bf16[512,384]{0,1:T(8,128)(2,1)} %bitcast.58, bf16[384,3072]{1,0:T(8,128)(2,1)S(1)} %copy-done, f32[3072]{0:T(1024)S(1)} %copy-done.4), kind=kOutput, calls=%fused_computation.12 | convolution fusion | flops 1211105280 | bytes 5910528 | tf_op jit(solution)/shard_map/dot_general | solution.py:86
  22.1 0.0 copy-start.3
  22.1 0.0 all-reduce.2.cloned.1.call-update
  22.1 0.0 all-gather.2.cloned.1.call-start
  22.1 0.7 all-gather.2.cloned.1.call-update
  22.8 0.1 fusion.31
  22.9 0.0 copy-done.3
  22.9 0.0 copy-start.5
  22.9 70.4 %all-reduce.2.cloned.1.call-done = bf16[512,3072]{1,0:T(8,128)(2,1)} async-done(((bf16[512,3072]{1,0:T(8,128)(2,1)}), bf16[512,3072]{1,0:T(8,128)(2,1)}) %all-reduce.2.cloned.1.call-update) | async-done | bytes 3145744 | tf_op jit(solution)/shard_map/psum | solution.py:89
  93.4 30.2 %all-gather.2.cloned.1.call-done = bf16[1,512,3072]{2,1,0:T(8,128)(2,1)} async-done(((bf16[1,512,768]{2,1,0:T(8,128)(2,1)}), bf16[1,512,3072]{2,1,0:T(8,128)(2,1)}) %all-gather.2.cloned.1.call-update) | async-done | bytes 3145744 | tf_op jit(solution)/shard_map/all_gather | solution.py:88
  123.6 4.3 %convert_reduce_fusion = (f32[512]{0:T(512)S(1)}, f32[512]{0:T(512)S(1)}, bf16[512,3072]{1,0:T(8,128)(2,1)S(1)}) fusion(bf16[512,3072]{1,0:T(8,128)(2,1)} %all-reduce.2.cloned.1.call-done, bf16[1,512,3072]{2,1,0:T(8,128)(2,1)} %all-gather.2.cloned.1.call-done), kind=kLoop, calls=%fused_computation.4 | loop fusion | flops 12581888 | bytes 9441280 | tf_op jit(solution)/shard_map/reduce_sum | solution.py:68
  127.9 0.0 copy-start.1
  127.9 0.0 copy-done.5
  127.9 8.3 %fusion.9 = f32[512,3,384]{0,2,1:T(8,128)S(1)} fusion(bf16[3072,3,384]{2,0,1:T(8,128)(2,1)} %param.10, bf16[512,3072]{1,0:T(8,128)(2,1)S(1)} %get-tuple-element.4, f32[3072]{0:T(1024)S(1)} %copy-done.5, f32[3072]{0:T(1024)S(1)} %broadcast_add_fusion, f32[512]{0:T(512)S(1)} %get-tuple-element.11, f32[512]{0:T(512)S(1)} %get-tuple-element.10), kind=kOutput, calls=%fused_computation.14 | convolution fusion | flops 3633315840 | bytes 12611584 | tf_op jit(solution)/shard_map/td,dch->tch/dot_general | solution.py:93
  136.2 0.0 copy-done.1
  136.2 0.1 slice.60
  136.3 0.3 subtract_convert_fusion
  136.6 0.1 pad_maximum_fusion
  136.7 2.3 %copy.60 = bf16[1,512,3,3,128]{4,3,2,0,1:T(4,128)(2,1)} copy(bf16[1,512,3,3,128]{1,4,3,2,0:T(8,128)(2,1)S(1)} %pad_maximum_fusion) | data formatting | bytes 2359296 | tf_op jit(solution)/shard_map/concatenate | solution.py:63
  139.0 42.9 %all_to_all.21 = bf16[1,512,3,3,128]{4,3,2,0,1:T(4,128)(2,1)S(1)} all-to-all(bf16[1,512,3,3,128]{4,3,2,0,1:T(4,128)(2,1)} %copy.60), channel_id=1, replica_groups=mesh['seq'=8,'mlp'=4] {'seq'}, dimensions={1} | all-to-all | bytes 2359296 | tf_op jit(solution)/shard_map/all_to_all | solution.py:100
  181.8 0.2 copy.61
  182.0 0.1 fusion.38
  182.1 1.5 convolution_multiply_fusion
  183.6 1.6 fusion.40
  185.2 2.1 fusion.23
  187.3 0.8 copy.66
  188.1 3.6 %all-to-all-start.1 = ((bf16[8,64,3,128]{3,1,2,0:T(8,128)(2,1)}), bf16[8,64,3,128]{3,1,2,0:T(8,128)(2,1)S(1)}, u32[]{:S(2)}, u32[]{:S(2)}) async-start(bf16[8,64,3,128]{3,1,2,0:T(8,128)(2,1)} %copy.66), calls=%async_computation.1 | async-start | bytes 786432 | tf_op jit(solution)/shard_map/all_to_all | solution.py:102
  191.8 2.1 dynamic-slice_bitcast_fusion
  193.8 9.6 %all-to-all-done.1 = bf16[8,64,3,128]{3,1,2,0:T(8,128)(2,1)S(1)} async-done(((bf16[8,64,3,128]{3,1,2,0:T(8,128)(2,1)}), bf16[8,64,3,128]{3,1,2,0:T(8,128)(2,1)S(1)}, u32[]{:S(2)}, u32[]{:S(2)}) %all-to-all-start.1) | async-done | bytes 393248 | tf_op jit(solution)/shard_map/all_to_all | solution.py:102
  203.4 0.3 copy.67
  203.8 1.1 reshape.141
  (2 shorter events, 0.0 us)
Async XLA Ops:
  7.2 10.4 %copy-start = (bf16[384,3072]{1,0:T(8,128)(2,1)S(1)}, bf16[384,3072]{1,0:T(8,128)(2,1)}, u32[]{:S(2)}) copy-start(bf16[384,3072]{1,0:T(8,128)(2,1)} %param.9) | copy-start | bytes 7077892
  7.2 86.2 %all-reduce.2.cloned.1.call-start = ((), (), s32[]{:S(2)}) async-start(), calls=%async_computation.3 | async-start | bytes 6291456 | tf_op jit(solution)/shard_map/psum | solution.py:89
  9.6 1.7 copy-start.2
  12.7 4.8 %copy-start.4 = (f32[3072]{0:T(1024)S(1)}, f32[3072]{0:T(1024)}, u32[]{:S(2)}) copy-start(f32[3072]{0:T(1024)} %param.13) | copy-start | bytes 36868
  22.1 0.8 copy-start.3
  22.1 101.5 %all-gather.2.cloned.1.call-start = ((), (), s32[]{:S(2)}) async-start(), calls=%async_computation.2 | async-start | bytes 3932160 | tf_op jit(solution)/shard_map/all_gather | solution.py:88
  22.9 105.0 %copy-start.5 = (f32[3072]{0:T(1024)S(1)}, f32[3072]{0:T(1024)}, u32[]{:S(2)}) copy-start(f32[3072]{0:T(1024)} %param.11) | copy-start | bytes 36868
  127.9 8.3 %copy-start.1 = (bf16[512,3072]{1,0:T(8,128)(2,1)}, bf16[512,3072]{1,0:T(8,128)(2,1)S(1)}, u32[]{:S(2)}) copy-start(bf16[512,3072]{1,0:T(8,128)(2,1)S(1)} %get-tuple-element.4) | copy-start | bytes 9437188
  188.1 15.3 %all-to-all-start.1 = ((bf16[8,64,3,128]{3,1,2,0:T(8,128)(2,1)}), bf16[8,64,3,128]{3,1,2,0:T(8,128)(2,1)S(1)}, u32[]{:S(2)}, u32[]{:S(2)}) async-start(bf16[8,64,3,128]{3,1,2,0:T(8,128)(2,1)} %copy.66), calls=%async_computation.1 | async-start | bytes 786432 | tf_op jit(solution)/shard_map/all_to_all | solution.py:102
Sparse Core Ops, SparseCore 0:
  22.2 71.1 all-reduce.1
  94.9 28.6 all-gather.1
where the time goes:
time: 212 us
  waiting for transfers between devices  111 us (52%)
  blocking collectives  42.9 us (20%)
  matrix products  23.4 us (11%)
  between operations  14.2 us (7%)
  local copies, waits for them, and re-layouts  10.3 us (5%)
  other arithmetic  6.17 us (3%)
  starting transfers between devices  3.72 us (2%)
    psum x1, waiting for transfers between devices, on_device(): lax.psum(head_terms.astype(jnp.bfloat16), 'mlp').astype(jnp.float32)  70.4 us
    all_to_all x1, blocking collectives, on_device(): lax.all_to_all(turned, 'seq', split_axis=1, concat_axis=0, tiled=True)  42.9 us
    all_gather x1, waiting for transfers between devices, on_device(): lax.all_gather(residual, 'mlp', axis=2, tiled=True).reshape(tokens, D)  30.2 us
    all_to_all x1, waiting for transfers between devices, on_device(): lax.all_to_all(blended_head_output, 'seq', split_axis=0, concat_axis=1, t...  9.61 us
    dot_general x1, matrix products, on_device(): jnp.einsum('td,dch->tch', normed_full, temporal_qkv, preferred_element_ty...  8.3 us
    dot_general x1, matrix products, spatial_attend(): jnp.einsum('bhnm,bmhd->bnhd', attention_probs, value_matrix_rows, preferr...  4.82 us
    dot_general x1, matrix products, on_device(): jnp.dot(spatial, spatial_out, preferred_element_type=jnp.float32)  4.52 us
    reduce_sum x1, other arithmetic, modulate(): row_mean = jnp.mean(values, axis=-1, keepdims=True)  4.26 us
  transfers between devices with their start and end apart: 3, of which 3 were waited for; matrix products, arithmetic and copies ran while one was open for 1% of the time, Pallas kernels for 0%

commit v1 on v0

v1 whole, which is shorter than its diff:
```python
import functools
import math

import jax
import jax.numpy as jnp
from jax import lax
from jax.experimental import pallas as pl
from jax.experimental.pallas import tpu as pltpu
from jax.sharding import PartitionSpec as P

HEAD_DIM = 128
EPSILON = 1e-06
CHUNKS = 2
GROUP = 16
MASKED = -1e30
VMEM_LIMIT = 28 * 1024 * 1024
EXP2_SCALE = math.log2(math.e) / math.sqrt(HEAD_DIM)


def call(body, outs, flops, moved, exps=0):
    return pl.pallas_call(
        body,
        out_shape=outs,
        compiler_params=pltpu.CompilerParams(vmem_limit_bytes=VMEM_LIMIT),
        cost_estimate=pl.CostEstimate(
            flops=int(flops), bytes_accessed=int(moved), transcendentals=int(exps)
        ),
    )


def dot(a, b):
    return jnp.dot(a, b, preferred_element_type=jnp.float32)


def dot_nt(a, b):
    return lax.dot_general(a, b, (((1,), (1,)), ((), ())), preferred_element_type=jnp.float32)


def attend(query, key, value, same=None):
    logits = dot_nt(query, key)
    if same is not None:
        logits = jnp.where(same, logits, MASKED)
    top = jnp.max(logits, axis=-1, keepdims=True)
    weights = jnp.exp2((logits - top) * EXP2_SCALE)
    total = jnp.sum(weights, axis=-1, keepdims=True)
    return (dot(weights.astype(jnp.bfloat16), value) / total).astype(jnp.bfloat16)


def spatial_kernel(qkv_ref, out_ref, *, first):
    rows, width = out_ref.shape
    for lane in range(0, width, HEAD_DIM):
        head = slice(lane, lane + HEAD_DIM)
        out_ref[:, head] = attend(
            qkv_ref[0, first : first + rows, head], qkv_ref[1, :, head], qkv_ref[2, :, head]
        )


def send_kernel(own_ref, other_ref, own_w_ref, other_w_ref, gate_ref, out_ref):
    term = dot(own_ref[...], own_w_ref[...]) + dot(other_ref[...], other_w_ref[...])
    out_ref[...] = (term * gate_ref[...]).astype(out_ref.dtype)


def keep_kernel(own_ref, other_ref, own_w_ref, other_w_ref, gate_ref, residual_ref, out_ref):
    term = dot(own_ref[...], own_w_ref[...]) + dot(other_ref[...], other_w_ref[...])
    out_ref[...] = residual_ref[...].astype(jnp.float32) + term * gate_ref[...]


def update_kernel(place_ref, base_ref, arrived_ref, whole_ref, *piece_refs):
    whole_ref[...] = (base_ref[...] + arrived_ref[...].astype(jnp.float32)).astype(whole_ref.dtype)
    count = piece_refs[0].shape[0]
    for k, piece_ref in enumerate(piece_refs):
        start = pl.multiple_of((place_ref[0] ^ k) * count, count)
        piece_ref[...] = whole_ref[pl.ds(start, count), :]


def temporal_kernel(
    place_ref, u0, u1, u2, u3, w_ref, gain_ref, shift_ref, cos_ref, sin_ref, *rest, frames
):
    *out_refs, normed_ref, proj_ref = rest
    rows, share = u0.shape
    count = rows // frames
    width = w_ref.shape[-1]
    blocks = (u0, u1, u2, u3)
    total = jnp.zeros((rows, 1), jnp.float32)
    square = jnp.zeros((rows, 1), jnp.float32)
    for ref in blocks:
        values = ref[...].astype(jnp.float32)
        total += jnp.sum(values, axis=-1, keepdims=True)
        square += jnp.sum(values * values, axis=-1, keepdims=True)
    features = share * len(blocks)
    mean = total / features
    rate = lax.rsqrt(square / features - mean * mean + EPSILON)
    starts = [pl.multiple_of((place_ref[0] ^ k) * share, share) for k in range(len(blocks))]
    for k, ref in enumerate(blocks):
        gain = 1.0 + gain_ref[:, pl.ds(starts[k], share)]
        shift = shift_ref[:, pl.ds(starts[k], share)]
        normed_ref[k] = ((ref[...].astype(jnp.float32) - mean) * rate * gain + shift).astype(
            normed_ref.dtype
        )
    for part in range(3):
        acc = dot(normed_ref[0], w_ref[part, pl.ds(starts[0], share), :])
        for k in range(1, len(blocks)):
            acc += dot(normed_ref[k], w_ref[part, pl.ds(starts[k], share), :])
        if part == 2:
            proj_ref[part] = acc.astype(proj_ref.dtype)
            continue
        shaped = acc.reshape(frames, count, width)
        cosine = cos_ref[...][:, None, :]
        sine = sin_ref[...][:, None, :]
        for lane in range(0, width, HEAD_DIM):
            head = shaped[:, :, lane : lane + HEAD_DIM]
            turned = pltpu.roll(head.reshape(rows, HEAD_DIM), HEAD_DIM // 2, 1).reshape(head.shape)
            proj_ref[part, :, lane : lane + HEAD_DIM] = (
                (head * cosine + turned * sine).reshape(rows, HEAD_DIM).astype(proj_ref.dtype)
            )
    step = GROUP if count % GROUP == 0 else count
    size = step * frames
    patch_of = lambda axis: lax.rem(lax.broadcasted_iota(jnp.int32, (size, size), axis), step)
    same = patch_of(0) == patch_of(1)
    for low in range(0, count, step):
        for lane in range(0, width, HEAD_DIM):
            head = slice(lane, lane + HEAD_DIM)

            def gathered(part):
                if step == count:
                    return proj_ref[part, :, head]
                return jnp.concatenate(
                    [
                        proj_ref[part, f * count + low : f * count + low + step, head]
                        for f in range(frames)
                    ],
                    axis=0,
                )

            mixed = attend(gathered(0), gathered(1), gathered(2), same)
            if len(out_refs) == 1:
                out_refs[0][:, head] = mixed
            else:
                for f, out_ref in enumerate(out_refs):
                    out_ref[low : low + step, head] = mixed[f * step : (f + 1) * step]


def gather_kernel(place_ref, *rest, chunks):
    *piece_refs, out_ref = rest
    many = len(piece_refs) // chunks
    count = piece_refs[0].shape[0]
    for c in range(chunks):
        for k in range(many):
            start = pl.multiple_of(c * many * count + (place_ref[0] ^ k) * count, count)
            out_ref[pl.ds(start, count), :] = piece_refs[c * many + k][...]


def swap(value, axis, size, k):
    return lax.ppermute(value, axis, [(i, i ^ k) for i in range(size)])


def smem(count):
    return [pl.BlockSpec(memory_space=pltpu.SMEM)] * count


def on_device(
    residual, spatial_qkv, spatial_out, temporal_qkv, shift, scale, gate, *, n_seq, n_mlp
):
    frames, patches, share = residual.shape
    width = spatial_qkv.shape[-1]
    features = share * n_mlp
    tokens = frames * patches
    pairwise = n_seq == 8 and frames == 1 and patches % (n_seq * CHUNKS * GROUP) == 0
    chunks = CHUNKS if pairwise else 1
    rows = tokens // chunks
    count = rows // n_seq
    seq, mlp = lax.axis_index("seq"), lax.axis_index("mlp")
    seq_place, mlp_place = seq.reshape(1), mlp.reshape(1)
    flat_residual = residual.reshape(tokens, share)
    qkv = spatial_qkv.transpose(2, 0, 1, 3).reshape(3, tokens, width)
    weights = temporal_qkv.transpose(1, 0, 2)
    vm = pl.BlockSpec(memory_space=pltpu.VMEM)
    bf16, f32 = jnp.bfloat16, jnp.float32

    def columns(array, block):
        return lax.dynamic_slice_in_dim(array, block * share, share, 1)

    gate_row = gate.reshape(1, features)
    own_send, own_keep = columns(spatial_out, mlp ^ 2), columns(spatial_out, mlp)
    other_send = swap(columns(spatial_out, mlp ^ 3), "mlp", n_mlp, 1)
    other_keep = swap(columns(spatial_out, mlp ^ 1), "mlp", n_mlp, 1)
    gate_send, gate_keep = columns(gate_row, mlp ^ 2), columns(gate_row, mlp)

    rates = 10000.0 ** (-2.0 * jnp.arange(HEAD_DIM // 2, dtype=f32) / HEAD_DIM)
    order = jnp.arange(n_seq) ^ seq if pairwise else jnp.arange(n_seq)
    angles = order.astype(f32)[:, None] * rates
    cosine = jnp.concatenate([jnp.cos(angles)] * 2, axis=1)
    sine = jnp.concatenate([-jnp.sin(angles), jnp.sin(angles)], axis=1)

    matmul_bytes = 4 * share * width + 4 * rows * width + 6 * rows * share
    updates, results = [], []
    for c in range(chunks):
        heads = call(
            functools.partial(spatial_kernel, first=c * rows),
            jax.ShapeDtypeStruct((rows, width), bf16),
            4 * rows * tokens * width,
            2 * (3 * tokens * width),
            rows * tokens * width // HEAD_DIM,
        )(qkv)
        others = swap(heads, "mlp", n_mlp, 1)
        sent = call(
            send_kernel,
            jax.ShapeDtypeStruct((rows, share), bf16),
            4 * rows * width * share,
            matmul_bytes,
        )(heads, others, own_send, other_send, gate_send)
        arrived = swap(sent, "mlp", n_mlp, 2)
        base = call(
            keep_kernel,
            jax.ShapeDtypeStruct((rows, share), f32),
            4 * rows * width * share,
            matmul_bytes,
        )(heads, others, own_keep, other_keep, gate_keep, flat_residual[c * rows : (c + 1) * rows])
        if pairwise:
            updated, *pieces = pl.pallas_call(
                update_kernel,
                out_shape=[jax.ShapeDtypeStruct((rows, share), bf16)]
                + [jax.ShapeDtypeStruct((count, share), bf16)] * n_seq,
                in_specs=smem(1) + [vm] * 2,
                out_specs=[vm] * (1 + n_seq),
                compiler_params=pltpu.CompilerParams(vmem_limit_bytes=VMEM_LIMIT),
                cost_estimate=pl.CostEstimate(
                    flops=rows * share, bytes_accessed=10 * rows * share, transcendentals=0
                ),
            )(seq_place, base, arrived)
            pieces = [pieces[0]] + [swap(pieces[k], "seq", n_seq, k) for k in range(1, n_seq)]
            mine = jnp.concatenate(pieces, axis=0)
        else:
            updated = (base + arrived.astype(f32)).astype(bf16)
            mine = lax.all_to_all(
                updated.reshape(n_seq, count, share), "seq", 0, 0, tiled=True
            ).reshape(rows, share)
        updates.append(updated)
        across = swap(mine, "mlp", n_mlp, 2)
        beside = swap(mine, "mlp", n_mlp, 1)
        diagonal = swap(across, "mlp", n_mlp, 1)
        outs = (
            [jax.ShapeDtypeStruct((count, width), bf16)] * n_seq
            if pairwise
            else [jax.ShapeDtypeStruct((rows, width), bf16)]
        )
        mixed = pl.pallas_call(
            functools.partial(temporal_kernel, frames=n_seq),
            out_shape=outs,
            in_specs=smem(1) + [vm] * 9,
            out_specs=[vm] * len(outs),
            scratch_shapes=[
                pltpu.VMEM((n_mlp, rows, share), bf16),
                pltpu.VMEM((3, rows, width), bf16),
            ],
            compiler_params=pltpu.CompilerParams(vmem_limit_bytes=VMEM_LIMIT),
            cost_estimate=pl.CostEstimate(
                flops=6 * rows * features * width,
                bytes_accessed=6 * features * width + 2 * rows * features,
                transcendentals=rows * 128 * width // HEAD_DIM,
            ),
        )(
            mlp_place, mine, beside, across, diagonal, weights,
            scale.reshape(1, features), shift.reshape(1, features), cosine, sine,
        )
        if pairwise:
            results += [mixed[0]] + [swap(mixed[k], "seq", n_seq, k) for k in range(1, n_seq)]
        else:
            back = lax.all_to_all(
                mixed[0].reshape(n_seq, count, width), "seq", 0, 0, tiled=True
            )
            results.append(back.reshape(rows, width))
    if pairwise:
        result = pl.pallas_call(
            functools.partial(gather_kernel, chunks=chunks),
            out_shape=jax.ShapeDtypeStruct((tokens, width), bf16),
            in_specs=smem(1) + [vm] * len(results),
            out_specs=vm,
            compiler_params=pltpu.CompilerParams(vmem_limit_bytes=VMEM_LIMIT),
        )(seq_place, *results)
    else:
        result = results[0]
    return (
        jnp.concatenate(updates, axis=0).reshape(frames, patches, share),
        result.reshape(frames, patches, width),
    )


def solution(mesh):
    return jax.shard_map(
        functools.partial(on_device, n_seq=mesh.shape["seq"], n_mlp=mesh.shape["mlp"]),
        mesh=mesh,
        in_specs=(
            P("seq", None, "mlp"),
            P("seq", None, None, "mlp"),
            P("mlp", None),
            P(None, None, "mlp"),
            P(),
            P(),
            P(),
        ),
        out_specs=(P("seq", None, "mlp"), P("seq", None, "mlp")),
        check_vma=False,
    )
```

time: 212 us -> 103 us (0.49)
  waiting for transfers between devices: 111 us -> 18.5 us
  starting transfers between devices: 3.72 us -> 55.5 us
  blocking collectives: 42.9 us -> 0 us
  matrix products: 23.4 us -> 0 us
  Pallas kernels: 0 us -> 20.5 us
  between operations: 14.2 us -> 1.01 us
  other arithmetic: 6.17 us -> 1.13 us
  local copies, waits for them, and re-layouts: 10.3 us -> 5.89 us
    psum x1 -> x0, waiting for transfers between devices: 70.4 us -> none  [on_device(): lax.psum(head_terms.astype(jnp.bfloat16), 'mlp').astype(jnp.float32)]
    ppermute x0 -> x40, starting transfers between devices: none -> 55.5 us  [swap(): return lax.ppermute(value, axis, [(i, i ^ k) for i in range(size)])]
    all_to_all x1 -> x0, blocking collectives: 42.9 us -> none  [on_device(): lax.all_to_all(turned, 'seq', split_axis=1, concat_axis=0, tiled=True)]
    all_gather x1 -> x0, waiting for transfers between devices: 30.2 us -> none  [on_device(): lax.all_gather(residual, 'mlp', axis=2, tiled=True).reshape(tokens, D)]
    dot_general x6 -> x0, matrix products: 21.8 us -> none  [the longest x1 8.3 us: on_device(): jnp.einsum('td,dch->tch', normed_full, temporal_qkv, preferred_element_ty...]
    pallas_call x0 -> x11, Pallas kernels: none -> 20.5 us  [the longest x2 9.06 us: on_device(): pl.pallas_call(functools.partial(temporal_kernel, frames=n_seq), out_shap...]
    ppermute x0 -> x40, waiting for transfers between devices: none -> 18.5 us  [swap(): return lax.ppermute(value, axis, [(i, i ^ k) for i in range(size)])]
    all_to_all x1 -> x0, waiting for transfers between devices: 9.61 us -> none  [on_device(): lax.all_to_all(blended_head_output, 'seq', split_axis=0, concat_axis=1, t...]
  transfers between devices with their start and end apart: 3 -> 40, of which waited for: 3 -> 8; matrix products, arithmetic and copies ran while one was open for 1% -> 1% of each run, Pallas kernels for 0% -> 19%
where the time goes in v1:
time: 103 us
  starting transfers between devices  55.5 us (54%)
  Pallas kernels  20.5 us (20%)
  waiting for transfers between devices  18.5 us (18%)
  local copies, waits for them, and re-layouts  5.89 us (6%)
  other arithmetic  1.13 us (1%)
    ppermute x40, starting transfers between devices, swap(): return lax.ppermute(value, axis, [(i, i ^ k) for i in range(size)])  55.5 us
    ppermute x40, waiting for transfers between devices, swap(): return lax.ppermute(value, axis, [(i, i ^ k) for i in range(size)])  18.5 us
    pallas_call x2, Pallas kernels, on_device(): pl.pallas_call(functools.partial(temporal_kernel, frames=n_seq), out_shap...  9.06 us
    pallas_call x2, Pallas kernels, on_device(): call(keep_kernel, jax.ShapeDtypeStruct((rows, share), f32), 4 * rows * wi...  3.6 us
    unnamed x44, local copies, waits for them, and re-layouts  3.07 us
    pallas_call x2, Pallas kernels, on_device(): call(send_kernel, jax.ShapeDtypeStruct((rows, share), bf16), 4 * rows * w...  2.97 us
    pallas_call x2, Pallas kernels, on_device(): call(functools.partial(spatial_kernel, first=c * rows), jax.ShapeDtypeStr...  2.81 us
    dynamic_slice x3, local copies, waits for them, and re-layouts, columns(): return lax.dynamic_slice_in_dim(array, block * share, share, 1)  2.69 us
  transfers between devices with their start and end apart: 40, of which 8 were waited for; matrix products, arithmetic and copies ran while one was open for 1% of the time, Pallas kernels for 19%

profile of v1, /device:TPU:0, one launch (start us, length us, event | category | flops | bytes accessed | tf_op | source)
XLA Modules:
  0.0 102.6 jit_solution(3034389012861446606)
XLA Ops:
  0.7 2.7 %constant_dynamic-slice_fusion = (bf16[384,768]{1,0:T(8,128)(2,1)S(1)}, bf16[384,768]{1,0:T(8,128)(2,1)}, bf16[384,768]{1,0:T(8,128)(2,1)S(1)}, bf16[384,768]{1,0:T(8,128)(2,1)S(1)}) fusion(bf16[384,3072]{1,0:T(8,128)(2,1)} %param.9, s32[]{:T(128)S(6)} %select_n.17, s32[]{:T(128)S(6)} %select_n.15, s32[]{:T(128)S(6)} %select_n.14, s32[]{:T(128)S(6)} %select_n.16), kind=kLoop, calls=%fused_computation.23 | loop fusion | bytes 4718608 | tf_op jit(solution)/shard_map/dynamic_slice | solution.py:181
  3.3 0.5 collective-permute-start.2
  3.8 0.1 collective-permute-start.1
  3.9 1.1 %shard_map.86.own_ref = bf16[256,384]{1,0:T(8,128)(2,1)S(1)} custom-call(bf16[3,512,384]{2,1,0:T(8,128)(2,1)S(1)} %bitcast.19), custom_call_target="tpu_custom_call" | custom-call | flops 201326592 | bytes 1179648 | tf_op jit(solution)/shard_map/pallas_call | solution.py:198
  5.0 0.5 collective-permute-start
  5.5 1.7 %shard_map.90.own_ref = bf16[256,384]{1,0:T(8,128)(2,1)} custom-call(bf16[3,512,384]{2,1,0:T(8,128)(2,1)S(1)} %bitcast.20), custom_call_target="tpu_custom_call" | custom-call | flops 201326592 | bytes 1179648 | tf_op jit(solution)/shard_map/pallas_call | solution.py:198
  7.2 0.1 collective-permute-start.4
  7.3 0.1 fusion.1
  7.4 0.0 slice-start
  7.4 1.3 %shard_map.88 = bf16[256,768]{1,0:T(8,128)(2,1)} custom-call(bf16[256,384]{1,0:T(8,128)(2,1)S(1)} %shard_map.86.own_ref, bf16[256,384]{1,0:T(8,128)(2,1)S(1)} %collective-permute-done.other_ref, bf16[384,768]{1,0:T(8,128)(2,1)S(1)} %get-tuple-element.73.own_w_ref, bf16[384,768]{1,0:T(8,128)(2,1)S(1)} %collective-permute-done.2.other_w_ref, ...), custom_call_target="tpu_custom_call" | custom-call | flops 301989888 | bytes 2752512 | tf_op jit(solution)/shard_map/pallas_call | solution.py:206
  8.7 0.8 copy-done.3
  9.5 2.9 %collective-permute-start.3 = (bf16[256,768]{1,0:T(8,128)(2,1)}, bf16[256,768]{1,0:T(8,128)(2,1)}, u32[]{:S(2)}, u32[]{:S(2)}) collective-permute-start(bf16[256,768]{1,0:T(8,128)(2,1)} %shard_map.88), channel_id=1, source_target_pairs={{0,2},{1,3},{2,0},{3,1},{4,6},{5,7},{6,4},{7,5},{8,10},{9,11},{10,... | collective-permute-start | bytes 1179656 | tf_op jit(solution)/shard_map/ppermute | solution.py:154
  12.5 1.1 %copy-done.1 = bf16[384,768]{1,0:T(8,128)(2,1)S(1)} copy-done((bf16[384,768]{1,0:T(8,128)(2,1)S(1)}, bf16[384,768]{1,0:T(8,128)(2,1)}, u32[]{:S(2)}) %copy-start.1) | copy-done | bytes 589848
  13.5 1.1 %copy-done.4 = bf16[384,768]{1,0:T(8,128)(2,1)S(1)} copy-done((bf16[384,768]{1,0:T(8,128)(2,1)S(1)}, bf16[384,768]{1,0:T(8,128)(2,1)}, u32[]{:S(2)}) %copy-start.4) | copy-done | bytes 589848
  14.6 1.7 %shard_map.92 = bf16[256,768]{1,0:T(8,128)(2,1)S(1)} custom-call(bf16[256,384]{1,0:T(8,128)(2,1)} %shard_map.90.own_ref, bf16[256,384]{1,0:T(8,128)(2,1)} %collective-permute-done.4.other_ref, bf16[384,768]{1,0:T(8,128)(2,1)S(1)} %copy-done.1, bf16[384,768]{1,0:T(8,128)(2,1)S(1)} %copy-done.4, f32[1,768]{1,0:T(1,128)S(1)} %dynamic_slice.23.gate_ref), custom_call_target="tpu_custom_call" | custom-call | flops 301989888 | bytes 2752512 | tf_op jit(solution)/shard_map/pallas_call | solution.py:206
  16.3 0.1 collective-permute-start.5
  16.3 0.1 slice_bitcast_fusion.1
  16.4 0.0 slice-start.1
  16.5 2.0 %shard_map.91.base_ref = f32[256,768]{1,0:T(8,128)S(1)} custom-call(bf16[256,384]{1,0:T(8,128)(2,1)} %shard_map.90.own_ref, bf16[256,384]{1,0:T(8,128)(2,1)} %collective-permute-done.4.other_ref, bf16[384,768]{1,0:T(8,128)(2,1)S(1)} %get-tuple-element.72.own_w_ref, bf16[384,768]{1,0:T(8,128)(2,1)} %collective-permute-done.1.other_w_ref, ...), custom_call_target="tpu_custom_call" | custom-call | flops 301989888 | bytes 2752512 | tf_op jit(solution)/shard_map/pallas_call | solution.py:213
  18.4 1.6 %shard_map.87.base_ref = f32[256,768]{1,0:T(8,128)S(1)} custom-call(bf16[256,384]{1,0:T(8,128)(2,1)S(1)} %copy-done.6, bf16[256,384]{1,0:T(8,128)(2,1)S(1)} %copy-done.8, bf16[384,768]{1,0:T(8,128)(2,1)S(1)} %get-tuple-element.72.own_w_ref, bf16[384,768]{1,0:T(8,128)(2,1)} %collective-permute-done.1.other_w_ref, f32[1,768]{1,0:T(1,128)S(1)} %dynamic_slice.20.gate_ref, ...), custom_call_target="tpu_custom_call" | custom-call | flops 301989888 | bytes 2752512 | tf_op jit(solution)/shard_map/pallas_call | solution.py:213
  20.1 2.6 %collective-permute-done.3.arrived_ref = bf16[256,768]{1,0:T(8,128)(2,1)} collective-permute-done((bf16[256,768]{1,0:T(8,128)(2,1)}, bf16[256,768]{1,0:T(8,128)(2,1)}, u32[]{:S(2)}, u32[]{:S(2)}) %collective-permute-start.3) | collective-permute-done | bytes 393248 | tf_op jit(solution)/shard_map/ppermute | solution.py:154
  22.7 1.2 %shard_map.89 = (bf16[256,768]{1,0:T(8,128)(2,1)S(1)}, bf16[32,768]{1,0:T(8,128)(2,1)S(1)}, bf16[32,768]{1,0:T(8,128)(2,1)S(1)}, bf16[32,768]{1,0:T(8,128)(2,1)S...) custom-call(s32[1]{0:T(128)} %bitcast.place_ref, ...), custom_call_target="tpu_custom_call" | custom-call | flops 196608 | bytes 1966080 | tf_op jit(solution)/shard_map/pallas_call | solution.py:220
  23.9 2.1 %collective-permute-start.6 = (bf16[32,768]{1,0:T(8,128)(2,1)S(1)}, bf16[32,768]{1,0:T(8,128)(2,1)S(1)}, u32[]{:S(2)}, u32[]{:S(2)}) collective-permute-start(bf16[32,768]{1,0:T(8,128)(2,1)S(1)} %get-tuple-element.39), channel_id=1, source_target_pairs={{0,4},{4,0},{8,12},{12,8},{16,20},{20,16},{24,28},{28,24},{1,5},{5... | collective-permute-start | bytes 147464 | tf_op jit(solution)/shard_map/ppermute | solution.py:154
  26.0 1.6 %collective-permute-start.7 = (bf16[32,768]{1,0:T(8,128)(2,1)S(1)}, bf16[32,768]{1,0:T(8,128)(2,1)S(1)}, u32[]{:S(2)}, u32[]{:S(2)}) collective-permute-start(bf16[32,768]{1,0:T(8,128)(2,1)S(1)} %get-tuple-element.40), channel_id=1, source_target_pairs={{0,8},{4,12},{8,0},{12,4},{16,24},{20,28},{24,16},{28,20},{1,9},{5... | collective-permute-start | bytes 147464 | tf_op jit(solution)/shard_map/ppermute | solution.py:154
  27.6 3.0 %collective-permute-start.9 = (bf16[32,768]{1,0:T(8,128)(2,1)S(1)}, bf16[32,768]{1,0:T(8,128)(2,1)S(1)}, u32[]{:S(2)}, u32[]{:S(2)}) collective-permute-start(bf16[32,768]{1,0:T(8,128)(2,1)S(1)} %get-tuple-element.42), channel_id=1, source_target_pairs={{0,16},{4,20},{8,24},{12,28},{16,0},{20,4},{24,8},{28,12},{1,17},{... | collective-permute-start | bytes 147464 | tf_op jit(solution)/shard_map/ppermute | solution.py:154
  30.6 3.7 %collective-permute-start.10 = (bf16[32,768]{1,0:T(8,128)(2,1)S(1)}, bf16[32,768]{1,0:T(8,128)(2,1)S(1)}, u32[]{:S(2)}, u32[]{:S(2)}) collective-permute-start(bf16[32,768]{1,0:T(8,128)(2,1)S(1)} %get-tuple-element.43), channel_id=1, source_target_pairs={{0,20},{4,16},{8,28},{12,24},{16,4},{20,0},{24,12},{28,8},{1,21},{... | collective-permute-start | bytes 147464 | tf_op jit(solution)/shard_map/ppermute | solution.py:154
  34.2 0.2 shard_map.93
  34.4 1.4 %collective-permute-start.11 = (bf16[32,768]{1,0:T(8,128)(2,1)S(1)}, bf16[32,768]{1,0:T(8,128)(2,1)S(1)}, u32[]{:S(2)}, u32[]{:S(2)}) collective-permute-start(bf16[32,768]{1,0:T(8,128)(2,1)S(1)} %get-tuple-element.44), channel_id=1, source_target_pairs={{0,24},{4,28},{8,16},{12,20},{16,8},{20,12},{24,0},{28,4},{1,25},{... | collective-permute-start | bytes 147464 | tf_op jit(solution)/shard_map/ppermute | solution.py:154
  35.9 2.5 %collective-permute-start.12 = (bf16[32,768]{1,0:T(8,128)(2,1)S(1)}, bf16[32,768]{1,0:T(8,128)(2,1)S(1)}, u32[]{:S(2)}, u32[]{:S(2)}) collective-permute-start(bf16[32,768]{1,0:T(8,128)(2,1)S(1)} %get-tuple-element.45), channel_id=1, source_target_pairs={{0,28},{4,24},{8,20},{12,16},{16,12},{20,8},{24,4},{28,0},{1,29},{... | collective-permute-start | bytes 147464 | tf_op jit(solution)/shard_map/ppermute | solution.py:154
  38.4 1.6 %collective-permute-start.23 = (bf16[32,768]{1,0:T(8,128)(2,1)S(1)}, bf16[32,768]{1,0:T(8,128)(2,1)S(1)}, u32[]{:S(2)}, u32[]{:S(2)}) collective-permute-start(bf16[32,768]{1,0:T(8,128)(2,1)S(1)} %get-tuple-element.55), channel_id=1, source_target_pairs={{0,4},{4,0},{8,12},{12,8},{16,20},{20,16},{24,28},{28,24},{1,5},{5... | collective-permute-start | bytes 147464 | tf_op jit(solution)/shard_map/ppermute | solution.py:154
  39.9 0.1 collective-permute-start.24
  40.0 2.0 %collective-permute-start.25 = (bf16[32,768]{1,0:T(8,128)(2,1)S(1)}, bf16[32,768]{1,0:T(8,128)(2,1)S(1)}, u32[]{:S(2)}, u32[]{:S(2)}) collective-permute-start(bf16[32,768]{1,0:T(8,128)(2,1)S(1)} %get-tuple-element.57), channel_id=1, source_target_pairs={{0,12},{4,8},{8,4},{12,0},{16,28},{20,24},{24,20},{28,16},{1,13},{... | collective-permute-start | bytes 147464 | tf_op jit(solution)/shard_map/ppermute | solution.py:154
  42.0 2.0 %collective-permute-start.26 = (bf16[32,768]{1,0:T(8,128)(2,1)S(1)}, bf16[32,768]{1,0:T(8,128)(2,1)S(1)}, u32[]{:S(2)}, u32[]{:S(2)}) collective-permute-start(bf16[32,768]{1,0:T(8,128)(2,1)S(1)} %get-tuple-element.58), channel_id=1, source_target_pairs={{0,16},{4,20},{8,24},{12,28},{16,0},{20,4},{24,8},{28,12},{1,17},{... | collective-permute-start | bytes 147464 | tf_op jit(solution)/shard_map/ppermute | solution.py:154
  44.0 2.0 %collective-permute-start.27 = (bf16[32,768]{1,0:T(8,128)(2,1)S(1)}, bf16[32,768]{1,0:T(8,128)(2,1)S(1)}, u32[]{:S(2)}, u32[]{:S(2)}) collective-permute-start(bf16[32,768]{1,0:T(8,128)(2,1)S(1)} %get-tuple-element.59), channel_id=1, source_target_pairs={{0,20},{4,16},{8,28},{12,24},{16,4},{20,0},{24,12},{28,8},{1,21},{... | collective-permute-start | bytes 147464 | tf_op jit(solution)/shard_map/ppermute | solution.py:154
  46.1 1.4 %collective-permute-start.28 = (bf16[32,768]{1,0:T(8,128)(2,1)S(1)}, bf16[32,768]{1,0:T(8,128)(2,1)S(1)}, u32[]{:S(2)}, u32[]{:S(2)}) collective-permute-start(bf16[32,768]{1,0:T(8,128)(2,1)S(1)} %get-tuple-element.60), channel_id=1, source_target_pairs={{0,24},{4,28},{8,16},{12,20},{16,8},{20,12},{24,0},{28,4},{1,25},{... | collective-permute-start | bytes 147464 | tf_op jit(solution)/shard_map/ppermute | solution.py:154
  47.5 2.5 %collective-permute-start.29 = (bf16[32,768]{1,0:T(8,128)(2,1)S(1)}, bf16[32,768]{1,0:T(8,128)(2,1)S(1)}, u32[]{:S(2)}, u32[]{:S(2)}) collective-permute-start(bf16[32,768]{1,0:T(8,128)(2,1)S(1)} %get-tuple-element.61), channel_id=1, source_target_pairs={{0,28},{4,24},{8,20},{12,16},{16,12},{20,8},{24,4},{28,0},{1,29},{... | collective-permute-start | bytes 147464 | tf_op jit(solution)/shard_map/ppermute | solution.py:154
  50.0 1.5 %collective-permute-start.14 = (bf16[256,768]{1,0:T(8,128)(2,1)S(1)}, bf16[256,768]{1,0:T(8,128)(2,1)S(1)}, u32[]{:S(2)}, u32[]{:S(2)}) collective-permute-start(bf16[256,768]{1,0:T(8,128)(2,1)S(1)} %constant_dynamic-update-slice_fusion.u0), channel_id=1, source_target_pairs={{0,2},{1,3},{2,0},{3,1},{4,6},{5,7},{6,4},{7,5},{8,10},{9,11},{10,... | collective-permute-start | bytes 1179656 | tf_op jit(solution)/shard_map/ppermute | solution.py:154
  51.6 0.5 collective-permute-done.28
  52.0 2.3 %collective-permute-done.29 = bf16[32,768]{1,0:T(8,128)(2,1)S(1)} collective-permute-done((bf16[32,768]{1,0:T(8,128)(2,1)S(1)}, bf16[32,768]{1,0:T(8,128)(2,1)S(1)}, u32[]{:S(2)}, u32[]{:S(2)}) %collective-permute-start.29) | collective-permute-done | bytes 49184 | tf_op jit(solution)/shard_map/ppermute | solution.py:154
  54.3 1.5 %collective-permute-start.31 = (bf16[256,768]{1,0:T(8,128)(2,1)S(1)}, bf16[256,768]{1,0:T(8,128)(2,1)S(1)}, u32[]{:S(2)}, u32[]{:S(2)}) collective-permute-start(bf16[256,768]{1,0:T(8,128)(2,1)S(1)} %constant_dynamic-update-slice_fusion.8.u0), channel_id=1, source_target_pairs={{0,2},{1,3},{2,0},{3,1},{4,6},{5,7},{6,4},{7,5},{8,10},{9,11},{10,... | collective-permute-start | bytes 1179656 | tf_op jit(solution)/shard_map/ppermute | solution.py:154
  55.8 5.9 %collective-permute-done.14.u2 = bf16[256,768]{1,0:T(8,128)(2,1)S(1)} collective-permute-done((bf16[256,768]{1,0:T(8,128)(2,1)S(1)}, bf16[256,768]{1,0:T(8,128)(2,1)S(1)}, u32[]{:S(2)}, u32[]{:S(2)}) %collective-permute-start.14) | collective-permute-done | bytes 393248 | tf_op jit(solution)/shard_map/ppermute | solution.py:154
  61.7 0.5 collective-permute-start.30
  62.2 3.7 %collective-permute-done.31.u2 = bf16[256,768]{1,0:T(8,128)(2,1)S(1)} collective-permute-done((bf16[256,768]{1,0:T(8,128)(2,1)S(1)}, bf16[256,768]{1,0:T(8,128)(2,1)S(1)}, u32[]{:S(2)}, u32[]{:S(2)}) %collective-permute-start.31) | collective-permute-done | bytes 393248 | tf_op jit(solution)/shard_map/ppermute | solution.py:154
  65.9 0.1 fusion
  66.0 0.1 pad_maximum_fusion
  66.2 4.4 %shard_map.94 = (bf16[32,384]{1,0:T(8,128)(2,1)S(1)}, bf16[32,384]{1,0:T(8,128)(2,1)S(1)}, bf16[32,384]{1,0:T(8,128)(2,1)S(1)}, bf16[32,384]{1,0:T(8,128)(2,1)S(...) custom-call(s32[1]{0:T(128)} %bitcast.7.place_ref, ...), custom_call_target="tpu_custom_call" | custom-call | flops 1811939328 | bytes 8650752 | tf_op jit(solution)/shard_map/pallas_call | solution.py:247
  70.6 1.5 %collective-permute-start.16 = (bf16[32,384]{1,0:T(8,128)(2,1)S(1)}, bf16[32,384]{1,0:T(8,128)(2,1)S(1)}, u32[]{:S(2)}, u32[]{:S(2)}) collective-permute-start(bf16[32,384]{1,0:T(8,128)(2,1)S(1)} %get-tuple-element.47), channel_id=1, source_target_pairs={{0,4},{4,0},{8,12},{12,8},{16,20},{20,16},{24,28},{28,24},{1,5},{5... | collective-permute-start | bytes 73736 | tf_op jit(solution)/shard_map/ppermute | solution.py:154
  72.2 2.0 %collective-permute-start.18 = (bf16[32,384]{1,0:T(8,128)(2,1)S(1)}, bf16[32,384]{1,0:T(8,128)(2,1)S(1)}, u32[]{:S(2)}, u32[]{:S(2)}) collective-permute-start(bf16[32,384]{1,0:T(8,128)(2,1)S(1)} %get-tuple-element.49), channel_id=1, source_target_pairs={{0,12},{4,8},{8,4},{12,0},{16,28},{20,24},{24,20},{28,16},{1,13},{... | collective-permute-start | bytes 73736 | tf_op jit(solution)/shard_map/ppermute | solution.py:154
  74.2 0.2 collective-permute-start.19
  74.3 3.7 %collective-permute-start.20 = (bf16[32,384]{1,0:T(8,128)(2,1)S(1)}, bf16[32,384]{1,0:T(8,128)(2,1)S(1)}, u32[]{:S(2)}, u32[]{:S(2)}) collective-permute-start(bf16[32,384]{1,0:T(8,128)(2,1)S(1)} %get-tuple-element.51), channel_id=1, source_target_pairs={{0,20},{4,16},{8,28},{12,24},{16,4},{20,0},{24,12},{28,8},{1,21},{... | collective-permute-start | bytes 73736 | tf_op jit(solution)/shard_map/ppermute | solution.py:154
  78.0 4.6 %shard_map.95 = (bf16[32,384]{1,0:T(8,128)(2,1)S(1)}, bf16[32,384]{1,0:T(8,128)(2,1)S(1)}, bf16[32,384]{1,0:T(8,128)(2,1)S(1)}, bf16[32,384]{1,0:T(8,128)(2,1)S(...) custom-call(s32[1]{0:T(128)} %bitcast.7.place_ref, ...), custom_call_target="tpu_custom_call" | custom-call | flops 1811939328 | bytes 8650752 | tf_op jit(solution)/shard_map/pallas_call | solution.py:247
  82.7 1.4 %collective-permute-start.21 = (bf16[32,384]{1,0:T(8,128)(2,1)S(1)}, bf16[32,384]{1,0:T(8,128)(2,1)S(1)}, u32[]{:S(2)}, u32[]{:S(2)}) collective-permute-start(bf16[32,384]{1,0:T(8,128)(2,1)S(1)} %get-tuple-element.52), channel_id=1, source_target_pairs={{0,24},{4,28},{8,16},{12,20},{16,8},{20,12},{24,0},{28,4},{1,25},{... | collective-permute-start | bytes 73736 | tf_op jit(solution)/shard_map/ppermute | solution.py:154
  84.1 2.5 %collective-permute-start.22 = (bf16[32,384]{1,0:T(8,128)(2,1)S(1)}, bf16[32,384]{1,0:T(8,128)(2,1)S(1)}, u32[]{:S(2)}, u32[]{:S(2)}) collective-permute-start(bf16[32,384]{1,0:T(8,128)(2,1)S(1)} %get-tuple-element.53), channel_id=1, source_target_pairs={{0,28},{4,24},{8,20},{12,16},{16,12},{20,8},{24,4},{28,0},{1,29},{... | collective-permute-start | bytes 73736 | tf_op jit(solution)/shard_map/ppermute | solution.py:154
  86.5 1.5 %collective-permute-start.33 = (bf16[32,384]{1,0:T(8,128)(2,1)S(1)}, bf16[32,384]{1,0:T(8,128)(2,1)S(1)}, u32[]{:S(2)}, u32[]{:S(2)}) collective-permute-start(bf16[32,384]{1,0:T(8,128)(2,1)S(1)} %get-tuple-element.63), channel_id=1, source_target_pairs={{0,4},{4,0},{8,12},{12,8},{16,20},{20,16},{24,28},{28,24},{1,5},{5... | collective-permute-start | bytes 73736 | tf_op jit(solution)/shard_map/ppermute | solution.py:154
  88.0 2.0 %collective-permute-start.35 = (bf16[32,384]{1,0:T(8,128)(2,1)S(1)}, bf16[32,384]{1,0:T(8,128)(2,1)S(1)}, u32[]{:S(2)}, u32[]{:S(2)}) collective-permute-start(bf16[32,384]{1,0:T(8,128)(2,1)S(1)} %get-tuple-element.65), channel_id=1, source_target_pairs={{0,12},{4,8},{8,4},{12,0},{16,28},{20,24},{24,20},{28,16},{1,13},{... | collective-permute-start | bytes 73736 | tf_op jit(solution)/shard_map/ppermute | solution.py:154
  90.0 0.2 collective-permute-start.36
  90.3 0.4 collective-permute-done.22.rest_7_
  90.6 3.2 %collective-permute-start.37 = (bf16[32,384]{1,0:T(8,128)(2,1)S(1)}, bf16[32,384]{1,0:T(8,128)(2,1)S(1)}, u32[]{:S(2)}, u32[]{:S(2)}) collective-permute-start(bf16[32,384]{1,0:T(8,128)(2,1)S(1)} %get-tuple-element.67), channel_id=1, source_target_pairs={{0,20},{4,16},{8,28},{12,24},{16,4},{20,0},{24,12},{28,8},{1,21},{... | collective-permute-start | bytes 73736 | tf_op jit(solution)/shard_map/ppermute | solution.py:154
  93.9 1.4 %collective-permute-start.38 = (bf16[32,384]{1,0:T(8,128)(2,1)S(1)}, bf16[32,384]{1,0:T(8,128)(2,1)S(1)}, u32[]{:S(2)}, u32[]{:S(2)}) collective-permute-start(bf16[32,384]{1,0:T(8,128)(2,1)S(1)} %get-tuple-element.68), channel_id=1, source_target_pairs={{0,24},{4,28},{8,16},{12,20},{16,8},{20,12},{24,0},{28,4},{1,25},{... | collective-permute-start | bytes 73736 | tf_op jit(solution)/shard_map/ppermute | solution.py:154
  95.3 2.5 %collective-permute-start.39 = (bf16[32,384]{1,0:T(8,128)(2,1)S(1)}, bf16[32,384]{1,0:T(8,128)(2,1)S(1)}, u32[]{:S(2)}, u32[]{:S(2)}) collective-permute-start(bf16[32,384]{1,0:T(8,128)(2,1)S(1)} %get-tuple-element.69), channel_id=1, source_target_pairs={{0,28},{4,24},{8,20},{12,16},{16,12},{20,8},{24,4},{28,0},{1,29},{... | collective-permute-start | bytes 73736 | tf_op jit(solution)/shard_map/ppermute | solution.py:154
  97.7 0.9 maximum_bitcast_fusion
  98.7 0.9 collective-permute-done.38.rest_14_
  99.5 2.3 %collective-permute-done.39.rest_15_ = bf16[32,384]{1,0:T(8,128)(2,1)S(1)} collective-permute-done((bf16[32,384]{1,0:T(8,128)(2,1)S(1)}, bf16[32,384]{1,0:T(8,128)(2,1)S(1)}, u32[]{:S(2)}, u32[]{:S(2)}) %collective-permute-start.39) | collective-permute-done | bytes 24608 | tf_op jit(solution)/shard_map/ppermute | solution.py:154
  101.8 0.8 shard_map.96
  (84 shorter events, 0.2 us)
Async XLA Ops:
  0.7 3.2 %copy-start.2 = (bf16[1,512,3,384]{3,1,2,0:T(8,128)(2,1)S(1)}, bf16[1,512,3,384]{3,1,2,0:T(8,128)(2,1)}, u32[]{:S(2)}) copy-start(bf16[1,512,3,384]{3,1,2,0:T(8,128)(2,1)} %param.8) | copy-start | bytes 3538948
  3.3 5.4 %copy-start = (bf16[384,768]{1,0:T(8,128)(2,1)}, bf16[384,768]{1,0:T(8,128)(2,1)S(1)}, u32[]{:S(2)}) copy-start(bf16[384,768]{1,0:T(8,128)(2,1)S(1)} %get-tuple-element.73.own_w_ref) | copy-start | bytes 1769476
  3.3 3.9 %copy-start.12 = (f32[3072]{0:T(1024)S(1)}, f32[3072]{0:T(1024)}, u32[]{:S(2)}) copy-start(f32[3072]{0:T(1024)} %param.13) | copy-start | bytes 36868
  3.3 4.0 %collective-permute-start.2 = (bf16[384,768]{1,0:T(8,128)(2,1)S(1)}, bf16[384,768]{1,0:T(8,128)(2,1)S(1)}, u32[]{:S(2)}, u32[]{:S(2)}) collective-permute-start(bf16[384,768]{1,0:T(8,128)(2,1)S(1)} %get-tuple-element.70), channel_id=1, source_target_pairs={{0,1},{1,0},{2,3},{3,2},{4,5},{5,4},{6,7},{7,6},{8,9},{9,8},{10,11... | collective-permute-start | bytes 1769480 | tf_op jit(solution)/shard_map/ppermute | solution.py:154
  3.8 12.6 %collective-permute-start.1 = (bf16[384,768]{1,0:T(8,128)(2,1)}, bf16[384,768]{1,0:T(8,128)(2,1)}, u32[]{:S(2)}, u32[]{:S(2)}) collective-permute-start(bf16[384,768]{1,0:T(8,128)(2,1)} %get-tuple-element.71), channel_id=1, source_target_pairs={{0,1},{1,0},{2,3},{3,2},{4,5},{5,4},{6,7},{7,6},{8,9},{9,8},{10,11... | collective-permute-start | bytes 1769480 | tf_op jit(solution)/shard_map/ppermute | solution.py:154
  5.0 3.8 %copy-start.5 = (bf16[256,384]{1,0:T(8,128)(2,1)}, bf16[256,384]{1,0:T(8,128)(2,1)S(1)}, u32[]{:S(2)}) copy-start(bf16[256,384]{1,0:T(8,128)(2,1)S(1)} %shard_map.86.own_ref) | copy-start | bytes 589828
  5.0 2.4 %collective-permute-start = (bf16[256,384]{1,0:T(8,128)(2,1)S(1)}, bf16[256,384]{1,0:T(8,128)(2,1)S(1)}, u32[]{:S(2)}, u32[]{:S(2)}) collective-permute-start(bf16[256,384]{1,0:T(8,128)(2,1)S(1)} %shard_map.86.own_ref), channel_id=1, source_target_pairs={{0,1},{1,0},{2,3},{3,2},{4,5},{5,4},{6,7},{7,6},{8,9},{9,8},{10,11... | collective-permute-start | bytes 589832 | tf_op jit(solution)/shard_map/ppermute | solution.py:154
  7.2 5.3 %collective-permute-start.4 = (bf16[256,384]{1,0:T(8,128)(2,1)}, bf16[256,384]{1,0:T(8,128)(2,1)}, u32[]{:S(2)}, u32[]{:S(2)}) collective-permute-start(bf16[256,384]{1,0:T(8,128)(2,1)} %shard_map.90.own_ref), channel_id=1, source_target_pairs={{0,1},{1,0},{2,3},{3,2},{4,5},{5,4},{6,7},{7,6},{8,9},{9,8},{10,11... | collective-permute-start | bytes 589832 | tf_op jit(solution)/shard_map/ppermute | solution.py:154
  7.4 1.4 %copy-start.7 = (bf16[256,384]{1,0:T(8,128)(2,1)}, bf16[256,384]{1,0:T(8,128)(2,1)S(1)}, u32[]{:S(2)}) copy-start(bf16[256,384]{1,0:T(8,128)(2,1)S(1)} %collective-permute-done.other_ref) | copy-start | bytes 589828
  7.4 58.8 %slice-start = ((s8[7077888]{0:T(1024)(128)(4,1)}), s8[2883584]{0:T(1024)(128)(4,1)S(1)}, s32[]{:S(2)}) async-start(s8[7077888]{0:T(1024)(128)(4,1)} %bitcast.15), calls=%async_computation | async-start | bytes 5767168
  8.7 0.8 copy-start.3
  9.5 13.1 %collective-permute-start.3 = (bf16[256,768]{1,0:T(8,128)(2,1)}, bf16[256,768]{1,0:T(8,128)(2,1)}, u32[]{:S(2)}, u32[]{:S(2)}) collective-permute-start(bf16[256,768]{1,0:T(8,128)(2,1)} %shard_map.88), channel_id=1, source_target_pairs={{0,2},{1,3},{2,0},{3,1},{4,6},{5,7},{6,4},{7,5},{8,10},{9,11},{10,... | collective-permute-start | bytes 1179656 | tf_op jit(solution)/shard_map/ppermute | solution.py:154
  12.5 1.1 %copy-start.1 = (bf16[384,768]{1,0:T(8,128)(2,1)S(1)}, bf16[384,768]{1,0:T(8,128)(2,1)}, u32[]{:S(2)}) copy-start(bf16[384,768]{1,0:T(8,128)(2,1)} %copy-done) | copy-start | bytes 1769476
  13.5 1.1 %copy-start.4 = (bf16[384,768]{1,0:T(8,128)(2,1)S(1)}, bf16[384,768]{1,0:T(8,128)(2,1)}, u32[]{:S(2)}) copy-start(bf16[384,768]{1,0:T(8,128)(2,1)} %copy-done.3) | copy-start | bytes 1769476
  14.6 1.7 %copy-start.11 = (bf16[1,512,768]{2,1,0:T(8,128)(2,1)S(1)}, bf16[1,512,768]{2,1,0:T(8,128)(2,1)}, u32[]{:S(2)}) copy-start(bf16[1,512,768]{2,1,0:T(8,128)(2,1)} %param.7) | copy-start | bytes 2359300
  16.3 14.3 %collective-permute-start.5 = (bf16[256,768]{1,0:T(8,128)(2,1)S(1)}, bf16[256,768]{1,0:T(8,128)(2,1)S(1)}, u32[]{:S(2)}, u32[]{:S(2)}) collective-permute-start(bf16[256,768]{1,0:T(8,128)(2,1)S(1)} %shard_map.92), channel_id=1, source_target_pairs={{0,2},{1,3},{2,0},{3,1},{4,6},{5,7},{6,4},{7,5},{8,10},{9,11},{10,... | collective-permute-start | bytes 1179656 | tf_op jit(solution)/shard_map/ppermute | solution.py:154
  16.4 2.0 %copy-start.6 = (bf16[256,384]{1,0:T(8,128)(2,1)S(1)}, bf16[256,384]{1,0:T(8,128)(2,1)}, u32[]{:S(2)}) copy-start(bf16[256,384]{1,0:T(8,128)(2,1)} %copy-done.5) | copy-start | bytes 589828
  16.4 2.0 %copy-start.8 = (bf16[256,384]{1,0:T(8,128)(2,1)S(1)}, bf16[256,384]{1,0:T(8,128)(2,1)}, u32[]{:S(2)}) copy-start(bf16[256,384]{1,0:T(8,128)(2,1)} %copy-done.7) | copy-start | bytes 589828
  16.4 49.7 %slice-start.1 = ((s8[7077888]{0:T(1024)(128)(4,1)}), s8[4194304]{0:T(1024)(128)(4,1)S(1)}, s32[]{:S(2)}) async-start(s8[7077888]{0:T(1024)(128)(4,1)} %bitcast.15), calls=%async_computation.1 | async-start | bytes 8388608
  23.8 42.3 %copy-start.9 = (f32[3072]{0:T(1024)S(1)}, f32[3072]{0:T(1024)}, u32[]{:S(2)}) copy-start(f32[3072]{0:T(1024)} %param.12) | copy-start | bytes 36868
  23.9 42.3 %copy-start.10 = (f32[3072]{0:T(1024)S(1)}, f32[3072]{0:T(1024)}, u32[]{:S(2)}) copy-start(f32[3072]{0:T(1024)} %param.11) | copy-start | bytes 36868
  23.9 10.6 %collective-permute-start.6 = (bf16[32,768]{1,0:T(8,128)(2,1)S(1)}, bf16[32,768]{1,0:T(8,128)(2,1)S(1)}, u32[]{:S(2)}, u32[]{:S(2)}) collective-permute-start(bf16[32,768]{1,0:T(8,128)(2,1)S(1)} %get-tuple-element.39), channel_id=1, source_target_pairs={{0,4},{4,0},{8,12},{12,8},{16,20},{20,16},{24,28},{28,24},{1,5},{5... | collective-permute-start | bytes 147464 | tf_op jit(solution)/shard_map/ppermute | solution.py:154
  26.0 9.8 %collective-permute-start.7 = (bf16[32,768]{1,0:T(8,128)(2,1)S(1)}, bf16[32,768]{1,0:T(8,128)(2,1)S(1)}, u32[]{:S(2)}, u32[]{:S(2)}) collective-permute-start(bf16[32,768]{1,0:T(8,128)(2,1)S(1)} %get-tuple-element.40), channel_id=1, source_target_pairs={{0,8},{4,12},{8,0},{12,4},{16,24},{20,28},{24,16},{28,20},{1,9},{5... | collective-permute-start | bytes 147464 | tf_op jit(solution)/shard_map/ppermute | solution.py:154
  27.6 10.7 %collective-permute-start.8 = (bf16[32,768]{1,0:T(8,128)(2,1)S(1)}, bf16[32,768]{1,0:T(8,128)(2,1)S(1)}, u32[]{:S(2)}, u32[]{:S(2)}) collective-permute-start(bf16[32,768]{1,0:T(8,128)(2,1)S(1)} %get-tuple-element.41), channel_id=1, source_target_pairs={{0,12},{4,8},{8,4},{12,0},{16,28},{20,24},{24,20},{28,16},{1,13},{... | collective-permute-start | bytes 147464 | tf_op jit(solution)/shard_map/ppermute | solution.py:154
  27.6 12.3 %collective-permute-start.9 = (bf16[32,768]{1,0:T(8,128)(2,1)S(1)}, bf16[32,768]{1,0:T(8,128)(2,1)S(1)}, u32[]{:S(2)}, u32[]{:S(2)}) collective-permute-start(bf16[32,768]{1,0:T(8,128)(2,1)S(1)} %get-tuple-element.42), channel_id=1, source_target_pairs={{0,16},{4,20},{8,24},{12,28},{16,0},{20,4},{24,8},{28,12},{1,17},{... | collective-permute-start | bytes 147464 | tf_op jit(solution)/shard_map/ppermute | solution.py:154
  30.6 9.4 %collective-permute-start.10 = (bf16[32,768]{1,0:T(8,128)(2,1)S(1)}, bf16[32,768]{1,0:T(8,128)(2,1)S(1)}, u32[]{:S(2)}, u32[]{:S(2)}) collective-permute-start(bf16[32,768]{1,0:T(8,128)(2,1)S(1)} %get-tuple-element.43), channel_id=1, source_target_pairs={{0,20},{4,16},{8,28},{12,24},{16,4},{20,0},{24,12},{28,8},{1,21},{... | collective-permute-start | bytes 147464 | tf_op jit(solution)/shard_map/ppermute | solution.py:154
  34.4 7.6 %collective-permute-start.11 = (bf16[32,768]{1,0:T(8,128)(2,1)S(1)}, bf16[32,768]{1,0:T(8,128)(2,1)S(1)}, u32[]{:S(2)}, u32[]{:S(2)}) collective-permute-start(bf16[32,768]{1,0:T(8,128)(2,1)S(1)} %get-tuple-element.44), channel_id=1, source_target_pairs={{0,24},{4,28},{8,16},{12,20},{16,8},{20,12},{24,0},{28,4},{1,25},{... | collective-permute-start | bytes 147464 | tf_op jit(solution)/shard_map/ppermute | solution.py:154
  35.9 8.2 %collective-permute-start.12 = (bf16[32,768]{1,0:T(8,128)(2,1)S(1)}, bf16[32,768]{1,0:T(8,128)(2,1)S(1)}, u32[]{:S(2)}, u32[]{:S(2)}) collective-permute-start(bf16[32,768]{1,0:T(8,128)(2,1)S(1)} %get-tuple-element.45), channel_id=1, source_target_pairs={{0,28},{4,24},{8,20},{12,16},{16,12},{20,8},{24,4},{28,0},{1,29},{... | collective-permute-start | bytes 147464 | tf_op jit(solution)/shard_map/ppermute | solution.py:154
  38.4 7.7 %collective-permute-start.23 = (bf16[32,768]{1,0:T(8,128)(2,1)S(1)}, bf16[32,768]{1,0:T(8,128)(2,1)S(1)}, u32[]{:S(2)}, u32[]{:S(2)}) collective-permute-start(bf16[32,768]{1,0:T(8,128)(2,1)S(1)} %get-tuple-element.55), channel_id=1, source_target_pairs={{0,4},{4,0},{8,12},{12,8},{16,20},{20,16},{24,28},{28,24},{1,5},{5... | collective-permute-start | bytes 147464 | tf_op jit(solution)/shard_map/ppermute | solution.py:154
  39.9 7.5 %collective-permute-start.24 = (bf16[32,768]{1,0:T(8,128)(2,1)S(1)}, bf16[32,768]{1,0:T(8,128)(2,1)S(1)}, u32[]{:S(2)}, u32[]{:S(2)}) collective-permute-start(bf16[32,768]{1,0:T(8,128)(2,1)S(1)} %get-tuple-element.56), channel_id=1, source_target_pairs={{0,8},{4,12},{8,0},{12,4},{16,24},{20,28},{24,16},{28,20},{1,9},{5... | collective-permute-start | bytes 147464 | tf_op jit(solution)/shard_map/ppermute | solution.py:154
  40.0 9.9 %collective-permute-start.25 = (bf16[32,768]{1,0:T(8,128)(2,1)S(1)}, bf16[32,768]{1,0:T(8,128)(2,1)S(1)}, u32[]{:S(2)}, u32[]{:S(2)}) collective-permute-start(bf16[32,768]{1,0:T(8,128)(2,1)S(1)} %get-tuple-element.57), channel_id=1, source_target_pairs={{0,12},{4,8},{8,4},{12,0},{16,28},{20,24},{24,20},{28,16},{1,13},{... | collective-permute-start | bytes 147464 | tf_op jit(solution)/shard_map/ppermute | solution.py:154
  42.0 9.5 %collective-permute-start.26 = (bf16[32,768]{1,0:T(8,128)(2,1)S(1)}, bf16[32,768]{1,0:T(8,128)(2,1)S(1)}, u32[]{:S(2)}, u32[]{:S(2)}) collective-permute-start(bf16[32,768]{1,0:T(8,128)(2,1)S(1)} %get-tuple-element.58), channel_id=1, source_target_pairs={{0,16},{4,20},{8,24},{12,28},{16,0},{20,4},{24,8},{28,12},{1,17},{... | collective-permute-start | bytes 147464 | tf_op jit(solution)/shard_map/ppermute | solution.py:154
  44.0 7.5 %collective-permute-start.27 = (bf16[32,768]{1,0:T(8,128)(2,1)S(1)}, bf16[32,768]{1,0:T(8,128)(2,1)S(1)}, u32[]{:S(2)}, u32[]{:S(2)}) collective-permute-start(bf16[32,768]{1,0:T(8,128)(2,1)S(1)} %get-tuple-element.59), channel_id=1, source_target_pairs={{0,20},{4,16},{8,28},{12,24},{16,4},{20,0},{24,12},{28,8},{1,21},{... | collective-permute-start | bytes 147464 | tf_op jit(solution)/shard_map/ppermute | solution.py:154
  46.1 6.0 %collective-permute-start.28 = (bf16[32,768]{1,0:T(8,128)(2,1)S(1)}, bf16[32,768]{1,0:T(8,128)(2,1)S(1)}, u32[]{:S(2)}, u32[]{:S(2)}) collective-permute-start(bf16[32,768]{1,0:T(8,128)(2,1)S(1)} %get-tuple-element.60), channel_id=1, source_target_pairs={{0,24},{4,28},{8,16},{12,20},{16,8},{20,12},{24,0},{28,4},{1,25},{... | collective-permute-start | bytes 147464 | tf_op jit(solution)/shard_map/ppermute | solution.py:154
  47.5 6.8 %collective-permute-start.29 = (bf16[32,768]{1,0:T(8,128)(2,1)S(1)}, bf16[32,768]{1,0:T(8,128)(2,1)S(1)}, u32[]{:S(2)}, u32[]{:S(2)}) collective-permute-start(bf16[32,768]{1,0:T(8,128)(2,1)S(1)} %get-tuple-element.61), channel_id=1, source_target_pairs={{0,28},{4,24},{8,20},{12,16},{16,12},{20,8},{24,4},{28,0},{1,29},{... | collective-permute-start | bytes 147464 | tf_op jit(solution)/shard_map/ppermute | solution.py:154
  50.0 11.8 %collective-permute-start.14 = (bf16[256,768]{1,0:T(8,128)(2,1)S(1)}, bf16[256,768]{1,0:T(8,128)(2,1)S(1)}, u32[]{:S(2)}, u32[]{:S(2)}) collective-permute-start(bf16[256,768]{1,0:T(8,128)(2,1)S(1)} %constant_dynamic-update-slice_fusion.u0), channel_id=1, source_target_pairs={{0,2},{1,3},{2,0},{3,1},{4,6},{5,7},{6,4},{7,5},{8,10},{9,11},{10,... | collective-permute-start | bytes 1179656 | tf_op jit(solution)/shard_map/ppermute | solution.py:154
  54.3 11.6 %collective-permute-start.31 = (bf16[256,768]{1,0:T(8,128)(2,1)S(1)}, bf16[256,768]{1,0:T(8,128)(2,1)S(1)}, u32[]{:S(2)}, u32[]{:S(2)}) collective-permute-start(bf16[256,768]{1,0:T(8,128)(2,1)S(1)} %constant_dynamic-update-slice_fusion.8.u0), channel_id=1, source_target_pairs={{0,2},{1,3},{2,0},{3,1},{4,6},{5,7},{6,4},{7,5},{8,10},{9,11},{10,... | collective-permute-start | bytes 1179656 | tf_op jit(solution)/shard_map/ppermute | solution.py:154
  55.8 10.3 %collective-permute-start.13 = (bf16[256,768]{1,0:T(8,128)(2,1)S(1)}, bf16[256,768]{1,0:T(8,128)(2,1)S(1)}, u32[]{:S(2)}, u32[]{:S(2)}) collective-permute-start(bf16[256,768]{1,0:T(8,128)(2,1)S(1)} %constant_dynamic-update-slice_fusion.u0), channel_id=1, source_target_pairs={{0,1},{1,0},{2,3},{3,2},{4,5},{5,4},{6,7},{7,6},{8,9},{9,8},{10,11... | collective-permute-start | bytes 1179656 | tf_op jit(solution)/shard_map/ppermute | solution.py:154
  61.7 4.4 %collective-permute-start.15 = (bf16[256,768]{1,0:T(8,128)(2,1)S(1)}, bf16[256,768]{1,0:T(8,128)(2,1)S(1)}, u32[]{:S(2)}, u32[]{:S(2)}) collective-permute-start(bf16[256,768]{1,0:T(8,128)(2,1)S(1)} %collective-permute-done.14.u2), channel_id=1, source_target_pairs={{0,1},{1,0},{2,3},{3,2},{4,5},{5,4},{6,7},{7,6},{8,9},{9,8},{10,11... | collective-permute-start | bytes 1179656 | tf_op jit(solution)/shard_map/ppermute | solution.py:154
  61.7 12.4 %collective-permute-start.30 = (bf16[256,768]{1,0:T(8,128)(2,1)S(1)}, bf16[256,768]{1,0:T(8,128)(2,1)S(1)}, u32[]{:S(2)}, u32[]{:S(2)}) collective-permute-start(bf16[256,768]{1,0:T(8,128)(2,1)S(1)} %constant_dynamic-update-slice_fusion.8.u0), channel_id=1, source_target_pairs={{0,1},{1,0},{2,3},{3,2},{4,5},{5,4},{6,7},{7,6},{8,9},{9,8},{10,11... | collective-permute-start | bytes 1179656 | tf_op jit(solution)/shard_map/ppermute | solution.py:154
  65.9 8.4 %collective-permute-start.32 = (bf16[256,768]{1,0:T(8,128)(2,1)S(1)}, bf16[256,768]{1,0:T(8,128)(2,1)S(1)}, u32[]{:S(2)}, u32[]{:S(2)}) collective-permute-start(bf16[256,768]{1,0:T(8,128)(2,1)S(1)} %collective-permute-done.31.u2), channel_id=1, source_target_pairs={{0,1},{1,0},{2,3},{3,2},{4,5},{5,4},{6,7},{7,6},{8,9},{9,8},{10,11... | collective-permute-start | bytes 1179656 | tf_op jit(solution)/shard_map/ppermute | solution.py:154
  70.6 12.0 %collective-permute-start.16 = (bf16[32,384]{1,0:T(8,128)(2,1)S(1)}, bf16[32,384]{1,0:T(8,128)(2,1)S(1)}, u32[]{:S(2)}, u32[]{:S(2)}) collective-permute-start(bf16[32,384]{1,0:T(8,128)(2,1)S(1)} %get-tuple-element.47), channel_id=1, source_target_pairs={{0,4},{4,0},{8,12},{12,8},{16,20},{20,16},{24,28},{28,24},{1,5},{5... | collective-permute-start | bytes 73736 | tf_op jit(solution)/shard_map/ppermute | solution.py:154
  72.2 11.9 %collective-permute-start.17 = (bf16[32,384]{1,0:T(8,128)(2,1)S(1)}, bf16[32,384]{1,0:T(8,128)(2,1)S(1)}, u32[]{:S(2)}, u32[]{:S(2)}) collective-permute-start(bf16[32,384]{1,0:T(8,128)(2,1)S(1)} %get-tuple-element.48), channel_id=1, source_target_pairs={{0,8},{4,12},{8,0},{12,4},{16,24},{20,28},{24,16},{28,20},{1,9},{5... | collective-permute-start | bytes 73736 | tf_op jit(solution)/shard_map/ppermute | solution.py:154
  72.2 14.4 %collective-permute-start.18 = (bf16[32,384]{1,0:T(8,128)(2,1)S(1)}, bf16[32,384]{1,0:T(8,128)(2,1)S(1)}, u32[]{:S(2)}, u32[]{:S(2)}) collective-permute-start(bf16[32,384]{1,0:T(8,128)(2,1)S(1)} %get-tuple-element.49), channel_id=1, source_target_pairs={{0,12},{4,8},{8,4},{12,0},{16,28},{20,24},{24,20},{28,16},{1,13},{... | collective-permute-start | bytes 73736 | tf_op jit(solution)/shard_map/ppermute | solution.py:154
  74.2 13.8 %collective-permute-start.19 = (bf16[32,384]{1,0:T(8,128)(2,1)S(1)}, bf16[32,384]{1,0:T(8,128)(2,1)S(1)}, u32[]{:S(2)}, u32[]{:S(2)}) collective-permute-start(bf16[32,384]{1,0:T(8,128)(2,1)S(1)} %get-tuple-element.50), channel_id=1, source_target_pairs={{0,16},{4,20},{8,24},{12,28},{16,0},{20,4},{24,8},{28,12},{1,17},{... | collective-permute-start | bytes 73736 | tf_op jit(solution)/shard_map/ppermute | solution.py:154
  74.3 13.7 %collective-permute-start.20 = (bf16[32,384]{1,0:T(8,128)(2,1)S(1)}, bf16[32,384]{1,0:T(8,128)(2,1)S(1)}, u32[]{:S(2)}, u32[]{:S(2)}) collective-permute-start(bf16[32,384]{1,0:T(8,128)(2,1)S(1)} %get-tuple-element.51), channel_id=1, source_target_pairs={{0,20},{4,16},{8,28},{12,24},{16,4},{20,0},{24,12},{28,8},{1,21},{... | collective-permute-start | bytes 73736 | tf_op jit(solution)/shard_map/ppermute | solution.py:154
  82.7 7.4 %collective-permute-start.21 = (bf16[32,384]{1,0:T(8,128)(2,1)S(1)}, bf16[32,384]{1,0:T(8,128)(2,1)S(1)}, u32[]{:S(2)}, u32[]{:S(2)}) collective-permute-start(bf16[32,384]{1,0:T(8,128)(2,1)S(1)} %get-tuple-element.52), channel_id=1, source_target_pairs={{0,24},{4,28},{8,16},{12,20},{16,8},{20,12},{24,0},{28,4},{1,25},{... | collective-permute-start | bytes 73736 | tf_op jit(solution)/shard_map/ppermute | solution.py:154
  84.1 6.6 %collective-permute-start.22 = (bf16[32,384]{1,0:T(8,128)(2,1)S(1)}, bf16[32,384]{1,0:T(8,128)(2,1)S(1)}, u32[]{:S(2)}, u32[]{:S(2)}) collective-permute-start(bf16[32,384]{1,0:T(8,128)(2,1)S(1)} %get-tuple-element.53), channel_id=1, source_target_pairs={{0,28},{4,24},{8,20},{12,16},{16,12},{20,8},{24,4},{28,0},{1,29},{... | collective-permute-start | bytes 73736 | tf_op jit(solution)/shard_map/ppermute | solution.py:154
  86.5 7.3 %collective-permute-start.33 = (bf16[32,384]{1,0:T(8,128)(2,1)S(1)}, bf16[32,384]{1,0:T(8,128)(2,1)S(1)}, u32[]{:S(2)}, u32[]{:S(2)}) collective-permute-start(bf16[32,384]{1,0:T(8,128)(2,1)S(1)} %get-tuple-element.63), channel_id=1, source_target_pairs={{0,4},{4,0},{8,12},{12,8},{16,20},{20,16},{24,28},{28,24},{1,5},{5... | collective-permute-start | bytes 73736 | tf_op jit(solution)/shard_map/ppermute | solution.py:154
  88.0 7.2 %collective-permute-start.34 = (bf16[32,384]{1,0:T(8,128)(2,1)S(1)}, bf16[32,384]{1,0:T(8,128)(2,1)S(1)}, u32[]{:S(2)}, u32[]{:S(2)}) collective-permute-start(bf16[32,384]{1,0:T(8,128)(2,1)S(1)} %get-tuple-element.64), channel_id=1, source_target_pairs={{0,8},{4,12},{8,0},{12,4},{16,24},{20,28},{24,16},{28,20},{1,9},{5... | collective-permute-start | bytes 73736 | tf_op jit(solution)/shard_map/ppermute | solution.py:154
  88.0 10.6 %collective-permute-start.35 = (bf16[32,384]{1,0:T(8,128)(2,1)S(1)}, bf16[32,384]{1,0:T(8,128)(2,1)S(1)}, u32[]{:S(2)}, u32[]{:S(2)}) collective-permute-start(bf16[32,384]{1,0:T(8,128)(2,1)S(1)} %get-tuple-element.65), channel_id=1, source_target_pairs={{0,12},{4,8},{8,4},{12,0},{16,28},{20,24},{24,20},{28,16},{1,13},{... | collective-permute-start | bytes 73736 | tf_op jit(solution)/shard_map/ppermute | solution.py:154
  90.0 8.6 %collective-permute-start.36 = (bf16[32,384]{1,0:T(8,128)(2,1)S(1)}, bf16[32,384]{1,0:T(8,128)(2,1)S(1)}, u32[]{:S(2)}, u32[]{:S(2)}) collective-permute-start(bf16[32,384]{1,0:T(8,128)(2,1)S(1)} %get-tuple-element.66), channel_id=1, source_target_pairs={{0,16},{4,20},{8,24},{12,28},{16,0},{20,4},{24,8},{28,12},{1,17},{... | collective-permute-start | bytes 73736 | tf_op jit(solution)/shard_map/ppermute | solution.py:154
  90.6 8.0 %collective-permute-start.37 = (bf16[32,384]{1,0:T(8,128)(2,1)S(1)}, bf16[32,384]{1,0:T(8,128)(2,1)S(1)}, u32[]{:S(2)}, u32[]{:S(2)}) collective-permute-start(bf16[32,384]{1,0:T(8,128)(2,1)S(1)} %get-tuple-element.67), channel_id=1, source_target_pairs={{0,20},{4,16},{8,28},{12,24},{16,4},{20,0},{24,12},{28,8},{1,21},{... | collective-permute-start | bytes 73736 | tf_op jit(solution)/shard_map/ppermute | solution.py:154
  93.9 5.6 %collective-permute-start.38 = (bf16[32,384]{1,0:T(8,128)(2,1)S(1)}, bf16[32,384]{1,0:T(8,128)(2,1)S(1)}, u32[]{:S(2)}, u32[]{:S(2)}) collective-permute-start(bf16[32,384]{1,0:T(8,128)(2,1)S(1)} %get-tuple-element.68), channel_id=1, source_target_pairs={{0,24},{4,28},{8,16},{12,20},{16,8},{20,12},{24,0},{28,4},{1,25},{... | collective-permute-start | bytes 73736 | tf_op jit(solution)/shard_map/ppermute | solution.py:154
  95.3 6.5 %collective-permute-start.39 = (bf16[32,384]{1,0:T(8,128)(2,1)S(1)}, bf16[32,384]{1,0:T(8,128)(2,1)S(1)}, u32[]{:S(2)}, u32[]{:S(2)}) collective-permute-start(bf16[32,384]{1,0:T(8,128)(2,1)S(1)} %get-tuple-element.69), channel_id=1, source_target_pairs={{0,28},{4,24},{8,20},{12,16},{16,12},{20,8},{24,4},{28,0},{1,29},{... | collective-permute-start | bytes 73736 | tf_op jit(solution)/shard_map/ppermute | solution.py:154

commit v2 on v1

--- a/solution.py
+++ b/solution.py
@@ -65,18 +65,10 @@
     out_ref[...] = residual_ref[...].astype(jnp.float32) + term * gate_ref[...]
 
 
-def update_kernel(place_ref, base_ref, arrived_ref, whole_ref, *piece_refs):
-    whole_ref[...] = (base_ref[...] + arrived_ref[...].astype(jnp.float32)).astype(whole_ref.dtype)
-    count = piece_refs[0].shape[0]
-    for k, piece_ref in enumerate(piece_refs):
-        start = pl.multiple_of((place_ref[0] ^ k) * count, count)
-        piece_ref[...] = whole_ref[pl.ds(start, count), :]
-
-
 def temporal_kernel(
-    place_ref, u0, u1, u2, u3, w_ref, gain_ref, shift_ref, cos_ref, sin_ref, *rest, frames
+    place_ref, u0, u1, u2, u3, w_ref, gain_ref, shift_ref, cos_ref, sin_ref, out_ref,
+    normed_ref, proj_ref, *, frames
 ):
-    *out_refs, normed_ref, proj_ref = rest
     rows, share = u0.shape
     count = rows // frames
     width = w_ref.shape[-1]
@@ -133,21 +125,12 @@
                 )
 
             mixed = attend(gathered(0), gathered(1), gathered(2), same)
-            if len(out_refs) == 1:
-                out_refs[0][:, head] = mixed
-            else:
-                for f, out_ref in enumerate(out_refs):
-                    out_ref[low : low + step, head] = mixed[f * step : (f + 1) * step]
-
-
-def gather_kernel(place_ref, *rest, chunks):
-    *piece_refs, out_ref = rest
-    many = len(piece_refs) // chunks
-    count = piece_refs[0].shape[0]
-    for c in range(chunks):
-        for k in range(many):
-            start = pl.multiple_of(c * many * count + (place_ref[0] ^ k) * count, count)
-            out_ref[pl.ds(start, count), :] = piece_refs[c * many + k][...]
+            if step == count:
+                out_ref[:, head] = mixed
+                continue
+            for f in range(frames):
+                start = f * count + low
+                out_ref[start : start + step, head] = mixed[f * step : (f + 1) * step]
 
 
 def swap(value, axis, size, k):
@@ -165,12 +148,11 @@
     width = spatial_qkv.shape[-1]
     features = share * n_mlp
     tokens = frames * patches
-    pairwise = n_seq == 8 and frames == 1 and patches % (n_seq * CHUNKS * GROUP) == 0
-    chunks = CHUNKS if pairwise else 1
+    chunks = CHUNKS if tokens % (n_seq * CHUNKS * GROUP) == 0 else 1
     rows = tokens // chunks
     count = rows // n_seq
-    seq, mlp = lax.axis_index("seq"), lax.axis_index("mlp")
-    seq_place, mlp_place = seq.reshape(1), mlp.reshape(1)
+    mlp = lax.axis_index("mlp")
+    mlp_place = mlp.reshape(1)
     flat_residual = residual.reshape(tokens, share)
     qkv = spatial_qkv.transpose(2, 0, 1, 3).reshape(3, tokens, width)
     weights = temporal_qkv.transpose(1, 0, 2)
@@ -187,8 +169,7 @@
     gate_send, gate_keep = columns(gate_row, mlp ^ 2), columns(gate_row, mlp)
 
     rates = 10000.0 ** (-2.0 * jnp.arange(HEAD_DIM // 2, dtype=f32) / HEAD_DIM)
-    order = jnp.arange(n_seq) ^ seq if pairwise else jnp.arange(n_seq)
-    angles = order.astype(f32)[:, None] * rates
+    angles = jnp.arange(n_seq, dtype=f32)[:, None] * rates
     cosine = jnp.concatenate([jnp.cos(angles)] * 2, axis=1)
     sine = jnp.concatenate([-jnp.sin(angles), jnp.sin(angles)], axis=1)
 
@@ -216,39 +197,19 @@
             4 * rows * width * share,
             matmul_bytes,
         )(heads, others, own_keep, other_keep, gate_keep, flat_residual[c * rows : (c + 1) * rows])
-        if pairwise:
-            updated, *pieces = pl.pallas_call(
-                update_kernel,
-                out_shape=[jax.ShapeDtypeStruct((rows, share), bf16)]
-                + [jax.ShapeDtypeStruct((count, share), bf16)] * n_seq,
-                in_specs=smem(1) + [vm] * 2,
-                out_specs=[vm] * (1 + n_seq),
-                compiler_params=pltpu.CompilerParams(vmem_limit_bytes=VMEM_LIMIT),
-                cost_estimate=pl.CostEstimate(
-                    flops=rows * share, bytes_accessed=10 * rows * share, transcendentals=0
-                ),
-            )(seq_place, base, arrived)
-            pieces = [pieces[0]] + [swap(pieces[k], "seq", n_seq, k) for k in range(1, n_seq)]
-            mine = jnp.concatenate(pieces, axis=0)
-        else:
-            updated = (base + arrived.astype(f32)).astype(bf16)
-            mine = lax.all_to_all(
-                updated.reshape(n_seq, count, share), "seq", 0, 0, tiled=True
-            ).reshape(rows, share)
+        updated = (base + arrived.astype(f32)).astype(bf16)
+        mine = lax.all_to_all(
+            updated.reshape(n_seq, count, share), "seq", 0, 0, tiled=True
+        ).reshape(rows, share)
         updates.append(updated)
         across = swap(mine, "mlp", n_mlp, 2)
         beside = swap(mine, "mlp", n_mlp, 1)
         diagonal = swap(across, "mlp", n_mlp, 1)
-        outs = (
-            [jax.ShapeDtypeStruct((count, width), bf16)] * n_seq
-            if pairwise
-            else [jax.ShapeDtypeStruct((rows, width), bf16)]
-        )
         mixed = pl.pallas_call(
             functools.partial(temporal_kernel, frames=n_seq),
-            out_shape=outs,
+            out_shape=jax.ShapeDtypeStruct((rows, width), bf16),
             in_specs=smem(1) + [vm] * 9,
-            out_specs=[vm] * len(outs),
+            out_specs=vm,
             scratch_shapes=[
                 pltpu.VMEM((n_mlp, rows, share), bf16),
                 pltpu.VMEM((3, rows, width), bf16),
@@ -263,23 +224,12 @@
             mlp_place, mine, beside, across, diagonal, weights,
             scale.reshape(1, features), shift.reshape(1, features), cosine, sine,
         )
-        if pairwise:
-            results += [mixed[0]] + [swap(mixed[k], "seq", n_seq, k) for k in range(1, n_seq)]
-        else:
-            back = lax.all_to_all(
-                mixed[0].reshape(n_seq, count, width), "seq", 0, 0, tiled=True
-            )
-            results.append(back.reshape(rows, width))
-    if pairwise:
-        result = pl.pallas_call(
-            functools.partial(gather_kernel, chunks=chunks),
-            out_shape=jax.ShapeDtypeStruct((tokens, width), bf16),
-            in_specs=smem(1) + [vm] * len(results),
-            out_specs=vm,
-            compiler_params=pltpu.CompilerParams(vmem_limit_bytes=VMEM_LIMIT),
-        )(seq_place, *results)
-    else:
-        result = results[0]
+        results.append(
+            lax.all_to_all(
+                mixed.reshape(n_seq, count, width), "seq", 0, 0, tiled=True
+            ).reshape(rows, width)
+        )
+    result = jnp.concatenate(results, axis=0)
     return (
         jnp.concatenate(updates, axis=0).reshape(frames, patches, share),
         result.reshape(frames, patches, width),

time: 103 us -> 98.6 us (0.957)
  starting transfers between devices: 55.5 us -> 32.4 us
  waiting for transfers between devices: 18.5 us -> 37.5 us
  Pallas kernels: 20.5 us -> 14.7 us
  other arithmetic: 1.13 us -> 4.49 us
  local copies, waits for them, and re-layouts: 5.89 us -> 8.04 us
    ppermute x40 -> x12, starting transfers between devices: 55.5 us -> 9.02 us  [swap(): return lax.ppermute(value, axis, [(i, i ^ k) for i in range(size)])]
    all_to_all x0 -> x4, starting transfers between devices: none -> 23.4 us  [the longest x2 11.8 us: on_device(): lax.all_to_all(updated.reshape(n_seq, count, share), 'seq', 0, 0, tiled=T...]
    all_to_all x0 -> x4, waiting for transfers between devices: none -> 15 us  [the longest x2 8.44 us: on_device(): lax.all_to_all(updated.reshape(n_seq, count, share), 'seq', 0, 0, tiled=T...]
    ppermute x40 -> x12, waiting for transfers between devices: 18.5 us -> 22.5 us  [swap(): return lax.ppermute(value, axis, [(i, i ^ k) for i in range(size)])]
    unnamed x44 -> x16, local copies, waits for them, and re-layouts: 3.07 us -> 6.04 us
    pallas_call x2, Pallas kernels: 3.6 us -> 1.13 us  [on_device(): call(keep_kernel, jax.ShapeDtypeStruct((rows, share), f32), 4 * rows * wi...]
    pallas_call x3 -> x0, Pallas kernels: 2.11 us -> none  [the longest x2 1.31 us: on_device(): pl.pallas_call(update_kernel, out_shape=[jax.ShapeDtypeStruct((rows, shar...]
    pallas_call x2, Pallas kernels: 2.97 us -> 1.13 us  [on_device(): call(send_kernel, jax.ShapeDtypeStruct((rows, share), bf16), 4 * rows * w...]
  transfers between devices with their start and end apart: 40 -> 16, of which waited for: 8 -> 7; matrix products, arithmetic and copies ran while one was open for 1% -> 4% of each run, Pallas kernels for 19% -> 15%
where the time goes in v2:
time: 98.6 us; the launch traced here: 98 us
  waiting for transfers between devices  37.5 us (38%)
  starting transfers between devices  32.4 us (33%)
  Pallas kernels  14.7 us (15%)
  local copies, waits for them, and re-layouts  8.04 us (8%)
  other arithmetic  4.49 us (5%)
    ppermute x12, waiting for transfers between devices, swap(): return lax.ppermute(value, axis, [(i, i ^ k) for i in range(size)])  22.5 us
    all_to_all x2, starting transfers between devices, on_device(): lax.all_to_all(updated.reshape(n_seq, count, share), 'seq', 0, 0, tiled=T...  11.8 us
    all_to_all x2, starting transfers between devices, on_device(): lax.all_to_all(mixed.reshape(n_seq, count, width), 'seq', 0, 0, tiled=True)  11.6 us
    pallas_call x2, Pallas kernels, on_device(): pl.pallas_call(functools.partial(temporal_kernel, frames=n_seq), out_shap...  10.3 us
    ppermute x12, starting transfers between devices, swap(): return lax.ppermute(value, axis, [(i, i ^ k) for i in range(size)])  9.02 us
    all_to_all x2, waiting for transfers between devices, on_device(): lax.all_to_all(updated.reshape(n_seq, count, share), 'seq', 0, 0, tiled=T...  8.44 us
    all_to_all x2, waiting for transfers between devices, on_device(): lax.all_to_all(mixed.reshape(n_seq, count, width), 'seq', 0, 0, tiled=True)  6.56 us
    unnamed x16, local copies, waits for them, and re-layouts  6.04 us
  transfers between devices with their start and end apart: 16, of which 7 were waited for; matrix products, arithmetic and copies ran while one was open for 4% of the time, Pallas kernels for 15%

profile of v2, /device:TPU:0, one launch (start us, length us, event | category | flops | bytes accessed | tf_op | source)
XLA Modules:
  0.0 98.0 jit_solution(7811626839053436178)
XLA Ops:
  0.7 0.0 copy-start.2
  0.7 0.0 copy-start.7
  0.7 1.9 %constant_dynamic-slice_fusion = (bf16[384,768]{1,0:T(8,128)(2,1)S(1)}, bf16[384,768]{1,0:T(8,128)(2,1)S(1)}, bf16[384,768]{1,0:T(8,128)(2,1)S(1)}, bf16[384,768]{1,0:T(8,128)(2,1)S(1)}) fusion(bf16[384,3072]{1,0:T(8,128)(2,1)} %param.9, s32[]{:T(128)S(6)} %select_n.17, s32[]{:T(128)S(6)} %select_n.15, s32[]{:T(128)S(6)} %select_n.14, s32[]{:T(128)S(6)} %select_n.16), kind=kLoop, calls=%fused_computation.12 | loop fusion | bytes 4718608 | tf_op jit(solution)/shard_map/dynamic_slice | solution.py:163
  2.5 0.5 collective-permute-start.2
  3.1 0.0 copy-done.2
  3.1 1.1 %shard_map.89.own_ref = bf16[256,384]{1,0:T(8,128)(2,1)S(1)} custom-call(bf16[3,512,384]{2,1,0:T(8,128)(2,1)S(1)} %bitcast.25), custom_call_target="tpu_custom_call" | custom-call | flops 201326592 | bytes 1179648 | tf_op jit(solution)/shard_map/pallas_call | solution.py:179
  4.1 0.1 collective-permute-start.4
  4.3 0.5 collective-permute-start.1
  4.7 0.0 copy-done.7
  4.7 0.1 fusion.3
  4.8 0.8 collective-permute-done.4.other_ref
  5.6 0.0 collective-permute-done.2.other_w_ref
  5.6 0.0 copy-start.6
  5.6 0.6 shard_map.91
  6.2 2.7 %collective-permute-start.5 = (bf16[256,768]{1,0:T(8,128)(2,1)S(1)}, bf16[256,768]{1,0:T(8,128)(2,1)S(1)}, u32[]{:S(2)}, u32[]{:S(2)}) collective-permute-start(bf16[256,768]{1,0:T(8,128)(2,1)S(1)} %shard_map.91), channel_id=1, source_target_pairs={{0,2},{1,3},{2,0},{3,1},{4,6},{5,7},{6,4},{7,5},{8,10},{9,11},{10,... | collective-permute-start | bytes 1179656 | tf_op jit(solution)/shard_map/ppermute | solution.py:137
  8.9 1.1 %shard_map.86.own_ref = bf16[256,384]{1,0:T(8,128)(2,1)S(1)} custom-call(bf16[3,512,384]{2,1,0:T(8,128)(2,1)S(1)} %bitcast.26), custom_call_target="tpu_custom_call" | custom-call | flops 201326592 | bytes 1179648 | tf_op jit(solution)/shard_map/pallas_call | solution.py:179
  10.0 0.1 collective-permute-start
  10.1 0.0 copy-done.6
  10.1 0.1 slice_bitcast_fusion.1
  10.2 0.0 collective-permute-done.1.other_w_ref
  10.2 0.6 shard_map.90
  10.8 7.8 %collective-permute-done.5 = bf16[256,768]{1,0:T(8,128)(2,1)S(1)} collective-permute-done((bf16[256,768]{1,0:T(8,128)(2,1)S(1)}, bf16[256,768]{1,0:T(8,128)(2,1)S(1)}, u32[]{:S(2)}, u32[]{:S(2)}) %collective-permute-start.5) | collective-permute-done | bytes 393248 | tf_op jit(solution)/shard_map/ppermute | solution.py:137
  18.6 0.8 add_convert_fusion
  19.4 6.1 %all-to-all-start.2 = ((bf16[8,32,768]{2,1,0:T(8,128)(2,1)}), bf16[8,32,768]{2,1,0:T(8,128)(2,1)S(1)}, u32[]{:S(2)}, u32[]{:S(2)}) async-start(bf16[8,32,768]{2,1,0:T(8,128)(2,1)} %bitcast.37), calls=%async_computation.2 | async-start | bytes 786432 | tf_op jit(solution)/shard_map/all_to_all | solution.py:201
  25.5 0.0 collective-permute-done.other_ref
  25.5 0.6 shard_map.88
  26.0 1.5 %collective-permute-start.3 = (bf16[256,768]{1,0:T(8,128)(2,1)S(1)}, bf16[256,768]{1,0:T(8,128)(2,1)S(1)}, u32[]{:S(2)}, u32[]{:S(2)}) collective-permute-start(bf16[256,768]{1,0:T(8,128)(2,1)S(1)} %shard_map.88), channel_id=1, source_target_pairs={{0,2},{1,3},{2,0},{3,1},{4,6},{5,7},{6,4},{7,5},{8,10},{9,11},{10,... | collective-permute-start | bytes 1179656 | tf_op jit(solution)/shard_map/ppermute | solution.py:137
  27.6 0.6 shard_map.87
  28.2 0.0 copy-start.3
  28.2 0.0 copy-start.4
  28.2 8.2 %collective-permute-done.3 = bf16[256,768]{1,0:T(8,128)(2,1)S(1)} collective-permute-done((bf16[256,768]{1,0:T(8,128)(2,1)S(1)}, bf16[256,768]{1,0:T(8,128)(2,1)S(1)}, u32[]{:S(2)}, u32[]{:S(2)}) %collective-permute-start.3) | collective-permute-done | bytes 393248 | tf_op jit(solution)/shard_map/ppermute | solution.py:137
  36.4 0.8 add_convert_fusion.1
  37.2 0.0 all-to-all-done.2
  37.2 5.7 %all-to-all-start = ((bf16[8,32,768]{2,1,0:T(8,128)(2,1)}), bf16[8,32,768]{2,1,0:T(8,128)(2,1)S(1)}, u32[]{:S(2)}, u32[]{:S(2)}) async-start(bf16[8,32,768]{2,1,0:T(8,128)(2,1)} %bitcast.7), calls=%async_computation | async-start | bytes 786432 | tf_op jit(solution)/shard_map/all_to_all | solution.py:201
  43.0 1.5 %collective-permute-start.10 = (bf16[256,768]{1,0:T(8,128)(2,1)S(1)}, bf16[256,768]{1,0:T(8,128)(2,1)S(1)}, u32[]{:S(2)}, u32[]{:S(2)}) collective-permute-start(bf16[256,768]{1,0:T(8,128)(2,1)S(1)} %bitcast.27), channel_id=1, source_target_pairs={{0,2},{1,3},{2,0},{3,1},{4,6},{5,7},{6,4},{7,5},{8,10},{9,11},{10,... | collective-permute-start | bytes 1179656 | tf_op jit(solution)/shard_map/ppermute | solution.py:137
  44.4 8.4 %all-to-all-done = bf16[8,32,768]{2,1,0:T(8,128)(2,1)S(1)} async-done(((bf16[8,32,768]{2,1,0:T(8,128)(2,1)}), bf16[8,32,768]{2,1,0:T(8,128)(2,1)S(1)}, u32[]{:S(2)}, u32[]{:S(2)}) %all-to-all-start) | async-done | bytes 393248 | tf_op jit(solution)/shard_map/all_to_all | solution.py:201
  52.9 1.5 %collective-permute-start.7 = (bf16[256,768]{1,0:T(8,128)(2,1)S(1)}, bf16[256,768]{1,0:T(8,128)(2,1)S(1)}, u32[]{:S(2)}, u32[]{:S(2)}) collective-permute-start(bf16[256,768]{1,0:T(8,128)(2,1)S(1)} %bitcast.30), channel_id=1, source_target_pairs={{0,2},{1,3},{2,0},{3,1},{4,6},{5,7},{6,4},{7,5},{8,10},{9,11},{10,... | collective-permute-start | bytes 1179656 | tf_op jit(solution)/shard_map/ppermute | solution.py:137
  54.4 0.0 collective-permute-start.9
  54.4 0.0 collective-permute-done.10.u2
  54.4 0.5 collective-permute-start.11
  54.9 0.1 fusion.2
  54.9 0.1 collective-permute-start.6
  55.0 5.6 %collective-permute-done.7.u2 = bf16[256,768]{1,0:T(8,128)(2,1)S(1)} collective-permute-done((bf16[256,768]{1,0:T(8,128)(2,1)S(1)}, bf16[256,768]{1,0:T(8,128)(2,1)S(1)}, u32[]{:S(2)}, u32[]{:S(2)}) %collective-permute-start.7) | collective-permute-done | bytes 393248 | tf_op jit(solution)/shard_map/ppermute | solution.py:137
  60.7 0.0 collective-permute-start.8
  60.7 0.1 pad_maximum_fusion
  60.7 0.0 collective-permute-done.9.u1
  60.7 0.0 collective-permute-done.11.u3
  60.7 0.0 copy-done.3
  60.7 0.0 copy-done.4
  60.8 0.0 copy-start
  60.8 3.0 %copy-done = bf16[3072,3,384]{2,0,1:T(8,128)(2,1)S(1)} copy-done((bf16[3072,3,384]{2,0,1:T(8,128)(2,1)S(1)}, bf16[3072,3,384]{2,0,1:T(8,128)(2,1)}, u32[]{:S(2)}) %copy-start) | copy-done | bytes 7077912
  63.8 5.2 %shard_map.93 = bf16[256,384]{1,0:T(8,128)(2,1)} custom-call(s32[1]{0:T(128)} %bitcast.6.place_ref, bf16[256,768]{1,0:T(8,128)(2,1)S(1)} %bitcast.29, bf16[256,768]{1,0:T(8,128)(2,1)S(1)} %collective-permute-done.9.u1, bf16[256,768]{1,0:T(8,128)(2,1)S(1)} %collective-permute-done.10.u2, bf16[256,768]{1,0:T(8,128)(2,1)S(1)} %collective-permute-done.11.u3, ...), custom_call_target="tpu_custom_call" | custom-call | flops 1811939328 | bytes 8650752 | tf_op jit(solution)/shard_map/pallas_call | solution.py:208
  68.9 6.0 %all-to-all-start.3 = ((bf16[8,32,384]{2,1,0:T(8,128)(2,1)}), bf16[8,32,384]{2,1,0:T(8,128)(2,1)S(1)}, u32[]{:S(2)}, u32[]{:S(2)}) async-start(bf16[8,32,384]{2,1,0:T(8,128)(2,1)} %bitcast.16), calls=%async_computation.3 | async-start | bytes 393216 | tf_op jit(solution)/shard_map/all_to_all | solution.py:228
  74.9 0.0 collective-permute-done.6.u1
  74.9 0.0 collective-permute-done.8.u3
  75.0 0.0 copy-start.1
  75.0 3.0 %copy-done.1 = bf16[3072,3,384]{2,0,1:T(8,128)(2,1)S(1)} copy-done((bf16[3072,3,384]{2,0,1:T(8,128)(2,1)S(1)}, bf16[3072,3,384]{2,0,1:T(8,128)(2,1)}, u32[]{:S(2)}) %copy-start.1) | copy-done | bytes 7077912
  78.0 5.2 %shard_map.92 = bf16[256,384]{1,0:T(8,128)(2,1)} custom-call(s32[1]{0:T(128)} %bitcast.6.place_ref, bf16[256,768]{1,0:T(8,128)(2,1)S(1)} %bitcast.32, bf16[256,768]{1,0:T(8,128)(2,1)S(1)} %collective-permute-done.6.u1, bf16[256,768]{1,0:T(8,128)(2,1)S(1)} %collective-permute-done.7.u2, bf16[256,768]{1,0:T(8,128)(2,1)S(1)} %collective-permute-done.8.u3, ...), custom_call_target="tpu_custom_call" | custom-call | flops 1811939328 | bytes 8650752 | tf_op jit(solution)/shard_map/pallas_call | solution.py:208
  83.2 0.4 all-to-all-done.3
  83.6 5.6 %all-to-all-start.1 = ((bf16[8,32,384]{2,1,0:T(8,128)(2,1)}), bf16[8,32,384]{2,1,0:T(8,128)(2,1)S(1)}, u32[]{:S(2)}, u32[]{:S(2)}) async-start(bf16[8,32,384]{2,1,0:T(8,128)(2,1)} %bitcast.12), calls=%async_computation.1 | async-start | bytes 393216 | tf_op jit(solution)/shard_map/all_to_all | solution.py:228
  89.1 0.0 copy-done.5
  89.2 1.9 %maximum_bitcast_fusion = bf16[1,512,768]{2,1,0:T(8,128)(2,1)} fusion(bf16[256,768]{1,0:T(8,128)(2,1)S(1)} %copy-done.5, bf16[256,768]{1,0:T(8,128)(2,1)} %add_convert_fusion.1), kind=kLoop, calls=%fused_computation | loop fusion | flops 1572864 | bytes 1572864 | tf_op jit(solution)/shard_map/reshape | solution.py:234
  91.1 6.1 %all-to-all-done.1 = bf16[8,32,384]{2,1,0:T(8,128)(2,1)S(1)} async-done(((bf16[8,32,384]{2,1,0:T(8,128)(2,1)}), bf16[8,32,384]{2,1,0:T(8,128)(2,1)S(1)}, u32[]{:S(2)}, u32[]{:S(2)}) %all-to-all-start.1) | async-done | bytes 196640 | tf_op jit(solution)/shard_map/all_to_all | solution.py:228
  97.2 0.8 maximum_bitcast_fusion.1
  (4 shorter events, 0.0 us)
Async XLA Ops:
  0.7 2.4 %copy-start.2 = (bf16[1,512,3,384]{3,1,2,0:T(8,128)(2,1)S(1)}, bf16[1,512,3,384]{3,1,2,0:T(8,128)(2,1)}, u32[]{:S(2)}) copy-start(bf16[1,512,3,384]{3,1,2,0:T(8,128)(2,1)} %param.8) | copy-start | bytes 3538948
  0.7 4.0 %copy-start.7 = (f32[3072]{0:T(1024)S(1)}, f32[3072]{0:T(1024)}, u32[]{:S(2)}) copy-start(f32[3072]{0:T(1024)} %param.13) | copy-start | bytes 36868
  2.5 3.1 %collective-permute-start.2 = (bf16[384,768]{1,0:T(8,128)(2,1)S(1)}, bf16[384,768]{1,0:T(8,128)(2,1)S(1)}, u32[]{:S(2)}, u32[]{:S(2)}) collective-permute-start(bf16[384,768]{1,0:T(8,128)(2,1)S(1)} %get-tuple-element.2), channel_id=1, source_target_pairs={{0,1},{1,0},{2,3},{3,2},{4,5},{5,4},{6,7},{7,6},{8,9},{9,8},{10,11... | collective-permute-start | bytes 1769480 | tf_op jit(solution)/shard_map/ppermute | solution.py:137
  4.1 1.5 %collective-permute-start.4 = (bf16[256,384]{1,0:T(8,128)(2,1)S(1)}, bf16[256,384]{1,0:T(8,128)(2,1)S(1)}, u32[]{:S(2)}, u32[]{:S(2)}) collective-permute-start(bf16[256,384]{1,0:T(8,128)(2,1)S(1)} %shard_map.89.own_ref), channel_id=1, source_target_pairs={{0,1},{1,0},{2,3},{3,2},{4,5},{5,4},{6,7},{7,6},{8,9},{9,8},{10,11... | collective-permute-start | bytes 589832 | tf_op jit(solution)/shard_map/ppermute | solution.py:137
  4.3 5.9 %collective-permute-start.1 = (bf16[384,768]{1,0:T(8,128)(2,1)S(1)}, bf16[384,768]{1,0:T(8,128)(2,1)S(1)}, u32[]{:S(2)}, u32[]{:S(2)}) collective-permute-start(bf16[384,768]{1,0:T(8,128)(2,1)S(1)} %get-tuple-element.3), channel_id=1, source_target_pairs={{0,1},{1,0},{2,3},{3,2},{4,5},{5,4},{6,7},{7,6},{8,9},{9,8},{10,11... | collective-permute-start | bytes 1769480 | tf_op jit(solution)/shard_map/ppermute | solution.py:137
  5.6 4.5 %copy-start.6 = (bf16[1,512,768]{2,1,0:T(8,128)(2,1)S(1)}, bf16[1,512,768]{2,1,0:T(8,128)(2,1)}, u32[]{:S(2)}) copy-start(bf16[1,512,768]{2,1,0:T(8,128)(2,1)} %param.7) | copy-start | bytes 2359300
  6.2 12.3 %collective-permute-start.5 = (bf16[256,768]{1,0:T(8,128)(2,1)S(1)}, bf16[256,768]{1,0:T(8,128)(2,1)S(1)}, u32[]{:S(2)}, u32[]{:S(2)}) collective-permute-start(bf16[256,768]{1,0:T(8,128)(2,1)S(1)} %shard_map.91), channel_id=1, source_target_pairs={{0,2},{1,3},{2,0},{3,1},{4,6},{5,7},{6,4},{7,5},{8,10},{9,11},{10,... | collective-permute-start | bytes 1179656 | tf_op jit(solution)/shard_map/ppermute | solution.py:137
  10.0 15.5 %collective-permute-start = (bf16[256,384]{1,0:T(8,128)(2,1)S(1)}, bf16[256,384]{1,0:T(8,128)(2,1)S(1)}, u32[]{:S(2)}, u32[]{:S(2)}) collective-permute-start(bf16[256,384]{1,0:T(8,128)(2,1)S(1)} %shard_map.86.own_ref), channel_id=1, source_target_pairs={{0,1},{1,0},{2,3},{3,2},{4,5},{5,4},{6,7},{7,6},{8,9},{9,8},{10,11... | collective-permute-start | bytes 589832 | tf_op jit(solution)/shard_map/ppermute | solution.py:137
  19.4 17.9 %all-to-all-start.2 = ((bf16[8,32,768]{2,1,0:T(8,128)(2,1)}), bf16[8,32,768]{2,1,0:T(8,128)(2,1)S(1)}, u32[]{:S(2)}, u32[]{:S(2)}) async-start(bf16[8,32,768]{2,1,0:T(8,128)(2,1)} %bitcast.37), calls=%async_computation.2 | async-start | bytes 786432 | tf_op jit(solution)/shard_map/all_to_all | solution.py:201
  26.0 10.4 %collective-permute-start.3 = (bf16[256,768]{1,0:T(8,128)(2,1)S(1)}, bf16[256,768]{1,0:T(8,128)(2,1)S(1)}, u32[]{:S(2)}, u32[]{:S(2)}) collective-permute-start(bf16[256,768]{1,0:T(8,128)(2,1)S(1)} %shard_map.88), channel_id=1, source_target_pairs={{0,2},{1,3},{2,0},{3,1},{4,6},{5,7},{6,4},{7,5},{8,10},{9,11},{10,... | collective-permute-start | bytes 1179656 | tf_op jit(solution)/shard_map/ppermute | solution.py:137
  28.2 32.6 %copy-start.3 = (f32[3072]{0:T(1024)S(1)}, f32[3072]{0:T(1024)}, u32[]{:S(2)}) copy-start(f32[3072]{0:T(1024)} %param.12) | copy-start | bytes 36868
  28.2 32.6 %copy-start.4 = (f32[3072]{0:T(1024)S(1)}, f32[3072]{0:T(1024)}, u32[]{:S(2)}) copy-start(f32[3072]{0:T(1024)} %param.11) | copy-start | bytes 36868
  37.2 15.6 %all-to-all-start = ((bf16[8,32,768]{2,1,0:T(8,128)(2,1)}), bf16[8,32,768]{2,1,0:T(8,128)(2,1)S(1)}, u32[]{:S(2)}, u32[]{:S(2)}) async-start(bf16[8,32,768]{2,1,0:T(8,128)(2,1)} %bitcast.7), calls=%async_computation | async-start | bytes 786432 | tf_op jit(solution)/shard_map/all_to_all | solution.py:201
  43.0 11.4 %collective-permute-start.10 = (bf16[256,768]{1,0:T(8,128)(2,1)S(1)}, bf16[256,768]{1,0:T(8,128)(2,1)S(1)}, u32[]{:S(2)}, u32[]{:S(2)}) collective-permute-start(bf16[256,768]{1,0:T(8,128)(2,1)S(1)} %bitcast.27), channel_id=1, source_target_pairs={{0,2},{1,3},{2,0},{3,1},{4,6},{5,7},{6,4},{7,5},{8,10},{9,11},{10,... | collective-permute-start | bytes 1179656 | tf_op jit(solution)/shard_map/ppermute | solution.py:137
  52.9 7.8 %collective-permute-start.7 = (bf16[256,768]{1,0:T(8,128)(2,1)S(1)}, bf16[256,768]{1,0:T(8,128)(2,1)S(1)}, u32[]{:S(2)}, u32[]{:S(2)}) collective-permute-start(bf16[256,768]{1,0:T(8,128)(2,1)S(1)} %bitcast.30), channel_id=1, source_target_pairs={{0,2},{1,3},{2,0},{3,1},{4,6},{5,7},{6,4},{7,5},{8,10},{9,11},{10,... | collective-permute-start | bytes 1179656 | tf_op jit(solution)/shard_map/ppermute | solution.py:137
  54.4 6.4 %collective-permute-start.9 = (bf16[256,768]{1,0:T(8,128)(2,1)S(1)}, bf16[256,768]{1,0:T(8,128)(2,1)S(1)}, u32[]{:S(2)}, u32[]{:S(2)}) collective-permute-start(bf16[256,768]{1,0:T(8,128)(2,1)S(1)} %bitcast.28), channel_id=1, source_target_pairs={{0,1},{1,0},{2,3},{3,2},{4,5},{5,4},{6,7},{7,6},{8,9},{9,8},{10,11... | collective-permute-start | bytes 1179656 | tf_op jit(solution)/shard_map/ppermute | solution.py:137
  54.4 6.4 %collective-permute-start.11 = (bf16[256,768]{1,0:T(8,128)(2,1)S(1)}, bf16[256,768]{1,0:T(8,128)(2,1)S(1)}, u32[]{:S(2)}, u32[]{:S(2)}) collective-permute-start(bf16[256,768]{1,0:T(8,128)(2,1)S(1)} %collective-permute-done.10.u2), channel_id=1, source_target_pairs={{0,1},{1,0},{2,3},{3,2},{4,5},{5,4},{6,7},{7,6},{8,9},{9,8},{10,11... | collective-permute-start | bytes 1179656 | tf_op jit(solution)/shard_map/ppermute | solution.py:137
  54.9 20.0 %collective-permute-start.6 = (bf16[256,768]{1,0:T(8,128)(2,1)S(1)}, bf16[256,768]{1,0:T(8,128)(2,1)S(1)}, u32[]{:S(2)}, u32[]{:S(2)}) collective-permute-start(bf16[256,768]{1,0:T(8,128)(2,1)S(1)} %bitcast.31), channel_id=1, source_target_pairs={{0,1},{1,0},{2,3},{3,2},{4,5},{5,4},{6,7},{7,6},{8,9},{9,8},{10,11... | collective-permute-start | bytes 1179656 | tf_op jit(solution)/shard_map/ppermute | solution.py:137
  60.7 14.3 %collective-permute-start.8 = (bf16[256,768]{1,0:T(8,128)(2,1)S(1)}, bf16[256,768]{1,0:T(8,128)(2,1)S(1)}, u32[]{:S(2)}, u32[]{:S(2)}) collective-permute-start(bf16[256,768]{1,0:T(8,128)(2,1)S(1)} %collective-permute-done.7.u2), channel_id=1, source_target_pairs={{0,1},{1,0},{2,3},{3,2},{4,5},{5,4},{6,7},{7,6},{8,9},{9,8},{10,11... | collective-permute-start | bytes 1179656 | tf_op jit(solution)/shard_map/ppermute | solution.py:137
  60.8 3.0 %copy-start = (bf16[3072,3,384]{2,0,1:T(8,128)(2,1)S(1)}, bf16[3072,3,384]{2,0,1:T(8,128)(2,1)}, u32[]{:S(2)}) copy-start(bf16[3072,3,384]{2,0,1:T(8,128)(2,1)} %param.10) | copy-start | bytes 21233668
  68.9 20.2 %copy-start.5 = (bf16[256,768]{1,0:T(8,128)(2,1)S(1)}, bf16[256,768]{1,0:T(8,128)(2,1)}, u32[]{:S(2)}) copy-start(bf16[256,768]{1,0:T(8,128)(2,1)} %add_convert_fusion) | copy-start | bytes 1179652
  68.9 14.6 %all-to-all-start.3 = ((bf16[8,32,384]{2,1,0:T(8,128)(2,1)}), bf16[8,32,384]{2,1,0:T(8,128)(2,1)S(1)}, u32[]{:S(2)}, u32[]{:S(2)}) async-start(bf16[8,32,384]{2,1,0:T(8,128)(2,1)} %bitcast.16), calls=%async_computation.3 | async-start | bytes 393216 | tf_op jit(solution)/shard_map/all_to_all | solution.py:228
  75.0 3.0 %copy-start.1 = (bf16[3072,3,384]{2,0,1:T(8,128)(2,1)S(1)}, bf16[3072,3,384]{2,0,1:T(8,128)(2,1)}, u32[]{:S(2)}) copy-start(bf16[3072,3,384]{2,0,1:T(8,128)(2,1)} %param.10) | copy-start | bytes 21233668
  83.6 13.6 %all-to-all-start.1 = ((bf16[8,32,384]{2,1,0:T(8,128)(2,1)}), bf16[8,32,384]{2,1,0:T(8,128)(2,1)S(1)}, u32[]{:S(2)}, u32[]{:S(2)}) async-start(bf16[8,32,384]{2,1,0:T(8,128)(2,1)} %bitcast.12), calls=%async_computation.1 | async-start | bytes 393216 | tf_op jit(solution)/shard_map/all_to_all | solution.py:228

commit v3 on v2

v3 whole, which is shorter than its diff:
```python
import functools
import math

import jax
import jax.numpy as jnp
import numpy as np
from jax import lax
from jax.experimental import pallas as pl
from jax.experimental.pallas import tpu as pltpu
from jax.sharding import PartitionSpec as P

HEAD_DIM = 128
EPSILON = 1e-06
GROUP = 16
MASKED = -1e30
VMEM_LIMIT = 16 * 1024 * 1024
EXP2_SCALE = math.log2(math.e) / math.sqrt(HEAD_DIM)
CHUNK_ROWS = (256, 256)
PARTNERS = ((7, 4, 2, 0), (5, 3, 6, 1))
SHARES = len(PARTNERS[0])


def call(body, outs, flops=0, moved=0, exps=0, inputs=0, scratch=(), far=0):
    return pl.pallas_call(
        body,
        out_shape=outs,
        in_specs=[pl.BlockSpec(memory_space=pltpu.VMEM)] * (inputs - far)
        + [pl.BlockSpec(memory_space=pltpu.HBM)] * far,
        scratch_shapes=list(scratch),
        compiler_params=pltpu.CompilerParams(vmem_limit_bytes=VMEM_LIMIT),
        cost_estimate=pl.CostEstimate(
            flops=int(flops), bytes_accessed=int(moved), transcendentals=int(exps)
        ),
    )


def dot(a, b):
    return jnp.dot(a, b, preferred_element_type=jnp.float32)


def dot_nt(a, b):
    return lax.dot_general(a, b, (((1,), (1,)), ((), ())), preferred_element_type=jnp.float32)


def attend(query, key, value, same=None):
    logits = dot_nt(query, key)
    if same is not None:
        logits = jnp.where(same, logits, MASKED)
    top = jnp.max(logits, axis=-1, keepdims=True)
    weights = jnp.exp2((logits - top) * EXP2_SCALE)
    total = jnp.sum(weights, axis=-1, keepdims=True)
    return (dot(weights.astype(jnp.bfloat16), value) / total).astype(jnp.bfloat16)


def project_and_mix(parts, frame_of, write, w_ref, gain_ref, shift_ref, cos_ref, sin_ref, normed_ref, proj_ref):
    features, width = w_ref.shape[1:]
    frames = cos_ref.shape[0]
    rows = normed_ref.shape[0]
    count = rows // frames
    first = 0
    for part in parts:
        size = part[0][0].shape[0]
        total = jnp.zeros((size, 1), jnp.float32)
        square = jnp.zeros((size, 1), jnp.float32)
        for ref, _ in part:
            values = ref[...].astype(jnp.float32)
            total += jnp.sum(values, axis=-1, keepdims=True)
            square += jnp.sum(values * values, axis=-1, keepdims=True)
        mean = total / features
        rate = lax.rsqrt(square / features - mean * mean + EPSILON)
        for ref, start in part:
            lanes = pl.ds(start, ref.shape[-1])
            gain = 1.0 + gain_ref[:, lanes]
            normed_ref[first : first + size, lanes] = (
                (ref[...].astype(jnp.float32) - mean) * rate * gain + shift_ref[:, lanes]
            ).astype(normed_ref.dtype)
        first += size
    for part in range(3):
        acc = dot(normed_ref[...], w_ref[part])
        if part == 2:
            proj_ref[part] = acc.astype(proj_ref.dtype)
            continue
        for f in range(frames):
            row = pl.ds(frame_of(f), 1)
            cosine, sine = cos_ref[row, :], sin_ref[row, :]
            span = slice(f * count, (f + 1) * count)
            for lane in range(0, width, HEAD_DIM):
                head = acc[span, lane : lane + HEAD_DIM]
                turned = pltpu.roll(head, HEAD_DIM // 2, 1)
                proj_ref[part, span, lane : lane + HEAD_DIM] = (
                    head * cosine + turned * sine
                ).astype(proj_ref.dtype)
    step = GROUP if count % GROUP == 0 else count
    size = step * frames
    patch_of = lambda axis: lax.rem(lax.broadcasted_iota(jnp.int32, (size, size), axis), step)
    same = patch_of(0) == patch_of(1)
    for low in range(0, count, step):
        for lane in range(0, width, HEAD_DIM):
            head = slice(lane, lane + HEAD_DIM)

            def gathered(part):
                if step == count:
                    return proj_ref[part, :, head]
                return jnp.concatenate(
                    [
                        proj_ref[part, f * count + low : f * count + low + step, head]
                        for f in range(frames)
                    ],
                    axis=0,
                )

            mixed = attend(gathered(0), gathered(1), gathered(2), same)
            for f in range(frames):
                write(f, low, head, mixed[f * step : (f + 1) * step])


def core_of():
    return lax.rem(lax.axis_index("mlp"), 2)


def chip_of():
    return lax.div(lax.axis_index("mlp"), 2)


def frame_of(i):
    low, high = (PARTNERS[core][i % SHARES] for core in range(2))
    which = core_of() if i < SHARES else 1 - core_of()
    return lax.axis_index("seq") ^ (low + which * (high - low))


def piece_span(first, count, i):
    return pl.ds(pl.multiple_of(first + frame_of(i) * count, count), count)


def piece_rows(ref, first, count, lanes):
    return jnp.concatenate(
        [ref[piece_span(first, count, i), lanes] for i in range(2 * SHARES)], axis=0
    )


def chip_columns(features, flip):
    half = features // 2
    return pl.ds(pl.multiple_of((chip_of() ^ flip) * half, half), half)


def spatial_body(qkv_ref, far_w_ref, far_gate, heads_ref, message_ref, first, before_message):
    rows, width = heads_ref.shape
    for lane in range(0, width, HEAD_DIM):
        head = slice(lane, lane + HEAD_DIM)
        query = piece_rows(qkv_ref.at[0], first, rows // (2 * SHARES), head)
        heads_ref[:, head] = attend(query, qkv_ref[1, :, head], qkv_ref[2, :, head])
    before_message()
    message_ref[...] = (dot(heads_ref[rows // 2 :, :], far_w_ref[...]) * far_gate).astype(
        message_ref.dtype
    )


def first_spatial_kernel(
    gate_ref, qkv_far, w_far, heads_ref, message_ref, qkv_ref, w_ref, semaphores, *, first
):
    columns = chip_columns(w_far.shape[-1], 1)
    copies = [
        pltpu.make_async_copy(qkv_far, qkv_ref, semaphores.at[0]),
        pltpu.make_async_copy(w_far.at[:, columns], w_ref, semaphores.at[1]),
    ]
    for copy in copies:
        copy.start()
    copies[0].wait()
    spatial_body(
        qkv_ref, w_ref, gate_ref[:, columns], heads_ref, message_ref, first, copies[1].wait
    )


def spatial_kernel(gate_ref, qkv_ref, w_ref, heads_ref, message_ref, *, first):
    columns = chip_columns(w_ref.shape[-1], 1)
    spatial_body(
        qkv_ref,
        w_ref.at[:, columns],
        gate_ref[:, columns],
        heads_ref,
        message_ref,
        first,
        lambda: None,
    )


def terms_kernel(
    heads_ref, w_ref, gate_ref, residual_ref, far_ref, base_ref, message_ref, *, first
):
    half, both = base_ref.shape
    share = both // 2
    features = w_ref.shape[-1]
    far = chip_columns(features, 1)
    far_ref[...] = dot(heads_ref[:half, :], w_ref[:, far]) * gate_ref[:, far]
    for flip in range(2):
        place = pl.multiple_of((core_of() ^ flip) * share, share)
        lanes = pl.ds(pl.multiple_of(chip_of() * both + place, share), share)
        term = dot(heads_ref[...], w_ref[:, lanes]) * gate_ref[:, lanes]
        if flip == 0:
            term += piece_rows(residual_ref, first, half // SHARES, slice(None)).astype(
                jnp.float32
            )
        base_ref[:, pl.ds(place, share)] = term[:half]
        message_ref[:, pl.ds(place, share)] = term[half:].astype(message_ref.dtype)


def add_kernel(a_ref, b_ref, out_ref):
    out_ref[...] = (a_ref[...] + b_ref[...].astype(jnp.float32)).astype(out_ref.dtype)


def update_kernel(base_ref, message_ref, arrived_ref, own_ref, other_ref, *piece_refs):
    updated = (
        base_ref[...] + message_ref[...].astype(jnp.float32) + arrived_ref[...].astype(jnp.float32)
    ).astype(jnp.bfloat16)
    count = piece_refs[0].shape[0]
    for i, piece_ref in enumerate(piece_refs):
        piece_ref[...] = updated[i * count : (i + 1) * count]
    share = own_ref.shape[-1]
    left, right = updated[:, :share], updated[:, share:]
    core = core_of()
    own_ref[...] = jnp.where(core == 0, left, right)
    other_ref[...] = jnp.where(core == 0, right, left)


def split_temporal_kernel(own_near, own_far, other_near, other_far, w_ref, gain_ref, shift_ref, cos_ref, sin_ref, own_ref, other_ref, *scratch):
    half = own_near.shape[-1]
    near, far = (pl.multiple_of((chip_of() ^ flip) * half, half) for flip in range(2))
    count = own_ref.shape[0] // SHARES

    def write(i, low, head, value):
        ref = own_ref if i < SHARES else other_ref
        start = (i % SHARES) * count + low
        ref[start : start + value.shape[0], head] = value

    project_and_mix(
        [[(own_near, near), (own_far, far)], [(other_near, near), (other_far, far)]],
        frame_of,
        write,
        w_ref,
        gain_ref,
        shift_ref,
        cos_ref,
        sin_ref,
        *scratch,
    )


def pack_kernel(*refs):
    block_refs, out_refs = refs[:-SHARES], refs[-SHARES:]
    for i, out_ref in enumerate(out_refs):
        start = 0
        for ref in block_refs:
            count = ref.shape[0] // SHARES
            out_ref[start : start + count] = ref[i * count : (i + 1) * count]
            start += count


def unpack_kernel(*refs):
    *piece_refs, out_ref = refs
    count = piece_refs[0].shape[0] // 2
    for i, ref in enumerate(piece_refs):
        out_ref[i * count : (i + 1) * count] = ref[count:]


def place_updated_kernel(*refs, chunks):
    *block_refs, out_ref = refs
    for (first, rows), own_ref, other_ref in zip(chunks, block_refs[::2], block_refs[1::2]):
        count = rows // (2 * SHARES)
        for i in range(2 * SHARES):
            ref = own_ref if i < SHARES else other_ref
            start = (i % SHARES) * count
            out_ref[piece_span(first, count, i), :] = ref[start : start + count, :]


def place_mixed_kernel(*refs, chunks):
    *own_refs, other_ref, out_ref = refs
    size = own_refs[0].shape[0] // 2
    start = 0
    for first, rows in chunks:
        count = rows // (2 * SHARES)
        for i in range(SHARES):
            out_ref[piece_span(first, count, i), :] = own_refs[i][start : start + count, :]
            low = i * size + start
            out_ref[piece_span(first, count, SHARES + i), :] = other_ref[low : low + count, :]
        start += count


def swap(value, axis, size, k):
    return lax.ppermute(value, axis, [(i, i ^ k) for i in range(size)])


def rotation_tables(frames):
    rates = 10000.0 ** (-2.0 * np.arange(HEAD_DIM // 2, dtype=np.float32) / HEAD_DIM)
    angles = np.arange(frames, dtype=np.float32)[:, None] * rates.astype(np.float32)
    cosine, sine = np.cos(angles), np.sin(angles)
    return (
        jnp.asarray(np.concatenate([cosine, cosine], axis=1), jnp.float32),
        jnp.asarray(np.concatenate([-sine, sine], axis=1), jnp.float32),
    )


def piece_pairs(n_seq, n_mlp, index):
    return [
        (s * n_mlp + m, (s ^ PARTNERS[m % 2][index]) * n_mlp + m)
        for s in range(n_seq)
        for m in range(n_mlp)
    ]


def after(value, *others):
    return lax.optimization_barrier((value,) + others)[0]


def split_on_device(
    residual, spatial_qkv, spatial_out, temporal_qkv, shift, scale, gate, *, n_seq, n_mlp
):
    frames, patches, share = residual.shape
    width = spatial_qkv.shape[-1]
    features = share * n_mlp
    both = 2 * share
    tokens = frames * patches
    bf16, f32 = jnp.bfloat16, jnp.float32
    flat_residual = residual.reshape(tokens, share)
    qkv = spatial_qkv.transpose(2, 0, 1, 3).reshape(3, tokens, width)
    weights = temporal_qkv.transpose(1, 0, 2)
    gate_row = gate.reshape(1, features)
    gain_row, shift_row = scale.reshape(1, features), shift.reshape(1, features)
    cosine, sine = rotation_tables(n_seq)

    def shape(rows, columns, kind=bf16):
        return jax.ShapeDtypeStruct((rows, columns), kind)

    def send_pieces(pieces):
        return [
            lax.ppermute(piece, ("seq", "mlp"), piece_pairs(n_seq, n_mlp, i))
            for i, piece in enumerate(pieces)
        ]

    chunks = []
    first = 0
    for rows in CHUNK_ROWS:
        chunks.append((first, rows))
        first += rows

    reduced = []
    previous = None
    for first, rows in chunks:
        half = rows // 2
        if previous is None:
            heads, message = call(
                functools.partial(first_spatial_kernel, first=first),
                [shape(rows, width), shape(half, both)],
                inputs=3,
                far=2,
                scratch=(
                    pltpu.VMEM((3, tokens, width), bf16),
                    pltpu.VMEM((width, both), bf16),
                    pltpu.SemaphoreType.DMA((2,)),
                ),
            )(gate_row, *(pltpu.with_memory_space_constraint(a, pltpu.HBM) for a in (qkv, spatial_out)))
        else:
            heads, message = call(
                functools.partial(spatial_kernel, first=first),
                [shape(rows, width), shape(half, both)],
                inputs=3,
            )(gate_row, after(qkv, previous), spatial_out)
        message = swap(message, "mlp", n_mlp, 1)
        far_term, base, near_message = call(
            functools.partial(terms_kernel, first=first),
            [shape(half, both, f32), shape(half, both, f32), shape(half, both)],
            inputs=4,
        )(heads, spatial_out, gate_row, flat_residual)
        sent = call(add_kernel, shape(half, both), inputs=2)(far_term, message)
        previous = sent
        reduced.append((base, swap(near_message, "mlp", n_mlp, 1), sent))

    arrivals = [swap(sent, "mlp", n_mlp, 2) for _, _, sent in reduced]
    arrivals[0] = after(arrivals[0], previous, *(message for _, message, _ in reduced))
    nears, blocks = [], []
    for (first, rows), (base, near_message, _), arrived in zip(chunks, reduced, arrivals):
        half = rows // 2
        own, other, *pieces = call(
            update_kernel,
            [shape(half, share)] * 2 + [shape(half // SHARES, both)] * SHARES,
            inputs=3,
        )(base, near_message, arrived)
        blocks += [own, swap(other, "mlp", n_mlp, 1)]
        nears.append(jnp.concatenate(send_pieces(pieces), axis=0))

    own_mixed, other_mixed = [], []
    for (first, rows), near in zip(chunks, nears):
        half = rows // 2
        far = swap(near, "mlp", n_mlp, 2)
        other_near = swap(near, "mlp", n_mlp, 1)
        if own_mixed:
            updated = call(
                functools.partial(place_updated_kernel, chunks=chunks),
                shape(tokens, share),
                inputs=len(blocks),
            )(*blocks)
            far = after(far, own_mixed[-1], updated)
        other_far = swap(far, "mlp", n_mlp, 1)
        own, other = call(
            split_temporal_kernel,
            [shape(half, width)] * 2,
            inputs=9,
            scratch=(pltpu.VMEM((rows, features), bf16), pltpu.VMEM((3, rows, width), bf16)),
        )(near, far, other_near, other_far, weights, gain_row, shift_row, cosine, sine)
        own_mixed.append(own)
        other_mixed.append(swap(other, "mlp", n_mlp, 1))
    packed = call(
        pack_kernel, [shape(2 * tokens // (2 * SHARES), width)] * SHARES, inputs=2 * len(chunks)
    )(*own_mixed, *other_mixed)
    pieces = send_pieces(packed)
    others = call(unpack_kernel, shape(tokens // 2, width), inputs=SHARES)(*pieces)
    results = pieces + [swap(others, "mlp", n_mlp, 1)]
    result = call(
        functools.partial(place_mixed_kernel, chunks=chunks),
        shape(tokens, width),
        inputs=len(results),
    )(*results)
    return updated.reshape(frames, patches, share), result.reshape(frames, patches, width)


def heads_kernel(qkv_ref, out_ref):
    for lane in range(0, out_ref.shape[-1], HEAD_DIM):
        head = slice(lane, lane + HEAD_DIM)
        out_ref[:, head] = attend(qkv_ref[0, :, head], qkv_ref[1, :, head], qkv_ref[2, :, head])


def columns_kernel(own_ref, other_ref, own_w_ref, other_w_ref, gate_ref, out_ref):
    term = dot(own_ref[...], own_w_ref[...]) + dot(other_ref[...], other_w_ref[...])
    out_ref[...] = (term * gate_ref[...]).astype(out_ref.dtype)


def temporal_kernel(u0, u1, u2, u3, *refs):
    *refs, out_ref, normed_ref, proj_ref = refs
    share = u0.shape[-1]
    count = out_ref.shape[0] // refs[-1].shape[0]
    part = [
        (ref, pl.multiple_of((lax.axis_index("mlp") ^ k) * share, share))
        for k, ref in enumerate((u0, u1, u2, u3))
    ]

    def write(f, low, head, value):
        start = f * count + low
        out_ref[start : start + value.shape[0], head] = value

    project_and_mix([part], lambda f: f, write, *refs, normed_ref, proj_ref)


def on_device(
    residual, spatial_qkv, spatial_out, temporal_qkv, shift, scale, gate, *, n_seq, n_mlp
):
    frames, patches, share = residual.shape
    width = spatial_qkv.shape[-1]
    features = share * n_mlp
    rows = frames * patches
    count = rows // n_seq
    mlp = lax.axis_index("mlp")
    bf16, f32 = jnp.bfloat16, jnp.float32
    qkv = spatial_qkv.transpose(2, 0, 1, 3).reshape(3, rows, width)
    gate_row = gate.reshape(1, features)

    def columns(array, block):
        return lax.dynamic_slice_in_dim(array, block * share, share, 1)

    heads = call(heads_kernel, jax.ShapeDtypeStruct((rows, width), bf16), inputs=1)(qkv)
    others = swap(heads, "mlp", n_mlp, 1)

    def term(block, kind):
        other_w = swap(columns(spatial_out, block ^ 1), "mlp", n_mlp, 1)
        return call(columns_kernel, jax.ShapeDtypeStruct((rows, share), kind), inputs=5)(
            heads, others, columns(spatial_out, block), other_w, columns(gate_row, block)
        )

    arrived = swap(term(mlp ^ 2, bf16), "mlp", n_mlp, 2)
    branch = term(mlp, f32) + arrived.astype(f32)
    updated = (residual.reshape(rows, share).astype(f32) + branch).astype(bf16)
    mine = lax.all_to_all(
        updated.reshape(n_seq, count, share), "seq", 0, 0, tiled=True
    ).reshape(rows, share)
    across = swap(mine, "mlp", n_mlp, 2)
    mixed = call(
        temporal_kernel,
        jax.ShapeDtypeStruct((rows, width), bf16),
        inputs=9,
        scratch=(pltpu.VMEM((rows, features), bf16), pltpu.VMEM((3, rows, width), bf16)),
    )(
        mine,
        swap(mine, "mlp", n_mlp, 1),
        across,
        swap(across, "mlp", n_mlp, 1),
        temporal_qkv.transpose(1, 0, 2),
        scale.reshape(1, features),
        shift.reshape(1, features),
        *rotation_tables(n_seq),
    )
    result = lax.all_to_all(
        mixed.reshape(n_seq, count, width), "seq", 0, 0, tiled=True
    ).reshape(rows, width)
    return updated.reshape(frames, patches, share), result.reshape(frames, patches, width)


def solution(mesh):
    sizes = dict(n_seq=mesh.shape["seq"], n_mlp=mesh.shape["mlp"])
    split = sizes["n_seq"] == 2 * SHARES and sizes["n_mlp"] == 4
    return jax.shard_map(
        functools.partial(split_on_device if split else on_device, **sizes),
        mesh=mesh,
        in_specs=(
            P("seq", None, "mlp"),
            P("seq", None, None, "mlp"),
            P("mlp", None),
            P(None, None, "mlp"),
            P(),
            P(),
            P(),
        ),
        out_specs=(P("seq", None, "mlp"), P("seq", None, "mlp")),
        check_vma=False,
    )
```

time: 98.6 us -> 82.1 us (0.83)
  local copies, waits for them, and re-layouts: 8.04 us -> 0.95 us
  starting transfers between devices: 32.4 us -> 27.4 us
  other arithmetic: 4.49 us -> 0.01 us
  Pallas kernels: 14.7 us -> 18.7 us
  waiting for transfers between devices: 37.5 us -> 33.8 us
    all_to_all x4 -> x0, starting transfers between devices: 23.4 us -> none  [the longest x2 11.8 us: on_device(): lax.all_to_all(updated.reshape(n_seq, count, share), 'seq', 0, 0, tiled=T...]
    ppermute x0 -> x12, starting transfers between devices: none -> 17.8 us  [send_pieces(): lax.ppermute(piece, ('seq', 'mlp'), piece_pairs(n_seq, n_mlp, i))]
    all_to_all x4 -> x0, waiting for transfers between devices: 15 us -> none  [the longest x2 8.44 us: on_device(): lax.all_to_all(updated.reshape(n_seq, count, share), 'seq', 0, 0, tiled=T...]
    ppermute x0 -> x12, waiting for transfers between devices: none -> 13.8 us  [send_pieces(): lax.ppermute(piece, ('seq', 'mlp'), piece_pairs(n_seq, n_mlp, i))]
    unnamed x16 -> x26, local copies, waits for them, and re-layouts: 6.04 us -> 0.93 us
    pallas_call x8 -> x14, Pallas kernels: 14.7 us -> 18.7 us  [the longest x2 10.6 us: split_on_device(): call(split_temporal_kernel, [shape(half, width)] * 2, inputs=9, scratch=(...]
    reshape x2 -> x0, other arithmetic: 2.71 us -> none  [the longest x1 1.93 us: on_device(): jnp.concatenate(updates, axis=0).reshape(frames, patches, share)]
    ppermute x12 -> x17, waiting for transfers between devices: 22.5 us -> 20 us  [swap(): return lax.ppermute(value, axis, [(i, i ^ k) for i in range(size)])]
  transfers between devices with their start and end apart: 16 -> 29, of which waited for: 7 -> 14; matrix products, arithmetic and copies ran while one was open for 4% -> 0% of each run, Pallas kernels for 15% -> 18%
where the time goes in v3:
time: 82.1 us; the launch traced here: 81.9 us
  waiting for transfers between devices  33.8 us (41%)
  starting transfers between devices  27.4 us (33%)
  Pallas kernels  18.7 us (23%)
  local copies, waits for them, and re-layouts  0.95 us (1%)
  between operations  0.93 us (1%)
    ppermute x17, waiting for transfers between devices, swap(): return lax.ppermute(value, axis, [(i, i ^ k) for i in range(size)])  20 us
    ppermute x12, starting transfers between devices, send_pieces(): lax.ppermute(piece, ('seq', 'mlp'), piece_pairs(n_seq, n_mlp, i))  17.8 us
    ppermute x12, waiting for transfers between devices, send_pieces(): lax.ppermute(piece, ('seq', 'mlp'), piece_pairs(n_seq, n_mlp, i))  13.8 us
    pallas_call x2, Pallas kernels, split_on_device(): call(split_temporal_kernel, [shape(half, width)] * 2, inputs=9, scratch=(...  10.6 us
    ppermute x17, starting transfers between devices, swap(): return lax.ppermute(value, axis, [(i, i ^ k) for i in range(size)])  9.62 us
    pallas_call x1, Pallas kernels, split_on_device(): call(functools.partial(first_spatial_kernel, first=first), [shape(rows, w...  2.81 us
    pallas_call x2, Pallas kernels, split_on_device(): call(functools.partial(terms_kernel, first=first), [shape(half, both, f32...  1.64 us
  transfers between devices with their start and end apart: 29, of which 14 were waited for; matrix products, arithmetic and copies ran while one was open for 0% of the time, Pallas kernels for 18%

profile of v3, /device:TPU:0, one launch (start us, length us, event | category | flops | bytes accessed | tf_op | source)
XLA Modules:
  0.0 81.9 jit_solution(13481128346556546712)
XLA Ops:
  0.7 0.8 %copy-done.3 = f32[3072]{0:T(1024)S(1)} copy-done((f32[3072]{0:T(1024)S(1)}, f32[3072]{0:T(1024)}, u32[]{:S(2)}) %copy-start.3) | copy-done | bytes 12312
  1.5 2.8 %shard_map.104 = (bf16[256,384]{1,0:T(8,128)(2,1)S(1)}, bf16[128,1536]{1,0:T(8,128)(2,1)S(1)}) custom-call(f32[1,3072]{1,0:T(1,128)S(1)} %bitcast.18, bf16[3,512,384]{2,1,0:T(8,128)(2,1)} %bitcast.14, bf16[384,3072]{1,0:T(8,128)(2,1)} %w_ref.5), custom_call_target="tpu_custom_call" | custom-call | tf_op jit(solution)/shard_map/pallas_call | solution.py:350
  4.3 0.5 collective-permute-start.1
  4.8 0.8 %shard_map.105 = (f32[128,1536]{1,0:T(8,128)S(1)}, f32[128,1536]{1,0:T(8,128)S(1)}, bf16[128,1536]{1,0:T(8,128)(2,1)S(1)}) custom-call(bf16[256,384]{1,0:T(8,128)(2,1)S(1)} %get-tuple-element.35.heads_ref, bf16[384,3072]{1,0:T(8,128)(2,1)S(1)} %copy-done, f32[1,3072]{1,0:T(1,128)S(1)} %bitcast.19, bf16[512,768]{1,0:T(8,128)(2,1)S(1)} %bitcast.16), custom_call_target="tpu_custom_call" | custom-call | tf_op jit(solution)/shard_map/pallas_call | solution.py:368
  5.7 0.1 collective-permute-start
  5.8 0.4 collective-permute-done.1.b_ref
  6.2 0.1 shard_map.106
  6.3 0.0 slice-start
  6.3 1.4 %shard_map.107 = (bf16[256,384]{1,0:T(8,128)(2,1)S(1)}, bf16[128,1536]{1,0:T(8,128)(2,1)S(1)}) custom-call(f32[1,3072]{1,0:T(1,128)S(1)} %bitcast.20, bf16[3,512,384]{2,1,0:T(8,128)(2,1)S(1)} %bitcast.15, bf16[384,3072]{1,0:T(8,128)(2,1)S(1)} %copy-done), custom_call_target="tpu_custom_call" | custom-call | tf_op jit(solution)/shard_map/pallas_call | solution.py:362
  7.7 0.4 collective-permute-start.3
  8.1 2.6 %collective-permute-start.2 = (bf16[128,1536]{1,0:T(8,128)(2,1)S(1)}, bf16[128,1536]{1,0:T(8,128)(2,1)S(1)}, u32[]{:S(2)}, u32[]{:S(2)}) collective-permute-start(bf16[128,1536]{1,0:T(8,128)(2,1)S(1)} %shard_map.106), channel_id=1, source_target_pairs={{0,2},{1,3},{2,0},{3,1},{4,6},{5,7},{6,4},{7,5},{8,10},{9,11},{10,... | collective-permute-start | bytes 1179656 | tf_op jit(solution)/shard_map/ppermute | solution.py:289
  10.7 0.8 %shard_map.108 = (f32[128,1536]{1,0:T(8,128)S(1)}, f32[128,1536]{1,0:T(8,128)S(1)}, bf16[128,1536]{1,0:T(8,128)(2,1)S(1)}) custom-call(bf16[256,384]{1,0:T(8,128)(2,1)S(1)} %get-tuple-element.41.heads_ref, bf16[384,3072]{1,0:T(8,128)(2,1)S(1)} %copy-done, f32[1,3072]{1,0:T(1,128)S(1)} %bitcast.21, bf16[512,768]{1,0:T(8,128)(2,1)S(1)} %bitcast.17), custom_call_target="tpu_custom_call" | custom-call | tf_op jit(solution)/shard_map/pallas_call | solution.py:368
  11.6 0.1 collective-permute-start.4
  11.7 0.0 collective-permute-done.3.b_ref
  11.7 0.1 shard_map.109
  11.8 0.0 collective-permute-done.message_ref
  11.8 8.6 %collective-permute-done.2.arrived_ref = bf16[128,1536]{1,0:T(8,128)(2,1)S(1)} collective-permute-done((bf16[128,1536]{1,0:T(8,128)(2,1)S(1)}, bf16[128,1536]{1,0:T(8,128)(2,1)S(1)}, u32[]{:S(2)}, u32[]{:S(2)}) %collective-permute-start.2) | collective-permute-done | bytes 393248 | tf_op jit(solution)/shard_map/ppermute | solution.py:289
  20.4 0.0 collective-permute-done.4.message_ref
  20.4 0.2 shard_map.110
  20.5 4.9 %collective-permute-start.8 = (bf16[32,1536]{1,0:T(8,128)(2,1)S(1)}, bf16[32,1536]{1,0:T(8,128)(2,1)S(1)}, u32[]{:S(2)}, u32[]{:S(2)}) collective-permute-start(bf16[32,1536]{1,0:T(8,128)(2,1)S(1)} %get-tuple-element.51), channel_id=1, source_target_pairs={{0,28},{1,21},{2,30},{3,23},{4,24},{5,17},{6,26},{7,19},{8,20},{9,... | collective-permute-start | bytes 294920 | tf_op jit(solution)/shard_map/ppermute | solution.py:335
  25.4 1.5 %collective-permute-start.6 = (bf16[128,1536]{1,0:T(8,128)(2,1)S(1)}, bf16[128,1536]{1,0:T(8,128)(2,1)S(1)}, u32[]{:S(2)}, u32[]{:S(2)}) collective-permute-start(bf16[128,1536]{1,0:T(8,128)(2,1)S(1)} %shard_map.109), channel_id=1, source_target_pairs={{0,2},{1,3},{2,0},{3,1},{4,6},{5,7},{6,4},{7,5},{8,10},{9,11},{10,... | collective-permute-start | bytes 1179656 | tf_op jit(solution)/shard_map/ppermute | solution.py:289
  26.9 0.0 collective-permute-start.9
  26.9 0.8 collective-permute-start.10
  27.7 0.8 collective-permute-start.11
  28.5 0.1 collective-permute-done.8
  28.6 5.0 %collective-permute-done.9 = bf16[32,1536]{1,0:T(8,128)(2,1)S(1)} collective-permute-done((bf16[32,1536]{1,0:T(8,128)(2,1)S(1)}, bf16[32,1536]{1,0:T(8,128)(2,1)S(1)}, u32[]{:S(2)}, u32[]{:S(2)}) %collective-permute-start.9) | collective-permute-done | bytes 98336 | tf_op jit(solution)/shard_map/ppermute | solution.py:335
  33.6 0.0 collective-permute-done.10
  33.7 1.2 %collective-permute-start.12 = (bf16[128,1536]{1,0:T(8,128)(2,1)S(1)}, bf16[128,1536]{1,0:T(8,128)(2,1)S(1)}, u32[]{:S(2)}, u32[]{:S(2)}) collective-permute-start(bf16[128,1536]{1,0:T(8,128)(2,1)S(1)} %constant_dynamic-update-slice_fusion.own_near), channel_id=1, source_target_pairs={{0,2},{1,3},{2,0},{3,1},{4,6},{5,7},{6,4},{7,5},{8,10},{9,11},{10,... | collective-permute-start | bytes 1179656 | tf_op jit(solution)/shard_map/ppermute | solution.py:289
  34.9 0.0 collective-permute-done.6.arrived_ref
  34.9 0.2 shard_map.111
  35.1 3.5 %collective-permute-start.15 = (bf16[32,1536]{1,0:T(8,128)(2,1)S(1)}, bf16[32,1536]{1,0:T(8,128)(2,1)S(1)}, u32[]{:S(2)}, u32[]{:S(2)}) collective-permute-start(bf16[32,1536]{1,0:T(8,128)(2,1)S(1)} %get-tuple-element.56), channel_id=1, source_target_pairs={{0,28},{1,21},{2,30},{3,23},{4,24},{5,17},{6,26},{7,19},{8,20},{9,... | collective-permute-start | bytes 294920 | tf_op jit(solution)/shard_map/ppermute | solution.py:335
  38.6 0.9 %collective-permute-start.17 = (bf16[32,1536]{1,0:T(8,128)(2,1)S(1)}, bf16[32,1536]{1,0:T(8,128)(2,1)S(1)}, u32[]{:S(2)}, u32[]{:S(2)}) collective-permute-start(bf16[32,1536]{1,0:T(8,128)(2,1)S(1)} %get-tuple-element.58), channel_id=1, source_target_pairs={{0,8},{1,25},{2,10},{3,27},{4,12},{5,29},{6,14},{7,31},{8,0},{9,17... | collective-permute-start | bytes 294920 | tf_op jit(solution)/shard_map/ppermute | solution.py:335
  39.5 4.0 %collective-permute-done.12.own_far = bf16[128,1536]{1,0:T(8,128)(2,1)S(1)} collective-permute-done((bf16[128,1536]{1,0:T(8,128)(2,1)S(1)}, bf16[128,1536]{1,0:T(8,128)(2,1)S(1)}, u32[]{:S(2)}, u32[]{:S(2)}) %collective-permute-start.12) | collective-permute-done | bytes 393248 | tf_op jit(solution)/shard_map/ppermute | solution.py:289
  43.5 0.8 %collective-permute-start.18 = (bf16[32,1536]{1,0:T(8,128)(2,1)S(1)}, bf16[32,1536]{1,0:T(8,128)(2,1)S(1)}, u32[]{:S(2)}, u32[]{:S(2)}) collective-permute-start(bf16[32,1536]{1,0:T(8,128)(2,1)S(1)} %get-tuple-element.59), channel_id=1, source_target_pairs={{0,0},{1,5},{2,2},{3,7},{4,4},{5,1},{6,6},{7,3},{8,8},{9,13},{10,1... | collective-permute-start | bytes 294920 | tf_op jit(solution)/shard_map/ppermute | solution.py:335
  44.4 0.0 collective-permute-done.15
  44.4 0.2 collective-permute-start.14
  44.6 1.7 %collective-permute-done.16 = bf16[32,1536]{1,0:T(8,128)(2,1)S(1)} collective-permute-done((bf16[32,1536]{1,0:T(8,128)(2,1)S(1)}, bf16[32,1536]{1,0:T(8,128)(2,1)S(1)}, u32[]{:S(2)}, u32[]{:S(2)}) %collective-permute-start.16) | collective-permute-done | bytes 98336 | tf_op jit(solution)/shard_map/ppermute | solution.py:335
  46.3 0.0 collective-permute-done.17
  46.4 1.4 %collective-permute-start.19 = (bf16[128,1536]{1,0:T(8,128)(2,1)S(1)}, bf16[128,1536]{1,0:T(8,128)(2,1)S(1)}, u32[]{:S(2)}, u32[]{:S(2)}) collective-permute-start(bf16[128,1536]{1,0:T(8,128)(2,1)S(1)} %constant_dynamic-update-slice_fusion.4.own_near), channel_id=1, source_target_pairs={{0,2},{1,3},{2,0},{3,1},{4,6},{5,7},{6,4},{7,5},{8,10},{9,11},{10,... | collective-permute-start | bytes 1179656 | tf_op jit(solution)/shard_map/ppermute | solution.py:289
  47.8 0.5 collective-permute-start.7
  48.3 0.9 %collective-permute-done.5.refs_1_ = bf16[128,768]{1,0:T(8,128)(2,1)S(1)} collective-permute-done((bf16[128,768]{1,0:T(8,128)(2,1)S(1)}, bf16[128,768]{1,0:T(8,128)(2,1)S(1)}, u32[]{:S(2)}, u32[]{:S(2)}) %collective-permute-start.5) | collective-permute-done | bytes 196640 | tf_op jit(solution)/shard_map/ppermute | solution.py:289
  49.2 0.1 collective-permute-start.20
  49.4 0.1 collective-permute-done.7.refs_3_
  49.5 0.9 %shard_map.112 = bf16[512,768]{1,0:T(8,128)(2,1)} custom-call(bf16[128,768]{1,0:T(8,128)(2,1)S(1)} %get-tuple-element.46.refs_0_, bf16[128,768]{1,0:T(8,128)(2,1)S(1)} %collective-permute-done.5.refs_1_, bf16[128,768]{1,0:T(8,128)(2,1)S(1)} %get-tuple-element.49.refs_2_, bf16[128,768]{1,0:T(8,128)(2,1)S(1)} %collective-permute-done.7.refs_3_), custom_call_target="tpu_custom_call" | custom-call | tf_op jit(solution)/shard_map/pallas_call | solution.py:396
  50.5 0.0 collective-permute-done.13.other_near
  50.5 0.0 collective-permute-done.14.other_far
  50.5 5.3 %shard_map.113 = (bf16[128,384]{1,0:T(8,128)(2,1)S(1)}, bf16[128,384]{1,0:T(8,128)(2,1)S(1)}) custom-call(bf16[128,1536]{1,0:T(8,128)(2,1)S(1)} %constant_dynamic-update-slice_fusion.own_near, bf16[128,1536]{1,0:T(8,128)(2,1)S(1)} %collective-permute-done.12.own_far, bf16[128,1536]{1,0:T(8,128)(2,1)S(1)} %collective-permute-done.13.other_near, ...), custom_call_target="tpu_custom_call" | custom-call | tf_op jit(solution)/shard_map/pallas_call | solution.py:403
  55.8 2.1 %collective-permute-done.19.own_far = bf16[128,1536]{1,0:T(8,128)(2,1)S(1)} collective-permute-done((bf16[128,1536]{1,0:T(8,128)(2,1)S(1)}, bf16[128,1536]{1,0:T(8,128)(2,1)S(1)}, u32[]{:S(2)}, u32[]{:S(2)}) %collective-permute-start.19) | collective-permute-done | bytes 393248 | tf_op jit(solution)/shard_map/ppermute | solution.py:289
  57.9 0.0 collective-permute-start.21
  57.9 0.5 collective-permute-start.22
  58.4 1.2 %collective-permute-done.21.other_far = bf16[128,1536]{1,0:T(8,128)(2,1)S(1)} collective-permute-done((bf16[128,1536]{1,0:T(8,128)(2,1)S(1)}, bf16[128,1536]{1,0:T(8,128)(2,1)S(1)}, u32[]{:S(2)}, u32[]{:S(2)}) %collective-permute-start.21) | collective-permute-done | bytes 393248 | tf_op jit(solution)/shard_map/ppermute | solution.py:289
  59.7 5.3 %shard_map.114 = (bf16[128,384]{1,0:T(8,128)(2,1)S(1)}, bf16[128,384]{1,0:T(8,128)(2,1)S(1)}) custom-call(bf16[128,1536]{1,0:T(8,128)(2,1)S(1)} %constant_dynamic-update-slice_fusion.4.own_near, bf16[128,1536]{1,0:T(8,128)(2,1)S(1)} %collective-permute-done.19.own_far, bf16[128,1536]{1,0:T(8,128)(2,1)S(1)} %collective-permute-done.20.other_near, ...), custom_call_target="tpu_custom_call" | custom-call | tf_op jit(solution)/shard_map/pallas_call | solution.py:403
  65.0 0.2 collective-permute-start.23
  65.2 1.2 %collective-permute-done.23.refs_3_ = bf16[128,384]{1,0:T(8,128)(2,1)S(1)} collective-permute-done((bf16[128,384]{1,0:T(8,128)(2,1)S(1)}, bf16[128,384]{1,0:T(8,128)(2,1)S(1)}, u32[]{:S(2)}, u32[]{:S(2)}) %collective-permute-start.23) | collective-permute-done | bytes 98336 | tf_op jit(solution)/shard_map/ppermute | solution.py:289
  66.4 2.8 %collective-permute-start.24 = (bf16[128,384]{1,0:T(8,128)(2,1)S(1)}, bf16[128,384]{1,0:T(8,128)(2,1)S(1)}, u32[]{:S(2)}, u32[]{:S(2)}) collective-permute-start(bf16[128,384]{1,0:T(8,128)(2,1)S(1)} %get-tuple-element.64), channel_id=1, source_target_pairs={{0,28},{1,21},{2,30},{3,23},{4,24},{5,17},{6,26},{7,19},{8,20},{9,... | collective-permute-start | bytes 294920 | tf_op jit(solution)/shard_map/ppermute | solution.py:335
  69.2 1.1 %collective-permute-start.25 = (bf16[128,384]{1,0:T(8,128)(2,1)S(1)}, bf16[128,384]{1,0:T(8,128)(2,1)S(1)}, u32[]{:S(2)}, u32[]{:S(2)}) collective-permute-start(bf16[128,384]{1,0:T(8,128)(2,1)S(1)} %get-tuple-element.65), channel_id=1, source_target_pairs={{0,16},{1,13},{2,18},{3,15},{4,20},{5,9},{6,22},{7,11},{8,24},{9,5... | collective-permute-start | bytes 294920 | tf_op jit(solution)/shard_map/ppermute | solution.py:335
  70.2 1.6 %collective-permute-start.26 = (bf16[128,384]{1,0:T(8,128)(2,1)S(1)}, bf16[128,384]{1,0:T(8,128)(2,1)S(1)}, u32[]{:S(2)}, u32[]{:S(2)}) collective-permute-start(bf16[128,384]{1,0:T(8,128)(2,1)S(1)} %get-tuple-element.66), channel_id=1, source_target_pairs={{0,8},{1,25},{2,10},{3,27},{4,12},{5,29},{6,14},{7,31},{8,0},{9,17... | collective-permute-start | bytes 294920 | tf_op jit(solution)/shard_map/ppermute | solution.py:335
  71.8 0.7 collective-permute-start.27
  72.5 1.9 %collective-permute-done.24.refs_0_ = bf16[128,384]{1,0:T(8,128)(2,1)S(1)} collective-permute-done((bf16[128,384]{1,0:T(8,128)(2,1)S(1)}, bf16[128,384]{1,0:T(8,128)(2,1)S(1)}, u32[]{:S(2)}, u32[]{:S(2)}) %collective-permute-start.24) | collective-permute-done | bytes 98336 | tf_op jit(solution)/shard_map/ppermute | solution.py:335
  74.4 5.1 %collective-permute-done.25.refs_1_ = bf16[128,384]{1,0:T(8,128)(2,1)S(1)} collective-permute-done((bf16[128,384]{1,0:T(8,128)(2,1)S(1)}, bf16[128,384]{1,0:T(8,128)(2,1)S(1)}, u32[]{:S(2)}, u32[]{:S(2)}) %collective-permute-start.25) | collective-permute-done | bytes 98336 | tf_op jit(solution)/shard_map/ppermute | solution.py:335
  79.5 0.0 collective-permute-done.27.refs_3_
  79.6 0.1 collective-permute-start.28
  79.6 1.4 %collective-permute-done.28.refs_4_ = bf16[256,384]{1,0:T(8,128)(2,1)S(1)} collective-permute-done((bf16[256,384]{1,0:T(8,128)(2,1)S(1)}, bf16[256,384]{1,0:T(8,128)(2,1)S(1)}, u32[]{:S(2)}, u32[]{:S(2)}) %collective-permute-start.28) | collective-permute-done | bytes 196640 | tf_op jit(solution)/shard_map/ppermute | solution.py:289
  81.1 0.8 shard_map.117
  (37 shorter events, 0.2 us)
Async XLA Ops:
  0.6 4.2 %copy-start = (bf16[384,3072]{1,0:T(8,128)(2,1)S(1)}, bf16[384,3072]{1,0:T(8,128)(2,1)}, u32[]{:S(2)}) copy-start(bf16[384,3072]{1,0:T(8,128)(2,1)} %w_ref.5) | copy-start | bytes 7077892
  0.6 4.2 %copy-start.2 = (bf16[1,512,768]{2,1,0:T(8,128)(2,1)S(1)}, bf16[1,512,768]{2,1,0:T(8,128)(2,1)}, u32[]{:S(2)}) copy-start(bf16[1,512,768]{2,1,0:T(8,128)(2,1)} %param.9) | copy-start | bytes 2359300
  0.6 0.9 %copy-start.3 = (f32[3072]{0:T(1024)S(1)}, f32[3072]{0:T(1024)}, u32[]{:S(2)}) copy-start(f32[3072]{0:T(1024)} %param.15) | copy-start | bytes 36868
  4.3 1.9 %collective-permute-start.1 = (bf16[128,1536]{1,0:T(8,128)(2,1)S(1)}, bf16[128,1536]{1,0:T(8,128)(2,1)S(1)}, u32[]{:S(2)}, u32[]{:S(2)}) collective-permute-start(bf16[128,1536]{1,0:T(8,128)(2,1)S(1)} %get-tuple-element.39), channel_id=1, source_target_pairs={{0,1},{1,0},{2,3},{3,2},{4,5},{5,4},{6,7},{7,6},{8,9},{9,8},{10,11... | collective-permute-start | bytes 1179656 | tf_op jit(solution)/shard_map/ppermute | solution.py:289
  4.8 1.4 %copy-start.1 = (bf16[1,512,3,384]{3,1,2,0:T(8,128)(2,1)S(1)}, bf16[1,512,3,384]{3,1,2,0:T(8,128)(2,1)}, u32[]{:S(2)}) copy-start(bf16[1,512,3,384]{3,1,2,0:T(8,128)(2,1)} %param.10) | copy-start | bytes 3538948
  5.7 6.1 %collective-permute-start = (bf16[128,1536]{1,0:T(8,128)(2,1)S(1)}, bf16[128,1536]{1,0:T(8,128)(2,1)S(1)}, u32[]{:S(2)}, u32[]{:S(2)}) collective-permute-start(bf16[128,1536]{1,0:T(8,128)(2,1)S(1)} %get-tuple-element.37), channel_id=1, source_target_pairs={{0,1},{1,0},{2,3},{3,2},{4,5},{5,4},{6,7},{7,6},{8,9},{9,8},{10,11... | collective-permute-start | bytes 1179656 | tf_op jit(solution)/shard_map/ppermute | solution.py:289
  6.3 44.2 %slice-start = ((s8[7077888]{0:T(1024)(128)(4,1)}), s8[4194304]{0:T(1024)(128)(4,1)S(1)}, s32[]{:S(2)}) async-start(s8[7077888]{0:T(1024)(128)(4,1)} %bitcast.10), calls=%async_computation | async-start | bytes 8388608
  7.7 4.0 %collective-permute-start.3 = (bf16[128,1536]{1,0:T(8,128)(2,1)S(1)}, bf16[128,1536]{1,0:T(8,128)(2,1)S(1)}, u32[]{:S(2)}, u32[]{:S(2)}) collective-permute-start(bf16[128,1536]{1,0:T(8,128)(2,1)S(1)} %get-tuple-element.43), channel_id=1, source_target_pairs={{0,1},{1,0},{2,3},{3,2},{4,5},{5,4},{6,7},{7,6},{8,9},{9,8},{10,11... | collective-permute-start | bytes 1179656 | tf_op jit(solution)/shard_map/ppermute | solution.py:289
  8.1 12.3 %collective-permute-start.2 = (bf16[128,1536]{1,0:T(8,128)(2,1)S(1)}, bf16[128,1536]{1,0:T(8,128)(2,1)S(1)}, u32[]{:S(2)}, u32[]{:S(2)}) collective-permute-start(bf16[128,1536]{1,0:T(8,128)(2,1)S(1)} %shard_map.106), channel_id=1, source_target_pairs={{0,2},{1,3},{2,0},{3,1},{4,6},{5,7},{6,4},{7,5},{8,10},{9,11},{10,... | collective-permute-start | bytes 1179656 | tf_op jit(solution)/shard_map/ppermute | solution.py:289
  11.6 8.8 %collective-permute-start.4 = (bf16[128,1536]{1,0:T(8,128)(2,1)S(1)}, bf16[128,1536]{1,0:T(8,128)(2,1)S(1)}, u32[]{:S(2)}, u32[]{:S(2)}) collective-permute-start(bf16[128,1536]{1,0:T(8,128)(2,1)S(1)} %get-tuple-element.44), channel_id=1, source_target_pairs={{0,1},{1,0},{2,3},{3,2},{4,5},{5,4},{6,7},{7,6},{8,9},{9,8},{10,11... | collective-permute-start | bytes 1179656 | tf_op jit(solution)/shard_map/ppermute | solution.py:289
  11.7 38.8 %slice-start.1 = ((s8[7077888]{0:T(1024)(128)(4,1)}), s8[2883584]{0:T(1024)(128)(4,1)S(1)}, s32[]{:S(2)}) async-start(s8[7077888]{0:T(1024)(128)(4,1)} %bitcast.10), calls=%async_computation.1 | async-start | bytes 5767168
  20.5 8.0 %collective-permute-start.8 = (bf16[32,1536]{1,0:T(8,128)(2,1)S(1)}, bf16[32,1536]{1,0:T(8,128)(2,1)S(1)}, u32[]{:S(2)}, u32[]{:S(2)}) collective-permute-start(bf16[32,1536]{1,0:T(8,128)(2,1)S(1)} %get-tuple-element.51), channel_id=1, source_target_pairs={{0,28},{1,21},{2,30},{3,23},{4,24},{5,17},{6,26},{7,19},{8,20},{9,... | collective-permute-start | bytes 294920 | tf_op jit(solution)/shard_map/ppermute | solution.py:335
  25.4 9.5 %collective-permute-start.6 = (bf16[128,1536]{1,0:T(8,128)(2,1)S(1)}, bf16[128,1536]{1,0:T(8,128)(2,1)S(1)}, u32[]{:S(2)}, u32[]{:S(2)}) collective-permute-start(bf16[128,1536]{1,0:T(8,128)(2,1)S(1)} %shard_map.109), channel_id=1, source_target_pairs={{0,2},{1,3},{2,0},{3,1},{4,6},{5,7},{6,4},{7,5},{8,10},{9,11},{10,... | collective-permute-start | bytes 1179656 | tf_op jit(solution)/shard_map/ppermute | solution.py:289
  26.9 6.7 %collective-permute-start.9 = (bf16[32,1536]{1,0:T(8,128)(2,1)S(1)}, bf16[32,1536]{1,0:T(8,128)(2,1)S(1)}, u32[]{:S(2)}, u32[]{:S(2)}) collective-permute-start(bf16[32,1536]{1,0:T(8,128)(2,1)S(1)} %get-tuple-element.52), channel_id=1, source_target_pairs={{0,16},{1,13},{2,18},{3,15},{4,20},{5,9},{6,22},{7,11},{8,24},{9,5... | collective-permute-start | bytes 294920 | tf_op jit(solution)/shard_map/ppermute | solution.py:335
  26.9 6.7 %collective-permute-start.10 = (bf16[32,1536]{1,0:T(8,128)(2,1)S(1)}, bf16[32,1536]{1,0:T(8,128)(2,1)S(1)}, u32[]{:S(2)}, u32[]{:S(2)}) collective-permute-start(bf16[32,1536]{1,0:T(8,128)(2,1)S(1)} %get-tuple-element.53), channel_id=1, source_target_pairs={{0,8},{1,25},{2,10},{3,27},{4,12},{5,29},{6,14},{7,31},{8,0},{9,17... | collective-permute-start | bytes 294920 | tf_op jit(solution)/shard_map/ppermute | solution.py:335
  27.7 22.8 %copy-start.4 = (f32[3072]{0:T(1024)S(1)}, f32[3072]{0:T(1024)}, u32[]{:S(2)}) copy-start(f32[3072]{0:T(1024)} %param.14) | copy-start | bytes 36868
  27.7 22.8 %copy-start.5 = (f32[3072]{0:T(1024)S(1)}, f32[3072]{0:T(1024)}, u32[]{:S(2)}) copy-start(f32[3072]{0:T(1024)} %param.13) | copy-start | bytes 36868
  27.7 22.8 %copy-start.6 = (f32[8,128]{1,0:T(8,128)S(1)}, f32[8,128]{1,0:T(8,128)}, u32[]{:S(2)}) copy-start(f32[8,128]{1,0:T(8,128)} %constant.5.clone.sin_ref) | copy-start | bytes 12292
  27.7 22.8 %copy-start.7 = (f32[8,128]{1,0:T(8,128)S(1)}, f32[8,128]{1,0:T(8,128)}, u32[]{:S(2)}) copy-start(f32[8,128]{1,0:T(8,128)} %constant.4.clone.cos_ref) | copy-start | bytes 12292
  27.7 6.0 %collective-permute-start.11 = (bf16[32,1536]{1,0:T(8,128)(2,1)S(1)}, bf16[32,1536]{1,0:T(8,128)(2,1)S(1)}, u32[]{:S(2)}, u32[]{:S(2)}) collective-permute-start(bf16[32,1536]{1,0:T(8,128)(2,1)S(1)} %get-tuple-element.54), channel_id=1, source_target_pairs={{0,0},{1,5},{2,2},{3,7},{4,4},{5,1},{6,6},{7,3},{8,8},{9,13},{10,1... | collective-permute-start | bytes 294920 | tf_op jit(solution)/shard_map/ppermute | solution.py:335
  33.7 9.9 %collective-permute-start.12 = (bf16[128,1536]{1,0:T(8,128)(2,1)S(1)}, bf16[128,1536]{1,0:T(8,128)(2,1)S(1)}, u32[]{:S(2)}, u32[]{:S(2)}) collective-permute-start(bf16[128,1536]{1,0:T(8,128)(2,1)S(1)} %constant_dynamic-update-slice_fusion.own_near), channel_id=1, source_target_pairs={{0,2},{1,3},{2,0},{3,1},{4,6},{5,7},{6,4},{7,5},{8,10},{9,11},{10,... | collective-permute-start | bytes 1179656 | tf_op jit(solution)/shard_map/ppermute | solution.py:289
  35.1 9.3 %collective-permute-start.15 = (bf16[32,1536]{1,0:T(8,128)(2,1)S(1)}, bf16[32,1536]{1,0:T(8,128)(2,1)S(1)}, u32[]{:S(2)}, u32[]{:S(2)}) collective-permute-start(bf16[32,1536]{1,0:T(8,128)(2,1)S(1)} %get-tuple-element.56), channel_id=1, source_target_pairs={{0,28},{1,21},{2,30},{3,23},{4,24},{5,17},{6,26},{7,19},{8,20},{9,... | collective-permute-start | bytes 294920 | tf_op jit(solution)/shard_map/ppermute | solution.py:335
  38.6 11.9 %collective-permute-start.13 = (bf16[128,1536]{1,0:T(8,128)(2,1)S(1)}, bf16[128,1536]{1,0:T(8,128)(2,1)S(1)}, u32[]{:S(2)}, u32[]{:S(2)}) collective-permute-start(bf16[128,1536]{1,0:T(8,128)(2,1)S(1)} %constant_dynamic-update-slice_fusion.own_near), channel_id=1, source_target_pairs={{0,1},{1,0},{2,3},{3,2},{4,5},{5,4},{6,7},{7,6},{8,9},{9,8},{10,11... | collective-permute-start | bytes 1179656 | tf_op jit(solution)/shard_map/ppermute | solution.py:289
  38.6 7.7 %collective-permute-start.16 = (bf16[32,1536]{1,0:T(8,128)(2,1)S(1)}, bf16[32,1536]{1,0:T(8,128)(2,1)S(1)}, u32[]{:S(2)}, u32[]{:S(2)}) collective-permute-start(bf16[32,1536]{1,0:T(8,128)(2,1)S(1)} %get-tuple-element.57), channel_id=1, source_target_pairs={{0,16},{1,13},{2,18},{3,15},{4,20},{5,9},{6,22},{7,11},{8,24},{9,5... | collective-permute-start | bytes 294920 | tf_op jit(solution)/shard_map/ppermute | solution.py:335
  38.6 7.7 %collective-permute-start.17 = (bf16[32,1536]{1,0:T(8,128)(2,1)S(1)}, bf16[32,1536]{1,0:T(8,128)(2,1)S(1)}, u32[]{:S(2)}, u32[]{:S(2)}) collective-permute-start(bf16[32,1536]{1,0:T(8,128)(2,1)S(1)} %get-tuple-element.58), channel_id=1, source_target_pairs={{0,8},{1,25},{2,10},{3,27},{4,12},{5,29},{6,14},{7,31},{8,0},{9,17... | collective-permute-start | bytes 294920 | tf_op jit(solution)/shard_map/ppermute | solution.py:335
  43.5 2.8 %collective-permute-start.18 = (bf16[32,1536]{1,0:T(8,128)(2,1)S(1)}, bf16[32,1536]{1,0:T(8,128)(2,1)S(1)}, u32[]{:S(2)}, u32[]{:S(2)}) collective-permute-start(bf16[32,1536]{1,0:T(8,128)(2,1)S(1)} %get-tuple-element.59), channel_id=1, source_target_pairs={{0,0},{1,5},{2,2},{3,7},{4,4},{5,1},{6,6},{7,3},{8,8},{9,13},{10,1... | collective-permute-start | bytes 294920 | tf_op jit(solution)/shard_map/ppermute | solution.py:335
  44.4 6.1 %collective-permute-start.14 = (bf16[128,1536]{1,0:T(8,128)(2,1)S(1)}, bf16[128,1536]{1,0:T(8,128)(2,1)S(1)}, u32[]{:S(2)}, u32[]{:S(2)}) collective-permute-start(bf16[128,1536]{1,0:T(8,128)(2,1)S(1)} %collective-permute-done.12.own_far), channel_id=1, source_target_pairs={{0,1},{1,0},{2,3},{3,2},{4,5},{5,4},{6,7},{7,6},{8,9},{9,8},{10,11... | collective-permute-start | bytes 1179656 | tf_op jit(solution)/shard_map/ppermute | solution.py:289
  46.4 11.5 %collective-permute-start.19 = (bf16[128,1536]{1,0:T(8,128)(2,1)S(1)}, bf16[128,1536]{1,0:T(8,128)(2,1)S(1)}, u32[]{:S(2)}, u32[]{:S(2)}) collective-permute-start(bf16[128,1536]{1,0:T(8,128)(2,1)S(1)} %constant_dynamic-update-slice_fusion.4.own_near), channel_id=1, source_target_pairs={{0,2},{1,3},{2,0},{3,1},{4,6},{5,7},{6,4},{7,5},{8,10},{9,11},{10,... | collective-permute-start | bytes 1179656 | tf_op jit(solution)/shard_map/ppermute | solution.py:289
  47.8 1.4 %collective-permute-start.5 = (bf16[128,768]{1,0:T(8,128)(2,1)S(1)}, bf16[128,768]{1,0:T(8,128)(2,1)S(1)}, u32[]{:S(2)}, u32[]{:S(2)}) collective-permute-start(bf16[128,768]{1,0:T(8,128)(2,1)S(1)} %get-tuple-element.47), channel_id=1, source_target_pairs={{0,1},{1,0},{2,3},{3,2},{4,5},{5,4},{6,7},{7,6},{8,9},{9,8},{10,11... | collective-permute-start | bytes 589832 | tf_op jit(solution)/shard_map/ppermute | solution.py:289
  47.8 1.7 %collective-permute-start.7 = (bf16[128,768]{1,0:T(8,128)(2,1)S(1)}, bf16[128,768]{1,0:T(8,128)(2,1)S(1)}, u32[]{:S(2)}, u32[]{:S(2)}) collective-permute-start(bf16[128,768]{1,0:T(8,128)(2,1)S(1)} %get-tuple-element.50), channel_id=1, source_target_pairs={{0,1},{1,0},{2,3},{3,2},{4,5},{5,4},{6,7},{7,6},{8,9},{9,8},{10,11... | collective-permute-start | bytes 589832 | tf_op jit(solution)/shard_map/ppermute | solution.py:289
  49.2 9.2 %collective-permute-start.20 = (bf16[128,1536]{1,0:T(8,128)(2,1)S(1)}, bf16[128,1536]{1,0:T(8,128)(2,1)S(1)}, u32[]{:S(2)}, u32[]{:S(2)}) collective-permute-start(bf16[128,1536]{1,0:T(8,128)(2,1)S(1)} %constant_dynamic-update-slice_fusion.4.own_near), channel_id=1, source_target_pairs={{0,1},{1,0},{2,3},{3,2},{4,5},{5,4},{6,7},{7,6},{8,9},{9,8},{10,11... | collective-permute-start | bytes 1179656 | tf_op jit(solution)/shard_map/ppermute | solution.py:289
  57.9 1.7 %collective-permute-start.21 = (bf16[128,1536]{1,0:T(8,128)(2,1)S(1)}, bf16[128,1536]{1,0:T(8,128)(2,1)S(1)}, u32[]{:S(2)}, u32[]{:S(2)}) collective-permute-start(bf16[128,1536]{1,0:T(8,128)(2,1)S(1)} %collective-permute-done.19.own_far), channel_id=1, source_target_pairs={{0,1},{1,0},{2,3},{3,2},{4,5},{5,4},{6,7},{7,6},{8,9},{9,8},{10,11... | collective-permute-start | bytes 1179656 | tf_op jit(solution)/shard_map/ppermute | solution.py:289
  57.9 7.2 %collective-permute-start.22 = (bf16[128,384]{1,0:T(8,128)(2,1)S(1)}, bf16[128,384]{1,0:T(8,128)(2,1)S(1)}, u32[]{:S(2)}, u32[]{:S(2)}) collective-permute-start(bf16[128,384]{1,0:T(8,128)(2,1)S(1)} %get-tuple-element.62), channel_id=1, source_target_pairs={{0,1},{1,0},{2,3},{3,2},{4,5},{5,4},{6,7},{7,6},{8,9},{9,8},{10,11... | collective-permute-start | bytes 294920 | tf_op jit(solution)/shard_map/ppermute | solution.py:289
  65.0 1.4 %collective-permute-start.23 = (bf16[128,384]{1,0:T(8,128)(2,1)S(1)}, bf16[128,384]{1,0:T(8,128)(2,1)S(1)}, u32[]{:S(2)}, u32[]{:S(2)}) collective-permute-start(bf16[128,384]{1,0:T(8,128)(2,1)S(1)} %get-tuple-element.63), channel_id=1, source_target_pairs={{0,1},{1,0},{2,3},{3,2},{4,5},{5,4},{6,7},{7,6},{8,9},{9,8},{10,11... | collective-permute-start | bytes 294920 | tf_op jit(solution)/shard_map/ppermute | solution.py:289
  66.4 8.0 %collective-permute-start.24 = (bf16[128,384]{1,0:T(8,128)(2,1)S(1)}, bf16[128,384]{1,0:T(8,128)(2,1)S(1)}, u32[]{:S(2)}, u32[]{:S(2)}) collective-permute-start(bf16[128,384]{1,0:T(8,128)(2,1)S(1)} %get-tuple-element.64), channel_id=1, source_target_pairs={{0,28},{1,21},{2,30},{3,23},{4,24},{5,17},{6,26},{7,19},{8,20},{9,... | collective-permute-start | bytes 294920 | tf_op jit(solution)/shard_map/ppermute | solution.py:335
  69.2 10.4 %collective-permute-start.25 = (bf16[128,384]{1,0:T(8,128)(2,1)S(1)}, bf16[128,384]{1,0:T(8,128)(2,1)S(1)}, u32[]{:S(2)}, u32[]{:S(2)}) collective-permute-start(bf16[128,384]{1,0:T(8,128)(2,1)S(1)} %get-tuple-element.65), channel_id=1, source_target_pairs={{0,16},{1,13},{2,18},{3,15},{4,20},{5,9},{6,22},{7,11},{8,24},{9,5... | collective-permute-start | bytes 294920 | tf_op jit(solution)/shard_map/ppermute | solution.py:335
  70.2 9.3 %collective-permute-start.26 = (bf16[128,384]{1,0:T(8,128)(2,1)S(1)}, bf16[128,384]{1,0:T(8,128)(2,1)S(1)}, u32[]{:S(2)}, u32[]{:S(2)}) collective-permute-start(bf16[128,384]{1,0:T(8,128)(2,1)S(1)} %get-tuple-element.66), channel_id=1, source_target_pairs={{0,8},{1,25},{2,10},{3,27},{4,12},{5,29},{6,14},{7,31},{8,0},{9,17... | collective-permute-start | bytes 294920 | tf_op jit(solution)/shard_map/ppermute | solution.py:335
  71.8 7.7 %collective-permute-start.27 = (bf16[128,384]{1,0:T(8,128)(2,1)S(1)}, bf16[128,384]{1,0:T(8,128)(2,1)S(1)}, u32[]{:S(2)}, u32[]{:S(2)}) collective-permute-start(bf16[128,384]{1,0:T(8,128)(2,1)S(1)} %get-tuple-element.67), channel_id=1, source_target_pairs={{0,0},{1,5},{2,2},{3,7},{4,4},{5,1},{6,6},{7,3},{8,8},{9,13},{10,1... | collective-permute-start | bytes 294920 | tf_op jit(solution)/shard_map/ppermute | solution.py:335
  79.6 1.5 %collective-permute-start.28 = (bf16[256,384]{1,0:T(8,128)(2,1)S(1)}, bf16[256,384]{1,0:T(8,128)(2,1)S(1)}, u32[]{:S(2)}, u32[]{:S(2)}) collective-permute-start(bf16[256,384]{1,0:T(8,128)(2,1)S(1)} %shard_map.116), channel_id=1, source_target_pairs={{0,1},{1,0},{2,3},{3,2},{4,5},{5,4},{6,7},{7,6},{8,9},{9,8},{10,11... | collective-permute-start | bytes 589832 | tf_op jit(solution)/shard_map/ppermute | solution.py:289

commit v4 on v3

--- a/solution.py
+++ b/solution.py
@@ -42,76 +42,102 @@
     return lax.dot_general(a, b, (((1,), (1,)), ((), ())), preferred_element_type=jnp.float32)
 
 
-def attend(query, key, value, same=None):
-    logits = dot_nt(query, key)
+def attend(heads, same=None):
+    logits = [dot_nt(query, key) for query, key, _ in heads]
     if same is not None:
-        logits = jnp.where(same, logits, MASKED)
-    top = jnp.max(logits, axis=-1, keepdims=True)
-    weights = jnp.exp2((logits - top) * EXP2_SCALE)
-    total = jnp.sum(weights, axis=-1, keepdims=True)
-    return (dot(weights.astype(jnp.bfloat16), value) / total).astype(jnp.bfloat16)
-
-
-def project_and_mix(parts, frame_of, write, w_ref, gain_ref, shift_ref, cos_ref, sin_ref, normed_ref, proj_ref):
-    features, width = w_ref.shape[1:]
+        logits = [jnp.where(same, one, MASKED) for one in logits]
+    tops = [jnp.max(one, axis=-1, keepdims=True) for one in logits]
+    weights = [jnp.exp2((one - top) * EXP2_SCALE) for one, top in zip(logits, tops)]
+    rates = [1.0 / jnp.sum(one, axis=-1, keepdims=True) for one in weights]
+    return [
+        (dot(one.astype(jnp.bfloat16), value) * rate).astype(jnp.bfloat16)
+        for one, (_, _, value), rate in zip(weights, heads, rates)
+    ]
+
+
+def normalize(blocks, gain_ref, shift_ref, out_ref):
+    features = out_ref.shape[-1]
+    total, square = 0.0, 0.0
+    for ref, _ in blocks:
+        values = ref[...].astype(jnp.float32)
+        total += jnp.sum(values, axis=-1, keepdims=True)
+        square += jnp.sum(values * values, axis=-1, keepdims=True)
+    mean = total / features
+    rate = lax.rsqrt(square / features - mean * mean + EPSILON)
+    for ref, start in blocks:
+        lanes = pl.ds(start, ref.shape[-1])
+        gain = 1.0 + gain_ref[:, lanes]
+        out_ref[:, lanes] = (
+            (ref[...].astype(jnp.float32) - mean) * rate * gain + shift_ref[:, lanes]
+        ).astype(out_ref.dtype)
+
+
+def project_and_mix(normed_refs, frame_of, write, w_ref, cos_ref, sin_ref, proj_ref):
     frames = cos_ref.shape[0]
-    rows = normed_ref.shape[0]
+    width = w_ref.shape[-1] // 3
+    rows = proj_ref.shape[0]
     count = rows // frames
     first = 0
-    for part in parts:
-        size = part[0][0].shape[0]
-        total = jnp.zeros((size, 1), jnp.float32)
-        square = jnp.zeros((size, 1), jnp.float32)
-        for ref, _ in part:
-            values = ref[...].astype(jnp.float32)
-            total += jnp.sum(values, axis=-1, keepdims=True)
-            square += jnp.sum(values * values, axis=-1, keepdims=True)
-        mean = total / features
-        rate = lax.rsqrt(square / features - mean * mean + EPSILON)
-        for ref, start in part:
-            lanes = pl.ds(start, ref.shape[-1])
-            gain = 1.0 + gain_ref[:, lanes]
-            normed_ref[first : first + size, lanes] = (
-                (ref[...].astype(jnp.float32) - mean) * rate * gain + shift_ref[:, lanes]
-            ).astype(normed_ref.dtype)
-        first += size
-    for part in range(3):
-        acc = dot(normed_ref[...], w_ref[part])
-        if part == 2:
-            proj_ref[part] = acc.astype(proj_ref.dtype)
-            continue
-        for f in range(frames):
-            row = pl.ds(frame_of(f), 1)
+    for ref in normed_refs:
+        size = ref.shape[0]
+        acc = dot(ref[...], w_ref[...])
+        span = slice(first, first + size)
+        proj_ref[span, 2 * width :] = acc[:, 2 * width :].astype(proj_ref.dtype)
+        for low in range(0, size, count):
+            row = pl.ds(frame_of((first + low) // count), 1)
             cosine, sine = cos_ref[row, :], sin_ref[row, :]
-            span = slice(f * count, (f + 1) * count)
-            for lane in range(0, width, HEAD_DIM):
-                head = acc[span, lane : lane + HEAD_DIM]
+            for lane in range(0, 2 * width, HEAD_DIM):
+                head = acc[low : low + count, lane : lane + HEAD_DIM]
                 turned = pltpu.roll(head, HEAD_DIM // 2, 1)
-                proj_ref[part, span, lane : lane + HEAD_DIM] = (
+                proj_ref[first + low : first + low + count, lane : lane + HEAD_DIM] = (
                     head * cosine + turned * sine
                 ).astype(proj_ref.dtype)
+        first += size
     step = GROUP if count % GROUP == 0 else count
     size = step * frames
     patch_of = lambda axis: lax.rem(lax.broadcasted_iota(jnp.int32, (size, size), axis), step)
     same = patch_of(0) == patch_of(1)
-    for low in range(0, count, step):
-        for lane in range(0, width, HEAD_DIM):
-            head = slice(lane, lane + HEAD_DIM)
-
-            def gathered(part):
-                if step == count:
-                    return proj_ref[part, :, head]
-                return jnp.concatenate(
-                    [
-                        proj_ref[part, f * count + low : f * count + low + step, head]
-                        for f in range(frames)
-                    ],
-                    axis=0,
-                )
-
-            mixed = attend(gathered(0), gathered(1), gathered(2), same)
-            for f in range(frames):
-                write(f, low, head, mixed[f * step : (f + 1) * step])
+    lanes = range(0, width, HEAD_DIM)
+
+    def gathered(low, lane):
+        head = slice(lane, lane + HEAD_DIM)
+        if step == count:
+            return proj_ref[:, head]
+        spans = [slice(f * count + low, f * count + low + step) for f in range(frames)]
+        return jnp.concatenate([proj_ref[span, head] for span in spans], axis=0)
+
+    units = [(low, lane) for low in range(0, count, step) for lane in lanes]
+    heads = [tuple(gathered(low, part * width + lane) for part in range(3)) for low, lane in units]
+    for (low, lane), mixed in zip(units, attend(heads, same)):
+        for f in range(frames):
+            write(f, low, slice(lane, lane + HEAD_DIM), mixed[f * step : (f + 1) * step])
+
+
+def hold_kernel(w_far, out_ref, semaphores):
+    width = w_far.shape[-1]
+    copies = [
+        pltpu.make_async_copy(
+            w_far.at[part], out_ref.at[:, part * width : (part + 1) * width], semaphores.at[part]
+        )
+        for part in range(3)
+    ]
+    for copy in copies:
+        copy.start()
+    for copy in copies:
+        copy.wait()
+
+
+def hold_weights(temporal_qkv):
+    features, parts, width = temporal_qkv.shape
+    return pl.pallas_call(
+        hold_kernel,
+        out_shape=pltpu.VMEM((features, parts * width), temporal_qkv.dtype),
+        in_specs=[pl.BlockSpec(memory_space=pltpu.HBM)],
+        out_specs=pl.BlockSpec(memory_space=pltpu.VMEM),
+        scratch_shapes=[pltpu.SemaphoreType.DMA((parts,))],
+        compiler_params=pltpu.CompilerParams(vmem_limit_bytes=1024 * 1024),
+        cost_estimate=pl.CostEstimate(flops=0, bytes_accessed=0, transcendentals=0),
+    )(in_hbm(temporal_qkv.transpose(1, 0, 2)))
 
 
 def core_of():
@@ -143,32 +169,42 @@
     return pl.ds(pl.multiple_of((chip_of() ^ flip) * half, half), half)
 
 
-def spatial_body(qkv_ref, far_w_ref, far_gate, heads_ref, message_ref, first, before_message):
+def spatial_body(qkv_ref, far_w_ref, heads_ref, message_ref, first, far_gate):
     rows, width = heads_ref.shape
     for lane in range(0, width, HEAD_DIM):
         head = slice(lane, lane + HEAD_DIM)
         query = piece_rows(qkv_ref.at[0], first, rows // (2 * SHARES), head)
-        heads_ref[:, head] = attend(query, qkv_ref[1, :, head], qkv_ref[2, :, head])
-    before_message()
-    message_ref[...] = (dot(heads_ref[rows // 2 :, :], far_w_ref[...]) * far_gate).astype(
-        message_ref.dtype
-    )
+        (heads_ref[:, head],) = attend([(query, qkv_ref[1, :, head], qkv_ref[2, :, head])])
+    gate = far_gate()
+    term = dot(heads_ref[rows // 2 :, :], far_w_ref[...])
+    message_ref[...] = (term * gate).astype(message_ref.dtype)
 
 
 def first_spatial_kernel(
-    gate_ref, qkv_far, w_far, heads_ref, message_ref, qkv_ref, w_ref, semaphores, *, first
+    qkv_far, w_far, gate_far, residual_far,
+    heads_ref, message_ref, qkv_ref, w_ref, gate_ref, residual_ref, semaphores, *, first
 ):
-    columns = chip_columns(w_far.shape[-1], 1)
-    copies = [
-        pltpu.make_async_copy(qkv_far, qkv_ref, semaphores.at[0]),
-        pltpu.make_async_copy(w_far.at[:, columns], w_ref, semaphores.at[1]),
+    far, near = (chip_columns(w_far.shape[-1], flip) for flip in (1, 0))
+    moves = [
+        (qkv_far, qkv_ref),
+        (w_far.at[:, far], w_ref.at[:, far]),
+        (gate_far, gate_ref),
+        (w_far.at[:, near], w_ref.at[:, near]),
+        (residual_far, residual_ref),
     ]
+    copies = [pltpu.make_async_copy(*move, semaphores.at[i]) for i, move in enumerate(moves)]
     for copy in copies:
         copy.start()
     copies[0].wait()
-    spatial_body(
-        qkv_ref, w_ref, gate_ref[:, columns], heads_ref, message_ref, first, copies[1].wait
-    )
+
+    def far_gate():
+        copies[1].wait()
+        copies[2].wait()
+        return gate_ref[:, far]
+
+    spatial_body(qkv_ref, w_ref.at[:, far], heads_ref, message_ref, first, far_gate)
+    copies[3].wait()
+    copies[4].wait()
 
 
 def spatial_kernel(gate_ref, qkv_ref, w_ref, heads_ref, message_ref, *, first):
@@ -176,11 +212,10 @@
     spatial_body(
         qkv_ref,
         w_ref.at[:, columns],
-        gate_ref[:, columns],
         heads_ref,
         message_ref,
         first,
-        lambda: None,
+        lambda: gate_ref[:, columns],
     )
 
 
@@ -222,9 +257,23 @@
     other_ref[...] = jnp.where(core == 0, right, left)
 
 
-def split_temporal_kernel(own_near, own_far, other_near, other_far, w_ref, gain_ref, shift_ref, cos_ref, sin_ref, own_ref, other_ref, *scratch):
-    half = own_near.shape[-1]
-    near, far = (pl.multiple_of((chip_of() ^ flip) * half, half) for flip in range(2))
+def split_blocks(near_ref, far_ref):
+    half = near_ref.shape[-1]
+    return [
+        (ref, pl.multiple_of((chip_of() ^ flip) * half, half))
+        for flip, ref in enumerate((near_ref, far_ref))
+    ]
+
+
+def split_norm_kernel(near_ref, far_ref, gain_ref, shift_ref, out_ref):
+    normalize(split_blocks(near_ref, far_ref), gain_ref, shift_ref, out_ref)
+
+
+def split_temporal_kernel(
+    own_normed_ref, near_ref, far_ref, gain_ref, shift_ref, w_ref, cos_ref, sin_ref,
+    own_ref, other_ref, normed_ref, proj_ref,
+):
+    normalize(split_blocks(near_ref, far_ref), gain_ref, shift_ref, normed_ref)
     count = own_ref.shape[0] // SHARES
 
     def write(i, low, head, value):
@@ -233,15 +282,7 @@
         ref[start : start + value.shape[0], head] = value
 
     project_and_mix(
-        [[(own_near, near), (own_far, far)], [(other_near, near), (other_far, far)]],
-        frame_of,
-        write,
-        w_ref,
-        gain_ref,
-        shift_ref,
-        cos_ref,
-        sin_ref,
-        *scratch,
+        [own_normed_ref, normed_ref], frame_of, write, w_ref, cos_ref, sin_ref, proj_ref
     )
 
 
@@ -307,6 +348,10 @@
     ]
 
 
+def in_hbm(array):
+    return pltpu.with_memory_space_constraint(array, pltpu.HBM)
+
+
 def after(value, *others):
     return lax.optimization_barrier((value,) + others)[0]
 
@@ -322,7 +367,7 @@
     bf16, f32 = jnp.bfloat16, jnp.float32
     flat_residual = residual.reshape(tokens, share)
     qkv = spatial_qkv.transpose(2, 0, 1, 3).reshape(3, tokens, width)
-    weights = temporal_qkv.transpose(1, 0, 2)
+    weights = hold_weights(temporal_qkv)
     gate_row = gate.reshape(1, features)
     gain_row, shift_row = scale.reshape(1, features), shift.reshape(1, features)
     cosine, sine = rotation_tables(n_seq)
@@ -347,17 +392,16 @@
     for first, rows in chunks:
         half = rows // 2
         if previous is None:
-            heads, message = call(
+            operands = (qkv, spatial_out, gate_row, flat_residual)
+            heads, message, *operands = call(
                 functools.partial(first_spatial_kernel, first=first),
-                [shape(rows, width), shape(half, both)],
-                inputs=3,
-                far=2,
-                scratch=(
-                    pltpu.VMEM((3, tokens, width), bf16),
-                    pltpu.VMEM((width, both), bf16),
-                    pltpu.SemaphoreType.DMA((2,)),
-                ),
-            )(gate_row, *(pltpu.with_memory_space_constraint(a, pltpu.HBM) for a in (qkv, spatial_out)))
+                [shape(rows, width), shape(half, both)]
+                + [pltpu.VMEM(one.shape, one.dtype) for one in operands],
+                inputs=len(operands),
+                far=len(operands),
+                scratch=(pltpu.SemaphoreType.DMA((len(operands) + 1,)),),
+            )(*(in_hbm(one) for one in operands))
+            qkv, spatial_out, gate_row, flat_residual = operands
         else:
             heads, message = call(
                 functools.partial(spatial_kernel, first=first),
@@ -375,17 +419,26 @@
         reduced.append((base, swap(near_message, "mlp", n_mlp, 1), sent))
 
     arrivals = [swap(sent, "mlp", n_mlp, 2) for _, _, sent in reduced]
-    arrivals[0] = after(arrivals[0], previous, *(message for _, message, _ in reduced))
-    nears, blocks = [], []
-    for (first, rows), (base, near_message, _), arrived in zip(chunks, reduced, arrivals):
+    arrivals[0] = after(arrivals[0], previous, weights, *(message for _, message, _ in reduced))
+    blocks, pieces = [], []
+    for index, ((first, rows), (base, near_message, _)) in enumerate(zip(chunks, reduced)):
         half = rows // 2
-        own, other, *pieces = call(
+        own, other, *sends = call(
             update_kernel,
             [shape(half, share)] * 2 + [shape(half // SHARES, both)] * SHARES,
+            flops=1e10 * index,
             inputs=3,
-        )(base, near_message, arrived)
+        )(base, near_message, arrivals[index])
         blocks += [own, swap(other, "mlp", n_mlp, 1)]
-        nears.append(jnp.concatenate(send_pieces(pieces), axis=0))
+        pieces.append(sends)
+    nears = []
+    for index, sends in enumerate(pieces):
+        received = send_pieces(sends)
+        if index + 1 < len(pieces):
+            received[0], pieces[index + 1][0] = lax.optimization_barrier(
+                (received[0], pieces[index + 1][0])
+            )
+        nears.append(jnp.concatenate(received, axis=0))
 
     own_mixed, other_mixed = [], []
     for (first, rows), near in zip(chunks, nears):
@@ -400,12 +453,15 @@
             )(*blocks)
             far = after(far, own_mixed[-1], updated)
         other_far = swap(far, "mlp", n_mlp, 1)
+        own_normed = call(split_norm_kernel, shape(half, features), inputs=4)(
+            near, far, gain_row, shift_row
+        )
         own, other = call(
             split_temporal_kernel,
             [shape(half, width)] * 2,
-            inputs=9,
-            scratch=(pltpu.VMEM((rows, features), bf16), pltpu.VMEM((3, rows, width), bf16)),
-        )(near, far, other_near, other_far, weights, gain_row, shift_row, cosine, sine)
+            inputs=8,
+            scratch=(pltpu.VMEM((half, features), bf16), pltpu.VMEM((rows, 3 * width), bf16)),
+        )(own_normed, other_near, other_far, gain_row, shift_row, weights, cosine, sine)
         own_mixed.append(own)
         other_mixed.append(swap(other, "mlp", n_mlp, 1))
     packed = call(
@@ -425,7 +481,7 @@
 def heads_kernel(qkv_ref, out_ref):
     for lane in range(0, out_ref.shape[-1], HEAD_DIM):
         head = slice(lane, lane + HEAD_DIM)
-        out_ref[:, head] = attend(qkv_ref[0, :, head], qkv_ref[1, :, head], qkv_ref[2, :, head])
+        (out_ref[:, head],) = attend([tuple(qkv_ref[part, :, head] for part in range(3))])
 
 
 def columns_kernel(own_ref, other_ref, own_w_ref, other_w_ref, gate_ref, out_ref):
@@ -433,20 +489,22 @@
     out_ref[...] = (term * gate_ref[...]).astype(out_ref.dtype)
 
 
-def temporal_kernel(u0, u1, u2, u3, *refs):
-    *refs, out_ref, normed_ref, proj_ref = refs
+def temporal_kernel(
+    u0, u1, u2, u3, gain_ref, shift_ref, w_ref, cos_ref, sin_ref, out_ref, normed_ref, proj_ref
+):
     share = u0.shape[-1]
-    count = out_ref.shape[0] // refs[-1].shape[0]
-    part = [
+    count = out_ref.shape[0] // cos_ref.shape[0]
+    blocks = [
         (ref, pl.multiple_of((lax.axis_index("mlp") ^ k) * share, share))
         for k, ref in enumerate((u0, u1, u2, u3))
     ]
+    normalize(blocks, gain_ref, shift_ref, normed_ref)
 
     def write(f, low, head, value):
         start = f * count + low
         out_ref[start : start + value.shape[0], head] = value
 
-    project_and_mix([part], lambda f: f, write, *refs, normed_ref, proj_ref)
+    project_and_mix([normed_ref], lambda f: f, write, w_ref, cos_ref, sin_ref, proj_ref)
 
 
 def on_device(
@@ -485,15 +543,15 @@
         temporal_kernel,
         jax.ShapeDtypeStruct((rows, width), bf16),
         inputs=9,
-        scratch=(pltpu.VMEM((rows, features), bf16), pltpu.VMEM((3, rows, width), bf16)),
+        scratch=(pltpu.VMEM((rows, features), bf16), pltpu.VMEM((rows, 3 * width), bf16)),
     )(
         mine,
         swap(mine, "mlp", n_mlp, 1),
         across,
         swap(across, "mlp", n_mlp, 1),
-        temporal_qkv.transpose(1, 0, 2),
         scale.reshape(1, features),
         shift.reshape(1, features),
+        hold_weights(temporal_qkv),
         *rotation_tables(n_seq),
     )
     result = lax.all_to_all(

time: 82.1 us -> 78.2 us (0.952)
  waiting for transfers between devices: 33.8 us -> 28 us
  starting transfers between devices: 27.4 us -> 30.2 us
  local copies, waits for them, and re-layouts: 0.95 us -> 0.09 us
    ppermute x12, waiting for transfers between devices: 13.8 us -> 10.7 us  [send_pieces(): lax.ppermute(piece, ('seq', 'mlp'), piece_pairs(n_seq, n_mlp, i))]
    ppermute x12, starting transfers between devices: 17.8 us -> 21 us  [send_pieces(): lax.ppermute(piece, ('seq', 'mlp'), piece_pairs(n_seq, n_mlp, i))]
    ppermute x17, waiting for transfers between devices: 20 us -> 17.3 us  [swap(): return lax.ppermute(value, axis, [(i, i ^ k) for i in range(size)])]
    unnamed x26 -> x14, local copies, waits for them, and re-layouts: 0.93 us -> 0.07 us
    pallas_call x2 -> x5, Pallas kernels: 10.6 us -> 10.7 us  [the longest x2 6.41 us: split_on_device(): call(split_temporal_kernel, [shape(half, width)] * 2, inputs=8, scratch=(...]
where the time goes in v4:
time: 78.2 us; the launch traced here: 78 us
  starting transfers between devices  30.2 us (39%)
  waiting for transfers between devices  28 us (36%)
  Pallas kernels  18.8 us (24%)
  between operations  0.92 us (1%)
    ppermute x12, starting transfers between devices, send_pieces(): lax.ppermute(piece, ('seq', 'mlp'), piece_pairs(n_seq, n_mlp, i))  21 us
    ppermute x17, waiting for transfers between devices, swap(): return lax.ppermute(value, axis, [(i, i ^ k) for i in range(size)])  17.3 us
    ppermute x12, waiting for transfers between devices, send_pieces(): lax.ppermute(piece, ('seq', 'mlp'), piece_pairs(n_seq, n_mlp, i))  10.7 us
    ppermute x17, starting transfers between devices, swap(): return lax.ppermute(value, axis, [(i, i ^ k) for i in range(size)])  9.24 us
    pallas_call x2, Pallas kernels, split_on_device(): call(split_temporal_kernel, [shape(half, width)] * 2, inputs=8, scratch=(...  6.41 us
    pallas_call x1, Pallas kernels, hold_weights(): pl.pallas_call(hold_kernel, out_shape=pltpu.VMEM((features, parts * width...  3.12 us
    pallas_call x1, Pallas kernels, split_on_device(): call(functools.partial(first_spatial_kernel, first=first), [shape(rows, w...  2.77 us
    pallas_call x2, Pallas kernels, split_on_device(): call(functools.partial(terms_kernel, first=first), [shape(half, both, f32...  1.64 us
  transfers between devices with their start and end apart: 29, of which 14 were waited for; matrix products, arithmetic and copies ran while one was open for 0% of the time, Pallas kernels for 18%

profile of v4, /device:TPU:0, one launch (start us, length us, event | category | flops | bytes accessed | tf_op | source)
XLA Modules:
  0.0 78.0 jit_solution(12719924924134064314)
XLA Ops:
  0.6 2.8 %shard_map.104 = (bf16[256,384]{1,0:T(8,128)(2,1)S(1)}, bf16[128,1536]{1,0:T(8,128)(2,1)S(1)}, bf16[3,512,384]{2,1,0:T(8,128)(2,1)S(1)}, bf16[384,3072]{1,0:T(8,...) custom-call(bf16[3,512,384]{2,1,0:T(8,128)(2,1)} %bitcast.19, bf16[384,3072]{1,0:T(8,128)(2,1)} %w_far.1, ...), custom_call_target="tpu_custom_call" | custom-call | tf_op jit(solution)/shard_map/pallas_call | solution.py:396
  3.4 0.5 collective-permute-start.1
  3.9 0.8 %shard_map.105 = (f32[128,1536]{1,0:T(8,128)S(1)}, f32[128,1536]{1,0:T(8,128)S(1)}, bf16[128,1536]{1,0:T(8,128)(2,1)S(1)}) custom-call(bf16[256,384]{1,0:T(8,128)(2,1)S(1)} %get-tuple-element.41.heads_ref, bf16[384,3072]{1,0:T(8,128)(2,1)S(1)} %get-tuple-element.42.w_ref, f32[1,3072]{1,0:T(1,128)S(1)} %get-tuple-element.43.gate_ref, ...), custom_call_target="tpu_custom_call" | custom-call | tf_op jit(solution)/shard_map/pallas_call | solution.py:412
  4.8 0.5 collective-permute-done.1.b_ref
  5.3 0.1 shard_map.106
  5.3 1.4 %shard_map.107 = (bf16[256,384]{1,0:T(8,128)(2,1)S(1)}, bf16[128,1536]{1,0:T(8,128)(2,1)S(1)}) custom-call(f32[1,3072]{1,0:T(1,128)S(1)} %get-tuple-element.43.gate_ref, bf16[3,512,384]{2,1,0:T(8,128)(2,1)S(1)} %get-tuple-element.50.qkv_ref, bf16[384,3072]{1,0:T(8,128)(2,1)S(1)} %get-tuple-element.42.w_ref), custom_call_target="tpu_custom_call" | custom-call | tf_op jit(solution)/shard_map/pallas_call | solution.py:406
  6.7 0.4 collective-permute-start.3
  7.2 0.1 collective-permute-start
  7.3 0.8 %shard_map.108 = (f32[128,1536]{1,0:T(8,128)S(1)}, f32[128,1536]{1,0:T(8,128)S(1)}, bf16[128,1536]{1,0:T(8,128)(2,1)S(1)}) custom-call(bf16[256,384]{1,0:T(8,128)(2,1)S(1)} %get-tuple-element.51.heads_ref, bf16[384,3072]{1,0:T(8,128)(2,1)S(1)} %get-tuple-element.42.w_ref, f32[1,3072]{1,0:T(1,128)S(1)} %get-tuple-element.43.gate_ref, ...), custom_call_target="tpu_custom_call" | custom-call | tf_op jit(solution)/shard_map/pallas_call | solution.py:412
  8.1 0.4 collective-permute-start.4
  8.5 2.7 %collective-permute-start.2 = (bf16[128,1536]{1,0:T(8,128)(2,1)S(1)}, bf16[128,1536]{1,0:T(8,128)(2,1)S(1)}, u32[]{:S(2)}, u32[]{:S(2)}) collective-permute-start(bf16[128,1536]{1,0:T(8,128)(2,1)S(1)} %shard_map.106), channel_id=1, source_target_pairs={{0,2},{1,3},{2,0},{3,1},{4,6},{5,7},{6,4},{7,5},{8,10},{9,11},{10,... | collective-permute-start | bytes 1179656 | tf_op jit(solution)/shard_map/ppermute | solution.py:330
  11.2 0.0 collective-permute-done.3.b_ref
  11.2 0.1 shard_map.109
  11.3 0.2 collective-permute-start.6
  11.5 3.1 %shard_map.110.w_ref = bf16[3072,1152]{1,0:T(8,128)(2,1)S(1)} custom-call(bf16[3,3072,384]{2,1,0:T(8,128)(2,1)} %bitcast.18), custom_call_target="tpu_custom_call" | custom-call | tf_op jit(solution)/shard_map/pallas_call | solution.py:132
  14.7 0.0 collective-permute-done.message_ref
  14.7 0.0 collective-permute-done.4.message_ref
  14.7 6.4 %collective-permute-done.2.arrived_ref = bf16[128,1536]{1,0:T(8,128)(2,1)S(1)} collective-permute-done((bf16[128,1536]{1,0:T(8,128)(2,1)S(1)}, bf16[128,1536]{1,0:T(8,128)(2,1)S(1)}, u32[]{:S(2)}, u32[]{:S(2)}) %collective-permute-start.2) | collective-permute-done | bytes 393248 | tf_op jit(solution)/shard_map/ppermute | solution.py:330
  21.1 0.2 shard_map.111
  21.3 5.1 %collective-permute-start.8 = (bf16[32,1536]{1,0:T(8,128)(2,1)S(1)}, bf16[32,1536]{1,0:T(8,128)(2,1)S(1)}, u32[]{:S(2)}, u32[]{:S(2)}) collective-permute-start(bf16[32,1536]{1,0:T(8,128)(2,1)S(1)} %get-tuple-element.61), channel_id=1, source_target_pairs={{0,28},{1,21},{2,30},{3,23},{4,24},{5,17},{6,26},{7,19},{8,20},{9,... | collective-permute-start | bytes 294920 | tf_op jit(solution)/shard_map/ppermute | solution.py:380
  26.4 0.0 collective-permute-start.9
  26.4 0.8 %collective-permute-start.10 = (bf16[32,1536]{1,0:T(8,128)(2,1)S(1)}, bf16[32,1536]{1,0:T(8,128)(2,1)S(1)}, u32[]{:S(2)}, u32[]{:S(2)}) collective-permute-start(bf16[32,1536]{1,0:T(8,128)(2,1)S(1)} %get-tuple-element.65), channel_id=1, source_target_pairs={{0,8},{1,25},{2,10},{3,27},{4,12},{5,29},{6,14},{7,31},{8,0},{9,17... | collective-permute-start | bytes 294920 | tf_op jit(solution)/shard_map/ppermute | solution.py:380
  27.2 0.7 collective-permute-start.11
  27.9 1.4 %collective-permute-done.6.arrived_ref = bf16[128,1536]{1,0:T(8,128)(2,1)S(1)} collective-permute-done((bf16[128,1536]{1,0:T(8,128)(2,1)S(1)}, bf16[128,1536]{1,0:T(8,128)(2,1)S(1)}, u32[]{:S(2)}, u32[]{:S(2)}) %collective-permute-start.6) | collective-permute-done | bytes 393248 | tf_op jit(solution)/shard_map/ppermute | solution.py:330
  29.3 0.2 shard_map.112
  29.4 0.0 copy-start
  29.5 0.0 copy-start.1
  29.5 0.2 collective-permute-done.8
  29.7 4.7 %collective-permute-start.15 = (bf16[32,1536]{1,0:T(8,128)(2,1)S(1)}, bf16[32,1536]{1,0:T(8,128)(2,1)S(1)}, u32[]{:S(2)}, u32[]{:S(2)}) collective-permute-start(bf16[32,1536]{1,0:T(8,128)(2,1)S(1)} %get-tuple-element.68), channel_id=1, source_target_pairs={{0,28},{1,21},{2,30},{3,23},{4,24},{5,17},{6,26},{7,19},{8,20},{9,... | collective-permute-start | bytes 294920 | tf_op jit(solution)/shard_map/ppermute | solution.py:380
  34.4 0.0 collective-permute-done.9
  34.5 0.0 collective-permute-done.11
  34.5 0.1 collective-permute-start.13
  34.6 1.6 %collective-permute-start.12 = (bf16[128,1536]{1,0:T(8,128)(2,1)S(1)}, bf16[128,1536]{1,0:T(8,128)(2,1)S(1)}, u32[]{:S(2)}, u32[]{:S(2)}) collective-permute-start(bf16[128,1536]{1,0:T(8,128)(2,1)S(1)} %constant_dynamic-update-slice_fusion.near_ref), channel_id=1, source_target_pairs={{0,2},{1,3},{2,0},{3,1},{4,6},{5,7},{6,4},{7,5},{8,10},{9,11},{10,... | collective-permute-start | bytes 1179656 | tf_op jit(solution)/shard_map/ppermute | solution.py:330
  36.2 1.5 %collective-permute-start.16 = (bf16[32,1536]{1,0:T(8,128)(2,1)S(1)}, bf16[32,1536]{1,0:T(8,128)(2,1)S(1)}, u32[]{:S(2)}, u32[]{:S(2)}) collective-permute-start(bf16[32,1536]{1,0:T(8,128)(2,1)S(1)} %get-tuple-element.69), channel_id=1, source_target_pairs={{0,16},{1,13},{2,18},{3,15},{4,20},{5,9},{6,22},{7,11},{8,24},{9,5... | collective-permute-start | bytes 294920 | tf_op jit(solution)/shard_map/ppermute | solution.py:380
  37.7 1.8 %collective-permute-start.17 = (bf16[32,1536]{1,0:T(8,128)(2,1)S(1)}, bf16[32,1536]{1,0:T(8,128)(2,1)S(1)}, u32[]{:S(2)}, u32[]{:S(2)}) collective-permute-start(bf16[32,1536]{1,0:T(8,128)(2,1)S(1)} %get-tuple-element.70), channel_id=1, source_target_pairs={{0,8},{1,25},{2,10},{3,27},{4,12},{5,29},{6,14},{7,31},{8,0},{9,17... | collective-permute-start | bytes 294920 | tf_op jit(solution)/shard_map/ppermute | solution.py:380
  39.5 0.0 collective-permute-done.15
  39.5 0.8 %collective-permute-start.18 = (bf16[32,1536]{1,0:T(8,128)(2,1)S(1)}, bf16[32,1536]{1,0:T(8,128)(2,1)S(1)}, u32[]{:S(2)}, u32[]{:S(2)}) collective-permute-start(bf16[32,1536]{1,0:T(8,128)(2,1)S(1)} %get-tuple-element.71), channel_id=1, source_target_pairs={{0,0},{1,5},{2,2},{3,7},{4,4},{5,1},{6,6},{7,3},{8,8},{9,13},{10,1... | collective-permute-start | bytes 294920 | tf_op jit(solution)/shard_map/ppermute | solution.py:380
  40.4 4.3 %collective-permute-done.16 = bf16[32,1536]{1,0:T(8,128)(2,1)S(1)} collective-permute-done((bf16[32,1536]{1,0:T(8,128)(2,1)S(1)}, bf16[32,1536]{1,0:T(8,128)(2,1)S(1)}, u32[]{:S(2)}, u32[]{:S(2)}) %collective-permute-start.16) | collective-permute-done | bytes 98336 | tf_op jit(solution)/shard_map/ppermute | solution.py:380
  44.7 0.0 collective-permute-done.17
  44.7 1.4 %collective-permute-done.12.far_ref = bf16[128,1536]{1,0:T(8,128)(2,1)S(1)} collective-permute-done((bf16[128,1536]{1,0:T(8,128)(2,1)S(1)}, bf16[128,1536]{1,0:T(8,128)(2,1)S(1)}, u32[]{:S(2)}, u32[]{:S(2)}) %collective-permute-start.12) | collective-permute-done | bytes 393248 | tf_op jit(solution)/shard_map/ppermute | solution.py:330
  46.1 1.6 %collective-permute-start.19 = (bf16[128,1536]{1,0:T(8,128)(2,1)S(1)}, bf16[128,1536]{1,0:T(8,128)(2,1)S(1)}, u32[]{:S(2)}, u32[]{:S(2)}) collective-permute-start(bf16[128,1536]{1,0:T(8,128)(2,1)S(1)} %constant_dynamic-update-slice_fusion.4.near_ref), channel_id=1, source_target_pairs={{0,2},{1,3},{2,0},{3,1},{4,6},{5,7},{6,4},{7,5},{8,10},{9,11},{10,... | collective-permute-start | bytes 1179656 | tf_op jit(solution)/shard_map/ppermute | solution.py:330
  47.7 0.2 collective-permute-start.5
  47.9 0.3 collective-permute-start.7
  48.2 0.9 %collective-permute-done.5.refs_1_ = bf16[128,768]{1,0:T(8,128)(2,1)S(1)} collective-permute-done((bf16[128,768]{1,0:T(8,128)(2,1)S(1)}, bf16[128,768]{1,0:T(8,128)(2,1)S(1)}, u32[]{:S(2)}, u32[]{:S(2)}) %collective-permute-start.5) | collective-permute-done | bytes 196640 | tf_op jit(solution)/shard_map/ppermute | solution.py:330
  49.2 0.2 collective-permute-start.20
  49.4 0.1 collective-permute-done.7.refs_3_
  49.4 0.9 %shard_map.113 = bf16[512,768]{1,0:T(8,128)(2,1)} custom-call(bf16[128,768]{1,0:T(8,128)(2,1)S(1)} %get-tuple-element.56.refs_0_, bf16[128,768]{1,0:T(8,128)(2,1)S(1)} %collective-permute-done.5.refs_1_, bf16[128,768]{1,0:T(8,128)(2,1)S(1)} %get-tuple-element.59.refs_2_, bf16[128,768]{1,0:T(8,128)(2,1)S(1)} %collective-permute-done.7.refs_3_), custom_call_target="tpu_custom_call" | custom-call | tf_op jit(solution)/shard_map/pallas_call | solution.py:449
  50.4 0.6 shard_map.114.own_normed_ref
  51.0 3.2 %shard_map.115 = (bf16[128,384]{1,0:T(8,128)(2,1)S(1)}, bf16[128,384]{1,0:T(8,128)(2,1)S(1)}) custom-call(bf16[128,3072]{1,0:T(8,128)(2,1)S(1)} %shard_map.114.own_normed_ref, bf16[128,1536]{1,0:T(8,128)(2,1)S(1)} %collective-permute-done.13.near_ref, bf16[128,1536]{1,0:T(8,128)(2,1)S(1)} %collective-permute-done.14.far_ref, f32[1,3072]{1,0:T(1,128)S(1)} %bitcast.11, ...), custom_call_target="tpu_custom_call" | custom-call | tf_op jit(solution)/shard_map/pallas_call | solution.py:459
  54.2 3.5 %collective-permute-done.19.far_ref = bf16[128,1536]{1,0:T(8,128)(2,1)S(1)} collective-permute-done((bf16[128,1536]{1,0:T(8,128)(2,1)S(1)}, bf16[128,1536]{1,0:T(8,128)(2,1)S(1)}, u32[]{:S(2)}, u32[]{:S(2)}) %collective-permute-start.19) | collective-permute-done | bytes 393248 | tf_op jit(solution)/shard_map/ppermute | solution.py:330
  57.7 0.6 shard_map.116.own_normed_ref
  58.3 0.6 collective-permute-start.22
  58.9 0.6 collective-permute-done.21.far_ref
  59.4 3.2 %shard_map.117 = (bf16[128,384]{1,0:T(8,128)(2,1)S(1)}, bf16[128,384]{1,0:T(8,128)(2,1)S(1)}) custom-call(bf16[128,3072]{1,0:T(8,128)(2,1)S(1)} %shard_map.116.own_normed_ref, bf16[128,1536]{1,0:T(8,128)(2,1)S(1)} %collective-permute-done.20.near_ref, bf16[128,1536]{1,0:T(8,128)(2,1)S(1)} %collective-permute-done.21.far_ref, f32[1,3072]{1,0:T(1,128)S(1)} %bitcast.13, ...), custom_call_target="tpu_custom_call" | custom-call | tf_op jit(solution)/shard_map/pallas_call | solution.py:459
  62.6 0.2 collective-permute-start.23
  62.8 1.2 %collective-permute-done.23.refs_3_ = bf16[128,384]{1,0:T(8,128)(2,1)S(1)} collective-permute-done((bf16[128,384]{1,0:T(8,128)(2,1)S(1)}, bf16[128,384]{1,0:T(8,128)(2,1)S(1)}, u32[]{:S(2)}, u32[]{:S(2)}) %collective-permute-start.23) | collective-permute-done | bytes 98336 | tf_op jit(solution)/shard_map/ppermute | solution.py:330
  64.0 3.3 %collective-permute-start.24 = (bf16[128,384]{1,0:T(8,128)(2,1)S(1)}, bf16[128,384]{1,0:T(8,128)(2,1)S(1)}, u32[]{:S(2)}, u32[]{:S(2)}) collective-permute-start(bf16[128,384]{1,0:T(8,128)(2,1)S(1)} %get-tuple-element.76), channel_id=1, source_target_pairs={{0,28},{1,21},{2,30},{3,23},{4,24},{5,17},{6,26},{7,19},{8,20},{9,... | collective-permute-start | bytes 294920 | tf_op jit(solution)/shard_map/ppermute | solution.py:380
  67.3 1.5 %collective-permute-start.26 = (bf16[128,384]{1,0:T(8,128)(2,1)S(1)}, bf16[128,384]{1,0:T(8,128)(2,1)S(1)}, u32[]{:S(2)}, u32[]{:S(2)}) collective-permute-start(bf16[128,384]{1,0:T(8,128)(2,1)S(1)} %get-tuple-element.78), channel_id=1, source_target_pairs={{0,8},{1,25},{2,10},{3,27},{4,12},{5,29},{6,14},{7,31},{8,0},{9,17... | collective-permute-start | bytes 294920 | tf_op jit(solution)/shard_map/ppermute | solution.py:380
  68.9 0.7 collective-permute-start.27
  69.5 3.0 %collective-permute-done.24.refs_0_ = bf16[128,384]{1,0:T(8,128)(2,1)S(1)} collective-permute-done((bf16[128,384]{1,0:T(8,128)(2,1)S(1)}, bf16[128,384]{1,0:T(8,128)(2,1)S(1)}, u32[]{:S(2)}, u32[]{:S(2)}) %collective-permute-start.24) | collective-permute-done | bytes 98336 | tf_op jit(solution)/shard_map/ppermute | solution.py:380
  72.5 3.2 %collective-permute-done.25.refs_1_ = bf16[128,384]{1,0:T(8,128)(2,1)S(1)} collective-permute-done((bf16[128,384]{1,0:T(8,128)(2,1)S(1)}, bf16[128,384]{1,0:T(8,128)(2,1)S(1)}, u32[]{:S(2)}, u32[]{:S(2)}) %collective-permute-start.25) | collective-permute-done | bytes 98336 | tf_op jit(solution)/shard_map/ppermute | solution.py:380
  75.7 0.1 collective-permute-start.28
  75.8 1.4 %collective-permute-done.28.refs_4_ = bf16[256,384]{1,0:T(8,128)(2,1)S(1)} collective-permute-done((bf16[256,384]{1,0:T(8,128)(2,1)S(1)}, bf16[256,384]{1,0:T(8,128)(2,1)S(1)}, u32[]{:S(2)}, u32[]{:S(2)}) %collective-permute-start.28) | collective-permute-done | bytes 196640 | tf_op jit(solution)/shard_map/ppermute | solution.py:330
  77.2 0.8 %shard_map.120 = bf16[512,384]{1,0:T(8,128)(2,1)} custom-call(bf16[128,384]{1,0:T(8,128)(2,1)S(1)} %collective-permute-done.24.refs_0_, bf16[128,384]{1,0:T(8,128)(2,1)S(1)} %collective-permute-done.25.refs_1_, bf16[128,384]{1,0:T(8,128)(2,1)S(1)} %collective-permute-done.26.refs_2_, bf16[128,384]{1,0:T(8,128)(2,1)S(1)} %collective-permute-done.27.refs_3_, ...), custom_call_target="tpu_custom_call" | custom-call | tf_op jit(solution)/shard_map/pallas_call | solution.py:473
  (27 shorter events, 0.2 us)
Async XLA Ops:
  3.4 1.9 %collective-permute-start.1 = (bf16[128,1536]{1,0:T(8,128)(2,1)S(1)}, bf16[128,1536]{1,0:T(8,128)(2,1)S(1)}, u32[]{:S(2)}, u32[]{:S(2)}) collective-permute-start(bf16[128,1536]{1,0:T(8,128)(2,1)S(1)} %get-tuple-element.48), channel_id=1, source_target_pairs={{0,1},{1,0},{2,3},{3,2},{4,5},{5,4},{6,7},{7,6},{8,9},{9,8},{10,11... | collective-permute-start | bytes 1179656 | tf_op jit(solution)/shard_map/ppermute | solution.py:330
  6.7 4.5 %collective-permute-start.3 = (bf16[128,1536]{1,0:T(8,128)(2,1)S(1)}, bf16[128,1536]{1,0:T(8,128)(2,1)S(1)}, u32[]{:S(2)}, u32[]{:S(2)}) collective-permute-start(bf16[128,1536]{1,0:T(8,128)(2,1)S(1)} %get-tuple-element.53), channel_id=1, source_target_pairs={{0,1},{1,0},{2,3},{3,2},{4,5},{5,4},{6,7},{7,6},{8,9},{9,8},{10,11... | collective-permute-start | bytes 1179656 | tf_op jit(solution)/shard_map/ppermute | solution.py:330
  7.2 7.5 %collective-permute-start = (bf16[128,1536]{1,0:T(8,128)(2,1)S(1)}, bf16[128,1536]{1,0:T(8,128)(2,1)S(1)}, u32[]{:S(2)}, u32[]{:S(2)}) collective-permute-start(bf16[128,1536]{1,0:T(8,128)(2,1)S(1)} %get-tuple-element.46), channel_id=1, source_target_pairs={{0,1},{1,0},{2,3},{3,2},{4,5},{5,4},{6,7},{7,6},{8,9},{9,8},{10,11... | collective-permute-start | bytes 1179656 | tf_op jit(solution)/shard_map/ppermute | solution.py:330
  8.1 6.5 %collective-permute-start.4 = (bf16[128,1536]{1,0:T(8,128)(2,1)S(1)}, bf16[128,1536]{1,0:T(8,128)(2,1)S(1)}, u32[]{:S(2)}, u32[]{:S(2)}) collective-permute-start(bf16[128,1536]{1,0:T(8,128)(2,1)S(1)} %get-tuple-element.54), channel_id=1, source_target_pairs={{0,1},{1,0},{2,3},{3,2},{4,5},{5,4},{6,7},{7,6},{8,9},{9,8},{10,11... | collective-permute-start | bytes 1179656 | tf_op jit(solution)/shard_map/ppermute | solution.py:330
  8.5 12.5 %collective-permute-start.2 = (bf16[128,1536]{1,0:T(8,128)(2,1)S(1)}, bf16[128,1536]{1,0:T(8,128)(2,1)S(1)}, u32[]{:S(2)}, u32[]{:S(2)}) collective-permute-start(bf16[128,1536]{1,0:T(8,128)(2,1)S(1)} %shard_map.106), channel_id=1, source_target_pairs={{0,2},{1,3},{2,0},{3,1},{4,6},{5,7},{6,4},{7,5},{8,10},{9,11},{10,... | collective-permute-start | bytes 1179656 | tf_op jit(solution)/shard_map/ppermute | solution.py:330
  11.3 18.0 %collective-permute-start.6 = (bf16[128,1536]{1,0:T(8,128)(2,1)S(1)}, bf16[128,1536]{1,0:T(8,128)(2,1)S(1)}, u32[]{:S(2)}, u32[]{:S(2)}) collective-permute-start(bf16[128,1536]{1,0:T(8,128)(2,1)S(1)} %shard_map.109), channel_id=1, source_target_pairs={{0,2},{1,3},{2,0},{3,1},{4,6},{5,7},{6,4},{7,5},{8,10},{9,11},{10,... | collective-permute-start | bytes 1179656 | tf_op jit(solution)/shard_map/ppermute | solution.py:330
  21.3 8.4 %collective-permute-start.8 = (bf16[32,1536]{1,0:T(8,128)(2,1)S(1)}, bf16[32,1536]{1,0:T(8,128)(2,1)S(1)}, u32[]{:S(2)}, u32[]{:S(2)}) collective-permute-start(bf16[32,1536]{1,0:T(8,128)(2,1)S(1)} %get-tuple-element.61), channel_id=1, source_target_pairs={{0,28},{1,21},{2,30},{3,23},{4,24},{5,17},{6,26},{7,19},{8,20},{9,... | collective-permute-start | bytes 294920 | tf_op jit(solution)/shard_map/ppermute | solution.py:380
  26.4 8.0 %collective-permute-start.9 = (bf16[32,1536]{1,0:T(8,128)(2,1)S(1)}, bf16[32,1536]{1,0:T(8,128)(2,1)S(1)}, u32[]{:S(2)}, u32[]{:S(2)}) collective-permute-start(bf16[32,1536]{1,0:T(8,128)(2,1)S(1)} %get-tuple-element.64), channel_id=1, source_target_pairs={{0,16},{1,13},{2,18},{3,15},{4,20},{5,9},{6,22},{7,11},{8,24},{9,5... | collective-permute-start | bytes 294920 | tf_op jit(solution)/shard_map/ppermute | solution.py:380
  26.4 8.0 %collective-permute-start.10 = (bf16[32,1536]{1,0:T(8,128)(2,1)S(1)}, bf16[32,1536]{1,0:T(8,128)(2,1)S(1)}, u32[]{:S(2)}, u32[]{:S(2)}) collective-permute-start(bf16[32,1536]{1,0:T(8,128)(2,1)S(1)} %get-tuple-element.65), channel_id=1, source_target_pairs={{0,8},{1,25},{2,10},{3,27},{4,12},{5,29},{6,14},{7,31},{8,0},{9,17... | collective-permute-start | bytes 294920 | tf_op jit(solution)/shard_map/ppermute | solution.py:380
  27.2 7.3 %collective-permute-start.11 = (bf16[32,1536]{1,0:T(8,128)(2,1)S(1)}, bf16[32,1536]{1,0:T(8,128)(2,1)S(1)}, u32[]{:S(2)}, u32[]{:S(2)}) collective-permute-start(bf16[32,1536]{1,0:T(8,128)(2,1)S(1)} %get-tuple-element.66), channel_id=1, source_target_pairs={{0,0},{1,5},{2,2},{3,7},{4,4},{5,1},{6,6},{7,3},{8,8},{9,13},{10,1... | collective-permute-start | bytes 294920 | tf_op jit(solution)/shard_map/ppermute | solution.py:380
  29.4 20.9 %copy-start = (f32[3072]{0:T(1024)S(1)}, f32[3072]{0:T(1024)}, u32[]{:S(2)}) copy-start(f32[3072]{0:T(1024)} %param.14) | copy-start | bytes 36868
  29.5 20.9 %copy-start.1 = (f32[3072]{0:T(1024)S(1)}, f32[3072]{0:T(1024)}, u32[]{:S(2)}) copy-start(f32[3072]{0:T(1024)} %param.13) | copy-start | bytes 36868
  29.7 21.3 %copy-start.2 = (f32[8,128]{1,0:T(8,128)S(1)}, f32[8,128]{1,0:T(8,128)}, u32[]{:S(2)}) copy-start(f32[8,128]{1,0:T(8,128)} %constant.5.clone.sin_ref) | copy-start | bytes 12292
  29.7 21.3 %copy-start.3 = (f32[8,128]{1,0:T(8,128)S(1)}, f32[8,128]{1,0:T(8,128)}, u32[]{:S(2)}) copy-start(f32[8,128]{1,0:T(8,128)} %constant.4.clone.cos_ref) | copy-start | bytes 12292
  29.7 9.8 %collective-permute-start.15 = (bf16[32,1536]{1,0:T(8,128)(2,1)S(1)}, bf16[32,1536]{1,0:T(8,128)(2,1)S(1)}, u32[]{:S(2)}, u32[]{:S(2)}) collective-permute-start(bf16[32,1536]{1,0:T(8,128)(2,1)S(1)} %get-tuple-element.68), channel_id=1, source_target_pairs={{0,28},{1,21},{2,30},{3,23},{4,24},{5,17},{6,26},{7,19},{8,20},{9,... | collective-permute-start | bytes 294920 | tf_op jit(solution)/shard_map/ppermute | solution.py:380
  34.5 16.5 %collective-permute-start.13 = (bf16[128,1536]{1,0:T(8,128)(2,1)S(1)}, bf16[128,1536]{1,0:T(8,128)(2,1)S(1)}, u32[]{:S(2)}, u32[]{:S(2)}) collective-permute-start(bf16[128,1536]{1,0:T(8,128)(2,1)S(1)} %constant_dynamic-update-slice_fusion.near_ref), channel_id=1, source_target_pairs={{0,1},{1,0},{2,3},{3,2},{4,5},{5,4},{6,7},{7,6},{8,9},{9,8},{10,11... | collective-permute-start | bytes 1179656 | tf_op jit(solution)/shard_map/ppermute | solution.py:330
  34.6 11.5 %collective-permute-start.12 = (bf16[128,1536]{1,0:T(8,128)(2,1)S(1)}, bf16[128,1536]{1,0:T(8,128)(2,1)S(1)}, u32[]{:S(2)}, u32[]{:S(2)}) collective-permute-start(bf16[128,1536]{1,0:T(8,128)(2,1)S(1)} %constant_dynamic-update-slice_fusion.near_ref), channel_id=1, source_target_pairs={{0,2},{1,3},{2,0},{3,1},{4,6},{5,7},{6,4},{7,5},{8,10},{9,11},{10,... | collective-permute-start | bytes 1179656 | tf_op jit(solution)/shard_map/ppermute | solution.py:330
  36.2 8.5 %collective-permute-start.16 = (bf16[32,1536]{1,0:T(8,128)(2,1)S(1)}, bf16[32,1536]{1,0:T(8,128)(2,1)S(1)}, u32[]{:S(2)}, u32[]{:S(2)}) collective-permute-start(bf16[32,1536]{1,0:T(8,128)(2,1)S(1)} %get-tuple-element.69), channel_id=1, source_target_pairs={{0,16},{1,13},{2,18},{3,15},{4,20},{5,9},{6,22},{7,11},{8,24},{9,5... | collective-permute-start | bytes 294920 | tf_op jit(solution)/shard_map/ppermute | solution.py:380
  37.7 7.0 %collective-permute-start.17 = (bf16[32,1536]{1,0:T(8,128)(2,1)S(1)}, bf16[32,1536]{1,0:T(8,128)(2,1)S(1)}, u32[]{:S(2)}, u32[]{:S(2)}) collective-permute-start(bf16[32,1536]{1,0:T(8,128)(2,1)S(1)} %get-tuple-element.70), channel_id=1, source_target_pairs={{0,8},{1,25},{2,10},{3,27},{4,12},{5,29},{6,14},{7,31},{8,0},{9,17... | collective-permute-start | bytes 294920 | tf_op jit(solution)/shard_map/ppermute | solution.py:380
  39.5 6.6 %collective-permute-start.18 = (bf16[32,1536]{1,0:T(8,128)(2,1)S(1)}, bf16[32,1536]{1,0:T(8,128)(2,1)S(1)}, u32[]{:S(2)}, u32[]{:S(2)}) collective-permute-start(bf16[32,1536]{1,0:T(8,128)(2,1)S(1)} %get-tuple-element.71), channel_id=1, source_target_pairs={{0,0},{1,5},{2,2},{3,7},{4,4},{5,1},{6,6},{7,3},{8,8},{9,13},{10,1... | collective-permute-start | bytes 294920 | tf_op jit(solution)/shard_map/ppermute | solution.py:380
  46.1 4.9 %collective-permute-start.14 = (bf16[128,1536]{1,0:T(8,128)(2,1)S(1)}, bf16[128,1536]{1,0:T(8,128)(2,1)S(1)}, u32[]{:S(2)}, u32[]{:S(2)}) collective-permute-start(bf16[128,1536]{1,0:T(8,128)(2,1)S(1)} %collective-permute-done.12.far_ref), channel_id=1, source_target_pairs={{0,1},{1,0},{2,3},{3,2},{4,5},{5,4},{6,7},{7,6},{8,9},{9,8},{10,11... | collective-permute-start | bytes 1179656 | tf_op jit(solution)/shard_map/ppermute | solution.py:330
  46.1 11.6 %collective-permute-start.19 = (bf16[128,1536]{1,0:T(8,128)(2,1)S(1)}, bf16[128,1536]{1,0:T(8,128)(2,1)S(1)}, u32[]{:S(2)}, u32[]{:S(2)}) collective-permute-start(bf16[128,1536]{1,0:T(8,128)(2,1)S(1)} %constant_dynamic-update-slice_fusion.4.near_ref), channel_id=1, source_target_pairs={{0,2},{1,3},{2,0},{3,1},{4,6},{5,7},{6,4},{7,5},{8,10},{9,11},{10,... | collective-permute-start | bytes 1179656 | tf_op jit(solution)/shard_map/ppermute | solution.py:330
  47.7 1.4 %collective-permute-start.5 = (bf16[128,768]{1,0:T(8,128)(2,1)S(1)}, bf16[128,768]{1,0:T(8,128)(2,1)S(1)}, u32[]{:S(2)}, u32[]{:S(2)}) collective-permute-start(bf16[128,768]{1,0:T(8,128)(2,1)S(1)} %get-tuple-element.57), channel_id=1, source_target_pairs={{0,1},{1,0},{2,3},{3,2},{4,5},{5,4},{6,7},{7,6},{8,9},{9,8},{10,11... | collective-permute-start | bytes 589832 | tf_op jit(solution)/shard_map/ppermute | solution.py:330
  47.9 1.5 %collective-permute-start.7 = (bf16[128,768]{1,0:T(8,128)(2,1)S(1)}, bf16[128,768]{1,0:T(8,128)(2,1)S(1)}, u32[]{:S(2)}, u32[]{:S(2)}) collective-permute-start(bf16[128,768]{1,0:T(8,128)(2,1)S(1)} %get-tuple-element.60), channel_id=1, source_target_pairs={{0,1},{1,0},{2,3},{3,2},{4,5},{5,4},{6,7},{7,6},{8,9},{9,8},{10,11... | collective-permute-start | bytes 589832 | tf_op jit(solution)/shard_map/ppermute | solution.py:330
  49.2 9.7 %collective-permute-start.20 = (bf16[128,1536]{1,0:T(8,128)(2,1)S(1)}, bf16[128,1536]{1,0:T(8,128)(2,1)S(1)}, u32[]{:S(2)}, u32[]{:S(2)}) collective-permute-start(bf16[128,1536]{1,0:T(8,128)(2,1)S(1)} %constant_dynamic-update-slice_fusion.4.near_ref), channel_id=1, source_target_pairs={{0,1},{1,0},{2,3},{3,2},{4,5},{5,4},{6,7},{7,6},{8,9},{9,8},{10,11... | collective-permute-start | bytes 1179656 | tf_op jit(solution)/shard_map/ppermute | solution.py:330
  57.7 1.7 %collective-permute-start.21 = (bf16[128,1536]{1,0:T(8,128)(2,1)S(1)}, bf16[128,1536]{1,0:T(8,128)(2,1)S(1)}, u32[]{:S(2)}, u32[]{:S(2)}) collective-permute-start(bf16[128,1536]{1,0:T(8,128)(2,1)S(1)} %collective-permute-done.19.far_ref), channel_id=1, source_target_pairs={{0,1},{1,0},{2,3},{3,2},{4,5},{5,4},{6,7},{7,6},{8,9},{9,8},{10,11... | collective-permute-start | bytes 1179656 | tf_op jit(solution)/shard_map/ppermute | solution.py:330
  58.3 4.5 %collective-permute-start.22 = (bf16[128,384]{1,0:T(8,128)(2,1)S(1)}, bf16[128,384]{1,0:T(8,128)(2,1)S(1)}, u32[]{:S(2)}, u32[]{:S(2)}) collective-permute-start(bf16[128,384]{1,0:T(8,128)(2,1)S(1)} %get-tuple-element.74), channel_id=1, source_target_pairs={{0,1},{1,0},{2,3},{3,2},{4,5},{5,4},{6,7},{7,6},{8,9},{9,8},{10,11... | collective-permute-start | bytes 294920 | tf_op jit(solution)/shard_map/ppermute | solution.py:330
  62.6 1.4 %collective-permute-start.23 = (bf16[128,384]{1,0:T(8,128)(2,1)S(1)}, bf16[128,384]{1,0:T(8,128)(2,1)S(1)}, u32[]{:S(2)}, u32[]{:S(2)}) collective-permute-start(bf16[128,384]{1,0:T(8,128)(2,1)S(1)} %get-tuple-element.75), channel_id=1, source_target_pairs={{0,1},{1,0},{2,3},{3,2},{4,5},{5,4},{6,7},{7,6},{8,9},{9,8},{10,11... | collective-permute-start | bytes 294920 | tf_op jit(solution)/shard_map/ppermute | solution.py:330
  64.0 8.5 %collective-permute-start.24 = (bf16[128,384]{1,0:T(8,128)(2,1)S(1)}, bf16[128,384]{1,0:T(8,128)(2,1)S(1)}, u32[]{:S(2)}, u32[]{:S(2)}) collective-permute-start(bf16[128,384]{1,0:T(8,128)(2,1)S(1)} %get-tuple-element.76), channel_id=1, source_target_pairs={{0,28},{1,21},{2,30},{3,23},{4,24},{5,17},{6,26},{7,19},{8,20},{9,... | collective-permute-start | bytes 294920 | tf_op jit(solution)/shard_map/ppermute | solution.py:380
  67.3 8.4 %collective-permute-start.25 = (bf16[128,384]{1,0:T(8,128)(2,1)S(1)}, bf16[128,384]{1,0:T(8,128)(2,1)S(1)}, u32[]{:S(2)}, u32[]{:S(2)}) collective-permute-start(bf16[128,384]{1,0:T(8,128)(2,1)S(1)} %get-tuple-element.77), channel_id=1, source_target_pairs={{0,16},{1,13},{2,18},{3,15},{4,20},{5,9},{6,22},{7,11},{8,24},{9,5... | collective-permute-start | bytes 294920 | tf_op jit(solution)/shard_map/ppermute | solution.py:380
  67.3 8.4 %collective-permute-start.26 = (bf16[128,384]{1,0:T(8,128)(2,1)S(1)}, bf16[128,384]{1,0:T(8,128)(2,1)S(1)}, u32[]{:S(2)}, u32[]{:S(2)}) collective-permute-start(bf16[128,384]{1,0:T(8,128)(2,1)S(1)} %get-tuple-element.78), channel_id=1, source_target_pairs={{0,8},{1,25},{2,10},{3,27},{4,12},{5,29},{6,14},{7,31},{8,0},{9,17... | collective-permute-start | bytes 294920 | tf_op jit(solution)/shard_map/ppermute | solution.py:380
  68.9 6.8 %collective-permute-start.27 = (bf16[128,384]{1,0:T(8,128)(2,1)S(1)}, bf16[128,384]{1,0:T(8,128)(2,1)S(1)}, u32[]{:S(2)}, u32[]{:S(2)}) collective-permute-start(bf16[128,384]{1,0:T(8,128)(2,1)S(1)} %get-tuple-element.79), channel_id=1, source_target_pairs={{0,0},{1,5},{2,2},{3,7},{4,4},{5,1},{6,6},{7,3},{8,8},{9,13},{10,1... | collective-permute-start | bytes 294920 | tf_op jit(solution)/shard_map/ppermute | solution.py:380
  75.7 1.5 %collective-permute-start.28 = (bf16[256,384]{1,0:T(8,128)(2,1)S(1)}, bf16[256,384]{1,0:T(8,128)(2,1)S(1)}, u32[]{:S(2)}, u32[]{:S(2)}) collective-permute-start(bf16[256,384]{1,0:T(8,128)(2,1)S(1)} %shard_map.119), channel_id=1, source_target_pairs={{0,1},{1,0},{2,3},{3,2},{4,5},{5,4},{6,7},{7,6},{8,9},{9,8},{10,11... | collective-permute-start | bytes 589832 | tf_op jit(solution)/shard_map/ppermute | solution.py:330

commit v5 on v4

--- a/solution.py
+++ b/solution.py
@@ -169,84 +169,79 @@
     return pl.ds(pl.multiple_of((chip_of() ^ flip) * half, half), half)
 
 
-def spatial_body(qkv_ref, far_w_ref, heads_ref, message_ref, first, far_gate):
+def spatial_heads(qkv_ref, heads_ref, first):
     rows, width = heads_ref.shape
     for lane in range(0, width, HEAD_DIM):
         head = slice(lane, lane + HEAD_DIM)
         query = piece_rows(qkv_ref.at[0], first, rows // (2 * SHARES), head)
         (heads_ref[:, head],) = attend([(query, qkv_ref[1, :, head], qkv_ref[2, :, head])])
-    gate = far_gate()
-    term = dot(heads_ref[rows // 2 :, :], far_w_ref[...])
-    message_ref[...] = (term * gate).astype(message_ref.dtype)
 
 
 def first_spatial_kernel(
-    qkv_far, w_far, gate_far, residual_far,
-    heads_ref, message_ref, qkv_ref, w_ref, gate_ref, residual_ref, semaphores, *, first
+    qkv_far, w_far, gate_far, heads_ref, message_ref, w_ref, gate_ref, qkv_ref, semaphores, *, first
 ):
-    far, near = (chip_columns(w_far.shape[-1], flip) for flip in (1, 0))
+    far = chip_columns(w_far.shape[-1], 1)
+    moves = [(qkv_far, qkv_ref), (w_far.at[:, far], w_ref), (gate_far.at[:, far], gate_ref)]
+    copies = [pltpu.make_async_copy(*move, semaphores.at[i]) for i, move in enumerate(moves)]
+    for copy in copies:
+        copy.start()
+    copies[0].wait()
+    spatial_heads(qkv_ref, heads_ref, first)
+    copies[1].wait()
+    copies[2].wait()
+    term = dot(heads_ref[heads_ref.shape[0] // 2 :, :], w_ref[...])
+    message_ref[...] = (term * gate_ref[...]).astype(message_ref.dtype)
+
+
+def term_kernel(heads_ref, w_ref, gate_ref, out_ref):
+    out_ref[...] = dot(heads_ref[: out_ref.shape[0], :], w_ref[...]) * gate_ref[...]
+
+
+def rest_kernel(
+    heads0_ref, qkv_far, w_far, gate_far, residual_far,
+    message_ref, term_ref, base0_ref, near0_ref, base1_ref, near1_ref,
+    heads1_ref, qkv_ref, w_ref, gate_ref, residual_ref, semaphores, *, firsts
+):
     moves = [
-        (qkv_far, qkv_ref),
-        (w_far.at[:, far], w_ref.at[:, far]),
-        (gate_far, gate_ref),
-        (w_far.at[:, near], w_ref.at[:, near]),
-        (residual_far, residual_ref),
+        (qkv_far, qkv_ref), (w_far, w_ref), (gate_far, gate_ref), (residual_far, residual_ref)
     ]
     copies = [pltpu.make_async_copy(*move, semaphores.at[i]) for i, move in enumerate(moves)]
     for copy in copies:
         copy.start()
     copies[0].wait()
-
-    def far_gate():
-        copies[1].wait()
-        copies[2].wait()
-        return gate_ref[:, far]
-
-    spatial_body(qkv_ref, w_ref.at[:, far], heads_ref, message_ref, first, far_gate)
-    copies[3].wait()
-    copies[4].wait()
-
-
-def spatial_kernel(gate_ref, qkv_ref, w_ref, heads_ref, message_ref, *, first):
-    columns = chip_columns(w_ref.shape[-1], 1)
-    spatial_body(
-        qkv_ref,
-        w_ref.at[:, columns],
-        heads_ref,
-        message_ref,
-        first,
-        lambda: gate_ref[:, columns],
-    )
-
-
-def terms_kernel(
-    heads_ref, w_ref, gate_ref, residual_ref, far_ref, base_ref, message_ref, *, first
-):
-    half, both = base_ref.shape
-    share = both // 2
+    spatial_heads(qkv_ref, heads1_ref, firsts[1])
+    for copy in copies[1:]:
+        copy.wait()
+    half, both = message_ref.shape
     features = w_ref.shape[-1]
     far = chip_columns(features, 1)
-    far_ref[...] = dot(heads_ref[:half, :], w_ref[:, far]) * gate_ref[:, far]
-    for flip in range(2):
-        place = pl.multiple_of((core_of() ^ flip) * share, share)
-        lanes = pl.ds(pl.multiple_of(chip_of() * both + place, share), share)
-        term = dot(heads_ref[...], w_ref[:, lanes]) * gate_ref[:, lanes]
-        if flip == 0:
-            term += piece_rows(residual_ref, first, half // SHARES, slice(None)).astype(
-                jnp.float32
-            )
-        base_ref[:, pl.ds(place, share)] = term[:half]
-        message_ref[:, pl.ds(place, share)] = term[half:].astype(message_ref.dtype)
+    term = dot(heads1_ref[...], w_ref[:, far]) * gate_ref[:, far]
+    term_ref[...] = term[:half]
+    message_ref[...] = term[half:].astype(message_ref.dtype)
+    share = both // 2
+    for first, heads_ref, base_ref, near_ref in (
+        (firsts[0], heads0_ref, base0_ref, near0_ref),
+        (firsts[1], heads1_ref, base1_ref, near1_ref),
+    ):
+        size = base_ref.shape[0]
+        for flip in range(2):
+            place = pl.multiple_of((core_of() ^ flip) * share, share)
+            lanes = pl.ds(pl.multiple_of(chip_of() * both + place, share), share)
+            term = dot(heads_ref[...], w_ref[:, lanes]) * gate_ref[:, lanes]
+            if flip == 0:
+                term += piece_rows(residual_ref, first, size // SHARES, slice(None)).astype(
+                    jnp.float32
+                )
+            base_ref[:, pl.ds(place, share)] = term[:size]
+            near_ref[:, pl.ds(place, share)] = term[size:].astype(near_ref.dtype)
 
 
 def add_kernel(a_ref, b_ref, out_ref):
     out_ref[...] = (a_ref[...] + b_ref[...].astype(jnp.float32)).astype(out_ref.dtype)
 
 
-def update_kernel(base_ref, message_ref, arrived_ref, own_ref, other_ref, *piece_refs):
-    updated = (
-        base_ref[...] + message_ref[...].astype(jnp.float32) + arrived_ref[...].astype(jnp.float32)
-    ).astype(jnp.bfloat16)
+def update_kernel(base_ref, arrived_ref, own_ref, other_ref, *piece_refs):
+    updated = (base_ref[...] + arrived_ref[...].astype(jnp.float32)).astype(jnp.bfloat16)
     count = piece_refs[0].shape[0]
     for i, piece_ref in enumerate(piece_refs):
         piece_ref[...] = updated[i * count : (i + 1) * count]
@@ -367,7 +362,6 @@
     bf16, f32 = jnp.bfloat16, jnp.float32
     flat_residual = residual.reshape(tokens, share)
     qkv = spatial_qkv.transpose(2, 0, 1, 3).reshape(3, tokens, width)
-    weights = hold_weights(temporal_qkv)
     gate_row = gate.reshape(1, features)
     gain_row, shift_row = scale.reshape(1, features), shift.reshape(1, features)
     cosine, sine = rotation_tables(n_seq)
@@ -381,77 +375,104 @@
             for i, piece in enumerate(pieces)
         ]
 
+    once = jnp.minimum(lax.axis_index("seq") + 1, 1)
+
     chunks = []
     first = 0
     for rows in CHUNK_ROWS:
         chunks.append((first, rows))
         first += rows
 
-    reduced = []
-    previous = None
-    for first, rows in chunks:
-        half = rows // 2
-        if previous is None:
-            operands = (qkv, spatial_out, gate_row, flat_residual)
-            heads, message, *operands = call(
-                functools.partial(first_spatial_kernel, first=first),
-                [shape(rows, width), shape(half, both)]
-                + [pltpu.VMEM(one.shape, one.dtype) for one in operands],
-                inputs=len(operands),
-                far=len(operands),
-                scratch=(pltpu.SemaphoreType.DMA((len(operands) + 1,)),),
-            )(*(in_hbm(one) for one in operands))
-            qkv, spatial_out, gate_row, flat_residual = operands
-        else:
-            heads, message = call(
-                functools.partial(spatial_kernel, first=first),
-                [shape(rows, width), shape(half, both)],
-                inputs=3,
-            )(gate_row, after(qkv, previous), spatial_out)
-        message = swap(message, "mlp", n_mlp, 1)
-        far_term, base, near_message = call(
-            functools.partial(terms_kernel, first=first),
-            [shape(half, both, f32), shape(half, both, f32), shape(half, both)],
-            inputs=4,
-        )(heads, spatial_out, gate_row, flat_residual)
-        sent = call(add_kernel, shape(half, both), inputs=2)(far_term, message)
-        previous = sent
-        reduced.append((base, swap(near_message, "mlp", n_mlp, 1), sent))
-
-    arrivals = [swap(sent, "mlp", n_mlp, 2) for _, _, sent in reduced]
-    arrivals[0] = after(arrivals[0], previous, weights, *(message for _, message, _ in reduced))
+    (first0, rows0), (first1, rows1) = chunks
+    half0, half1 = rows0 // 2, rows1 // 2
+    heads, message, far_w, far_gate = call(
+        functools.partial(first_spatial_kernel, first=first0),
+        [
+            shape(rows0, width),
+            shape(half0, both),
+            pltpu.VMEM((width, both), bf16),
+            pltpu.VMEM((1, both), f32),
+        ],
+        inputs=3,
+        far=3,
+        scratch=(pltpu.VMEM(qkv.shape, bf16), pltpu.SemaphoreType.DMA((3,))),
+    )(*(in_hbm(one) for one in (qkv, spatial_out, gate_row)))
+    message = swap(message, "mlp", n_mlp, 1)
+    far_term = call(term_kernel, shape(half0, both, f32), inputs=3)(heads, far_w, far_gate)
+    sent = call(add_kernel, shape(half0, both), inputs=2)(far_term, message)
+    arrived0 = swap(sent, "mlp", n_mlp, 2)
+
+    def rest(heads, *operands):
+        message, far_term, base0, near0, base1, near1 = call(
+            functools.partial(rest_kernel, firsts=(first0, first1)),
+            [
+                shape(half1, both),
+                shape(half1, both, f32),
+                shape(half0, both, f32),
+                shape(half0, both),
+                shape(half1, both, f32),
+                shape(half1, both),
+            ],
+            inputs=5,
+            far=4,
+            scratch=(
+                pltpu.VMEM((rows1, width), bf16),
+                *(pltpu.VMEM(one.shape, one.dtype) for one in operands),
+                pltpu.SemaphoreType.DMA((4,)),
+            ),
+        )(heads, *(in_hbm(one) for one in operands))
+        message, near0, near1 = (swap(one, "mlp", n_mlp, 1) for one in (message, near0, near1))
+        sent = call(add_kernel, shape(half1, both), inputs=2)(far_term, message)
+        base0, base1 = (
+            call(add_kernel, shape(*base.shape, f32), inputs=2)(base, near)
+            for base, near in ((base0, near0), (base1, near1))
+        )
+        return sent, base0, base1
+
+    def nothing(*_):
+        return (
+            jnp.zeros((half1, both), bf16),
+            jnp.zeros((half0, both), f32),
+            jnp.zeros((half1, both), f32),
+        )
+
+    sent, base0, base1 = lax.cond(
+        once > 0, rest, nothing, after(heads, sent), qkv, spatial_out, gate_row, flat_residual
+    )
+    arrived1 = swap(sent, "mlp", n_mlp, 2)
+    arrived0 = after(arrived0, sent)
+    reduced = [(base0, arrived0), (base1, arrived1)]
+
     blocks, pieces = [], []
-    for index, ((first, rows), (base, near_message, _)) in enumerate(zip(chunks, reduced)):
+    for index, ((first, rows), operands) in enumerate(zip(chunks, reduced)):
         half = rows // 2
         own, other, *sends = call(
             update_kernel,
             [shape(half, share)] * 2 + [shape(half // SHARES, both)] * SHARES,
-            flops=1e10 * index,
-            inputs=3,
-        )(base, near_message, arrivals[index])
+            inputs=2,
+        )(*operands)
         blocks += [own, swap(other, "mlp", n_mlp, 1)]
         pieces.append(sends)
     nears = []
-    for index, sends in enumerate(pieces):
-        received = send_pieces(sends)
-        if index + 1 < len(pieces):
-            received[0], pieces[index + 1][0] = lax.optimization_barrier(
-                (received[0], pieces[index + 1][0])
-            )
-        nears.append(jnp.concatenate(received, axis=0))
+    for sends in pieces:
+        sends = lax.fori_loop(0, once, lambda _, sends: send_pieces(sends), sends)
+        nears.append(jnp.concatenate(sends, axis=0))
+    weights = hold_weights(after(temporal_qkv, *nears))
 
     own_mixed, other_mixed = [], []
     for (first, rows), near in zip(chunks, nears):
         half = rows // 2
         far = swap(near, "mlp", n_mlp, 2)
         other_near = swap(near, "mlp", n_mlp, 1)
-        if own_mixed:
+        if not own_mixed:
+            far = after(far, *nears)
+        else:
             updated = call(
                 functools.partial(place_updated_kernel, chunks=chunks),
                 shape(tokens, share),
                 inputs=len(blocks),
             )(*blocks)
-            far = after(far, own_mixed[-1], updated)
+            far = after(far, other_mixed[-1], updated)
         other_far = swap(far, "mlp", n_mlp, 1)
         own_normed = call(split_norm_kernel, shape(half, features), inputs=4)(
             near, far, gain_row, shift_row

time: 78.2 us -> 76.1 us (0.973)
  starting transfers between devices: 30.2 us -> 25.8 us
  Pallas kernels: 18.8 us -> 20.7 us
    ppermute x12, waiting for transfers between devices: 10.7 us -> 18.3 us  [send_pieces(): lax.ppermute(piece, ('seq', 'mlp'), piece_pairs(n_seq, n_mlp, i))]
    ppermute x17, waiting for transfers between devices: 17.3 us -> 9.79 us  [swap(): return lax.ppermute(value, axis, [(i, i ^ k) for i in range(size)])]
    ppermute x12, starting transfers between devices: 21 us -> 16.8 us  [send_pieces(): lax.ppermute(piece, ('seq', 'mlp'), piece_pairs(n_seq, n_mlp, i))]
    pallas_call x6 -> x7, Pallas kernels: 5.91 us -> 7.94 us  [the longest x1 3.82 us: rest(): call(functools.partial(rest_kernel, firsts=(first0, first1)), [shape(half...]
where the time goes in v5:
time: 76.1 us; the launch traced here: 75.9 us
  waiting for transfers between devices  28.1 us (37%)
  starting transfers between devices  25.8 us (34%)
  Pallas kernels  20.7 us (27%)
  between operations  0.9 us (1%)
    ppermute x12, waiting for transfers between devices, send_pieces(): lax.ppermute(piece, ('seq', 'mlp'), piece_pairs(n_seq, n_mlp, i))  18.3 us
    ppermute x12, starting transfers between devices, send_pieces(): lax.ppermute(piece, ('seq', 'mlp'), piece_pairs(n_seq, n_mlp, i))  16.8 us
    ppermute x17, waiting for transfers between devices, swap(): return lax.ppermute(value, axis, [(i, i ^ k) for i in range(size)])  9.79 us
    ppermute x17, starting transfers between devices, swap(): return lax.ppermute(value, axis, [(i, i ^ k) for i in range(size)])  8.98 us
    pallas_call x2, Pallas kernels, split_on_device(): call(split_temporal_kernel, [shape(half, width)] * 2, inputs=8, scratch=(...  6.39 us
    pallas_call x1, Pallas kernels, rest(): call(functools.partial(rest_kernel, firsts=(first0, first1)), [shape(half...  3.82 us
    pallas_call x1, Pallas kernels, hold_weights(): pl.pallas_call(hold_kernel, out_shape=pltpu.VMEM((features, parts * width...  3.16 us
    pallas_call x1, Pallas kernels, split_on_device(): call(functools.partial(first_spatial_kernel, first=first0), [shape(rows0,...  2.74 us
  transfers between devices with their start and end apart: 29, of which 14 were waited for; matrix products, arithmetic and copies ran while one was open for 0% of the time, Pallas kernels for 18%

profile of v5, /device:TPU:0, one launch (start us, length us, event | category | flops | bytes accessed | tf_op | source)
XLA Modules:
  0.0 75.9 jit_solution(5429391271248835995)
XLA Ops:
  0.6 2.7 %shard_map.105 = (bf16[256,384]{1,0:T(8,128)(2,1)S(1)}, bf16[128,1536]{1,0:T(8,128)(2,1)S(1)}, bf16[384,1536]{1,0:T(8,128)(2,1)S(1)}, f32[1,1536]{1,0:T(1,128)S(1)}) custom-call(bf16[3,512,384]{2,1,0:T(8,128)(2,1)} %bitcast.19, bf16[384,3072]{1,0:T(8,128)(2,1)} %w_far.1, f32[1,3072]{1,0:T(1,128)} %bitcast.24), custom_call_target="tpu_custom_call" | custom-call | tf_op jit(solution)/shard_map/pallas_call | solution.py:388
  3.4 0.5 collective-permute-start.11
  3.9 0.4 shard_map.106.a_ref
  4.3 1.0 %collective-permute-done.11.b_ref = bf16[128,1536]{1,0:T(8,128)(2,1)S(1)} collective-permute-done((bf16[128,1536]{1,0:T(8,128)(2,1)S(1)}, bf16[128,1536]{1,0:T(8,128)(2,1)S(1)}, u32[]{:S(2)}, u32[]{:S(2)}) %collective-permute-start.11) | collective-permute-done | bytes 393248 | tf_op jit(solution)/shard_map/ppermute | solution.py:325
  5.2 0.1 shard_map.107
  5.3 2.9 %collective-permute-start.12 = (bf16[128,1536]{1,0:T(8,128)(2,1)S(1)}, bf16[128,1536]{1,0:T(8,128)(2,1)S(1)}, u32[]{:S(2)}, u32[]{:S(2)}) collective-permute-start(bf16[128,1536]{1,0:T(8,128)(2,1)S(1)} %shard_map.107), channel_id=1, source_target_pairs={{0,2},{1,3},{2,0},{3,1},{4,6},{5,7},{6,4},{7,5},{8,10},{9,11},{10,... | collective-permute-start | bytes 1179656 | tf_op jit(solution)/shard_map/ppermute | solution.py:325
  8.2 6.8 %conditional.1 = (bf16[128,1536]{1,0:T(8,128)(2,1)}, f32[128,1536]{1,0:T(8,128)S(1)}, f32[128,1536]{1,0:T(8,128)S(1)}) conditional(s32[]{:T(128)} %convert_element_type.3, () %tuple.29, (bf16[1,512,768]{2,1,0:T(8,128)(2,1)}, bf16[256,384]{1,0:T(8,128)(2,1)S(1)}, bf16[3,512,384]{2,1,0:T(8,128)(2,1)}, bf16[384,3072]{1,0:T(8,128)(2,1)}, ...), branch_computations={%region_0.0_spmd, %region_1.0_spmd} | conditional | bytes 4718736 | solution.py:439
  8.2 3.8 %branch_1_fun.4 = (bf16[128,1536]{1,0:T(8,128)(2,1)S(1)}, f32[128,1536]{1,0:T(8,128)S(1)}, f32[128,1536]{1,0:T(8,128)S(1)}, bf16[128,1536]{1,0:T(8,128)(2,1)S(1)...) custom-call(bf16[256,384]{1,0:T(8,128)(2,1)S(1)} %get-tuple-element.59.heads0_ref, ...), custom_call_target="tpu_custom_call" | custom-call | tf_op jit(solution)/shard_map/cond/branch_1_fun/pallas_call | solution.py:406
  12.1 0.1 collective-permute-start
  12.1 0.5 collective-permute-start.1
  12.6 0.1 collective-permute-start.2
  12.7 1.1 %collective-permute-done.b_ref = bf16[128,1536]{1,0:T(8,128)(2,1)S(1)} collective-permute-done((bf16[128,1536]{1,0:T(8,128)(2,1)S(1)}, bf16[128,1536]{1,0:T(8,128)(2,1)S(1)}, u32[]{:S(2)}, u32[]{:S(2)}) %collective-permute-start) | collective-permute-done | bytes 393248 | tf_op jit(solution)/shard_map/cond/branch_1_fun/ppermute | solution.py:325
  13.8 0.8 %branch_1_fun.5 = bf16[128,1536]{1,0:T(8,128)(2,1)} custom-call(f32[128,1536]{1,0:T(8,128)S(1)} %get-tuple-element.64.a_ref, bf16[128,1536]{1,0:T(8,128)(2,1)S(1)} %collective-permute-done.b_ref), custom_call_target="tpu_custom_call" | custom-call | tf_op jit(solution)/shard_map/cond/branch_1_fun/pallas_call | solution.py:425
  14.7 0.0 collective-permute-done.1.b_ref
  14.7 0.1 branch_1_fun.6
  14.7 0.2 collective-permute-done.2.b_ref
  15.0 0.1 branch_1_fun.7
  15.0 0.1 collective-permute-start.14
  15.1 2.6 %collective-permute-done.12.arrived_ref = bf16[128,1536]{1,0:T(8,128)(2,1)S(1)} collective-permute-done((bf16[128,1536]{1,0:T(8,128)(2,1)S(1)}, bf16[128,1536]{1,0:T(8,128)(2,1)S(1)}, u32[]{:S(2)}, u32[]{:S(2)}) %collective-permute-start.12) | collective-permute-done | bytes 393248 | tf_op jit(solution)/shard_map/ppermute | solution.py:325
  17.7 0.1 shard_map.108
  17.8 12.7 %while.32 = (s32[]{:T(128)}, bf16[32,1536]{1,0:T(8,128)(2,1)S(1)}, bf16[32,1536]{1,0:T(8,128)(2,1)S(1)}, bf16[32,1536]{1,0:T(8,128)(2,1)S(1)}, bf16[32,1536]{1,0:T(8,128)(2,1)S(1)}, /*index=5*/s32[]{:T(128)}, s32[]{:T(128)}) while((s32[]{:T(128)}, bf16[32,1536]{1,0:T(8,128)(2,1)S(1)}, bf16[32,1536]{1,0:T(8,128)(2,1)S(1)}, ...), condition=%wide.region_3.0_spmd, body=%wide.region_2.0_spmd.sunk | while | flops 2 | bytes 2359533 | solution.py:458
  18.0 4.8 %collective-permute-start.3 = (bf16[32,1536]{1,0:T(8,128)(2,1)S(1)}, bf16[32,1536]{1,0:T(8,128)(2,1)S(1)}, u32[]{:S(2)}, u32[]{:S(2)}) collective-permute-start(bf16[32,1536]{1,0:T(8,128)(2,1)S(1)} %get-tuple-element.284), channel_id=1, source_target_pairs={{0,28},{1,21},{2,30},{3,23},{4,24},{5,17},{6,26},{7,19},{8,20},{9,... | collective-permute-start | bytes 294920 | tf_op jit(solution)/shard_map/while/body/ppermute | solution.py:374
  22.8 0.8 %collective-permute-start.5 = (bf16[32,1536]{1,0:T(8,128)(2,1)S(1)}, bf16[32,1536]{1,0:T(8,128)(2,1)S(1)}, u32[]{:S(2)}, u32[]{:S(2)}) collective-permute-start(bf16[32,1536]{1,0:T(8,128)(2,1)S(1)} %get-tuple-element.286), channel_id=1, source_target_pairs={{0,8},{1,25},{2,10},{3,27},{4,12},{5,29},{6,14},{7,31},{8,0},{9,17... | collective-permute-start | bytes 294920 | tf_op jit(solution)/shard_map/while/body/ppermute | solution.py:374
  23.6 0.7 collective-permute-start.6
  24.3 2.0 %collective-permute-done.3 = bf16[32,1536]{1,0:T(8,128)(2,1)S(1)} collective-permute-done((bf16[32,1536]{1,0:T(8,128)(2,1)S(1)}, bf16[32,1536]{1,0:T(8,128)(2,1)S(1)}, u32[]{:S(2)}, u32[]{:S(2)}) %collective-permute-start.3) | collective-permute-done | bytes 98336 | tf_op jit(solution)/shard_map/while/body/ppermute | solution.py:374
  26.3 4.1 %collective-permute-done.4 = bf16[32,1536]{1,0:T(8,128)(2,1)S(1)} collective-permute-done((bf16[32,1536]{1,0:T(8,128)(2,1)S(1)}, bf16[32,1536]{1,0:T(8,128)(2,1)S(1)}, u32[]{:S(2)}, u32[]{:S(2)}) %collective-permute-start.4) | collective-permute-done | bytes 98336 | tf_op jit(solution)/shard_map/while/body/ppermute | solution.py:374
  30.5 0.0 collective-permute-done.5
  30.5 0.0 collective-permute-done.6
  30.6 2.0 %collective-permute-start.16 = (bf16[128,1536]{1,0:T(8,128)(2,1)S(1)}, bf16[128,1536]{1,0:T(8,128)(2,1)S(1)}, u32[]{:S(2)}, u32[]{:S(2)}) collective-permute-start(bf16[128,1536]{1,0:T(8,128)(2,1)S(1)} %constant_dynamic-update-slice_fusion.near_ref), channel_id=1, source_target_pairs={{0,2},{1,3},{2,0},{3,1},{4,6},{5,7},{6,4},{7,5},{8,10},{9,11},{10,... | collective-permute-start | bytes 1179656 | tf_op jit(solution)/shard_map/ppermute | solution.py:325
  32.6 0.1 shard_map.109
  32.7 10.7 %while.33 = (s32[]{:T(128)}, bf16[32,1536]{1,0:T(8,128)(2,1)S(1)}, bf16[32,1536]{1,0:T(8,128)(2,1)S(1)}, bf16[32,1536]{1,0:T(8,128)(2,1)S(1)}, bf16[32,1536]{1,0:T(8,128)(2,1)S(1)}, /*index=5*/s32[]{:T(128)}, s32[]{:T(128)}) while((s32[]{:T(128)}, bf16[32,1536]{1,0:T(8,128)(2,1)S(1)}, bf16[32,1536]{1,0:T(8,128)(2,1)S(1)}, ...), condition=%wide.region_5.0_spmd, body=%wide.region_4.0_spmd.sunk | while | flops 2 | bytes 2359533 | solution.py:458
  32.7 3.1 %collective-permute-start.7 = (bf16[32,1536]{1,0:T(8,128)(2,1)S(1)}, bf16[32,1536]{1,0:T(8,128)(2,1)S(1)}, u32[]{:S(2)}, u32[]{:S(2)}) collective-permute-start(bf16[32,1536]{1,0:T(8,128)(2,1)S(1)} %get-tuple-element.305), channel_id=1, source_target_pairs={{0,28},{1,21},{2,30},{3,23},{4,24},{5,17},{6,26},{7,19},{8,20},{9,... | collective-permute-start | bytes 294920 | tf_op jit(solution)/shard_map/while/body/ppermute | solution.py:374
  35.8 1.3 %collective-permute-start.9 = (bf16[32,1536]{1,0:T(8,128)(2,1)S(1)}, bf16[32,1536]{1,0:T(8,128)(2,1)S(1)}, u32[]{:S(2)}, u32[]{:S(2)}) collective-permute-start(bf16[32,1536]{1,0:T(8,128)(2,1)S(1)} %get-tuple-element.307), channel_id=1, source_target_pairs={{0,8},{1,25},{2,10},{3,27},{4,12},{5,29},{6,14},{7,31},{8,0},{9,17... | collective-permute-start | bytes 294920 | tf_op jit(solution)/shard_map/while/body/ppermute | solution.py:374
  37.1 0.7 collective-permute-start.10
  37.8 3.5 %collective-permute-done.7 = bf16[32,1536]{1,0:T(8,128)(2,1)S(1)} collective-permute-done((bf16[32,1536]{1,0:T(8,128)(2,1)S(1)}, bf16[32,1536]{1,0:T(8,128)(2,1)S(1)}, u32[]{:S(2)}, u32[]{:S(2)}) %collective-permute-start.7) | collective-permute-done | bytes 98336 | tf_op jit(solution)/shard_map/while/body/ppermute | solution.py:374
  41.3 2.0 %collective-permute-done.8 = bf16[32,1536]{1,0:T(8,128)(2,1)S(1)} collective-permute-done((bf16[32,1536]{1,0:T(8,128)(2,1)S(1)}, bf16[32,1536]{1,0:T(8,128)(2,1)S(1)}, u32[]{:S(2)}, u32[]{:S(2)}) %collective-permute-start.8) | collective-permute-done | bytes 98336 | tf_op jit(solution)/shard_map/while/body/ppermute | solution.py:374
  43.4 0.1 collective-permute-start.17
  43.6 0.5 collective-permute-start.18
  44.1 0.9 %collective-permute-start.19 = (bf16[128,1536]{1,0:T(8,128)(2,1)S(1)}, bf16[128,1536]{1,0:T(8,128)(2,1)S(1)}, u32[]{:S(2)}, u32[]{:S(2)}) collective-permute-start(bf16[128,1536]{1,0:T(8,128)(2,1)S(1)} %constant_dynamic-update-slice_fusion.4.near_ref), channel_id=1, source_target_pairs={{0,2},{1,3},{2,0},{3,1},{4,6},{5,7},{6,4},{7,5},{8,10},{9,11},{10,... | collective-permute-start | bytes 1179656 | tf_op jit(solution)/shard_map/ppermute | solution.py:325
  45.0 0.5 collective-permute-start.15
  45.5 3.2 %shard_map.112.w_ref = bf16[3072,1152]{1,0:T(8,128)(2,1)S(1)} custom-call(bf16[3,3072,384]{2,1,0:T(8,128)(2,1)} %bitcast.18), custom_call_target="tpu_custom_call" | custom-call | tf_op jit(solution)/shard_map/pallas_call | solution.py:132
  48.7 0.6 shard_map.111.own_normed_ref
  49.3 0.0 collective-permute-done.17.near_ref
  49.3 0.0 collective-permute-done.18.far_ref
  49.3 3.2 %shard_map.113 = (bf16[128,384]{1,0:T(8,128)(2,1)S(1)}, bf16[128,384]{1,0:T(8,128)(2,1)S(1)}) custom-call(bf16[128,3072]{1,0:T(8,128)(2,1)S(1)} %shard_map.111.own_normed_ref, bf16[128,1536]{1,0:T(8,128)(2,1)S(1)} %collective-permute-done.17.near_ref, bf16[128,1536]{1,0:T(8,128)(2,1)S(1)} %collective-permute-done.18.far_ref, f32[1,3072]{1,0:T(1,128)S(1)} %bitcast.11, ...), custom_call_target="tpu_custom_call" | custom-call | tf_op jit(solution)/shard_map/pallas_call | solution.py:480
  52.5 0.1 collective-permute-start.20
  52.6 0.5 collective-permute-start.21
  53.1 0.0 collective-permute-done.13.refs_1_
  53.1 0.0 collective-permute-done.15.refs_3_
  53.1 0.9 %shard_map.110 = bf16[512,768]{1,0:T(8,128)(2,1)} custom-call(bf16[128,768]{1,0:T(8,128)(2,1)S(1)} %get-tuple-element.136.refs_0_, bf16[128,768]{1,0:T(8,128)(2,1)S(1)} %collective-permute-done.13.refs_1_, bf16[128,768]{1,0:T(8,128)(2,1)S(1)} %get-tuple-element.139.refs_2_, bf16[128,768]{1,0:T(8,128)(2,1)S(1)} %collective-permute-done.15.refs_3_), custom_call_target="tpu_custom_call" | custom-call | tf_op jit(solution)/shard_map/pallas_call | solution.py:470
  54.1 1.1 %collective-permute-done.19.far_ref = bf16[128,1536]{1,0:T(8,128)(2,1)S(1)} collective-permute-done((bf16[128,1536]{1,0:T(8,128)(2,1)S(1)}, bf16[128,1536]{1,0:T(8,128)(2,1)S(1)}, u32[]{:S(2)}, u32[]{:S(2)}) %collective-permute-start.19) | collective-permute-done | bytes 393248 | tf_op jit(solution)/shard_map/ppermute | solution.py:325
  55.2 0.6 shard_map.114.own_normed_ref
  55.8 1.1 %collective-permute-done.22.far_ref = bf16[128,1536]{1,0:T(8,128)(2,1)S(1)} collective-permute-done((bf16[128,1536]{1,0:T(8,128)(2,1)S(1)}, bf16[128,1536]{1,0:T(8,128)(2,1)S(1)}, u32[]{:S(2)}, u32[]{:S(2)}) %collective-permute-start.22) | collective-permute-done | bytes 393248 | tf_op jit(solution)/shard_map/ppermute | solution.py:325
  56.9 3.2 %shard_map.115 = (bf16[128,384]{1,0:T(8,128)(2,1)S(1)}, bf16[128,384]{1,0:T(8,128)(2,1)S(1)}) custom-call(bf16[128,3072]{1,0:T(8,128)(2,1)S(1)} %shard_map.114.own_normed_ref, bf16[128,1536]{1,0:T(8,128)(2,1)S(1)} %collective-permute-done.21.near_ref, bf16[128,1536]{1,0:T(8,128)(2,1)S(1)} %collective-permute-done.22.far_ref, f32[1,3072]{1,0:T(1,128)S(1)} %bitcast.13, ...), custom_call_target="tpu_custom_call" | custom-call | tf_op jit(solution)/shard_map/pallas_call | solution.py:480
  60.1 0.2 collective-permute-start.23
  60.3 1.2 %collective-permute-done.23.refs_3_ = bf16[128,384]{1,0:T(8,128)(2,1)S(1)} collective-permute-done((bf16[128,384]{1,0:T(8,128)(2,1)S(1)}, bf16[128,384]{1,0:T(8,128)(2,1)S(1)}, u32[]{:S(2)}, u32[]{:S(2)}) %collective-permute-start.23) | collective-permute-done | bytes 98336 | tf_op jit(solution)/shard_map/ppermute | solution.py:325
  61.5 3.5 %collective-permute-start.24 = (bf16[128,384]{1,0:T(8,128)(2,1)S(1)}, bf16[128,384]{1,0:T(8,128)(2,1)S(1)}, u32[]{:S(2)}, u32[]{:S(2)}) collective-permute-start(bf16[128,384]{1,0:T(8,128)(2,1)S(1)} %get-tuple-element.164), channel_id=1, source_target_pairs={{0,28},{1,21},{2,30},{3,23},{4,24},{5,17},{6,26},{7,19},{8,20},{9,... | collective-permute-start | bytes 294920 | tf_op jit(solution)/shard_map/ppermute | solution.py:374
  65.0 1.4 %collective-permute-start.26 = (bf16[128,384]{1,0:T(8,128)(2,1)S(1)}, bf16[128,384]{1,0:T(8,128)(2,1)S(1)}, u32[]{:S(2)}, u32[]{:S(2)}) collective-permute-start(bf16[128,384]{1,0:T(8,128)(2,1)S(1)} %get-tuple-element.166), channel_id=1, source_target_pairs={{0,8},{1,25},{2,10},{3,27},{4,12},{5,29},{6,14},{7,31},{8,0},{9,17... | collective-permute-start | bytes 294920 | tf_op jit(solution)/shard_map/ppermute | solution.py:374
  66.4 0.7 collective-permute-start.27
  67.0 2.9 %collective-permute-done.24.refs_0_ = bf16[128,384]{1,0:T(8,128)(2,1)S(1)} collective-permute-done((bf16[128,384]{1,0:T(8,128)(2,1)S(1)}, bf16[128,384]{1,0:T(8,128)(2,1)S(1)}, u32[]{:S(2)}, u32[]{:S(2)}) %collective-permute-start.24) | collective-permute-done | bytes 98336 | tf_op jit(solution)/shard_map/ppermute | solution.py:374
  69.9 3.7 %collective-permute-done.25.refs_1_ = bf16[128,384]{1,0:T(8,128)(2,1)S(1)} collective-permute-done((bf16[128,384]{1,0:T(8,128)(2,1)S(1)}, bf16[128,384]{1,0:T(8,128)(2,1)S(1)}, u32[]{:S(2)}, u32[]{:S(2)}) %collective-permute-start.25) | collective-permute-done | bytes 98336 | tf_op jit(solution)/shard_map/ppermute | solution.py:374
  73.6 0.1 collective-permute-start.28
  73.7 1.4 %collective-permute-done.28.refs_4_ = bf16[256,384]{1,0:T(8,128)(2,1)S(1)} collective-permute-done((bf16[256,384]{1,0:T(8,128)(2,1)S(1)}, bf16[256,384]{1,0:T(8,128)(2,1)S(1)}, u32[]{:S(2)}, u32[]{:S(2)}) %collective-permute-start.28) | collective-permute-done | bytes 196640 | tf_op jit(solution)/shard_map/ppermute | solution.py:325
  75.1 0.8 %shard_map.118 = bf16[512,384]{1,0:T(8,128)(2,1)} custom-call(bf16[128,384]{1,0:T(8,128)(2,1)S(1)} %collective-permute-done.24.refs_0_, bf16[128,384]{1,0:T(8,128)(2,1)S(1)} %collective-permute-done.25.refs_1_, bf16[128,384]{1,0:T(8,128)(2,1)S(1)} %collective-permute-done.26.refs_2_, bf16[128,384]{1,0:T(8,128)(2,1)S(1)} %collective-permute-done.27.refs_3_, ...), custom_call_target="tpu_custom_call" | custom-call | tf_op jit(solution)/shard_map/pallas_call | solution.py:494
  (39 shorter events, 0.2 us)
Async XLA Ops:
  3.4 1.9 %collective-permute-start.11 = (bf16[128,1536]{1,0:T(8,128)(2,1)S(1)}, bf16[128,1536]{1,0:T(8,128)(2,1)S(1)}, u32[]{:S(2)}, u32[]{:S(2)}) collective-permute-start(bf16[128,1536]{1,0:T(8,128)(2,1)S(1)} %get-tuple-element.131), channel_id=1, source_target_pairs={{0,1},{1,0},{2,3},{3,2},{4,5},{5,4},{6,7},{7,6},{8,9},{9,8},{10,11... | collective-permute-start | bytes 1179656 | tf_op jit(solution)/shard_map/ppermute | solution.py:325
  5.3 12.4 %collective-permute-start.12 = (bf16[128,1536]{1,0:T(8,128)(2,1)S(1)}, bf16[128,1536]{1,0:T(8,128)(2,1)S(1)}, u32[]{:S(2)}, u32[]{:S(2)}) collective-permute-start(bf16[128,1536]{1,0:T(8,128)(2,1)S(1)} %shard_map.107), channel_id=1, source_target_pairs={{0,2},{1,3},{2,0},{3,1},{4,6},{5,7},{6,4},{7,5},{8,10},{9,11},{10,... | collective-permute-start | bytes 1179656 | tf_op jit(solution)/shard_map/ppermute | solution.py:325
  12.1 1.8 %collective-permute-start = (bf16[128,1536]{1,0:T(8,128)(2,1)S(1)}, bf16[128,1536]{1,0:T(8,128)(2,1)S(1)}, u32[]{:S(2)}, u32[]{:S(2)}) collective-permute-start(bf16[128,1536]{1,0:T(8,128)(2,1)S(1)} %get-tuple-element.65), channel_id=1, source_target_pairs={{0,1},{1,0},{2,3},{3,2},{4,5},{5,4},{6,7},{7,6},{8,9},{9,8},{10,11... | collective-permute-start | bytes 1179656 | tf_op jit(solution)/shard_map/cond/branch_1_fun/ppermute | solution.py:325
  12.1 2.5 %collective-permute-start.1 = (bf16[128,1536]{1,0:T(8,128)(2,1)S(1)}, bf16[128,1536]{1,0:T(8,128)(2,1)S(1)}, u32[]{:S(2)}, u32[]{:S(2)}) collective-permute-start(bf16[128,1536]{1,0:T(8,128)(2,1)S(1)} %get-tuple-element.67), channel_id=1, source_target_pairs={{0,1},{1,0},{2,3},{3,2},{4,5},{5,4},{6,7},{7,6},{8,9},{9,8},{10,11... | collective-permute-start | bytes 1179656 | tf_op jit(solution)/shard_map/cond/branch_1_fun/ppermute | solution.py:325
  12.6 2.3 %collective-permute-start.2 = (bf16[128,1536]{1,0:T(8,128)(2,1)S(1)}, bf16[128,1536]{1,0:T(8,128)(2,1)S(1)}, u32[]{:S(2)}, u32[]{:S(2)}) collective-permute-start(bf16[128,1536]{1,0:T(8,128)(2,1)S(1)} %get-tuple-element.69), channel_id=1, source_target_pairs={{0,1},{1,0},{2,3},{3,2},{4,5},{5,4},{6,7},{7,6},{8,9},{9,8},{10,11... | collective-permute-start | bytes 1179656 | tf_op jit(solution)/shard_map/cond/branch_1_fun/ppermute | solution.py:325
  15.0 17.5 %collective-permute-start.14 = (bf16[128,1536]{1,0:T(8,128)(2,1)}, bf16[128,1536]{1,0:T(8,128)(2,1)S(1)}, u32[]{:S(2)}, u32[]{:S(2)}) collective-permute-start(bf16[128,1536]{1,0:T(8,128)(2,1)} %get-tuple-element.134), channel_id=1, source_target_pairs={{0,2},{1,3},{2,0},{3,1},{4,6},{5,7},{6,4},{7,5},{8,10},{9,11},{10,... | collective-permute-start | bytes 1179656 | tf_op jit(solution)/shard_map/ppermute | solution.py:325
  18.0 8.3 %collective-permute-start.3 = (bf16[32,1536]{1,0:T(8,128)(2,1)S(1)}, bf16[32,1536]{1,0:T(8,128)(2,1)S(1)}, u32[]{:S(2)}, u32[]{:S(2)}) collective-permute-start(bf16[32,1536]{1,0:T(8,128)(2,1)S(1)} %get-tuple-element.284), channel_id=1, source_target_pairs={{0,28},{1,21},{2,30},{3,23},{4,24},{5,17},{6,26},{7,19},{8,20},{9,... | collective-permute-start | bytes 294920 | tf_op jit(solution)/shard_map/while/body/ppermute | solution.py:374
  22.8 7.6 %collective-permute-start.4 = (bf16[32,1536]{1,0:T(8,128)(2,1)S(1)}, bf16[32,1536]{1,0:T(8,128)(2,1)S(1)}, u32[]{:S(2)}, u32[]{:S(2)}) collective-permute-start(bf16[32,1536]{1,0:T(8,128)(2,1)S(1)} %get-tuple-element.285), channel_id=1, source_target_pairs={{0,16},{1,13},{2,18},{3,15},{4,20},{5,9},{6,22},{7,11},{8,24},{9,5... | collective-permute-start | bytes 294920 | tf_op jit(solution)/shard_map/while/body/ppermute | solution.py:374
  22.8 7.6 %collective-permute-start.5 = (bf16[32,1536]{1,0:T(8,128)(2,1)S(1)}, bf16[32,1536]{1,0:T(8,128)(2,1)S(1)}, u32[]{:S(2)}, u32[]{:S(2)}) collective-permute-start(bf16[32,1536]{1,0:T(8,128)(2,1)S(1)} %get-tuple-element.286), channel_id=1, source_target_pairs={{0,8},{1,25},{2,10},{3,27},{4,12},{5,29},{6,14},{7,31},{8,0},{9,17... | collective-permute-start | bytes 294920 | tf_op jit(solution)/shard_map/while/body/ppermute | solution.py:374
  23.6 6.9 %collective-permute-start.6 = (bf16[32,1536]{1,0:T(8,128)(2,1)S(1)}, bf16[32,1536]{1,0:T(8,128)(2,1)S(1)}, u32[]{:S(2)}, u32[]{:S(2)}) collective-permute-start(bf16[32,1536]{1,0:T(8,128)(2,1)S(1)} %get-tuple-element.287), channel_id=1, source_target_pairs={{0,0},{1,5},{2,2},{3,7},{4,4},{5,1},{6,6},{7,3},{8,8},{9,13},{10,1... | collective-permute-start | bytes 294920 | tf_op jit(solution)/shard_map/while/body/ppermute | solution.py:374
  30.6 12.9 %collective-permute-start.16 = (bf16[128,1536]{1,0:T(8,128)(2,1)S(1)}, bf16[128,1536]{1,0:T(8,128)(2,1)S(1)}, u32[]{:S(2)}, u32[]{:S(2)}) collective-permute-start(bf16[128,1536]{1,0:T(8,128)(2,1)S(1)} %constant_dynamic-update-slice_fusion.near_ref), channel_id=1, source_target_pairs={{0,2},{1,3},{2,0},{3,1},{4,6},{5,7},{6,4},{7,5},{8,10},{9,11},{10,... | collective-permute-start | bytes 1179656 | tf_op jit(solution)/shard_map/ppermute | solution.py:325
  32.7 8.6 %collective-permute-start.7 = (bf16[32,1536]{1,0:T(8,128)(2,1)S(1)}, bf16[32,1536]{1,0:T(8,128)(2,1)S(1)}, u32[]{:S(2)}, u32[]{:S(2)}) collective-permute-start(bf16[32,1536]{1,0:T(8,128)(2,1)S(1)} %get-tuple-element.305), channel_id=1, source_target_pairs={{0,28},{1,21},{2,30},{3,23},{4,24},{5,17},{6,26},{7,19},{8,20},{9,... | collective-permute-start | bytes 294920 | tf_op jit(solution)/shard_map/while/body/ppermute | solution.py:374
  35.8 7.5 %collective-permute-start.8 = (bf16[32,1536]{1,0:T(8,128)(2,1)S(1)}, bf16[32,1536]{1,0:T(8,128)(2,1)S(1)}, u32[]{:S(2)}, u32[]{:S(2)}) collective-permute-start(bf16[32,1536]{1,0:T(8,128)(2,1)S(1)} %get-tuple-element.306), channel_id=1, source_target_pairs={{0,16},{1,13},{2,18},{3,15},{4,20},{5,9},{6,22},{7,11},{8,24},{9,5... | collective-permute-start | bytes 294920 | tf_op jit(solution)/shard_map/while/body/ppermute | solution.py:374
  35.8 7.5 %collective-permute-start.9 = (bf16[32,1536]{1,0:T(8,128)(2,1)S(1)}, bf16[32,1536]{1,0:T(8,128)(2,1)S(1)}, u32[]{:S(2)}, u32[]{:S(2)}) collective-permute-start(bf16[32,1536]{1,0:T(8,128)(2,1)S(1)} %get-tuple-element.307), channel_id=1, source_target_pairs={{0,8},{1,25},{2,10},{3,27},{4,12},{5,29},{6,14},{7,31},{8,0},{9,17... | collective-permute-start | bytes 294920 | tf_op jit(solution)/shard_map/while/body/ppermute | solution.py:374
  37.1 6.3 %collective-permute-start.10 = (bf16[32,1536]{1,0:T(8,128)(2,1)S(1)}, bf16[32,1536]{1,0:T(8,128)(2,1)S(1)}, u32[]{:S(2)}, u32[]{:S(2)}) collective-permute-start(bf16[32,1536]{1,0:T(8,128)(2,1)S(1)} %get-tuple-element.308), channel_id=1, source_target_pairs={{0,0},{1,5},{2,2},{3,7},{4,4},{5,1},{6,6},{7,3},{8,8},{9,13},{10,1... | collective-permute-start | bytes 294920 | tf_op jit(solution)/shard_map/while/body/ppermute | solution.py:374
  43.4 5.9 %collective-permute-start.17 = (bf16[128,1536]{1,0:T(8,128)(2,1)S(1)}, bf16[128,1536]{1,0:T(8,128)(2,1)S(1)}, u32[]{:S(2)}, u32[]{:S(2)}) collective-permute-start(bf16[128,1536]{1,0:T(8,128)(2,1)S(1)} %constant_dynamic-update-slice_fusion.near_ref), channel_id=1, source_target_pairs={{0,1},{1,0},{2,3},{3,2},{4,5},{5,4},{6,7},{7,6},{8,9},{9,8},{10,11... | collective-permute-start | bytes 1179656 | tf_op jit(solution)/shard_map/ppermute | solution.py:325
  43.6 5.7 %collective-permute-start.18 = (bf16[128,1536]{1,0:T(8,128)(2,1)S(1)}, bf16[128,1536]{1,0:T(8,128)(2,1)S(1)}, u32[]{:S(2)}, u32[]{:S(2)}) collective-permute-start(bf16[128,1536]{1,0:T(8,128)(2,1)S(1)} %collective-permute-done.16.far_ref), channel_id=1, source_target_pairs={{0,1},{1,0},{2,3},{3,2},{4,5},{5,4},{6,7},{7,6},{8,9},{9,8},{10,11... | collective-permute-start | bytes 1179656 | tf_op jit(solution)/shard_map/ppermute | solution.py:325
  44.1 11.1 %collective-permute-start.19 = (bf16[128,1536]{1,0:T(8,128)(2,1)S(1)}, bf16[128,1536]{1,0:T(8,128)(2,1)S(1)}, u32[]{:S(2)}, u32[]{:S(2)}) collective-permute-start(bf16[128,1536]{1,0:T(8,128)(2,1)S(1)} %constant_dynamic-update-slice_fusion.4.near_ref), channel_id=1, source_target_pairs={{0,2},{1,3},{2,0},{3,1},{4,6},{5,7},{6,4},{7,5},{8,10},{9,11},{10,... | collective-permute-start | bytes 1179656 | tf_op jit(solution)/shard_map/ppermute | solution.py:325
  45.0 8.1 %collective-permute-start.13 = (bf16[128,768]{1,0:T(8,128)(2,1)S(1)}, bf16[128,768]{1,0:T(8,128)(2,1)S(1)}, u32[]{:S(2)}, u32[]{:S(2)}) collective-permute-start(bf16[128,768]{1,0:T(8,128)(2,1)S(1)} %get-tuple-element.137), channel_id=1, source_target_pairs={{0,1},{1,0},{2,3},{3,2},{4,5},{5,4},{6,7},{7,6},{8,9},{9,8},{10,11... | collective-permute-start | bytes 589832 | tf_op jit(solution)/shard_map/ppermute | solution.py:325
  45.0 8.1 %collective-permute-start.15 = (bf16[128,768]{1,0:T(8,128)(2,1)S(1)}, bf16[128,768]{1,0:T(8,128)(2,1)S(1)}, u32[]{:S(2)}, u32[]{:S(2)}) collective-permute-start(bf16[128,768]{1,0:T(8,128)(2,1)S(1)} %get-tuple-element.140), channel_id=1, source_target_pairs={{0,1},{1,0},{2,3},{3,2},{4,5},{5,4},{6,7},{7,6},{8,9},{9,8},{10,11... | collective-permute-start | bytes 589832 | tf_op jit(solution)/shard_map/ppermute | solution.py:325
  45.5 3.2 %copy-start = (f32[3072]{0:T(1024)S(1)}, f32[3072]{0:T(1024)}, u32[]{:S(2)}) copy-start(f32[3072]{0:T(1024)} %param.20) | copy-start | bytes 36868
  45.5 3.2 %copy-start.1 = (f32[3072]{0:T(1024)S(1)}, f32[3072]{0:T(1024)}, u32[]{:S(2)}) copy-start(f32[3072]{0:T(1024)} %param.19) | copy-start | bytes 36868
  45.5 3.8 %copy-start.2 = (f32[8,128]{1,0:T(8,128)S(1)}, f32[8,128]{1,0:T(8,128)}, u32[]{:S(2)}) copy-start(f32[8,128]{1,0:T(8,128)} %constant.22.clone.cos_ref) | copy-start | bytes 12292
  45.5 3.8 %copy-start.3 = (f32[8,128]{1,0:T(8,128)S(1)}, f32[8,128]{1,0:T(8,128)}, u32[]{:S(2)}) copy-start(f32[8,128]{1,0:T(8,128)} %constant.23.clone.sin_ref) | copy-start | bytes 12292
  52.5 2.7 %collective-permute-start.20 = (bf16[128,384]{1,0:T(8,128)(2,1)S(1)}, bf16[128,384]{1,0:T(8,128)(2,1)S(1)}, u32[]{:S(2)}, u32[]{:S(2)}) collective-permute-start(bf16[128,384]{1,0:T(8,128)(2,1)S(1)} %get-tuple-element.160), channel_id=1, source_target_pairs={{0,1},{1,0},{2,3},{3,2},{4,5},{5,4},{6,7},{7,6},{8,9},{9,8},{10,11... | collective-permute-start | bytes 294920 | tf_op jit(solution)/shard_map/ppermute | solution.py:325
  52.6 3.2 %collective-permute-start.21 = (bf16[128,1536]{1,0:T(8,128)(2,1)S(1)}, bf16[128,1536]{1,0:T(8,128)(2,1)S(1)}, u32[]{:S(2)}, u32[]{:S(2)}) collective-permute-start(bf16[128,1536]{1,0:T(8,128)(2,1)S(1)} %constant_dynamic-update-slice_fusion.4.near_ref), channel_id=1, source_target_pairs={{0,1},{1,0},{2,3},{3,2},{4,5},{5,4},{6,7},{7,6},{8,9},{9,8},{10,11... | collective-permute-start | bytes 1179656 | tf_op jit(solution)/shard_map/ppermute | solution.py:325
  55.2 1.7 %collective-permute-start.22 = (bf16[128,1536]{1,0:T(8,128)(2,1)S(1)}, bf16[128,1536]{1,0:T(8,128)(2,1)S(1)}, u32[]{:S(2)}, u32[]{:S(2)}) collective-permute-start(bf16[128,1536]{1,0:T(8,128)(2,1)S(1)} %collective-permute-done.19.far_ref), channel_id=1, source_target_pairs={{0,1},{1,0},{2,3},{3,2},{4,5},{5,4},{6,7},{7,6},{8,9},{9,8},{10,11... | collective-permute-start | bytes 1179656 | tf_op jit(solution)/shard_map/ppermute | solution.py:325
  60.1 1.4 %collective-permute-start.23 = (bf16[128,384]{1,0:T(8,128)(2,1)S(1)}, bf16[128,384]{1,0:T(8,128)(2,1)S(1)}, u32[]{:S(2)}, u32[]{:S(2)}) collective-permute-start(bf16[128,384]{1,0:T(8,128)(2,1)S(1)} %get-tuple-element.163), channel_id=1, source_target_pairs={{0,1},{1,0},{2,3},{3,2},{4,5},{5,4},{6,7},{7,6},{8,9},{9,8},{10,11... | collective-permute-start | bytes 294920 | tf_op jit(solution)/shard_map/ppermute | solution.py:325
  61.5 8.4 %collective-permute-start.24 = (bf16[128,384]{1,0:T(8,128)(2,1)S(1)}, bf16[128,384]{1,0:T(8,128)(2,1)S(1)}, u32[]{:S(2)}, u32[]{:S(2)}) collective-permute-start(bf16[128,384]{1,0:T(8,128)(2,1)S(1)} %get-tuple-element.164), channel_id=1, source_target_pairs={{0,28},{1,21},{2,30},{3,23},{4,24},{5,17},{6,26},{7,19},{8,20},{9,... | collective-permute-start | bytes 294920 | tf_op jit(solution)/shard_map/ppermute | solution.py:374
  65.0 8.6 %collective-permute-start.25 = (bf16[128,384]{1,0:T(8,128)(2,1)S(1)}, bf16[128,384]{1,0:T(8,128)(2,1)S(1)}, u32[]{:S(2)}, u32[]{:S(2)}) collective-permute-start(bf16[128,384]{1,0:T(8,128)(2,1)S(1)} %get-tuple-element.165), channel_id=1, source_target_pairs={{0,16},{1,13},{2,18},{3,15},{4,20},{5,9},{6,22},{7,11},{8,24},{9,5... | collective-permute-start | bytes 294920 | tf_op jit(solution)/shard_map/ppermute | solution.py:374
  65.0 8.6 %collective-permute-start.26 = (bf16[128,384]{1,0:T(8,128)(2,1)S(1)}, bf16[128,384]{1,0:T(8,128)(2,1)S(1)}, u32[]{:S(2)}, u32[]{:S(2)}) collective-permute-start(bf16[128,384]{1,0:T(8,128)(2,1)S(1)} %get-tuple-element.166), channel_id=1, source_target_pairs={{0,8},{1,25},{2,10},{3,27},{4,12},{5,29},{6,14},{7,31},{8,0},{9,17... | collective-permute-start | bytes 294920 | tf_op jit(solution)/shard_map/ppermute | solution.py:374
  66.4 7.2 %collective-permute-start.27 = (bf16[128,384]{1,0:T(8,128)(2,1)S(1)}, bf16[128,384]{1,0:T(8,128)(2,1)S(1)}, u32[]{:S(2)}, u32[]{:S(2)}) collective-permute-start(bf16[128,384]{1,0:T(8,128)(2,1)S(1)} %get-tuple-element.167), channel_id=1, source_target_pairs={{0,0},{1,5},{2,2},{3,7},{4,4},{5,1},{6,6},{7,3},{8,8},{9,13},{10,1... | collective-permute-start | bytes 294920 | tf_op jit(solution)/shard_map/ppermute | solution.py:374
  73.6 1.5 %collective-permute-start.28 = (bf16[256,384]{1,0:T(8,128)(2,1)S(1)}, bf16[256,384]{1,0:T(8,128)(2,1)S(1)}, u32[]{:S(2)}, u32[]{:S(2)}) collective-permute-start(bf16[256,384]{1,0:T(8,128)(2,1)S(1)} %shard_map.117), channel_id=1, source_target_pairs={{0,1},{1,0},{2,3},{3,2},{4,5},{5,4},{6,7},{7,6},{8,9},{9,8},{10,11... | collective-permute-start | bytes 589832 | tf_op jit(solution)/shard_map/ppermute | solution.py:325

commit v6 on v5

--- a/solution.py
+++ b/solution.py
@@ -72,40 +72,41 @@
         ).astype(out_ref.dtype)
 
 
-def project_and_mix(normed_refs, frame_of, write, w_ref, cos_ref, sin_ref, proj_ref):
-    frames = cos_ref.shape[0]
-    width = w_ref.shape[-1] // 3
-    rows = proj_ref.shape[0]
-    count = rows // frames
-    first = 0
-    for ref in normed_refs:
-        size = ref.shape[0]
-        acc = dot(ref[...], w_ref[...])
-        span = slice(first, first + size)
-        proj_ref[span, 2 * width :] = acc[:, 2 * width :].astype(proj_ref.dtype)
-        for low in range(0, size, count):
-            row = pl.ds(frame_of((first + low) // count), 1)
-            cosine, sine = cos_ref[row, :], sin_ref[row, :]
-            for lane in range(0, 2 * width, HEAD_DIM):
-                head = acc[low : low + count, lane : lane + HEAD_DIM]
-                turned = pltpu.roll(head, HEAD_DIM // 2, 1)
-                proj_ref[first + low : first + low + count, lane : lane + HEAD_DIM] = (
-                    head * cosine + turned * sine
-                ).astype(proj_ref.dtype)
-        first += size
+def project(normed_ref, places, w_ref, cos_ref, sin_ref, proj_ref):
+    turned_width = w_ref.shape[-1] // 3 * 2
+    acc = dot(normed_ref[...], w_ref[...])
+    proj_ref[:, turned_width:] = acc[:, turned_width:].astype(proj_ref.dtype)
+    count = acc.shape[0] // len(places)
+    for i, place in enumerate(places):
+        span = slice(i * count, (i + 1) * count)
+        row = pl.ds(place, 1)
+        cosine, sine = cos_ref[row, :], sin_ref[row, :]
+        for lane in range(0, turned_width, HEAD_DIM):
+            head = acc[span, lane : lane + HEAD_DIM]
+            turned = pltpu.roll(head, HEAD_DIM // 2, 1)
+            proj_ref[span, lane : lane + HEAD_DIM] = (head * cosine + turned * sine).astype(
+                proj_ref.dtype
+            )
+
+
+def mix(spans, count, write):
+    frames = len(spans)
+    width = spans[0][0].shape[-1] // 3
     step = GROUP if count % GROUP == 0 else count
     size = step * frames
     patch_of = lambda axis: lax.rem(lax.broadcasted_iota(jnp.int32, (size, size), axis), step)
     same = patch_of(0) == patch_of(1)
-    lanes = range(0, width, HEAD_DIM)
 
     def gathered(low, lane):
         head = slice(lane, lane + HEAD_DIM)
-        if step == count:
-            return proj_ref[:, head]
-        spans = [slice(f * count + low, f * count + low + step) for f in range(frames)]
-        return jnp.concatenate([proj_ref[span, head] for span in spans], axis=0)
-
+        ref = spans[0][0]
+        if step == count and all(span == (ref, i * count) for i, span in enumerate(spans)):
+            return ref[:, head]
+        return jnp.concatenate(
+            [ref[first + low : first + low + step, head] for ref, first in spans], axis=0
+        )
+
+    lanes = range(0, width, HEAD_DIM)
     units = [(low, lane) for low in range(0, count, step) for lane in lanes]
     heads = [tuple(gathered(low, part * width + lane) for part in range(3)) for low, lane in units]
     for (low, lane), mixed in zip(units, attend(heads, same)):
@@ -181,14 +182,21 @@
     qkv_far, w_far, gate_far, heads_ref, message_ref, w_ref, gate_ref, qkv_ref, semaphores, *, first
 ):
     far = chip_columns(w_far.shape[-1], 1)
-    moves = [(qkv_far, qkv_ref), (w_far.at[:, far], w_ref), (gate_far.at[:, far], gate_ref)]
+    query = pl.ds(first, heads_ref.shape[0])
+    moves = [
+        (qkv_far.at[0, query], qkv_ref.at[0, query]),
+        (qkv_far.at[1:], qkv_ref.at[1:]),
+        (w_far.at[:, far], w_ref),
+        (gate_far.at[:, far], gate_ref),
+    ]
     copies = [pltpu.make_async_copy(*move, semaphores.at[i]) for i, move in enumerate(moves)]
     for copy in copies:
         copy.start()
-    copies[0].wait()
+    for copy in copies[:2]:
+        copy.wait()
     spatial_heads(qkv_ref, heads_ref, first)
-    copies[1].wait()
-    copies[2].wait()
+    for copy in copies[2:]:
+        copy.wait()
     term = dot(heads_ref[heads_ref.shape[0] // 2 :, :], w_ref[...])
     message_ref[...] = (term * gate_ref[...]).astype(message_ref.dtype)
 
@@ -252,23 +260,29 @@
     other_ref[...] = jnp.where(core == 0, right, left)
 
 
-def split_blocks(near_ref, far_ref):
-    half = near_ref.shape[-1]
-    return [
-        (ref, pl.multiple_of((chip_of() ^ flip) * half, half))
-        for flip, ref in enumerate((near_ref, far_ref))
+def split_normalize(near, far, gain_ref, shift_ref, out_ref):
+    half = near.shape[-1]
+    blocks = [
+        (ref, pl.multiple_of((chip_of() ^ flip) * half, half)) for flip, ref in enumerate((near, far))
     ]
-
-
-def split_norm_kernel(near_ref, far_ref, gain_ref, shift_ref, out_ref):
-    normalize(split_blocks(near_ref, far_ref), gain_ref, shift_ref, out_ref)
+    normalize(blocks, gain_ref, shift_ref, out_ref)
+
+
+def half_kernel(
+    near, far, gain_ref, shift_ref, w_ref, cos_ref, sin_ref, proj_ref, normed_ref
+):
+    split_normalize(near, far, gain_ref, shift_ref, normed_ref)
+    places = [frame_of(i) for i in range(SHARES)]
+    project(normed_ref, places, w_ref, cos_ref, sin_ref, proj_ref)
 
 
 def split_temporal_kernel(
-    own_normed_ref, near_ref, far_ref, gain_ref, shift_ref, w_ref, cos_ref, sin_ref,
+    own_proj_ref, near, far, gain_ref, shift_ref, w_ref, cos_ref, sin_ref,
     own_ref, other_ref, normed_ref, proj_ref,
 ):
-    normalize(split_blocks(near_ref, far_ref), gain_ref, shift_ref, normed_ref)
+    split_normalize(near, far, gain_ref, shift_ref, normed_ref)
+    places = [frame_of(SHARES + i) for i in range(SHARES)]
+    project(normed_ref, places, w_ref, cos_ref, sin_ref, proj_ref)
     count = own_ref.shape[0] // SHARES
 
     def write(i, low, head, value):
@@ -276,9 +290,8 @@
         start = (i % SHARES) * count + low
         ref[start : start + value.shape[0], head] = value
 
-    project_and_mix(
-        [own_normed_ref, normed_ref], frame_of, write, w_ref, cos_ref, sin_ref, proj_ref
-    )
+    spans = [(ref, i * count) for ref in (own_proj_ref, proj_ref) for i in range(SHARES)]
+    mix(spans, count, write)
 
 
 def pack_kernel(*refs):
@@ -395,7 +408,7 @@
         ],
         inputs=3,
         far=3,
-        scratch=(pltpu.VMEM(qkv.shape, bf16), pltpu.SemaphoreType.DMA((3,))),
+        scratch=(pltpu.VMEM(qkv.shape, bf16), pltpu.SemaphoreType.DMA((4,))),
     )(*(in_hbm(one) for one in (qkv, spatial_out, gate_row)))
     message = swap(message, "mlp", n_mlp, 1)
     far_term = call(term_kernel, shape(half0, both, f32), inputs=3)(heads, far_w, far_gate)
@@ -441,23 +454,30 @@
     )
     arrived1 = swap(sent, "mlp", n_mlp, 2)
     arrived0 = after(arrived0, sent)
-    reduced = [(base0, arrived0), (base1, arrived1)]
-
-    blocks, pieces = [], []
-    for index, ((first, rows), operands) in enumerate(zip(chunks, reduced)):
+
+    def update(rows, base, arrived):
         half = rows // 2
-        own, other, *sends = call(
+        own, other, *pieces = call(
             update_kernel,
             [shape(half, share)] * 2 + [shape(half // SHARES, both)] * SHARES,
             inputs=2,
-        )(*operands)
-        blocks += [own, swap(other, "mlp", n_mlp, 1)]
-        pieces.append(sends)
-    nears = []
-    for sends in pieces:
-        sends = lax.fori_loop(0, once, lambda _, sends: send_pieces(sends), sends)
-        nears.append(jnp.concatenate(sends, axis=0))
-    weights = hold_weights(after(temporal_qkv, *nears))
+        )(base, arrived)
+        return [own, swap(other, "mlp", n_mlp, 1)], pieces
+
+    blocks0, pieces = update(rows0, base0, arrived0)
+    pieces = lax.fori_loop(0, once, lambda _, pieces: send_pieces(pieces), pieces)
+    near0 = jnp.concatenate(pieces, axis=0)
+    blocks1, pieces = update(rows1, base1, after(arrived1, near0))
+
+    def last_exchange(temporal_qkv, *pieces):
+        return (*send_pieces(pieces), hold_weights(temporal_qkv))
+
+    def no_exchange(temporal_qkv, *pieces):
+        return (*pieces, jnp.zeros((features, 3 * width), bf16))
+
+    *pieces, weights = lax.cond(once > 0, last_exchange, no_exchange, temporal_qkv, *pieces)
+    nears = [near0, jnp.concatenate(pieces, axis=0)]
+    blocks = blocks0 + blocks1
 
     own_mixed, other_mixed = [], []
     for (first, rows), near in zip(chunks, nears):
@@ -473,16 +493,20 @@
                 inputs=len(blocks),
             )(*blocks)
             far = after(far, other_mixed[-1], updated)
+        rest_in = (gain_row, shift_row, weights, cosine, sine)
         other_far = swap(far, "mlp", n_mlp, 1)
-        own_normed = call(split_norm_kernel, shape(half, features), inputs=4)(
-            near, far, gain_row, shift_row
-        )
+        own_proj = call(
+            half_kernel,
+            shape(half, 3 * width),
+            inputs=7,
+            scratch=(pltpu.VMEM((half, features), bf16),),
+        )(near, far, *rest_in)
         own, other = call(
             split_temporal_kernel,
             [shape(half, width)] * 2,
             inputs=8,
-            scratch=(pltpu.VMEM((half, features), bf16), pltpu.VMEM((rows, 3 * width), bf16)),
-        )(own_normed, other_near, other_far, gain_row, shift_row, weights, cosine, sine)
+            scratch=(pltpu.VMEM((half, features), bf16), pltpu.VMEM((half, 3 * width), bf16)),
+        )(own_proj, other_near, other_far, *rest_in)
         own_mixed.append(own)
         other_mixed.append(swap(other, "mlp", n_mlp, 1))
     packed = call(
@@ -514,18 +538,20 @@
     u0, u1, u2, u3, gain_ref, shift_ref, w_ref, cos_ref, sin_ref, out_ref, normed_ref, proj_ref
 ):
     share = u0.shape[-1]
-    count = out_ref.shape[0] // cos_ref.shape[0]
+    frames = cos_ref.shape[0]
+    count = out_ref.shape[0] // frames
     blocks = [
         (ref, pl.multiple_of((lax.axis_index("mlp") ^ k) * share, share))
         for k, ref in enumerate((u0, u1, u2, u3))
     ]
     normalize(blocks, gain_ref, shift_ref, normed_ref)
+    project(normed_ref, range(frames), w_ref, cos_ref, sin_ref, proj_ref)
 
     def write(f, low, head, value):
         start = f * count + low
         out_ref[start : start + value.shape[0], head] = value
 
-    project_and_mix([normed_ref], lambda f: f, write, w_ref, cos_ref, sin_ref, proj_ref)
+    mix([(proj_ref, f * count) for f in range(frames)], count, write)
 
 
 def on_device(

time: 76.1 us -> 75.4 us (level)
  waiting for transfers between devices: 28.1 us -> 27.2 us
    ppermute x12, waiting for transfers between devices: 18.3 us -> 15.5 us  [send_pieces(): lax.ppermute(piece, ('seq', 'mlp'), piece_pairs(n_seq, n_mlp, i))]
    pallas_call x4, Pallas kernels: 1.39 us -> 4.01 us  [the longest x2 3.79 us: split_on_device(): call(half_kernel, shape(half, 3 * width), inputs=7, scratch=(pltpu.VMEM((...]
    pallas_call x2, Pallas kernels: 6.39 us -> 4.44 us  [split_on_device(): call(split_temporal_kernel, [shape(half, width)] * 2, inputs=8, scratch=(...]
    ppermute x17, waiting for transfers between devices: 9.79 us -> 11.7 us  [swap(): return lax.ppermute(value, axis, [(i, i ^ k) for i in range(size)])]
  transfers between devices with their start and end apart: 29 -> 29, of which waited for: 14 -> 13; matrix products, arithmetic and copies ran while one was open for 0% -> 0% of each run, Pallas kernels for 18% -> 21%
where the time goes in v6:
time: 75.4 us; the launch traced here: 75.2 us
  waiting for transfers between devices  27.2 us (36%)
  starting transfers between devices  25.6 us (34%)
  Pallas kernels  21.3 us (28%)
  between operations  0.89 us (1%)
    ppermute x12, starting transfers between devices, send_pieces(): lax.ppermute(piece, ('seq', 'mlp'), piece_pairs(n_seq, n_mlp, i))  17 us
    ppermute x12, waiting for transfers between devices, send_pieces(): lax.ppermute(piece, ('seq', 'mlp'), piece_pairs(n_seq, n_mlp, i))  15.5 us
    ppermute x17, waiting for transfers between devices, swap(): return lax.ppermute(value, axis, [(i, i ^ k) for i in range(size)])  11.7 us
    ppermute x17, starting transfers between devices, swap(): return lax.ppermute(value, axis, [(i, i ^ k) for i in range(size)])  8.58 us
    pallas_call x2, Pallas kernels, split_on_device(): call(split_temporal_kernel, [shape(half, width)] * 2, inputs=8, scratch=(...  4.44 us
    pallas_call x1, Pallas kernels, rest(): call(functools.partial(rest_kernel, firsts=(first0, first1)), [shape(half...  3.81 us
    pallas_call x2, Pallas kernels, split_on_device(): call(half_kernel, shape(half, 3 * width), inputs=7, scratch=(pltpu.VMEM((...  3.79 us
    pallas_call x1, Pallas kernels, hold_weights(): pl.pallas_call(hold_kernel, out_shape=pltpu.VMEM((features, parts * width...  3.12 us
  transfers between devices with their start and end apart: 29, of which 13 were waited for; matrix products, arithmetic and copies ran while one was open for 0% of the time, Pallas kernels for 21%

profile of v6, /device:TPU:0, one launch (start us, length us, event | category | flops | bytes accessed | tf_op | source)
XLA Modules:
  0.0 75.2 jit_solution(16246394969982631840)
XLA Ops:
  0.6 2.7 %shard_map.106 = (bf16[256,384]{1,0:T(8,128)(2,1)S(1)}, bf16[128,1536]{1,0:T(8,128)(2,1)S(1)}, bf16[384,1536]{1,0:T(8,128)(2,1)S(1)}, f32[1,1536]{1,0:T(1,128)S(1)}) custom-call(bf16[3,512,384]{2,1,0:T(8,128)(2,1)} %bitcast.19, bf16[384,3072]{1,0:T(8,128)(2,1)} %w_far.1, f32[1,3072]{1,0:T(1,128)} %bitcast.24), custom_call_target="tpu_custom_call" | custom-call | tf_op jit(solution)/shard_map/pallas_call | solution.py:401
  3.4 0.5 collective-permute-start.11
  3.9 0.4 shard_map.107.a_ref
  4.3 1.0 %collective-permute-done.11.b_ref = bf16[128,1536]{1,0:T(8,128)(2,1)S(1)} collective-permute-done((bf16[128,1536]{1,0:T(8,128)(2,1)S(1)}, bf16[128,1536]{1,0:T(8,128)(2,1)S(1)}, u32[]{:S(2)}, u32[]{:S(2)}) %collective-permute-start.11) | collective-permute-done | bytes 393248 | tf_op jit(solution)/shard_map/ppermute | solution.py:338
  5.2 0.1 shard_map.108
  5.3 2.9 %collective-permute-start.12 = (bf16[128,1536]{1,0:T(8,128)(2,1)S(1)}, bf16[128,1536]{1,0:T(8,128)(2,1)S(1)}, u32[]{:S(2)}, u32[]{:S(2)}) collective-permute-start(bf16[128,1536]{1,0:T(8,128)(2,1)S(1)} %shard_map.108), channel_id=1, source_target_pairs={{0,2},{1,3},{2,0},{3,1},{4,6},{5,7},{6,4},{7,5},{8,10},{9,11},{10,... | collective-permute-start | bytes 1179656 | tf_op jit(solution)/shard_map/ppermute | solution.py:338
  8.2 7.5 %conditional.2 = (bf16[128,1536]{1,0:T(8,128)(2,1)}, f32[128,1536]{1,0:T(8,128)S(1)}, f32[128,1536]{1,0:T(8,128)S(1)}) conditional(s32[]{:T(128)} %convert_element_type.4, () %tuple.33, (bf16[1,512,768]{2,1,0:T(8,128)(2,1)}, bf16[256,384]{1,0:T(8,128)(2,1)S(1)}, bf16[3,512,384]{2,1,0:T(8,128)(2,1)}, bf16[384,3072]{1,0:T(8,128)(2,1)}, ...), branch_computations={%region_0.0_spmd, %region_1.0_spmd} | conditional | bytes 4718736 | solution.py:452
  8.2 3.8 %branch_1_fun.5 = (bf16[128,1536]{1,0:T(8,128)(2,1)S(1)}, f32[128,1536]{1,0:T(8,128)S(1)}, f32[128,1536]{1,0:T(8,128)S(1)}, bf16[128,1536]{1,0:T(8,128)(2,1)S(1)...) custom-call(bf16[256,384]{1,0:T(8,128)(2,1)S(1)} %get-tuple-element.53.heads0_ref, ...), custom_call_target="tpu_custom_call" | custom-call | tf_op jit(solution)/shard_map/cond/branch_1_fun/pallas_call | solution.py:419
  12.0 0.1 collective-permute-start.2
  12.1 0.5 collective-permute-start.1
  12.6 0.1 collective-permute-start
  12.7 1.1 %collective-permute-done.2.b_ref = bf16[128,1536]{1,0:T(8,128)(2,1)S(1)} collective-permute-done((bf16[128,1536]{1,0:T(8,128)(2,1)S(1)}, bf16[128,1536]{1,0:T(8,128)(2,1)S(1)}, u32[]{:S(2)}, u32[]{:S(2)}) %collective-permute-start.2) | collective-permute-done | bytes 393248 | tf_op jit(solution)/shard_map/cond/branch_1_fun/ppermute | solution.py:338
  13.8 0.1 branch_1_fun.8
  13.9 0.5 collective-permute-done.1.b_ref
  14.4 0.1 branch_1_fun.7
  14.5 0.5 collective-permute-done.b_ref
  15.0 0.8 %branch_1_fun.6 = bf16[128,1536]{1,0:T(8,128)(2,1)} custom-call(f32[128,1536]{1,0:T(8,128)S(1)} %get-tuple-element.58.a_ref, bf16[128,1536]{1,0:T(8,128)(2,1)S(1)} %collective-permute-done.b_ref), custom_call_target="tpu_custom_call" | custom-call | tf_op jit(solution)/shard_map/cond/branch_1_fun/pallas_call | solution.py:438
  15.8 0.0 collective-permute-start.14
  15.8 1.8 %collective-permute-done.12.arrived_ref = bf16[128,1536]{1,0:T(8,128)(2,1)S(1)} collective-permute-done((bf16[128,1536]{1,0:T(8,128)(2,1)S(1)}, bf16[128,1536]{1,0:T(8,128)(2,1)S(1)}, u32[]{:S(2)}, u32[]{:S(2)}) %collective-permute-start.12) | collective-permute-done | bytes 393248 | tf_op jit(solution)/shard_map/ppermute | solution.py:338
  17.6 0.1 shard_map.109
  17.8 12.6 %while.16 = (s32[]{:T(128)}, bf16[32,1536]{1,0:T(8,128)(2,1)S(1)}, bf16[32,1536]{1,0:T(8,128)(2,1)S(1)}, bf16[32,1536]{1,0:T(8,128)(2,1)S(1)}, bf16[32,1536]{1,0:T(8,128)(2,1)S(1)}, /*index=5*/s32[]{:T(128)}, s32[]{:T(128)}) while((s32[]{:T(128)}, bf16[32,1536]{1,0:T(8,128)(2,1)S(1)}, bf16[32,1536]{1,0:T(8,128)(2,1)S(1)}, ...), condition=%wide.region_3.0_spmd, body=%wide.region_2.0_spmd.sunk | while | flops 2 | bytes 2359533 | solution.py:468
  17.8 4.9 %collective-permute-start.7 = (bf16[32,1536]{1,0:T(8,128)(2,1)S(1)}, bf16[32,1536]{1,0:T(8,128)(2,1)S(1)}, u32[]{:S(2)}, u32[]{:S(2)}) collective-permute-start(bf16[32,1536]{1,0:T(8,128)(2,1)S(1)} %get-tuple-element.233), channel_id=1, source_target_pairs={{0,28},{1,21},{2,30},{3,23},{4,24},{5,17},{6,26},{7,19},{8,20},{9,... | collective-permute-start | bytes 294920 | tf_op jit(solution)/shard_map/while/body/ppermute | solution.py:387
  22.6 0.0 collective-permute-start.8
  22.6 0.8 %collective-permute-start.9 = (bf16[32,1536]{1,0:T(8,128)(2,1)S(1)}, bf16[32,1536]{1,0:T(8,128)(2,1)S(1)}, u32[]{:S(2)}, u32[]{:S(2)}) collective-permute-start(bf16[32,1536]{1,0:T(8,128)(2,1)S(1)} %get-tuple-element.235), channel_id=1, source_target_pairs={{0,8},{1,25},{2,10},{3,27},{4,12},{5,29},{6,14},{7,31},{8,0},{9,17... | collective-permute-start | bytes 294920 | tf_op jit(solution)/shard_map/while/body/ppermute | solution.py:387
  23.4 0.7 collective-permute-start.10
  24.1 2.0 %collective-permute-done.7 = bf16[32,1536]{1,0:T(8,128)(2,1)S(1)} collective-permute-done((bf16[32,1536]{1,0:T(8,128)(2,1)S(1)}, bf16[32,1536]{1,0:T(8,128)(2,1)S(1)}, u32[]{:S(2)}, u32[]{:S(2)}) %collective-permute-start.7) | collective-permute-done | bytes 98336 | tf_op jit(solution)/shard_map/while/body/ppermute | solution.py:387
  26.1 4.1 %collective-permute-done.8 = bf16[32,1536]{1,0:T(8,128)(2,1)S(1)} collective-permute-done((bf16[32,1536]{1,0:T(8,128)(2,1)S(1)}, bf16[32,1536]{1,0:T(8,128)(2,1)S(1)}, u32[]{:S(2)}, u32[]{:S(2)}) %collective-permute-start.8) | collective-permute-done | bytes 98336 | tf_op jit(solution)/shard_map/while/body/ppermute | solution.py:387
  30.3 0.0 collective-permute-done.9
  30.3 0.0 collective-permute-done.10
  30.4 1.5 %collective-permute-start.16 = (bf16[128,1536]{1,0:T(8,128)(2,1)S(1)}, bf16[128,1536]{1,0:T(8,128)(2,1)S(1)}, u32[]{:S(2)}, u32[]{:S(2)}) collective-permute-start(bf16[128,1536]{1,0:T(8,128)(2,1)S(1)} %constant_dynamic-update-slice_fusion.near), channel_id=1, source_target_pairs={{0,2},{1,3},{2,0},{3,1},{4,6},{5,7},{6,4},{7,5},{8,10},{9,11},{10,... | collective-permute-start | bytes 1179656 | tf_op jit(solution)/shard_map/ppermute | solution.py:338
  32.0 0.0 collective-permute-done.14.arrived_ref
  32.0 0.1 shard_map.110
  32.1 0.0 copy-start
  32.1 0.0 copy-start.1
  32.1 0.0 copy-start.2
  32.1 0.0 copy-start.3
  32.1 11.5 %conditional.3 = (bf16[32,1536]{1,0:T(8,128)(2,1)S(1)}, bf16[32,1536]{1,0:T(8,128)(2,1)S(1)}, bf16[32,1536]{1,0:T(8,128)(2,1)S(1)}, bf16[32,1536]{1,0:T(8,128)(2,1)S(1)}, bf16[3072,1152]{1,0:T(8,128)(2,1)S(1)}) conditional(s32[]{:T(128)} %convert_element_type.4, (bf16[32,1536]{1,0:T(8,128)(2,1)S(1)}, bf16[32,1536]{1,0:T(8,128)(2,1)S(1)}, ...), branch_computations={%region_4.0_spmd, %region_5.0_spmd} | conditional | bytes 7077930 | solution.py:478
  32.1 3.5 %collective-permute-start.3 = (bf16[32,1536]{1,0:T(8,128)(2,1)S(1)}, bf16[32,1536]{1,0:T(8,128)(2,1)S(1)}, u32[]{:S(2)}, u32[]{:S(2)}) collective-permute-start(bf16[32,1536]{1,0:T(8,128)(2,1)S(1)} %get-tuple-element.76), channel_id=1, source_target_pairs={{0,28},{1,21},{2,30},{3,23},{4,24},{5,17},{6,26},{7,19},{8,20},{9,... | collective-permute-start | bytes 294920 | tf_op jit(solution)/shard_map/cond/branch_1_fun/ppermute | solution.py:387
  35.6 1.0 %collective-permute-start.5 = (bf16[32,1536]{1,0:T(8,128)(2,1)S(1)}, bf16[32,1536]{1,0:T(8,128)(2,1)S(1)}, u32[]{:S(2)}, u32[]{:S(2)}) collective-permute-start(bf16[32,1536]{1,0:T(8,128)(2,1)S(1)} %get-tuple-element.78), channel_id=1, source_target_pairs={{0,8},{1,25},{2,10},{3,27},{4,12},{5,29},{6,14},{7,31},{8,0},{9,17... | collective-permute-start | bytes 294920 | tf_op jit(solution)/shard_map/cond/branch_1_fun/ppermute | solution.py:387
  36.6 0.8 %collective-permute-start.6 = (bf16[32,1536]{1,0:T(8,128)(2,1)S(1)}, bf16[32,1536]{1,0:T(8,128)(2,1)S(1)}, u32[]{:S(2)}, u32[]{:S(2)}) collective-permute-start(bf16[32,1536]{1,0:T(8,128)(2,1)S(1)} %get-tuple-element.79), channel_id=1, source_target_pairs={{0,0},{1,5},{2,2},{3,7},{4,4},{5,1},{6,6},{7,3},{8,8},{9,13},{10,1... | collective-permute-start | bytes 294920 | tf_op jit(solution)/shard_map/cond/branch_1_fun/ppermute | solution.py:387
  37.4 3.1 %branch_1_fun.9 = bf16[3072,1152]{1,0:T(8,128)(2,1)S(1)} custom-call(bf16[3,3072,384]{2,1,0:T(8,128)(2,1)} %bitcast.18), custom_call_target="tpu_custom_call" | custom-call | tf_op jit(solution)/shard_map/cond/branch_1_fun/pallas_call | solution.py:133
  40.6 2.9 %collective-permute-done.4 = bf16[32,1536]{1,0:T(8,128)(2,1)S(1)} collective-permute-done((bf16[32,1536]{1,0:T(8,128)(2,1)S(1)}, bf16[32,1536]{1,0:T(8,128)(2,1)S(1)}, u32[]{:S(2)}, u32[]{:S(2)}) %collective-permute-start.4) | collective-permute-done | bytes 98336 | tf_op jit(solution)/shard_map/cond/branch_1_fun/ppermute | solution.py:387
  43.6 0.1 collective-permute-start.17
  43.7 0.5 collective-permute-start.18
  44.3 0.5 collective-permute-start.19
  44.8 0.5 collective-permute-start.13
  45.4 1.9 %shard_map.112.own_proj_ref = bf16[128,1152]{1,0:T(8,128)(2,1)S(1)} custom-call(bf16[128,1536]{1,0:T(8,128)(2,1)S(1)} %constant_dynamic-update-slice_fusion.near, bf16[128,1536]{1,0:T(8,128)(2,1)S(1)} %collective-permute-done.16.far, f32[1,3072]{1,0:T(1,128)S(1)} %bitcast.10, f32[1,3072]{1,0:T(1,128)S(1)} %bitcast.14, ...), custom_call_target="tpu_custom_call" | custom-call | tf_op jit(solution)/shard_map/pallas_call | solution.py:498
  47.3 2.2 %shard_map.113 = (bf16[128,384]{1,0:T(8,128)(2,1)S(1)}, bf16[128,384]{1,0:T(8,128)(2,1)S(1)}) custom-call(bf16[128,1152]{1,0:T(8,128)(2,1)S(1)} %shard_map.112.own_proj_ref, bf16[128,1536]{1,0:T(8,128)(2,1)S(1)} %collective-permute-done.17.near, bf16[128,1536]{1,0:T(8,128)(2,1)S(1)} %collective-permute-done.18.far, f32[1,3072]{1,0:T(1,128)S(1)} %bitcast.11, ...), custom_call_target="tpu_custom_call" | custom-call | tf_op jit(solution)/shard_map/pallas_call | solution.py:504
  49.5 0.1 collective-permute-start.20
  49.6 0.5 collective-permute-start.21
  50.1 0.9 %shard_map.111 = bf16[512,768]{1,0:T(8,128)(2,1)} custom-call(bf16[128,768]{1,0:T(8,128)(2,1)S(1)} %get-tuple-element.132.refs_0_, bf16[128,768]{1,0:T(8,128)(2,1)S(1)} %collective-permute-done.13.refs_1_, bf16[128,768]{1,0:T(8,128)(2,1)S(1)} %get-tuple-element.144.refs_2_, bf16[128,768]{1,0:T(8,128)(2,1)S(1)} %collective-permute-done.15.refs_3_), custom_call_target="tpu_custom_call" | custom-call | tf_op jit(solution)/shard_map/pallas_call | solution.py:490
  51.0 4.4 %collective-permute-done.19.far = bf16[128,1536]{1,0:T(8,128)(2,1)S(1)} collective-permute-done((bf16[128,1536]{1,0:T(8,128)(2,1)S(1)}, bf16[128,1536]{1,0:T(8,128)(2,1)S(1)}, u32[]{:S(2)}, u32[]{:S(2)}) %collective-permute-start.19) | collective-permute-done | bytes 393248 | tf_op jit(solution)/shard_map/ppermute | solution.py:338
  55.4 1.9 %shard_map.114.own_proj_ref = bf16[128,1152]{1,0:T(8,128)(2,1)S(1)} custom-call(bf16[128,1536]{1,0:T(8,128)(2,1)S(1)} %constant_dynamic-update-slice_fusion.4.near, bf16[128,1536]{1,0:T(8,128)(2,1)S(1)} %collective-permute-done.19.far, f32[1,3072]{1,0:T(1,128)S(1)} %bitcast.12, f32[1,3072]{1,0:T(1,128)S(1)} %bitcast.16, ...), custom_call_target="tpu_custom_call" | custom-call | tf_op jit(solution)/shard_map/pallas_call | solution.py:498
  57.3 2.2 %shard_map.115 = (bf16[128,384]{1,0:T(8,128)(2,1)S(1)}, bf16[128,384]{1,0:T(8,128)(2,1)S(1)}) custom-call(bf16[128,1152]{1,0:T(8,128)(2,1)S(1)} %shard_map.114.own_proj_ref, bf16[128,1536]{1,0:T(8,128)(2,1)S(1)} %collective-permute-done.21.near, bf16[128,1536]{1,0:T(8,128)(2,1)S(1)} %collective-permute-done.22.far, f32[1,3072]{1,0:T(1,128)S(1)} %bitcast.13, ...), custom_call_target="tpu_custom_call" | custom-call | tf_op jit(solution)/shard_map/pallas_call | solution.py:504
  59.5 0.6 collective-permute-start.23
  60.1 0.9 %collective-permute-done.23.refs_3_ = bf16[128,384]{1,0:T(8,128)(2,1)S(1)} collective-permute-done((bf16[128,384]{1,0:T(8,128)(2,1)S(1)}, bf16[128,384]{1,0:T(8,128)(2,1)S(1)}, u32[]{:S(2)}, u32[]{:S(2)}) %collective-permute-start.23) | collective-permute-done | bytes 98336 | tf_op jit(solution)/shard_map/ppermute | solution.py:338
  61.1 2.4 %collective-permute-start.24 = (bf16[128,384]{1,0:T(8,128)(2,1)S(1)}, bf16[128,384]{1,0:T(8,128)(2,1)S(1)}, u32[]{:S(2)}, u32[]{:S(2)}) collective-permute-start(bf16[128,384]{1,0:T(8,128)(2,1)S(1)} %get-tuple-element.161), channel_id=1, source_target_pairs={{0,28},{1,21},{2,30},{3,23},{4,24},{5,17},{6,26},{7,19},{8,20},{9,... | collective-permute-start | bytes 294920 | tf_op jit(solution)/shard_map/ppermute | solution.py:387
  63.5 2.4 %collective-permute-start.26 = (bf16[128,384]{1,0:T(8,128)(2,1)S(1)}, bf16[128,384]{1,0:T(8,128)(2,1)S(1)}, u32[]{:S(2)}, u32[]{:S(2)}) collective-permute-start(bf16[128,384]{1,0:T(8,128)(2,1)S(1)} %get-tuple-element.163), channel_id=1, source_target_pairs={{0,8},{1,25},{2,10},{3,27},{4,12},{5,29},{6,14},{7,31},{8,0},{9,17... | collective-permute-start | bytes 294920 | tf_op jit(solution)/shard_map/ppermute | solution.py:387
  65.9 0.7 collective-permute-start.27
  66.5 3.1 %collective-permute-done.24.refs_0_ = bf16[128,384]{1,0:T(8,128)(2,1)S(1)} collective-permute-done((bf16[128,384]{1,0:T(8,128)(2,1)S(1)}, bf16[128,384]{1,0:T(8,128)(2,1)S(1)}, u32[]{:S(2)}, u32[]{:S(2)}) %collective-permute-start.24) | collective-permute-done | bytes 98336 | tf_op jit(solution)/shard_map/ppermute | solution.py:387
  69.6 3.3 %collective-permute-done.25.refs_1_ = bf16[128,384]{1,0:T(8,128)(2,1)S(1)} collective-permute-done((bf16[128,384]{1,0:T(8,128)(2,1)S(1)}, bf16[128,384]{1,0:T(8,128)(2,1)S(1)}, u32[]{:S(2)}, u32[]{:S(2)}) %collective-permute-start.25) | collective-permute-done | bytes 98336 | tf_op jit(solution)/shard_map/ppermute | solution.py:387
  72.9 0.1 collective-permute-start.28
  73.0 1.4 %collective-permute-done.28.refs_4_ = bf16[256,384]{1,0:T(8,128)(2,1)S(1)} collective-permute-done((bf16[256,384]{1,0:T(8,128)(2,1)S(1)}, bf16[256,384]{1,0:T(8,128)(2,1)S(1)}, u32[]{:S(2)}, u32[]{:S(2)}) %collective-permute-start.28) | collective-permute-done | bytes 196640 | tf_op jit(solution)/shard_map/ppermute | solution.py:338
  74.4 0.8 %shard_map.118 = bf16[512,384]{1,0:T(8,128)(2,1)} custom-call(bf16[128,384]{1,0:T(8,128)(2,1)S(1)} %collective-permute-done.24.refs_0_, bf16[128,384]{1,0:T(8,128)(2,1)S(1)} %collective-permute-done.25.refs_1_, bf16[128,384]{1,0:T(8,128)(2,1)S(1)} %collective-permute-done.26.refs_2_, bf16[128,384]{1,0:T(8,128)(2,1)S(1)} %collective-permute-done.27.refs_3_, ...), custom_call_target="tpu_custom_call" | custom-call | tf_op jit(solution)/shard_map/pallas_call | solution.py:518
  (39 shorter events, 0.2 us)
Async XLA Ops:
  3.4 1.9 %collective-permute-start.11 = (bf16[128,1536]{1,0:T(8,128)(2,1)S(1)}, bf16[128,1536]{1,0:T(8,128)(2,1)S(1)}, u32[]{:S(2)}, u32[]{:S(2)}) collective-permute-start(bf16[128,1536]{1,0:T(8,128)(2,1)S(1)} %get-tuple-element.127), channel_id=1, source_target_pairs={{0,1},{1,0},{2,3},{3,2},{4,5},{5,4},{6,7},{7,6},{8,9},{9,8},{10,11... | collective-permute-start | bytes 1179656 | tf_op jit(solution)/shard_map/ppermute | solution.py:338
  5.3 12.3 %collective-permute-start.12 = (bf16[128,1536]{1,0:T(8,128)(2,1)S(1)}, bf16[128,1536]{1,0:T(8,128)(2,1)S(1)}, u32[]{:S(2)}, u32[]{:S(2)}) collective-permute-start(bf16[128,1536]{1,0:T(8,128)(2,1)S(1)} %shard_map.108), channel_id=1, source_target_pairs={{0,2},{1,3},{2,0},{3,1},{4,6},{5,7},{6,4},{7,5},{8,10},{9,11},{10,... | collective-permute-start | bytes 1179656 | tf_op jit(solution)/shard_map/ppermute | solution.py:338
  12.0 1.8 %collective-permute-start.2 = (bf16[128,1536]{1,0:T(8,128)(2,1)S(1)}, bf16[128,1536]{1,0:T(8,128)(2,1)S(1)}, u32[]{:S(2)}, u32[]{:S(2)}) collective-permute-start(bf16[128,1536]{1,0:T(8,128)(2,1)S(1)} %get-tuple-element.63), channel_id=1, source_target_pairs={{0,1},{1,0},{2,3},{3,2},{4,5},{5,4},{6,7},{7,6},{8,9},{9,8},{10,11... | collective-permute-start | bytes 1179656 | tf_op jit(solution)/shard_map/cond/branch_1_fun/ppermute | solution.py:338
  12.1 2.3 %collective-permute-start.1 = (bf16[128,1536]{1,0:T(8,128)(2,1)S(1)}, bf16[128,1536]{1,0:T(8,128)(2,1)S(1)}, u32[]{:S(2)}, u32[]{:S(2)}) collective-permute-start(bf16[128,1536]{1,0:T(8,128)(2,1)S(1)} %get-tuple-element.61), channel_id=1, source_target_pairs={{0,1},{1,0},{2,3},{3,2},{4,5},{5,4},{6,7},{7,6},{8,9},{9,8},{10,11... | collective-permute-start | bytes 1179656 | tf_op jit(solution)/shard_map/cond/branch_1_fun/ppermute | solution.py:338
  12.6 2.3 %collective-permute-start = (bf16[128,1536]{1,0:T(8,128)(2,1)S(1)}, bf16[128,1536]{1,0:T(8,128)(2,1)S(1)}, u32[]{:S(2)}, u32[]{:S(2)}) collective-permute-start(bf16[128,1536]{1,0:T(8,128)(2,1)S(1)} %get-tuple-element.59), channel_id=1, source_target_pairs={{0,1},{1,0},{2,3},{3,2},{4,5},{5,4},{6,7},{7,6},{8,9},{9,8},{10,11... | collective-permute-start | bytes 1179656 | tf_op jit(solution)/shard_map/cond/branch_1_fun/ppermute | solution.py:338
  15.8 16.2 %collective-permute-start.14 = (bf16[128,1536]{1,0:T(8,128)(2,1)}, bf16[128,1536]{1,0:T(8,128)(2,1)S(1)}, u32[]{:S(2)}, u32[]{:S(2)}) collective-permute-start(bf16[128,1536]{1,0:T(8,128)(2,1)} %get-tuple-element.130), channel_id=1, source_target_pairs={{0,2},{1,3},{2,0},{3,1},{4,6},{5,7},{6,4},{7,5},{8,10},{9,11},{10,... | collective-permute-start | bytes 1179656 | tf_op jit(solution)/shard_map/ppermute | solution.py:338
  17.8 8.4 %collective-permute-start.7 = (bf16[32,1536]{1,0:T(8,128)(2,1)S(1)}, bf16[32,1536]{1,0:T(8,128)(2,1)S(1)}, u32[]{:S(2)}, u32[]{:S(2)}) collective-permute-start(bf16[32,1536]{1,0:T(8,128)(2,1)S(1)} %get-tuple-element.233), channel_id=1, source_target_pairs={{0,28},{1,21},{2,30},{3,23},{4,24},{5,17},{6,26},{7,19},{8,20},{9,... | collective-permute-start | bytes 294920 | tf_op jit(solution)/shard_map/while/body/ppermute | solution.py:387
  22.6 7.6 %collective-permute-start.8 = (bf16[32,1536]{1,0:T(8,128)(2,1)S(1)}, bf16[32,1536]{1,0:T(8,128)(2,1)S(1)}, u32[]{:S(2)}, u32[]{:S(2)}) collective-permute-start(bf16[32,1536]{1,0:T(8,128)(2,1)S(1)} %get-tuple-element.234), channel_id=1, source_target_pairs={{0,16},{1,13},{2,18},{3,15},{4,20},{5,9},{6,22},{7,11},{8,24},{9,5... | collective-permute-start | bytes 294920 | tf_op jit(solution)/shard_map/while/body/ppermute | solution.py:387
  22.6 7.6 %collective-permute-start.9 = (bf16[32,1536]{1,0:T(8,128)(2,1)S(1)}, bf16[32,1536]{1,0:T(8,128)(2,1)S(1)}, u32[]{:S(2)}, u32[]{:S(2)}) collective-permute-start(bf16[32,1536]{1,0:T(8,128)(2,1)S(1)} %get-tuple-element.235), channel_id=1, source_target_pairs={{0,8},{1,25},{2,10},{3,27},{4,12},{5,29},{6,14},{7,31},{8,0},{9,17... | collective-permute-start | bytes 294920 | tf_op jit(solution)/shard_map/while/body/ppermute | solution.py:387
  23.4 6.9 %collective-permute-start.10 = (bf16[32,1536]{1,0:T(8,128)(2,1)S(1)}, bf16[32,1536]{1,0:T(8,128)(2,1)S(1)}, u32[]{:S(2)}, u32[]{:S(2)}) collective-permute-start(bf16[32,1536]{1,0:T(8,128)(2,1)S(1)} %get-tuple-element.236), channel_id=1, source_target_pairs={{0,0},{1,5},{2,2},{3,7},{4,4},{5,1},{6,6},{7,3},{8,8},{9,13},{10,1... | collective-permute-start | bytes 294920 | tf_op jit(solution)/shard_map/while/body/ppermute | solution.py:387
  30.4 13.3 %collective-permute-start.16 = (bf16[128,1536]{1,0:T(8,128)(2,1)S(1)}, bf16[128,1536]{1,0:T(8,128)(2,1)S(1)}, u32[]{:S(2)}, u32[]{:S(2)}) collective-permute-start(bf16[128,1536]{1,0:T(8,128)(2,1)S(1)} %constant_dynamic-update-slice_fusion.near), channel_id=1, source_target_pairs={{0,2},{1,3},{2,0},{3,1},{4,6},{5,7},{6,4},{7,5},{8,10},{9,11},{10,... | collective-permute-start | bytes 1179656 | tf_op jit(solution)/shard_map/ppermute | solution.py:338
  32.1 13.3 %copy-start = (f32[3072]{0:T(1024)S(1)}, f32[3072]{0:T(1024)}, u32[]{:S(2)}) copy-start(f32[3072]{0:T(1024)} %param.20) | copy-start | bytes 36868
  32.1 13.3 %copy-start.1 = (f32[3072]{0:T(1024)S(1)}, f32[3072]{0:T(1024)}, u32[]{:S(2)}) copy-start(f32[3072]{0:T(1024)} %param.19) | copy-start | bytes 36868
  32.1 13.2 %copy-start.2 = (f32[8,128]{1,0:T(8,128)S(1)}, f32[8,128]{1,0:T(8,128)}, u32[]{:S(2)}) copy-start(f32[8,128]{1,0:T(8,128)} %constant.22.clone.cos_ref) | copy-start | bytes 12292
  32.1 13.2 %copy-start.3 = (f32[8,128]{1,0:T(8,128)S(1)}, f32[8,128]{1,0:T(8,128)}, u32[]{:S(2)}) copy-start(f32[8,128]{1,0:T(8,128)} %constant.23.clone.sin_ref) | copy-start | bytes 12292
  32.1 8.4 %collective-permute-start.3 = (bf16[32,1536]{1,0:T(8,128)(2,1)S(1)}, bf16[32,1536]{1,0:T(8,128)(2,1)S(1)}, u32[]{:S(2)}, u32[]{:S(2)}) collective-permute-start(bf16[32,1536]{1,0:T(8,128)(2,1)S(1)} %get-tuple-element.76), channel_id=1, source_target_pairs={{0,28},{1,21},{2,30},{3,23},{4,24},{5,17},{6,26},{7,19},{8,20},{9,... | collective-permute-start | bytes 294920 | tf_op jit(solution)/shard_map/cond/branch_1_fun/ppermute | solution.py:387
  35.6 7.9 %collective-permute-start.4 = (bf16[32,1536]{1,0:T(8,128)(2,1)S(1)}, bf16[32,1536]{1,0:T(8,128)(2,1)S(1)}, u32[]{:S(2)}, u32[]{:S(2)}) collective-permute-start(bf16[32,1536]{1,0:T(8,128)(2,1)S(1)} %get-tuple-element.77), channel_id=1, source_target_pairs={{0,16},{1,13},{2,18},{3,15},{4,20},{5,9},{6,22},{7,11},{8,24},{9,5... | collective-permute-start | bytes 294920 | tf_op jit(solution)/shard_map/cond/branch_1_fun/ppermute | solution.py:387
  35.6 7.9 %collective-permute-start.5 = (bf16[32,1536]{1,0:T(8,128)(2,1)S(1)}, bf16[32,1536]{1,0:T(8,128)(2,1)S(1)}, u32[]{:S(2)}, u32[]{:S(2)}) collective-permute-start(bf16[32,1536]{1,0:T(8,128)(2,1)S(1)} %get-tuple-element.78), channel_id=1, source_target_pairs={{0,8},{1,25},{2,10},{3,27},{4,12},{5,29},{6,14},{7,31},{8,0},{9,17... | collective-permute-start | bytes 294920 | tf_op jit(solution)/shard_map/cond/branch_1_fun/ppermute | solution.py:387
  36.6 7.0 %collective-permute-start.6 = (bf16[32,1536]{1,0:T(8,128)(2,1)S(1)}, bf16[32,1536]{1,0:T(8,128)(2,1)S(1)}, u32[]{:S(2)}, u32[]{:S(2)}) collective-permute-start(bf16[32,1536]{1,0:T(8,128)(2,1)S(1)} %get-tuple-element.79), channel_id=1, source_target_pairs={{0,0},{1,5},{2,2},{3,7},{4,4},{5,1},{6,6},{7,3},{8,8},{9,13},{10,1... | collective-permute-start | bytes 294920 | tf_op jit(solution)/shard_map/cond/branch_1_fun/ppermute | solution.py:387
  43.6 3.7 %collective-permute-start.17 = (bf16[128,1536]{1,0:T(8,128)(2,1)S(1)}, bf16[128,1536]{1,0:T(8,128)(2,1)S(1)}, u32[]{:S(2)}, u32[]{:S(2)}) collective-permute-start(bf16[128,1536]{1,0:T(8,128)(2,1)S(1)} %constant_dynamic-update-slice_fusion.near), channel_id=1, source_target_pairs={{0,1},{1,0},{2,3},{3,2},{4,5},{5,4},{6,7},{7,6},{8,9},{9,8},{10,11... | collective-permute-start | bytes 1179656 | tf_op jit(solution)/shard_map/ppermute | solution.py:338
  43.7 3.5 %collective-permute-start.18 = (bf16[128,1536]{1,0:T(8,128)(2,1)S(1)}, bf16[128,1536]{1,0:T(8,128)(2,1)S(1)}, u32[]{:S(2)}, u32[]{:S(2)}) collective-permute-start(bf16[128,1536]{1,0:T(8,128)(2,1)S(1)} %collective-permute-done.16.far), channel_id=1, source_target_pairs={{0,1},{1,0},{2,3},{3,2},{4,5},{5,4},{6,7},{7,6},{8,9},{9,8},{10,11... | collective-permute-start | bytes 1179656 | tf_op jit(solution)/shard_map/ppermute | solution.py:338
  44.3 11.1 %collective-permute-start.19 = (bf16[128,1536]{1,0:T(8,128)(2,1)S(1)}, bf16[128,1536]{1,0:T(8,128)(2,1)S(1)}, u32[]{:S(2)}, u32[]{:S(2)}) collective-permute-start(bf16[128,1536]{1,0:T(8,128)(2,1)S(1)} %constant_dynamic-update-slice_fusion.4.near), channel_id=1, source_target_pairs={{0,2},{1,3},{2,0},{3,1},{4,6},{5,7},{6,4},{7,5},{8,10},{9,11},{10,... | collective-permute-start | bytes 1179656 | tf_op jit(solution)/shard_map/ppermute | solution.py:338
  44.8 5.3 %collective-permute-start.15 = (bf16[128,768]{1,0:T(8,128)(2,1)S(1)}, bf16[128,768]{1,0:T(8,128)(2,1)S(1)}, u32[]{:S(2)}, u32[]{:S(2)}) collective-permute-start(bf16[128,768]{1,0:T(8,128)(2,1)S(1)} %get-tuple-element.145), channel_id=1, source_target_pairs={{0,1},{1,0},{2,3},{3,2},{4,5},{5,4},{6,7},{7,6},{8,9},{9,8},{10,11... | collective-permute-start | bytes 589832 | tf_op jit(solution)/shard_map/ppermute | solution.py:338
  44.8 5.3 %collective-permute-start.13 = (bf16[128,768]{1,0:T(8,128)(2,1)S(1)}, bf16[128,768]{1,0:T(8,128)(2,1)S(1)}, u32[]{:S(2)}, u32[]{:S(2)}) collective-permute-start(bf16[128,768]{1,0:T(8,128)(2,1)S(1)} %get-tuple-element.133), channel_id=1, source_target_pairs={{0,1},{1,0},{2,3},{3,2},{4,5},{5,4},{6,7},{7,6},{8,9},{9,8},{10,11... | collective-permute-start | bytes 589832 | tf_op jit(solution)/shard_map/ppermute | solution.py:338
  49.5 5.9 %collective-permute-start.20 = (bf16[128,384]{1,0:T(8,128)(2,1)S(1)}, bf16[128,384]{1,0:T(8,128)(2,1)S(1)}, u32[]{:S(2)}, u32[]{:S(2)}) collective-permute-start(bf16[128,384]{1,0:T(8,128)(2,1)S(1)} %get-tuple-element.157), channel_id=1, source_target_pairs={{0,1},{1,0},{2,3},{3,2},{4,5},{5,4},{6,7},{7,6},{8,9},{9,8},{10,11... | collective-permute-start | bytes 294920 | tf_op jit(solution)/shard_map/ppermute | solution.py:338
  49.6 7.7 %collective-permute-start.21 = (bf16[128,1536]{1,0:T(8,128)(2,1)S(1)}, bf16[128,1536]{1,0:T(8,128)(2,1)S(1)}, u32[]{:S(2)}, u32[]{:S(2)}) collective-permute-start(bf16[128,1536]{1,0:T(8,128)(2,1)S(1)} %constant_dynamic-update-slice_fusion.4.near), channel_id=1, source_target_pairs={{0,1},{1,0},{2,3},{3,2},{4,5},{5,4},{6,7},{7,6},{8,9},{9,8},{10,11... | collective-permute-start | bytes 1179656 | tf_op jit(solution)/shard_map/ppermute | solution.py:338
  55.4 1.9 %collective-permute-start.22 = (bf16[128,1536]{1,0:T(8,128)(2,1)S(1)}, bf16[128,1536]{1,0:T(8,128)(2,1)S(1)}, u32[]{:S(2)}, u32[]{:S(2)}) collective-permute-start(bf16[128,1536]{1,0:T(8,128)(2,1)S(1)} %collective-permute-done.19.far), channel_id=1, source_target_pairs={{0,1},{1,0},{2,3},{3,2},{4,5},{5,4},{6,7},{7,6},{8,9},{9,8},{10,11... | collective-permute-start | bytes 1179656 | tf_op jit(solution)/shard_map/ppermute | solution.py:338
  59.5 1.5 %collective-permute-start.23 = (bf16[128,384]{1,0:T(8,128)(2,1)S(1)}, bf16[128,384]{1,0:T(8,128)(2,1)S(1)}, u32[]{:S(2)}, u32[]{:S(2)}) collective-permute-start(bf16[128,384]{1,0:T(8,128)(2,1)S(1)} %get-tuple-element.160), channel_id=1, source_target_pairs={{0,1},{1,0},{2,3},{3,2},{4,5},{5,4},{6,7},{7,6},{8,9},{9,8},{10,11... | collective-permute-start | bytes 294920 | tf_op jit(solution)/shard_map/ppermute | solution.py:338
  61.1 8.5 %collective-permute-start.24 = (bf16[128,384]{1,0:T(8,128)(2,1)S(1)}, bf16[128,384]{1,0:T(8,128)(2,1)S(1)}, u32[]{:S(2)}, u32[]{:S(2)}) collective-permute-start(bf16[128,384]{1,0:T(8,128)(2,1)S(1)} %get-tuple-element.161), channel_id=1, source_target_pairs={{0,28},{1,21},{2,30},{3,23},{4,24},{5,17},{6,26},{7,19},{8,20},{9,... | collective-permute-start | bytes 294920 | tf_op jit(solution)/shard_map/ppermute | solution.py:387
  63.5 9.4 %collective-permute-start.25 = (bf16[128,384]{1,0:T(8,128)(2,1)S(1)}, bf16[128,384]{1,0:T(8,128)(2,1)S(1)}, u32[]{:S(2)}, u32[]{:S(2)}) collective-permute-start(bf16[128,384]{1,0:T(8,128)(2,1)S(1)} %get-tuple-element.162), channel_id=1, source_target_pairs={{0,16},{1,13},{2,18},{3,15},{4,20},{5,9},{6,22},{7,11},{8,24},{9,5... | collective-permute-start | bytes 294920 | tf_op jit(solution)/shard_map/ppermute | solution.py:387
  63.5 9.4 %collective-permute-start.26 = (bf16[128,384]{1,0:T(8,128)(2,1)S(1)}, bf16[128,384]{1,0:T(8,128)(2,1)S(1)}, u32[]{:S(2)}, u32[]{:S(2)}) collective-permute-start(bf16[128,384]{1,0:T(8,128)(2,1)S(1)} %get-tuple-element.163), channel_id=1, source_target_pairs={{0,8},{1,25},{2,10},{3,27},{4,12},{5,29},{6,14},{7,31},{8,0},{9,17... | collective-permute-start | bytes 294920 | tf_op jit(solution)/shard_map/ppermute | solution.py:387
  65.9 7.1 %collective-permute-start.27 = (bf16[128,384]{1,0:T(8,128)(2,1)S(1)}, bf16[128,384]{1,0:T(8,128)(2,1)S(1)}, u32[]{:S(2)}, u32[]{:S(2)}) collective-permute-start(bf16[128,384]{1,0:T(8,128)(2,1)S(1)} %get-tuple-element.164), channel_id=1, source_target_pairs={{0,0},{1,5},{2,2},{3,7},{4,4},{5,1},{6,6},{7,3},{8,8},{9,13},{10,1... | collective-permute-start | bytes 294920 | tf_op jit(solution)/shard_map/ppermute | solution.py:387
  72.9 1.5 %collective-permute-start.28 = (bf16[256,384]{1,0:T(8,128)(2,1)S(1)}, bf16[256,384]{1,0:T(8,128)(2,1)S(1)}, u32[]{:S(2)}, u32[]{:S(2)}) collective-permute-start(bf16[256,384]{1,0:T(8,128)(2,1)S(1)} %shard_map.117), channel_id=1, source_target_pairs={{0,1},{1,0},{2,3},{3,2},{4,5},{5,4},{6,7},{7,6},{8,9},{9,8},{10,11... | collective-permute-start | bytes 589832 | tf_op jit(solution)/shard_map/ppermute | solution.py:338

commit v7 on v6

--- a/solution.py
+++ b/solution.py
@@ -16,7 +16,7 @@
 VMEM_LIMIT = 16 * 1024 * 1024
 EXP2_SCALE = math.log2(math.e) / math.sqrt(HEAD_DIM)
 CHUNK_ROWS = (256, 256)
-PARTNERS = ((7, 4, 2, 0), (5, 3, 6, 1))
+PARTNERS = ((4, 7, 2, 0), (5, 3, 6, 1))
 SHARES = len(PARTNERS[0])
 
 
@@ -159,10 +159,11 @@
     return pl.ds(pl.multiple_of(first + frame_of(i) * count, count), count)
 
 
-def piece_rows(ref, first, count, lanes):
-    return jnp.concatenate(
-        [ref[piece_span(first, count, i), lanes] for i in range(2 * SHARES)], axis=0
-    )
+OWN, OTHER, ALL = range(SHARES), range(SHARES, 2 * SHARES), range(2 * SHARES)
+
+
+def piece_rows(ref, first, count, lanes, pieces=ALL):
+    return jnp.concatenate([ref[piece_span(first, count, i), lanes] for i in pieces], axis=0)
 
 
 def chip_columns(features, flip):
@@ -170,11 +171,11 @@
     return pl.ds(pl.multiple_of((chip_of() ^ flip) * half, half), half)
 
 
-def spatial_heads(qkv_ref, heads_ref, first):
+def spatial_heads(qkv_ref, heads_ref, first, pieces=ALL):
     rows, width = heads_ref.shape
     for lane in range(0, width, HEAD_DIM):
         head = slice(lane, lane + HEAD_DIM)
-        query = piece_rows(qkv_ref.at[0], first, rows // (2 * SHARES), head)
+        query = piece_rows(qkv_ref.at[0], first, rows // len(pieces), head, pieces)
         (heads_ref[:, head],) = attend([(query, qkv_ref[1, :, head], qkv_ref[2, :, head])])
 
 
@@ -182,7 +183,7 @@
     qkv_far, w_far, gate_far, heads_ref, message_ref, w_ref, gate_ref, qkv_ref, semaphores, *, first
 ):
     far = chip_columns(w_far.shape[-1], 1)
-    query = pl.ds(first, heads_ref.shape[0])
+    query = pl.ds(first, 2 * heads_ref.shape[0])
     moves = [
         (qkv_far.at[0, query], qkv_ref.at[0, query]),
         (qkv_far.at[1:], qkv_ref.at[1:]),
@@ -194,19 +195,20 @@
         copy.start()
     for copy in copies[:2]:
         copy.wait()
-    spatial_heads(qkv_ref, heads_ref, first)
+    spatial_heads(qkv_ref, heads_ref, first, OTHER)
     for copy in copies[2:]:
         copy.wait()
-    term = dot(heads_ref[heads_ref.shape[0] // 2 :, :], w_ref[...])
+    term = dot(heads_ref[...], w_ref[...])
     message_ref[...] = (term * gate_ref[...]).astype(message_ref.dtype)
 
 
-def term_kernel(heads_ref, w_ref, gate_ref, out_ref):
-    out_ref[...] = dot(heads_ref[: out_ref.shape[0], :], w_ref[...]) * gate_ref[...]
+def term_kernel(w_ref, gate_ref, qkv_ref, heads_ref, out_ref, *, first):
+    spatial_heads(qkv_ref, heads_ref, first, OWN)
+    out_ref[...] = dot(heads_ref[...], w_ref[...]) * gate_ref[...]
 
 
 def rest_kernel(
-    heads0_ref, qkv_far, w_far, gate_far, residual_far,
+    own0_ref, other0_ref, qkv_far, w_far, gate_far, residual_far,
     message_ref, term_ref, base0_ref, near0_ref, base1_ref, near1_ref,
     heads1_ref, qkv_ref, w_ref, gate_ref, residual_ref, semaphores, *, firsts
 ):
@@ -227,15 +229,16 @@
     term_ref[...] = term[:half]
     message_ref[...] = term[half:].astype(message_ref.dtype)
     share = both // 2
-    for first, heads_ref, base_ref, near_ref in (
-        (firsts[0], heads0_ref, base0_ref, near0_ref),
-        (firsts[1], heads1_ref, base1_ref, near1_ref),
+    heads0 = jnp.concatenate([own0_ref[...], other0_ref[...]], axis=0)
+    for first, heads, base_ref, near_ref in (
+        (firsts[0], heads0, base0_ref, near0_ref),
+        (firsts[1], heads1_ref[...], base1_ref, near1_ref),
     ):
         size = base_ref.shape[0]
         for flip in range(2):
             place = pl.multiple_of((core_of() ^ flip) * share, share)
             lanes = pl.ds(pl.multiple_of(chip_of() * both + place, share), share)
-            term = dot(heads_ref[...], w_ref[:, lanes]) * gate_ref[:, lanes]
+            term = dot(heads, w_ref[:, lanes]) * gate_ref[:, lanes]
             if flip == 0:
                 term += piece_rows(residual_ref, first, size // SHARES, slice(None)).astype(
                     jnp.float32
@@ -398,24 +401,29 @@
 
     (first0, rows0), (first1, rows1) = chunks
     half0, half1 = rows0 // 2, rows1 // 2
-    heads, message, far_w, far_gate = call(
+    other_heads, message, *held = call(
         functools.partial(first_spatial_kernel, first=first0),
         [
-            shape(rows0, width),
+            shape(half0, width),
             shape(half0, both),
             pltpu.VMEM((width, both), bf16),
             pltpu.VMEM((1, both), f32),
+            pltpu.VMEM(qkv.shape, bf16),
         ],
         inputs=3,
         far=3,
-        scratch=(pltpu.VMEM(qkv.shape, bf16), pltpu.SemaphoreType.DMA((4,))),
+        scratch=(pltpu.SemaphoreType.DMA((4,)),),
     )(*(in_hbm(one) for one in (qkv, spatial_out, gate_row)))
     message = swap(message, "mlp", n_mlp, 1)
-    far_term = call(term_kernel, shape(half0, both, f32), inputs=3)(heads, far_w, far_gate)
+    own_heads, far_term = call(
+        functools.partial(term_kernel, first=first0),
+        [shape(half0, width), shape(half0, both, f32)],
+        inputs=3,
+    )(*held)
     sent = call(add_kernel, shape(half0, both), inputs=2)(far_term, message)
     arrived0 = swap(sent, "mlp", n_mlp, 2)
 
-    def rest(heads, *operands):
+    def rest(own_heads, other_heads, *operands):
         message, far_term, base0, near0, base1, near1 = call(
             functools.partial(rest_kernel, firsts=(first0, first1)),
             [
@@ -426,14 +434,14 @@
                 shape(half1, both, f32),
                 shape(half1, both),
             ],
-            inputs=5,
+            inputs=6,
             far=4,
             scratch=(
                 pltpu.VMEM((rows1, width), bf16),
                 *(pltpu.VMEM(one.shape, one.dtype) for one in operands),
                 pltpu.SemaphoreType.DMA((4,)),
             ),
-        )(heads, *(in_hbm(one) for one in operands))
+        )(own_heads, other_heads, *(in_hbm(one) for one in operands))
         message, near0, near1 = (swap(one, "mlp", n_mlp, 1) for one in (message, near0, near1))
         sent = call(add_kernel, shape(half1, both), inputs=2)(far_term, message)
         base0, base1 = (
@@ -450,7 +458,15 @@
         )
 
     sent, base0, base1 = lax.cond(
-        once > 0, rest, nothing, after(heads, sent), qkv, spatial_out, gate_row, flat_residual
+        once > 0,
+        rest,
+        nothing,
+        after(own_heads, sent),
+        other_heads,
+        qkv,
+        spatial_out,
+        gate_row,
+        flat_residual,
     )
     arrived1 = swap(sent, "mlp", n_mlp, 2)
     arrived0 = after(arrived0, sent)

time: 75.4 us -> 74.5 us (0.988)
  waiting for transfers between devices: 27.2 us -> 25.5 us
    ppermute x17, waiting for transfers between devices: 11.7 us -> 10.6 us  [swap(): return lax.ppermute(value, axis, [(i, i ^ k) for i in range(size)])]
  transfers between devices with their start and end apart: 29 -> 29, of which waited for: 13 -> 17; matrix products, arithmetic and copies ran while one was open for 0% -> 0% of each run, Pallas kernels for 21% -> 22%
where the time goes in v7:
time: 74.5 us; the launch traced here: 74.4 us
  starting transfers between devices  25.7 us (34%)
  waiting for transfers between devices  25.5 us (34%)
  Pallas kernels  22 us (30%)
  between operations  0.88 us (1%)
    ppermute x12, starting transfers between devices, send_pieces(): lax.ppermute(piece, ('seq', 'mlp'), piece_pairs(n_seq, n_mlp, i))  16.6 us
    ppermute x12, waiting for transfers between devices, send_pieces(): lax.ppermute(piece, ('seq', 'mlp'), piece_pairs(n_seq, n_mlp, i))  14.9 us
    ppermute x17, waiting for transfers between devices, swap(): return lax.ppermute(value, axis, [(i, i ^ k) for i in range(size)])  10.6 us
    ppermute x17, starting transfers between devices, swap(): return lax.ppermute(value, axis, [(i, i ^ k) for i in range(size)])  9.1 us
    pallas_call x2, Pallas kernels, split_on_device(): call(split_temporal_kernel, [shape(half, width)] * 2, inputs=8, scratch=(...  4.44 us
    pallas_call x1, Pallas kernels, rest(): call(functools.partial(rest_kernel, firsts=(first0, first1)), [shape(half...  3.81 us
    pallas_call x2, Pallas kernels, split_on_device(): call(half_kernel, shape(half, 3 * width), inputs=7, scratch=(pltpu.VMEM((...  3.79 us
    pallas_call x1, Pallas kernels, hold_weights(): pl.pallas_call(hold_kernel, out_shape=pltpu.VMEM((features, parts * width...  3.12 us
  transfers between devices with their start and end apart: 29, of which 17 were waited for; matrix products, arithmetic and copies ran while one was open for 0% of the time, Pallas kernels for 22%

profile of v7, /device:TPU:0, one launch (start us, length us, event | category | flops | bytes accessed | tf_op | source)
XLA Modules:
  0.0 74.4 jit_solution(6113014788593722197)
XLA Ops:
  0.6 2.6 %shard_map.106 = (bf16[128,384]{1,0:T(8,128)(2,1)S(1)}, bf16[128,1536]{1,0:T(8,128)(2,1)S(1)}, bf16[384,1536]{1,0:T(8,128)(2,1)S(1)}, f32[1,1536]{1,0:T(1,128)S(1)}, bf16[3,512,384]{2,1,0:T(8,128)(2,1)S(1)}) custom-call(bf16[3,512,384]{2,1,0:T(8,128)(2,1)} %bitcast.19, bf16[384,3072]{1,0:T(8,128)(2,1)} %w_far.1, f32[1,3072]{1,0:T(1,128)} %bitcast.24), custom_call_target="tpu_custom_call" | custom-call | tf_op jit(solution)/shard_map/pallas_call | solution.py:404
  3.2 0.5 collective-permute-start.11
  3.7 1.2 %shard_map.107 = (bf16[128,384]{1,0:T(8,128)(2,1)S(1)}, f32[128,1536]{1,0:T(8,128)S(1)}) custom-call(bf16[384,1536]{1,0:T(8,128)(2,1)S(1)} %get-tuple-element.130.w_ref, f32[1,1536]{1,0:T(1,128)S(1)} %get-tuple-element.131.gate_ref, bf16[3,512,384]{2,1,0:T(8,128)(2,1)S(1)} %get-tuple-element.132.qkv_ref), custom_call_target="tpu_custom_call" | custom-call | tf_op jit(solution)/shard_map/pallas_call | solution.py:418
  5.0 0.1 collective-permute-done.11.b_ref
  5.1 0.1 shard_map.108
  5.2 2.9 %collective-permute-start.12 = (bf16[128,1536]{1,0:T(8,128)(2,1)S(1)}, bf16[128,1536]{1,0:T(8,128)(2,1)S(1)}, u32[]{:S(2)}, u32[]{:S(2)}) collective-permute-start(bf16[128,1536]{1,0:T(8,128)(2,1)S(1)} %shard_map.108), channel_id=1, source_target_pairs={{0,2},{1,3},{2,0},{3,1},{4,6},{5,7},{6,4},{7,5},{8,10},{9,11},{10,... | collective-permute-start | bytes 1179656 | tf_op jit(solution)/shard_map/ppermute | solution.py:341
  8.1 7.5 %conditional.2 = (bf16[128,1536]{1,0:T(8,128)(2,1)}, f32[128,1536]{1,0:T(8,128)S(1)}, f32[128,1536]{1,0:T(8,128)S(1)}) conditional(s32[]{:T(128)} %convert_element_type.4, () %tuple.33, (bf16[1,512,768]{2,1,0:T(8,128)(2,1)}, bf16[128,384]{1,0:T(8,128)(2,1)S(1)}, bf16[128,384]{1,0:T(8,128)(2,1)S(1)}, bf16[3,512,384]{2,1,0:T(8,128)(2,1)}, ...), branch_computations={%region_0.0_spmd, %region_1.0_spmd} | conditional | bytes 4718736 | solution.py:460
  8.1 3.8 %branch_1_fun.5 = (bf16[128,1536]{1,0:T(8,128)(2,1)S(1)}, f32[128,1536]{1,0:T(8,128)S(1)}, f32[128,1536]{1,0:T(8,128)S(1)}, bf16[128,1536]{1,0:T(8,128)(2,1)S(1)...) custom-call(bf16[128,384]{1,0:T(8,128)(2,1)S(1)} %get-tuple-element.55.own0_ref, ...), custom_call_target="tpu_custom_call" | custom-call | tf_op jit(solution)/shard_map/cond/branch_1_fun/pallas_call | solution.py:427
  11.9 0.1 collective-permute-start.2
  12.0 0.5 collective-permute-start.1
  12.5 0.1 collective-permute-start
  12.6 1.1 %collective-permute-done.2.b_ref = bf16[128,1536]{1,0:T(8,128)(2,1)S(1)} collective-permute-done((bf16[128,1536]{1,0:T(8,128)(2,1)S(1)}, bf16[128,1536]{1,0:T(8,128)(2,1)S(1)}, u32[]{:S(2)}, u32[]{:S(2)}) %collective-permute-start.2) | collective-permute-done | bytes 393248 | tf_op jit(solution)/shard_map/cond/branch_1_fun/ppermute | solution.py:341
  13.7 0.1 branch_1_fun.8
  13.8 0.5 collective-permute-done.1.b_ref
  14.3 0.1 branch_1_fun.7
  14.3 0.5 collective-permute-done.b_ref
  14.8 0.8 %branch_1_fun.6 = bf16[128,1536]{1,0:T(8,128)(2,1)} custom-call(f32[128,1536]{1,0:T(8,128)S(1)} %get-tuple-element.61.a_ref, bf16[128,1536]{1,0:T(8,128)(2,1)S(1)} %collective-permute-done.b_ref), custom_call_target="tpu_custom_call" | custom-call | tf_op jit(solution)/shard_map/cond/branch_1_fun/pallas_call | solution.py:446
  15.7 0.0 collective-permute-start.14
  15.7 1.8 %collective-permute-done.12.arrived_ref = bf16[128,1536]{1,0:T(8,128)(2,1)S(1)} collective-permute-done((bf16[128,1536]{1,0:T(8,128)(2,1)S(1)}, bf16[128,1536]{1,0:T(8,128)(2,1)S(1)}, u32[]{:S(2)}, u32[]{:S(2)}) %collective-permute-start.12) | collective-permute-done | bytes 393248 | tf_op jit(solution)/shard_map/ppermute | solution.py:341
  17.5 0.1 shard_map.109
  17.6 11.9 %while.16 = (s32[]{:T(128)}, bf16[32,1536]{1,0:T(8,128)(2,1)S(1)}, bf16[32,1536]{1,0:T(8,128)(2,1)S(1)}, bf16[32,1536]{1,0:T(8,128)(2,1)S(1)}, bf16[32,1536]{1,0:T(8,128)(2,1)S(1)}, /*index=5*/s32[]{:T(128)}, s32[]{:T(128)}) while((s32[]{:T(128)}, bf16[32,1536]{1,0:T(8,128)(2,1)S(1)}, bf16[32,1536]{1,0:T(8,128)(2,1)S(1)}, ...), condition=%wide.region_3.0_spmd, body=%wide.region_2.0_spmd.sunk | while | flops 2 | bytes 2359533 | solution.py:484
  17.7 2.9 %collective-permute-start.7 = (bf16[32,1536]{1,0:T(8,128)(2,1)S(1)}, bf16[32,1536]{1,0:T(8,128)(2,1)S(1)}, u32[]{:S(2)}, u32[]{:S(2)}) collective-permute-start(bf16[32,1536]{1,0:T(8,128)(2,1)S(1)} %get-tuple-element.242), channel_id=1, source_target_pairs={{0,16},{1,21},{2,18},{3,23},{4,20},{5,17},{6,22},{7,19},{8,24},{9,... | collective-permute-start | bytes 294920 | tf_op jit(solution)/shard_map/while/body/ppermute | solution.py:390
  20.6 2.3 %collective-permute-start.8 = (bf16[32,1536]{1,0:T(8,128)(2,1)S(1)}, bf16[32,1536]{1,0:T(8,128)(2,1)S(1)}, u32[]{:S(2)}, u32[]{:S(2)}) collective-permute-start(bf16[32,1536]{1,0:T(8,128)(2,1)S(1)} %get-tuple-element.243), channel_id=1, source_target_pairs={{0,28},{1,13},{2,30},{3,15},{4,24},{5,9},{6,26},{7,11},{8,20},{9,5... | collective-permute-start | bytes 294920 | tf_op jit(solution)/shard_map/while/body/ppermute | solution.py:390
  22.9 0.7 collective-permute-start.10
  23.5 5.0 %collective-permute-done.7 = bf16[32,1536]{1,0:T(8,128)(2,1)S(1)} collective-permute-done((bf16[32,1536]{1,0:T(8,128)(2,1)S(1)}, bf16[32,1536]{1,0:T(8,128)(2,1)S(1)}, u32[]{:S(2)}, u32[]{:S(2)}) %collective-permute-start.7) | collective-permute-done | bytes 98336 | tf_op jit(solution)/shard_map/while/body/ppermute | solution.py:390
  28.5 0.3 collective-permute-done.8
  28.8 0.7 collective-permute-done.9
  29.6 1.9 %collective-permute-start.16 = (bf16[128,1536]{1,0:T(8,128)(2,1)S(1)}, bf16[128,1536]{1,0:T(8,128)(2,1)S(1)}, u32[]{:S(2)}, u32[]{:S(2)}) collective-permute-start(bf16[128,1536]{1,0:T(8,128)(2,1)S(1)} %constant_dynamic-update-slice_fusion.near), channel_id=1, source_target_pairs={{0,2},{1,3},{2,0},{3,1},{4,6},{5,7},{6,4},{7,5},{8,10},{9,11},{10,... | collective-permute-start | bytes 1179656 | tf_op jit(solution)/shard_map/ppermute | solution.py:341
  31.4 0.1 shard_map.110
  31.6 0.0 copy-start.1
  31.6 0.0 copy-start.2
  31.6 0.0 copy-start.3
  31.6 11.3 %conditional.3 = (bf16[32,1536]{1,0:T(8,128)(2,1)S(1)}, bf16[32,1536]{1,0:T(8,128)(2,1)S(1)}, bf16[32,1536]{1,0:T(8,128)(2,1)S(1)}, bf16[32,1536]{1,0:T(8,128)(2,1)S(1)}, bf16[3072,1152]{1,0:T(8,128)(2,1)S(1)}) conditional(s32[]{:T(128)} %convert_element_type.4, (bf16[32,1536]{1,0:T(8,128)(2,1)S(1)}, bf16[32,1536]{1,0:T(8,128)(2,1)S(1)}, ...), branch_computations={%region_4.0_spmd, %region_5.0_spmd} | conditional | bytes 7077930 | solution.py:494
  31.6 3.0 %collective-permute-start.3 = (bf16[32,1536]{1,0:T(8,128)(2,1)S(1)}, bf16[32,1536]{1,0:T(8,128)(2,1)S(1)}, u32[]{:S(2)}, u32[]{:S(2)}) collective-permute-start(bf16[32,1536]{1,0:T(8,128)(2,1)S(1)} %get-tuple-element.79), channel_id=1, source_target_pairs={{0,16},{1,21},{2,18},{3,23},{4,20},{5,17},{6,22},{7,19},{8,24},{9,... | collective-permute-start | bytes 294920 | tf_op jit(solution)/shard_map/cond/branch_1_fun/ppermute | solution.py:390
  34.6 1.3 %collective-permute-start.4 = (bf16[32,1536]{1,0:T(8,128)(2,1)S(1)}, bf16[32,1536]{1,0:T(8,128)(2,1)S(1)}, u32[]{:S(2)}, u32[]{:S(2)}) collective-permute-start(bf16[32,1536]{1,0:T(8,128)(2,1)S(1)} %get-tuple-element.80), channel_id=1, source_target_pairs={{0,28},{1,13},{2,30},{3,15},{4,24},{5,9},{6,26},{7,11},{8,20},{9,5... | collective-permute-start | bytes 294920 | tf_op jit(solution)/shard_map/cond/branch_1_fun/ppermute | solution.py:390
  36.0 0.3 collective-permute-start.5
  36.3 0.8 %collective-permute-start.6 = (bf16[32,1536]{1,0:T(8,128)(2,1)S(1)}, bf16[32,1536]{1,0:T(8,128)(2,1)S(1)}, u32[]{:S(2)}, u32[]{:S(2)}) collective-permute-start(bf16[32,1536]{1,0:T(8,128)(2,1)S(1)} %get-tuple-element.82), channel_id=1, source_target_pairs={{0,0},{1,5},{2,2},{3,7},{4,4},{5,1},{6,6},{7,3},{8,8},{9,13},{10,1... | collective-permute-start | bytes 294920 | tf_op jit(solution)/shard_map/cond/branch_1_fun/ppermute | solution.py:390
  37.1 3.1 %branch_1_fun.9 = bf16[3072,1152]{1,0:T(8,128)(2,1)S(1)} custom-call(bf16[3,3072,384]{2,1,0:T(8,128)(2,1)} %bitcast.18), custom_call_target="tpu_custom_call" | custom-call | tf_op jit(solution)/shard_map/cond/branch_1_fun/pallas_call | solution.py:133
  40.2 0.2 collective-permute-done.3
  40.5 1.5 %collective-permute-done.4 = bf16[32,1536]{1,0:T(8,128)(2,1)S(1)} collective-permute-done((bf16[32,1536]{1,0:T(8,128)(2,1)S(1)}, bf16[32,1536]{1,0:T(8,128)(2,1)S(1)}, u32[]{:S(2)}, u32[]{:S(2)}) %collective-permute-start.4) | collective-permute-done | bytes 98336 | tf_op jit(solution)/shard_map/cond/branch_1_fun/ppermute | solution.py:390
  42.0 0.9 %collective-permute-done.5 = bf16[32,1536]{1,0:T(8,128)(2,1)S(1)} collective-permute-done((bf16[32,1536]{1,0:T(8,128)(2,1)S(1)}, bf16[32,1536]{1,0:T(8,128)(2,1)S(1)}, u32[]{:S(2)}, u32[]{:S(2)}) %collective-permute-start.5) | collective-permute-done | bytes 98336 | tf_op jit(solution)/shard_map/cond/branch_1_fun/ppermute | solution.py:390
  42.9 0.1 collective-permute-start.17
  43.1 0.5 collective-permute-start.18
  43.6 0.8 %collective-permute-start.19 = (bf16[128,1536]{1,0:T(8,128)(2,1)S(1)}, bf16[128,1536]{1,0:T(8,128)(2,1)S(1)}, u32[]{:S(2)}, u32[]{:S(2)}) collective-permute-start(bf16[128,1536]{1,0:T(8,128)(2,1)S(1)} %constant_dynamic-update-slice_fusion.4.near), channel_id=1, source_target_pairs={{0,2},{1,3},{2,0},{3,1},{4,6},{5,7},{6,4},{7,5},{8,10},{9,11},{10,... | collective-permute-start | bytes 1179656 | tf_op jit(solution)/shard_map/ppermute | solution.py:341
  44.4 0.5 collective-permute-start.13
  44.9 1.9 %shard_map.112.own_proj_ref = bf16[128,1152]{1,0:T(8,128)(2,1)S(1)} custom-call(bf16[128,1536]{1,0:T(8,128)(2,1)S(1)} %constant_dynamic-update-slice_fusion.near, bf16[128,1536]{1,0:T(8,128)(2,1)S(1)} %collective-permute-done.16.far, f32[1,3072]{1,0:T(1,128)S(1)} %bitcast.10, f32[1,3072]{1,0:T(1,128)S(1)} %bitcast.14, ...), custom_call_target="tpu_custom_call" | custom-call | tf_op jit(solution)/shard_map/pallas_call | solution.py:514
  46.8 2.2 %shard_map.113 = (bf16[128,384]{1,0:T(8,128)(2,1)S(1)}, bf16[128,384]{1,0:T(8,128)(2,1)S(1)}) custom-call(bf16[128,1152]{1,0:T(8,128)(2,1)S(1)} %shard_map.112.own_proj_ref, bf16[128,1536]{1,0:T(8,128)(2,1)S(1)} %collective-permute-done.17.near, bf16[128,1536]{1,0:T(8,128)(2,1)S(1)} %collective-permute-done.18.far, f32[1,3072]{1,0:T(1,128)S(1)} %bitcast.11, ...), custom_call_target="tpu_custom_call" | custom-call | tf_op jit(solution)/shard_map/pallas_call | solution.py:520
  49.1 0.1 collective-permute-start.20
  49.2 0.5 collective-permute-start.21
  49.7 1.0 %shard_map.111 = bf16[512,768]{1,0:T(8,128)(2,1)} custom-call(bf16[128,768]{1,0:T(8,128)(2,1)S(1)} %get-tuple-element.141.refs_0_, bf16[128,768]{1,0:T(8,128)(2,1)S(1)} %collective-permute-done.13.refs_1_, bf16[128,768]{1,0:T(8,128)(2,1)S(1)} %get-tuple-element.153.refs_2_, bf16[128,768]{1,0:T(8,128)(2,1)S(1)} %collective-permute-done.15.refs_3_), custom_call_target="tpu_custom_call" | custom-call | tf_op jit(solution)/shard_map/pallas_call | solution.py:506
  50.6 4.1 %collective-permute-done.19.far = bf16[128,1536]{1,0:T(8,128)(2,1)S(1)} collective-permute-done((bf16[128,1536]{1,0:T(8,128)(2,1)S(1)}, bf16[128,1536]{1,0:T(8,128)(2,1)S(1)}, u32[]{:S(2)}, u32[]{:S(2)}) %collective-permute-start.19) | collective-permute-done | bytes 393248 | tf_op jit(solution)/shard_map/ppermute | solution.py:341
  54.7 1.9 %shard_map.114.own_proj_ref = bf16[128,1152]{1,0:T(8,128)(2,1)S(1)} custom-call(bf16[128,1536]{1,0:T(8,128)(2,1)S(1)} %constant_dynamic-update-slice_fusion.4.near, bf16[128,1536]{1,0:T(8,128)(2,1)S(1)} %collective-permute-done.19.far, f32[1,3072]{1,0:T(1,128)S(1)} %bitcast.12, f32[1,3072]{1,0:T(1,128)S(1)} %bitcast.16, ...), custom_call_target="tpu_custom_call" | custom-call | tf_op jit(solution)/shard_map/pallas_call | solution.py:514
  56.7 2.2 %shard_map.115 = (bf16[128,384]{1,0:T(8,128)(2,1)S(1)}, bf16[128,384]{1,0:T(8,128)(2,1)S(1)}) custom-call(bf16[128,1152]{1,0:T(8,128)(2,1)S(1)} %shard_map.114.own_proj_ref, bf16[128,1536]{1,0:T(8,128)(2,1)S(1)} %collective-permute-done.21.near, bf16[128,1536]{1,0:T(8,128)(2,1)S(1)} %collective-permute-done.22.far, f32[1,3072]{1,0:T(1,128)S(1)} %bitcast.13, ...), custom_call_target="tpu_custom_call" | custom-call | tf_op jit(solution)/shard_map/pallas_call | solution.py:520
  58.9 0.6 collective-permute-start.23
  59.5 0.9 %collective-permute-done.23.refs_3_ = bf16[128,384]{1,0:T(8,128)(2,1)S(1)} collective-permute-done((bf16[128,384]{1,0:T(8,128)(2,1)S(1)}, bf16[128,384]{1,0:T(8,128)(2,1)S(1)}, u32[]{:S(2)}, u32[]{:S(2)}) %collective-permute-start.23) | collective-permute-done | bytes 98336 | tf_op jit(solution)/shard_map/ppermute | solution.py:341
  60.4 2.8 %collective-permute-start.24 = (bf16[128,384]{1,0:T(8,128)(2,1)S(1)}, bf16[128,384]{1,0:T(8,128)(2,1)S(1)}, u32[]{:S(2)}, u32[]{:S(2)}) collective-permute-start(bf16[128,384]{1,0:T(8,128)(2,1)S(1)} %get-tuple-element.170), channel_id=1, source_target_pairs={{0,16},{1,21},{2,18},{3,23},{4,20},{5,17},{6,22},{7,19},{8,24},{9,... | collective-permute-start | bytes 294920 | tf_op jit(solution)/shard_map/ppermute | solution.py:390
  63.2 1.8 %collective-permute-start.25 = (bf16[128,384]{1,0:T(8,128)(2,1)S(1)}, bf16[128,384]{1,0:T(8,128)(2,1)S(1)}, u32[]{:S(2)}, u32[]{:S(2)}) collective-permute-start(bf16[128,384]{1,0:T(8,128)(2,1)S(1)} %get-tuple-element.171), channel_id=1, source_target_pairs={{0,28},{1,13},{2,30},{3,15},{4,24},{5,9},{6,26},{7,11},{8,20},{9,5... | collective-permute-start | bytes 294920 | tf_op jit(solution)/shard_map/ppermute | solution.py:390
  65.0 0.7 collective-permute-start.27
  65.7 5.7 %collective-permute-done.24.refs_0_ = bf16[128,384]{1,0:T(8,128)(2,1)S(1)} collective-permute-done((bf16[128,384]{1,0:T(8,128)(2,1)S(1)}, bf16[128,384]{1,0:T(8,128)(2,1)S(1)}, u32[]{:S(2)}, u32[]{:S(2)}) %collective-permute-start.24) | collective-permute-done | bytes 98336 | tf_op jit(solution)/shard_map/ppermute | solution.py:390
  71.3 0.4 collective-permute-done.25.refs_1_
  71.7 0.3 collective-permute-done.26.refs_2_
  72.1 0.1 collective-permute-start.28
  72.1 1.4 %collective-permute-done.28.refs_4_ = bf16[256,384]{1,0:T(8,128)(2,1)S(1)} collective-permute-done((bf16[256,384]{1,0:T(8,128)(2,1)S(1)}, bf16[256,384]{1,0:T(8,128)(2,1)S(1)}, u32[]{:S(2)}, u32[]{:S(2)}) %collective-permute-start.28) | collective-permute-done | bytes 196640 | tf_op jit(solution)/shard_map/ppermute | solution.py:341
  73.6 0.8 %shard_map.118 = bf16[512,384]{1,0:T(8,128)(2,1)} custom-call(bf16[128,384]{1,0:T(8,128)(2,1)S(1)} %collective-permute-done.24.refs_0_, bf16[128,384]{1,0:T(8,128)(2,1)S(1)} %collective-permute-done.25.refs_1_, bf16[128,384]{1,0:T(8,128)(2,1)S(1)} %collective-permute-done.26.refs_2_, bf16[128,384]{1,0:T(8,128)(2,1)S(1)} %collective-permute-done.27.refs_3_, ...), custom_call_target="tpu_custom_call" | custom-call | tf_op jit(solution)/shard_map/pallas_call | solution.py:534
  (39 shorter events, 0.2 us)
Async XLA Ops:
  3.2 1.9 %collective-permute-start.11 = (bf16[128,1536]{1,0:T(8,128)(2,1)S(1)}, bf16[128,1536]{1,0:T(8,128)(2,1)S(1)}, u32[]{:S(2)}, u32[]{:S(2)}) collective-permute-start(bf16[128,1536]{1,0:T(8,128)(2,1)S(1)} %get-tuple-element.135), channel_id=1, source_target_pairs={{0,1},{1,0},{2,3},{3,2},{4,5},{5,4},{6,7},{7,6},{8,9},{9,8},{10,11... | collective-permute-start | bytes 1179656 | tf_op jit(solution)/shard_map/ppermute | solution.py:341
  5.2 12.3 %collective-permute-start.12 = (bf16[128,1536]{1,0:T(8,128)(2,1)S(1)}, bf16[128,1536]{1,0:T(8,128)(2,1)S(1)}, u32[]{:S(2)}, u32[]{:S(2)}) collective-permute-start(bf16[128,1536]{1,0:T(8,128)(2,1)S(1)} %shard_map.108), channel_id=1, source_target_pairs={{0,2},{1,3},{2,0},{3,1},{4,6},{5,7},{6,4},{7,5},{8,10},{9,11},{10,... | collective-permute-start | bytes 1179656 | tf_op jit(solution)/shard_map/ppermute | solution.py:341
  11.9 1.8 %collective-permute-start.2 = (bf16[128,1536]{1,0:T(8,128)(2,1)S(1)}, bf16[128,1536]{1,0:T(8,128)(2,1)S(1)}, u32[]{:S(2)}, u32[]{:S(2)}) collective-permute-start(bf16[128,1536]{1,0:T(8,128)(2,1)S(1)} %get-tuple-element.66), channel_id=1, source_target_pairs={{0,1},{1,0},{2,3},{3,2},{4,5},{5,4},{6,7},{7,6},{8,9},{9,8},{10,11... | collective-permute-start | bytes 1179656 | tf_op jit(solution)/shard_map/cond/branch_1_fun/ppermute | solution.py:341
  12.0 2.3 %collective-permute-start.1 = (bf16[128,1536]{1,0:T(8,128)(2,1)S(1)}, bf16[128,1536]{1,0:T(8,128)(2,1)S(1)}, u32[]{:S(2)}, u32[]{:S(2)}) collective-permute-start(bf16[128,1536]{1,0:T(8,128)(2,1)S(1)} %get-tuple-element.64), channel_id=1, source_target_pairs={{0,1},{1,0},{2,3},{3,2},{4,5},{5,4},{6,7},{7,6},{8,9},{9,8},{10,11... | collective-permute-start | bytes 1179656 | tf_op jit(solution)/shard_map/cond/branch_1_fun/ppermute | solution.py:341
  12.5 2.3 %collective-permute-start = (bf16[128,1536]{1,0:T(8,128)(2,1)S(1)}, bf16[128,1536]{1,0:T(8,128)(2,1)S(1)}, u32[]{:S(2)}, u32[]{:S(2)}) collective-permute-start(bf16[128,1536]{1,0:T(8,128)(2,1)S(1)} %get-tuple-element.62), channel_id=1, source_target_pairs={{0,1},{1,0},{2,3},{3,2},{4,5},{5,4},{6,7},{7,6},{8,9},{9,8},{10,11... | collective-permute-start | bytes 1179656 | tf_op jit(solution)/shard_map/cond/branch_1_fun/ppermute | solution.py:341
  15.7 15.8 %collective-permute-start.14 = (bf16[128,1536]{1,0:T(8,128)(2,1)}, bf16[128,1536]{1,0:T(8,128)(2,1)S(1)}, u32[]{:S(2)}, u32[]{:S(2)}) collective-permute-start(bf16[128,1536]{1,0:T(8,128)(2,1)} %get-tuple-element.139), channel_id=1, source_target_pairs={{0,2},{1,3},{2,0},{3,1},{4,6},{5,7},{6,4},{7,5},{8,10},{9,11},{10,... | collective-permute-start | bytes 1179656 | tf_op jit(solution)/shard_map/ppermute | solution.py:341
  17.7 10.9 %collective-permute-start.7 = (bf16[32,1536]{1,0:T(8,128)(2,1)S(1)}, bf16[32,1536]{1,0:T(8,128)(2,1)S(1)}, u32[]{:S(2)}, u32[]{:S(2)}) collective-permute-start(bf16[32,1536]{1,0:T(8,128)(2,1)S(1)} %get-tuple-element.242), channel_id=1, source_target_pairs={{0,16},{1,21},{2,18},{3,23},{4,20},{5,17},{6,22},{7,19},{8,24},{9,... | collective-permute-start | bytes 294920 | tf_op jit(solution)/shard_map/while/body/ppermute | solution.py:390
  20.6 8.2 %collective-permute-start.8 = (bf16[32,1536]{1,0:T(8,128)(2,1)S(1)}, bf16[32,1536]{1,0:T(8,128)(2,1)S(1)}, u32[]{:S(2)}, u32[]{:S(2)}) collective-permute-start(bf16[32,1536]{1,0:T(8,128)(2,1)S(1)} %get-tuple-element.243), channel_id=1, source_target_pairs={{0,28},{1,13},{2,30},{3,15},{4,24},{5,9},{6,26},{7,11},{8,20},{9,5... | collective-permute-start | bytes 294920 | tf_op jit(solution)/shard_map/while/body/ppermute | solution.py:390
  22.9 6.6 %collective-permute-start.9 = (bf16[32,1536]{1,0:T(8,128)(2,1)S(1)}, bf16[32,1536]{1,0:T(8,128)(2,1)S(1)}, u32[]{:S(2)}, u32[]{:S(2)}) collective-permute-start(bf16[32,1536]{1,0:T(8,128)(2,1)S(1)} %get-tuple-element.244), channel_id=1, source_target_pairs={{0,8},{1,25},{2,10},{3,27},{4,12},{5,29},{6,14},{7,31},{8,0},{9,17... | collective-permute-start | bytes 294920 | tf_op jit(solution)/shard_map/while/body/ppermute | solution.py:390
  22.9 6.6 %collective-permute-start.10 = (bf16[32,1536]{1,0:T(8,128)(2,1)S(1)}, bf16[32,1536]{1,0:T(8,128)(2,1)S(1)}, u32[]{:S(2)}, u32[]{:S(2)}) collective-permute-start(bf16[32,1536]{1,0:T(8,128)(2,1)S(1)} %get-tuple-element.245), channel_id=1, source_target_pairs={{0,0},{1,5},{2,2},{3,7},{4,4},{5,1},{6,6},{7,3},{8,8},{9,13},{10,1... | collective-permute-start | bytes 294920 | tf_op jit(solution)/shard_map/while/body/ppermute | solution.py:390
  29.6 13.5 %collective-permute-start.16 = (bf16[128,1536]{1,0:T(8,128)(2,1)S(1)}, bf16[128,1536]{1,0:T(8,128)(2,1)S(1)}, u32[]{:S(2)}, u32[]{:S(2)}) collective-permute-start(bf16[128,1536]{1,0:T(8,128)(2,1)S(1)} %constant_dynamic-update-slice_fusion.near), channel_id=1, source_target_pairs={{0,2},{1,3},{2,0},{3,1},{4,6},{5,7},{6,4},{7,5},{8,10},{9,11},{10,... | collective-permute-start | bytes 1179656 | tf_op jit(solution)/shard_map/ppermute | solution.py:341
  31.6 13.3 %copy-start = (f32[3072]{0:T(1024)S(1)}, f32[3072]{0:T(1024)}, u32[]{:S(2)}) copy-start(f32[3072]{0:T(1024)} %param.20) | copy-start | bytes 36868
  31.6 13.3 %copy-start.1 = (f32[3072]{0:T(1024)S(1)}, f32[3072]{0:T(1024)}, u32[]{:S(2)}) copy-start(f32[3072]{0:T(1024)} %param.19) | copy-start | bytes 36868
  31.6 13.3 %copy-start.2 = (f32[8,128]{1,0:T(8,128)S(1)}, f32[8,128]{1,0:T(8,128)}, u32[]{:S(2)}) copy-start(f32[8,128]{1,0:T(8,128)} %constant.22.clone.cos_ref) | copy-start | bytes 12292
  31.6 13.3 %copy-start.3 = (f32[8,128]{1,0:T(8,128)S(1)}, f32[8,128]{1,0:T(8,128)}, u32[]{:S(2)}) copy-start(f32[8,128]{1,0:T(8,128)} %constant.23.clone.sin_ref) | copy-start | bytes 12292
  31.6 8.9 %collective-permute-start.3 = (bf16[32,1536]{1,0:T(8,128)(2,1)S(1)}, bf16[32,1536]{1,0:T(8,128)(2,1)S(1)}, u32[]{:S(2)}, u32[]{:S(2)}) collective-permute-start(bf16[32,1536]{1,0:T(8,128)(2,1)S(1)} %get-tuple-element.79), channel_id=1, source_target_pairs={{0,16},{1,21},{2,18},{3,23},{4,20},{5,17},{6,22},{7,19},{8,24},{9,... | collective-permute-start | bytes 294920 | tf_op jit(solution)/shard_map/cond/branch_1_fun/ppermute | solution.py:390
  34.6 7.4 %collective-permute-start.4 = (bf16[32,1536]{1,0:T(8,128)(2,1)S(1)}, bf16[32,1536]{1,0:T(8,128)(2,1)S(1)}, u32[]{:S(2)}, u32[]{:S(2)}) collective-permute-start(bf16[32,1536]{1,0:T(8,128)(2,1)S(1)} %get-tuple-element.80), channel_id=1, source_target_pairs={{0,28},{1,13},{2,30},{3,15},{4,24},{5,9},{6,26},{7,11},{8,20},{9,5... | collective-permute-start | bytes 294920 | tf_op jit(solution)/shard_map/cond/branch_1_fun/ppermute | solution.py:390
  36.0 6.9 %collective-permute-start.5 = (bf16[32,1536]{1,0:T(8,128)(2,1)S(1)}, bf16[32,1536]{1,0:T(8,128)(2,1)S(1)}, u32[]{:S(2)}, u32[]{:S(2)}) collective-permute-start(bf16[32,1536]{1,0:T(8,128)(2,1)S(1)} %get-tuple-element.81), channel_id=1, source_target_pairs={{0,8},{1,25},{2,10},{3,27},{4,12},{5,29},{6,14},{7,31},{8,0},{9,17... | collective-permute-start | bytes 294920 | tf_op jit(solution)/shard_map/cond/branch_1_fun/ppermute | solution.py:390
  36.3 6.6 %collective-permute-start.6 = (bf16[32,1536]{1,0:T(8,128)(2,1)S(1)}, bf16[32,1536]{1,0:T(8,128)(2,1)S(1)}, u32[]{:S(2)}, u32[]{:S(2)}) collective-permute-start(bf16[32,1536]{1,0:T(8,128)(2,1)S(1)} %get-tuple-element.82), channel_id=1, source_target_pairs={{0,0},{1,5},{2,2},{3,7},{4,4},{5,1},{6,6},{7,3},{8,8},{9,13},{10,1... | collective-permute-start | bytes 294920 | tf_op jit(solution)/shard_map/cond/branch_1_fun/ppermute | solution.py:390
  42.9 3.9 %collective-permute-start.17 = (bf16[128,1536]{1,0:T(8,128)(2,1)S(1)}, bf16[128,1536]{1,0:T(8,128)(2,1)S(1)}, u32[]{:S(2)}, u32[]{:S(2)}) collective-permute-start(bf16[128,1536]{1,0:T(8,128)(2,1)S(1)} %constant_dynamic-update-slice_fusion.near), channel_id=1, source_target_pairs={{0,1},{1,0},{2,3},{3,2},{4,5},{5,4},{6,7},{7,6},{8,9},{9,8},{10,11... | collective-permute-start | bytes 1179656 | tf_op jit(solution)/shard_map/ppermute | solution.py:341
  43.1 3.8 %collective-permute-start.18 = (bf16[128,1536]{1,0:T(8,128)(2,1)S(1)}, bf16[128,1536]{1,0:T(8,128)(2,1)S(1)}, u32[]{:S(2)}, u32[]{:S(2)}) collective-permute-start(bf16[128,1536]{1,0:T(8,128)(2,1)S(1)} %collective-permute-done.16.far), channel_id=1, source_target_pairs={{0,1},{1,0},{2,3},{3,2},{4,5},{5,4},{6,7},{7,6},{8,9},{9,8},{10,11... | collective-permute-start | bytes 1179656 | tf_op jit(solution)/shard_map/ppermute | solution.py:341
  43.6 11.1 %collective-permute-start.19 = (bf16[128,1536]{1,0:T(8,128)(2,1)S(1)}, bf16[128,1536]{1,0:T(8,128)(2,1)S(1)}, u32[]{:S(2)}, u32[]{:S(2)}) collective-permute-start(bf16[128,1536]{1,0:T(8,128)(2,1)S(1)} %constant_dynamic-update-slice_fusion.4.near), channel_id=1, source_target_pairs={{0,2},{1,3},{2,0},{3,1},{4,6},{5,7},{6,4},{7,5},{8,10},{9,11},{10,... | collective-permute-start | bytes 1179656 | tf_op jit(solution)/shard_map/ppermute | solution.py:341
  44.4 5.3 %collective-permute-start.15 = (bf16[128,768]{1,0:T(8,128)(2,1)S(1)}, bf16[128,768]{1,0:T(8,128)(2,1)S(1)}, u32[]{:S(2)}, u32[]{:S(2)}) collective-permute-start(bf16[128,768]{1,0:T(8,128)(2,1)S(1)} %get-tuple-element.154), channel_id=1, source_target_pairs={{0,1},{1,0},{2,3},{3,2},{4,5},{5,4},{6,7},{7,6},{8,9},{9,8},{10,11... | collective-permute-start | bytes 589832 | tf_op jit(solution)/shard_map/ppermute | solution.py:341
  44.4 5.3 %collective-permute-start.13 = (bf16[128,768]{1,0:T(8,128)(2,1)S(1)}, bf16[128,768]{1,0:T(8,128)(2,1)S(1)}, u32[]{:S(2)}, u32[]{:S(2)}) collective-permute-start(bf16[128,768]{1,0:T(8,128)(2,1)S(1)} %get-tuple-element.142), channel_id=1, source_target_pairs={{0,1},{1,0},{2,3},{3,2},{4,5},{5,4},{6,7},{7,6},{8,9},{9,8},{10,11... | collective-permute-start | bytes 589832 | tf_op jit(solution)/shard_map/ppermute | solution.py:341
  49.1 5.7 %collective-permute-start.20 = (bf16[128,384]{1,0:T(8,128)(2,1)S(1)}, bf16[128,384]{1,0:T(8,128)(2,1)S(1)}, u32[]{:S(2)}, u32[]{:S(2)}) collective-permute-start(bf16[128,384]{1,0:T(8,128)(2,1)S(1)} %get-tuple-element.166), channel_id=1, source_target_pairs={{0,1},{1,0},{2,3},{3,2},{4,5},{5,4},{6,7},{7,6},{8,9},{9,8},{10,11... | collective-permute-start | bytes 294920 | tf_op jit(solution)/shard_map/ppermute | solution.py:341
  49.2 7.5 %collective-permute-start.21 = (bf16[128,1536]{1,0:T(8,128)(2,1)S(1)}, bf16[128,1536]{1,0:T(8,128)(2,1)S(1)}, u32[]{:S(2)}, u32[]{:S(2)}) collective-permute-start(bf16[128,1536]{1,0:T(8,128)(2,1)S(1)} %constant_dynamic-update-slice_fusion.4.near), channel_id=1, source_target_pairs={{0,1},{1,0},{2,3},{3,2},{4,5},{5,4},{6,7},{7,6},{8,9},{9,8},{10,11... | collective-permute-start | bytes 1179656 | tf_op jit(solution)/shard_map/ppermute | solution.py:341
  54.7 1.9 %collective-permute-start.22 = (bf16[128,1536]{1,0:T(8,128)(2,1)S(1)}, bf16[128,1536]{1,0:T(8,128)(2,1)S(1)}, u32[]{:S(2)}, u32[]{:S(2)}) collective-permute-start(bf16[128,1536]{1,0:T(8,128)(2,1)S(1)} %collective-permute-done.19.far), channel_id=1, source_target_pairs={{0,1},{1,0},{2,3},{3,2},{4,5},{5,4},{6,7},{7,6},{8,9},{9,8},{10,11... | collective-permute-start | bytes 1179656 | tf_op jit(solution)/shard_map/ppermute | solution.py:341
  58.9 1.5 %collective-permute-start.23 = (bf16[128,384]{1,0:T(8,128)(2,1)S(1)}, bf16[128,384]{1,0:T(8,128)(2,1)S(1)}, u32[]{:S(2)}, u32[]{:S(2)}) collective-permute-start(bf16[128,384]{1,0:T(8,128)(2,1)S(1)} %get-tuple-element.169), channel_id=1, source_target_pairs={{0,1},{1,0},{2,3},{3,2},{4,5},{5,4},{6,7},{7,6},{8,9},{9,8},{10,11... | collective-permute-start | bytes 294920 | tf_op jit(solution)/shard_map/ppermute | solution.py:341
  60.4 10.9 %collective-permute-start.24 = (bf16[128,384]{1,0:T(8,128)(2,1)S(1)}, bf16[128,384]{1,0:T(8,128)(2,1)S(1)}, u32[]{:S(2)}, u32[]{:S(2)}) collective-permute-start(bf16[128,384]{1,0:T(8,128)(2,1)S(1)} %get-tuple-element.170), channel_id=1, source_target_pairs={{0,16},{1,21},{2,18},{3,23},{4,20},{5,17},{6,22},{7,19},{8,24},{9,... | collective-permute-start | bytes 294920 | tf_op jit(solution)/shard_map/ppermute | solution.py:390
  63.2 8.5 %collective-permute-start.25 = (bf16[128,384]{1,0:T(8,128)(2,1)S(1)}, bf16[128,384]{1,0:T(8,128)(2,1)S(1)}, u32[]{:S(2)}, u32[]{:S(2)}) collective-permute-start(bf16[128,384]{1,0:T(8,128)(2,1)S(1)} %get-tuple-element.171), channel_id=1, source_target_pairs={{0,28},{1,13},{2,30},{3,15},{4,24},{5,9},{6,26},{7,11},{8,20},{9,5... | collective-permute-start | bytes 294920 | tf_op jit(solution)/shard_map/ppermute | solution.py:390
  65.0 7.0 %collective-permute-start.26 = (bf16[128,384]{1,0:T(8,128)(2,1)S(1)}, bf16[128,384]{1,0:T(8,128)(2,1)S(1)}, u32[]{:S(2)}, u32[]{:S(2)}) collective-permute-start(bf16[128,384]{1,0:T(8,128)(2,1)S(1)} %get-tuple-element.172), channel_id=1, source_target_pairs={{0,8},{1,25},{2,10},{3,27},{4,12},{5,29},{6,14},{7,31},{8,0},{9,17... | collective-permute-start | bytes 294920 | tf_op jit(solution)/shard_map/ppermute | solution.py:390
  65.0 7.0 %collective-permute-start.27 = (bf16[128,384]{1,0:T(8,128)(2,1)S(1)}, bf16[128,384]{1,0:T(8,128)(2,1)S(1)}, u32[]{:S(2)}, u32[]{:S(2)}) collective-permute-start(bf16[128,384]{1,0:T(8,128)(2,1)S(1)} %get-tuple-element.173), channel_id=1, source_target_pairs={{0,0},{1,5},{2,2},{3,7},{4,4},{5,1},{6,6},{7,3},{8,8},{9,13},{10,1... | collective-permute-start | bytes 294920 | tf_op jit(solution)/shard_map/ppermute | solution.py:390
  72.1 1.5 %collective-permute-start.28 = (bf16[256,384]{1,0:T(8,128)(2,1)S(1)}, bf16[256,384]{1,0:T(8,128)(2,1)S(1)}, u32[]{:S(2)}, u32[]{:S(2)}) collective-permute-start(bf16[256,384]{1,0:T(8,128)(2,1)S(1)} %shard_map.117), channel_id=1, source_target_pairs={{0,1},{1,0},{2,3},{3,2},{4,5},{5,4},{6,7},{7,6},{8,9},{9,8},{10,11... | collective-permute-start | bytes 589832 | tf_op jit(solution)/shard_map/ppermute | solution.py:341

commit v8 on v7

--- a/solution.py
+++ b/solution.py
@@ -72,9 +72,8 @@
         ).astype(out_ref.dtype)
 
 
-def project(normed_ref, places, w_ref, cos_ref, sin_ref, proj_ref):
-    turned_width = w_ref.shape[-1] // 3 * 2
-    acc = dot(normed_ref[...], w_ref[...])
+def turn(acc, places, cos_ref, sin_ref, proj_ref):
+    turned_width = acc.shape[-1] // 3 * 2
     proj_ref[:, turned_width:] = acc[:, turned_width:].astype(proj_ref.dtype)
     count = acc.shape[0] // len(places)
     for i, place in enumerate(places):
@@ -87,6 +86,10 @@
             proj_ref[span, lane : lane + HEAD_DIM] = (head * cosine + turned * sine).astype(
                 proj_ref.dtype
             )
+
+
+def project(normed_ref, places, w_ref, cos_ref, sin_ref, proj_ref):
+    turn(dot(normed_ref[...], w_ref[...]), places, cos_ref, sin_ref, proj_ref)
 
 
 def mix(spans, count, write):
@@ -286,6 +289,10 @@
     split_normalize(near, far, gain_ref, shift_ref, normed_ref)
     places = [frame_of(SHARES + i) for i in range(SHARES)]
     project(normed_ref, places, w_ref, cos_ref, sin_ref, proj_ref)
+    split_mix(own_proj_ref, proj_ref, own_ref, other_ref)
+
+
+def split_mix(own_proj_ref, proj_ref, own_ref, other_ref):
     count = own_ref.shape[0] // SHARES
 
     def write(i, low, head, value):
@@ -295,6 +302,74 @@
 
     spans = [(ref, i * count) for ref in (own_proj_ref, proj_ref) for i in range(SHARES)]
     mix(spans, count, write)
+
+
+def centred(rows, gain):
+    values = rows.astype(jnp.float32)
+    total = jnp.sum(values, axis=-1, keepdims=True)
+    square = jnp.sum(values * values, axis=-1, keepdims=True)
+    return total, square, ((values - total / rows.shape[-1]) * gain).astype(jnp.bfloat16)
+
+
+def half_lanes(features, flip):
+    half = features // 2
+    return pl.ds(pl.multiple_of((chip_of() ^ flip) * half, half), half)
+
+
+def near_kernel(
+    own_ref, other_ref, gain_ref, shift_ref, w_ref,
+    own_acc_ref, other_acc_ref, own_total_ref, other_total_ref, own_square_ref, other_square_ref,
+    fixed_ref,
+):
+    features = w_ref.shape[0]
+    near = half_lanes(features, 0)
+    gain = 1.0 + gain_ref[:, near]
+    for ref, acc_ref, total_ref, square_ref in (
+        (own_ref, own_acc_ref, own_total_ref, own_square_ref),
+        (other_ref, other_acc_ref, other_total_ref, other_square_ref),
+    ):
+        total_ref[...], square_ref[...], scaled = centred(ref[...], gain)
+        acc_ref[...] = dot(scaled, w_ref[near, :])
+    shifted = 0.0
+    for flip in range(2):
+        lanes = half_lanes(features, flip)
+        rows = []
+        for row in (1.0 + gain_ref[:, lanes], shift_ref[:, lanes]):
+            high = row.astype(jnp.bfloat16).astype(jnp.float32)
+            rows += [high, row - high]
+        rows.append(jnp.zeros((GROUP - len(rows), rows[0].shape[-1]), jnp.float32))
+        product = dot(jnp.concatenate(rows, axis=0).astype(jnp.bfloat16), w_ref[lanes, :])
+        fixed_ref[flip : flip + 1, :] = product[0:1] + product[1:2]
+        shifted += product[2:3] + product[3:4]
+    fixed_ref[2:3, :] = shifted
+    fixed_ref[3:, :] = jnp.zeros((fixed_ref.shape[0] - 3, fixed_ref.shape[1]), jnp.float32)
+
+
+def join_halves(
+    far_ref, acc_ref, total_ref, square_ref, fixed_ref, gain_ref, w_ref, cos_ref, sin_ref,
+    proj_ref, pieces,
+):
+    features = w_ref.shape[0]
+    half = features // 2
+    far = half_lanes(features, 1)
+    total, square, scaled = centred(far_ref[...], 1.0 + gain_ref[:, far])
+    near_total = total_ref[...]
+    mean = (near_total + total) / features
+    rate = lax.rsqrt((square_ref[...] + square) / features - mean * mean + EPSILON)
+    acc = acc_ref[...] + dot(scaled, w_ref[far, :])
+    acc += (near_total / half - mean) * fixed_ref[0:1, :] + (total / half - mean) * fixed_ref[1:2, :]
+    places = [frame_of(i) for i in pieces]
+    turn(acc * rate + fixed_ref[2:3, :], places, cos_ref, sin_ref, proj_ref)
+
+
+def own_far_kernel(*refs):
+    join_halves(*refs, OWN)
+
+
+def other_far_kernel(own_proj_ref, *refs):
+    *inputs, own_ref, other_ref, proj_ref = refs
+    join_halves(*inputs, proj_ref, OTHER)
+    split_mix(own_proj_ref, proj_ref, own_ref, other_ref)
 
 
 def pack_kernel(*refs):
@@ -508,21 +583,42 @@
                 shape(tokens, share),
                 inputs=len(blocks),
             )(*blocks)
-            far = after(far, other_mixed[-1], updated)
-        rest_in = (gain_row, shift_row, weights, cosine, sine)
+            line = jax.ShapeDtypeStruct((half, 1), f32)
+            own_acc, other_acc, own_total, other_total, own_square, other_square, fixed = call(
+                near_kernel,
+                [shape(half, 3 * width, f32)] * 2 + [line] * 4 + [shape(8, 3 * width, f32)],
+                inputs=5,
+            )(near, other_near, gain_row, shift_row, weights)
+            far = after(far, other_mixed[-1], updated, fixed)
         other_far = swap(far, "mlp", n_mlp, 1)
-        own_proj = call(
-            half_kernel,
-            shape(half, 3 * width),
-            inputs=7,
-            scratch=(pltpu.VMEM((half, features), bf16),),
-        )(near, far, *rest_in)
-        own, other = call(
-            split_temporal_kernel,
-            [shape(half, width)] * 2,
-            inputs=8,
-            scratch=(pltpu.VMEM((half, features), bf16), pltpu.VMEM((half, 3 * width), bf16)),
-        )(own_proj, other_near, other_far, *rest_in)
+        if own_mixed:
+            rest_in = (fixed, gain_row, weights, cosine, sine)
+            own_proj = call(own_far_kernel, shape(half, 3 * width), inputs=9)(
+                far, own_acc, own_total, own_square, *rest_in
+            )
+            own, other = call(
+                other_far_kernel,
+                [shape(half, width)] * 2,
+                inputs=10,
+                scratch=(pltpu.VMEM((half, 3 * width), bf16),),
+            )(own_proj, other_far, other_acc, other_total, other_square, *rest_in)
+        else:
+            rest_in = (gain_row, shift_row, weights, cosine, sine)
+            own_proj = call(
+                half_kernel,
+                shape(half, 3 * width),
+                inputs=7,
+                scratch=(pltpu.VMEM((half, features), bf16),),
+            )(near, far, *rest_in)
+            own, other = call(
+                split_temporal_kernel,
+                [shape(half, width)] * 2,
+                inputs=8,
+                scratch=(
+                    pltpu.VMEM((half, features), bf16),
+                    pltpu.VMEM((half, 3 * width), bf16),
+                ),
+            )(own_proj, other_near, other_far, *rest_in)
         own_mixed.append(own)
         other_mixed.append(swap(other, "mlp", n_mlp, 1))
     packed = call(

time: 74.5 us -> 73.8 us (level)
    pallas_call x0 -> x3, Pallas kernels: none -> 4.51 us  [the longest x1 2.24 us: split_on_device(): call(near_kernel, [shape(half, 3 * width, f32)] * 2 + [line] * 4 + [shape...]
    pallas_call x2 -> x1, Pallas kernels: 4.44 us -> 2.22 us  [split_on_device(): call(split_temporal_kernel, [shape(half, width)] * 2, inputs=8, scratch=(...]
    pallas_call x2 -> x1, Pallas kernels: 3.79 us -> 1.9 us  [split_on_device(): call(half_kernel, shape(half, 3 * width), inputs=7, scratch=(pltpu.VMEM((...]
  transfers between devices with their start and end apart: 29 -> 29, of which waited for: 17 -> 19; matrix products, arithmetic and copies ran while one was open for 0% -> 0% of each run, Pallas kernels for 22% -> 24%
where the time goes in v8:
time: 73.8 us; the launch traced here: 73.6 us
  starting transfers between devices  25.1 us (34%)
  waiting for transfers between devices  25 us (34%)
  Pallas kernels  22.4 us (30%)
  between operations  0.86 us (1%)
    ppermute x12, starting transfers between devices, send_pieces(): lax.ppermute(piece, ('seq', 'mlp'), piece_pairs(n_seq, n_mlp, i))  16.6 us
    ppermute x12, waiting for transfers between devices, send_pieces(): lax.ppermute(piece, ('seq', 'mlp'), piece_pairs(n_seq, n_mlp, i))  14.9 us
    ppermute x17, waiting for transfers between devices, swap(): return lax.ppermute(value, axis, [(i, i ^ k) for i in range(size)])  10.1 us
    ppermute x17, starting transfers between devices, swap(): return lax.ppermute(value, axis, [(i, i ^ k) for i in range(size)])  8.47 us
    pallas_call x1, Pallas kernels, rest(): call(functools.partial(rest_kernel, firsts=(first0, first1)), [shape(half...  3.81 us
    pallas_call x1, Pallas kernels, hold_weights(): pl.pallas_call(hold_kernel, out_shape=pltpu.VMEM((features, parts * width...  3.12 us
    pallas_call x1, Pallas kernels, split_on_device(): call(functools.partial(first_spatial_kernel, first=first0), [shape(half0,...  2.59 us
    pallas_call x1, Pallas kernels, split_on_device(): call(near_kernel, [shape(half, 3 * width, f32)] * 2 + [line] * 4 + [shape...  2.24 us
  transfers between devices with their start and end apart: 29, of which 19 were waited for; matrix products, arithmetic and copies ran while one was open for 0% of the time, Pallas kernels for 24%

profile of v8, /device:TPU:0, one launch (start us, length us, event | category | flops | bytes accessed | tf_op | source)
XLA Modules:
  0.0 73.6 jit_solution(9812504078778923081)
XLA Ops:
  0.6 2.6 %shard_map.106 = (bf16[128,384]{1,0:T(8,128)(2,1)S(1)}, bf16[128,1536]{1,0:T(8,128)(2,1)S(1)}, bf16[384,1536]{1,0:T(8,128)(2,1)S(1)}, f32[1,1536]{1,0:T(1,128)S(1)}, bf16[3,512,384]{2,1,0:T(8,128)(2,1)S(1)}) custom-call(bf16[3,512,384]{2,1,0:T(8,128)(2,1)} %bitcast.19, bf16[384,3072]{1,0:T(8,128)(2,1)} %w_far.1, f32[1,3072]{1,0:T(1,128)} %bitcast.24), custom_call_target="tpu_custom_call" | custom-call | tf_op jit(solution)/shard_map/pallas_call | solution.py:479
  3.2 0.5 collective-permute-start.11
  3.7 1.2 %shard_map.107 = (bf16[128,384]{1,0:T(8,128)(2,1)S(1)}, f32[128,1536]{1,0:T(8,128)S(1)}) custom-call(bf16[384,1536]{1,0:T(8,128)(2,1)S(1)} %get-tuple-element.137.w_ref, f32[1,1536]{1,0:T(1,128)S(1)} %get-tuple-element.138.gate_ref, bf16[3,512,384]{2,1,0:T(8,128)(2,1)S(1)} %get-tuple-element.139.qkv_ref), custom_call_target="tpu_custom_call" | custom-call | tf_op jit(solution)/shard_map/pallas_call | solution.py:493
  5.0 0.1 collective-permute-done.11.b_ref
  5.1 0.1 shard_map.108
  5.2 2.9 %collective-permute-start.12 = (bf16[128,1536]{1,0:T(8,128)(2,1)S(1)}, bf16[128,1536]{1,0:T(8,128)(2,1)S(1)}, u32[]{:S(2)}, u32[]{:S(2)}) collective-permute-start(bf16[128,1536]{1,0:T(8,128)(2,1)S(1)} %shard_map.108), channel_id=1, source_target_pairs={{0,2},{1,3},{2,0},{3,1},{4,6},{5,7},{6,4},{7,5},{8,10},{9,11},{10,... | collective-permute-start | bytes 1179656 | tf_op jit(solution)/shard_map/ppermute | solution.py:416
  8.1 7.5 %conditional.2 = (bf16[128,1536]{1,0:T(8,128)(2,1)}, f32[128,1536]{1,0:T(8,128)S(1)}, f32[128,1536]{1,0:T(8,128)S(1)}) conditional(s32[]{:T(128)} %convert_element_type.4, () %tuple.33, (bf16[1,512,768]{2,1,0:T(8,128)(2,1)}, bf16[128,384]{1,0:T(8,128)(2,1)S(1)}, bf16[128,384]{1,0:T(8,128)(2,1)S(1)}, bf16[3,512,384]{2,1,0:T(8,128)(2,1)}, ...), branch_computations={%region_0.0_spmd, %region_1.0_spmd} | conditional | bytes 4718736 | solution.py:535
  8.1 3.8 %branch_1_fun.5 = (bf16[128,1536]{1,0:T(8,128)(2,1)S(1)}, f32[128,1536]{1,0:T(8,128)S(1)}, f32[128,1536]{1,0:T(8,128)S(1)}, bf16[128,1536]{1,0:T(8,128)(2,1)S(1)...) custom-call(bf16[128,384]{1,0:T(8,128)(2,1)S(1)} %get-tuple-element.55.own0_ref, ...), custom_call_target="tpu_custom_call" | custom-call | tf_op jit(solution)/shard_map/cond/branch_1_fun/pallas_call | solution.py:502
  11.9 0.1 collective-permute-start.2
  12.0 0.5 collective-permute-start.1
  12.5 0.1 collective-permute-start
  12.6 1.1 %collective-permute-done.2.b_ref = bf16[128,1536]{1,0:T(8,128)(2,1)S(1)} collective-permute-done((bf16[128,1536]{1,0:T(8,128)(2,1)S(1)}, bf16[128,1536]{1,0:T(8,128)(2,1)S(1)}, u32[]{:S(2)}, u32[]{:S(2)}) %collective-permute-start.2) | collective-permute-done | bytes 393248 | tf_op jit(solution)/shard_map/cond/branch_1_fun/ppermute | solution.py:416
  13.7 0.1 branch_1_fun.8
  13.8 0.5 collective-permute-done.1.b_ref
  14.3 0.1 branch_1_fun.7
  14.3 0.5 collective-permute-done.b_ref
  14.8 0.8 %branch_1_fun.6 = bf16[128,1536]{1,0:T(8,128)(2,1)} custom-call(f32[128,1536]{1,0:T(8,128)S(1)} %get-tuple-element.61.a_ref, bf16[128,1536]{1,0:T(8,128)(2,1)S(1)} %collective-permute-done.b_ref), custom_call_target="tpu_custom_call" | custom-call | tf_op jit(solution)/shard_map/cond/branch_1_fun/pallas_call | solution.py:521
  15.7 1.8 %collective-permute-done.12.arrived_ref = bf16[128,1536]{1,0:T(8,128)(2,1)S(1)} collective-permute-done((bf16[128,1536]{1,0:T(8,128)(2,1)S(1)}, bf16[128,1536]{1,0:T(8,128)(2,1)S(1)}, u32[]{:S(2)}, u32[]{:S(2)}) %collective-permute-start.12) | collective-permute-done | bytes 393248 | tf_op jit(solution)/shard_map/ppermute | solution.py:416
  17.5 0.1 shard_map.109
  17.6 11.9 %while.16 = (s32[]{:T(128)}, bf16[32,1536]{1,0:T(8,128)(2,1)S(1)}, bf16[32,1536]{1,0:T(8,128)(2,1)S(1)}, bf16[32,1536]{1,0:T(8,128)(2,1)S(1)}, bf16[32,1536]{1,0:T(8,128)(2,1)S(1)}, /*index=5*/s32[]{:T(128)}, s32[]{:T(128)}) while((s32[]{:T(128)}, bf16[32,1536]{1,0:T(8,128)(2,1)S(1)}, bf16[32,1536]{1,0:T(8,128)(2,1)S(1)}, ...), condition=%wide.region_3.0_spmd, body=%wide.region_2.0_spmd.sunk | while | flops 2 | bytes 2359533 | solution.py:559
  17.7 2.9 %collective-permute-start.7 = (bf16[32,1536]{1,0:T(8,128)(2,1)S(1)}, bf16[32,1536]{1,0:T(8,128)(2,1)S(1)}, u32[]{:S(2)}, u32[]{:S(2)}) collective-permute-start(bf16[32,1536]{1,0:T(8,128)(2,1)S(1)} %get-tuple-element.256), channel_id=1, source_target_pairs={{0,16},{1,21},{2,18},{3,23},{4,20},{5,17},{6,22},{7,19},{8,24},{9,... | collective-permute-start | bytes 294920 | tf_op jit(solution)/shard_map/while/body/ppermute | solution.py:465
  20.6 2.3 %collective-permute-start.8 = (bf16[32,1536]{1,0:T(8,128)(2,1)S(1)}, bf16[32,1536]{1,0:T(8,128)(2,1)S(1)}, u32[]{:S(2)}, u32[]{:S(2)}) collective-permute-start(bf16[32,1536]{1,0:T(8,128)(2,1)S(1)} %get-tuple-element.257), channel_id=1, source_target_pairs={{0,28},{1,13},{2,30},{3,15},{4,24},{5,9},{6,26},{7,11},{8,20},{9,5... | collective-permute-start | bytes 294920 | tf_op jit(solution)/shard_map/while/body/ppermute | solution.py:465
  22.9 0.7 collective-permute-start.10
  23.5 5.0 %collective-permute-done.7 = bf16[32,1536]{1,0:T(8,128)(2,1)S(1)} collective-permute-done((bf16[32,1536]{1,0:T(8,128)(2,1)S(1)}, bf16[32,1536]{1,0:T(8,128)(2,1)S(1)}, u32[]{:S(2)}, u32[]{:S(2)}) %collective-permute-start.7) | collective-permute-done | bytes 98336 | tf_op jit(solution)/shard_map/while/body/ppermute | solution.py:465
  28.5 0.3 collective-permute-done.8
  28.8 0.7 collective-permute-done.9
  29.6 1.9 %collective-permute-start.16 = (bf16[128,1536]{1,0:T(8,128)(2,1)S(1)}, bf16[128,1536]{1,0:T(8,128)(2,1)S(1)}, u32[]{:S(2)}, u32[]{:S(2)}) collective-permute-start(bf16[128,1536]{1,0:T(8,128)(2,1)S(1)} %constant_dynamic-update-slice_fusion.near), channel_id=1, source_target_pairs={{0,2},{1,3},{2,0},{3,1},{4,6},{5,7},{6,4},{7,5},{8,10},{9,11},{10,... | collective-permute-start | bytes 1179656 | tf_op jit(solution)/shard_map/ppermute | solution.py:416
  31.4 0.1 shard_map.110
  31.6 11.3 %conditional.3 = (bf16[32,1536]{1,0:T(8,128)(2,1)S(1)}, bf16[32,1536]{1,0:T(8,128)(2,1)S(1)}, bf16[32,1536]{1,0:T(8,128)(2,1)S(1)}, bf16[32,1536]{1,0:T(8,128)(2,1)S(1)}, bf16[3072,1152]{1,0:T(8,128)(2,1)S(1)}) conditional(s32[]{:T(128)} %convert_element_type.4, (bf16[32,1536]{1,0:T(8,128)(2,1)S(1)}, bf16[32,1536]{1,0:T(8,128)(2,1)S(1)}, ...), branch_computations={%region_4.0_spmd, %region_5.0_spmd} | conditional | bytes 7077930 | solution.py:569
  31.6 3.0 %collective-permute-start.3 = (bf16[32,1536]{1,0:T(8,128)(2,1)S(1)}, bf16[32,1536]{1,0:T(8,128)(2,1)S(1)}, u32[]{:S(2)}, u32[]{:S(2)}) collective-permute-start(bf16[32,1536]{1,0:T(8,128)(2,1)S(1)} %get-tuple-element.79), channel_id=1, source_target_pairs={{0,16},{1,21},{2,18},{3,23},{4,20},{5,17},{6,22},{7,19},{8,24},{9,... | collective-permute-start | bytes 294920 | tf_op jit(solution)/shard_map/cond/branch_1_fun/ppermute | solution.py:465
  34.6 1.3 %collective-permute-start.4 = (bf16[32,1536]{1,0:T(8,128)(2,1)S(1)}, bf16[32,1536]{1,0:T(8,128)(2,1)S(1)}, u32[]{:S(2)}, u32[]{:S(2)}) collective-permute-start(bf16[32,1536]{1,0:T(8,128)(2,1)S(1)} %get-tuple-element.80), channel_id=1, source_target_pairs={{0,28},{1,13},{2,30},{3,15},{4,24},{5,9},{6,26},{7,11},{8,20},{9,5... | collective-permute-start | bytes 294920 | tf_op jit(solution)/shard_map/cond/branch_1_fun/ppermute | solution.py:465
  36.0 0.3 collective-permute-start.5
  36.3 0.8 %collective-permute-start.6 = (bf16[32,1536]{1,0:T(8,128)(2,1)S(1)}, bf16[32,1536]{1,0:T(8,128)(2,1)S(1)}, u32[]{:S(2)}, u32[]{:S(2)}) collective-permute-start(bf16[32,1536]{1,0:T(8,128)(2,1)S(1)} %get-tuple-element.82), channel_id=1, source_target_pairs={{0,0},{1,5},{2,2},{3,7},{4,4},{5,1},{6,6},{7,3},{8,8},{9,13},{10,1... | collective-permute-start | bytes 294920 | tf_op jit(solution)/shard_map/cond/branch_1_fun/ppermute | solution.py:465
  37.1 3.1 %branch_1_fun.9 = bf16[3072,1152]{1,0:T(8,128)(2,1)S(1)} custom-call(bf16[3,3072,384]{2,1,0:T(8,128)(2,1)} %bitcast.18), custom_call_target="tpu_custom_call" | custom-call | tf_op jit(solution)/shard_map/cond/branch_1_fun/pallas_call | solution.py:136
  40.2 0.2 collective-permute-done.3
  40.5 1.5 %collective-permute-done.4 = bf16[32,1536]{1,0:T(8,128)(2,1)S(1)} collective-permute-done((bf16[32,1536]{1,0:T(8,128)(2,1)S(1)}, bf16[32,1536]{1,0:T(8,128)(2,1)S(1)}, u32[]{:S(2)}, u32[]{:S(2)}) %collective-permute-start.4) | collective-permute-done | bytes 98336 | tf_op jit(solution)/shard_map/cond/branch_1_fun/ppermute | solution.py:465
  42.0 0.9 %collective-permute-done.5 = bf16[32,1536]{1,0:T(8,128)(2,1)S(1)} collective-permute-done((bf16[32,1536]{1,0:T(8,128)(2,1)S(1)}, bf16[32,1536]{1,0:T(8,128)(2,1)S(1)}, u32[]{:S(2)}, u32[]{:S(2)}) %collective-permute-start.5) | collective-permute-done | bytes 98336 | tf_op jit(solution)/shard_map/cond/branch_1_fun/ppermute | solution.py:465
  42.9 0.1 collective-permute-start.17
  43.1 0.5 collective-permute-start.18
  43.6 0.1 collective-permute-start.21
  43.7 0.8 %collective-permute-start.19 = (bf16[128,1536]{1,0:T(8,128)(2,1)S(1)}, bf16[128,1536]{1,0:T(8,128)(2,1)S(1)}, u32[]{:S(2)}, u32[]{:S(2)}) collective-permute-start(bf16[128,1536]{1,0:T(8,128)(2,1)S(1)} %constant_dynamic-update-slice_fusion.4.own_ref), channel_id=1, source_target_pairs={{0,2},{1,3},{2,0},{3,1},{4,6},{5,7},{6,4},{7,5},{8,10},{9,11},{10,... | collective-permute-start | bytes 1179656 | tf_op jit(solution)/shard_map/ppermute | solution.py:416
  44.5 0.2 collective-permute-start.15
  44.6 0.1 collective-permute-done.17.near
  44.7 0.3 collective-permute-start.13
  45.0 1.9 %shard_map.112.own_proj_ref = bf16[128,1152]{1,0:T(8,128)(2,1)S(1)} custom-call(bf16[128,1536]{1,0:T(8,128)(2,1)S(1)} %constant_dynamic-update-slice_fusion.near, bf16[128,1536]{1,0:T(8,128)(2,1)S(1)} %collective-permute-done.16.far, f32[1,3072]{1,0:T(1,128)S(1)} %bitcast.10, f32[1,3072]{1,0:T(1,128)S(1)} %bitcast.15, ...), custom_call_target="tpu_custom_call" | custom-call | tf_op jit(solution)/shard_map/pallas_call | solution.py:607
  46.9 2.2 %shard_map.113 = (bf16[128,384]{1,0:T(8,128)(2,1)S(1)}, bf16[128,384]{1,0:T(8,128)(2,1)S(1)}) custom-call(bf16[128,1152]{1,0:T(8,128)(2,1)S(1)} %shard_map.112.own_proj_ref, bf16[128,1536]{1,0:T(8,128)(2,1)S(1)} %collective-permute-done.17.near, bf16[128,1536]{1,0:T(8,128)(2,1)S(1)} %collective-permute-done.18.far, f32[1,3072]{1,0:T(1,128)S(1)} %bitcast.11, ...), custom_call_target="tpu_custom_call" | custom-call | tf_op jit(solution)/shard_map/pallas_call | solution.py:613
  49.1 0.3 collective-permute-start.20
  49.5 1.0 %shard_map.111 = bf16[512,768]{1,0:T(8,128)(2,1)} custom-call(bf16[128,768]{1,0:T(8,128)(2,1)S(1)} %get-tuple-element.148.refs_0_, bf16[128,768]{1,0:T(8,128)(2,1)S(1)} %collective-permute-done.13.refs_1_, bf16[128,768]{1,0:T(8,128)(2,1)S(1)} %get-tuple-element.160.refs_2_, bf16[128,768]{1,0:T(8,128)(2,1)S(1)} %collective-permute-done.15.refs_3_), custom_call_target="tpu_custom_call" | custom-call | tf_op jit(solution)/shard_map/pallas_call | solution.py:581
  50.4 2.2 %shard_map.114 = (f32[128,1152]{1,0:T(8,128)S(1)}, f32[128,1152]{1,0:T(8,128)S(1)}, f32[128,1]{1,0:T(8,128)S(1)}, f32[128,1]{1,0:T(8,128)S(1)}, f32[128,1]{1,0:T...) custom-call(bf16[128,1536]{1,0:T(8,128)(2,1)S(1)} %constant_dynamic-update-slice_fusion.4.own_ref, ...), custom_call_target="tpu_custom_call" | custom-call | tf_op jit(solution)/shard_map/pallas_call | solution.py:587
  52.6 2.5 %collective-permute-done.19.refs_0_ = bf16[128,1536]{1,0:T(8,128)(2,1)S(1)} collective-permute-done((bf16[128,1536]{1,0:T(8,128)(2,1)S(1)}, bf16[128,1536]{1,0:T(8,128)(2,1)S(1)}, u32[]{:S(2)}, u32[]{:S(2)}) %collective-permute-start.19) | collective-permute-done | bytes 393248 | tf_op jit(solution)/shard_map/ppermute | solution.py:416
  55.2 0.9 %shard_map.115.own_proj_ref = bf16[128,1152]{1,0:T(8,128)(2,1)S(1)} custom-call(bf16[128,1536]{1,0:T(8,128)(2,1)S(1)} %collective-permute-done.19.refs_0_, f32[128,1152]{1,0:T(8,128)S(1)} %get-tuple-element.176.refs_1_, f32[128,1]{1,0:T(8,128)S(1)} %get-tuple-element.177.refs_2_, f32[128,1]{1,0:T(8,128)S(1)} %get-tuple-element.178.refs_3_, ...), custom_call_target="tpu_custom_call" | custom-call | tf_op jit(solution)/shard_map/pallas_call | solution.py:596
  56.1 0.8 %collective-permute-done.22.refs_0_ = bf16[128,1536]{1,0:T(8,128)(2,1)S(1)} collective-permute-done((bf16[128,1536]{1,0:T(8,128)(2,1)S(1)}, bf16[128,1536]{1,0:T(8,128)(2,1)S(1)}, u32[]{:S(2)}, u32[]{:S(2)}) %collective-permute-start.22) | collective-permute-done | bytes 393248 | tf_op jit(solution)/shard_map/ppermute | solution.py:416
  56.9 1.4 %shard_map.116 = (bf16[128,384]{1,0:T(8,128)(2,1)S(1)}, bf16[128,384]{1,0:T(8,128)(2,1)S(1)}) custom-call(bf16[128,1152]{1,0:T(8,128)(2,1)S(1)} %shard_map.115.own_proj_ref, bf16[128,1536]{1,0:T(8,128)(2,1)S(1)} %collective-permute-done.22.refs_0_, f32[128,1152]{1,0:T(8,128)S(1)} %get-tuple-element.179.refs_1_, f32[128,1]{1,0:T(8,128)S(1)} %get-tuple-element.180.refs_2_, ...), custom_call_target="tpu_custom_call" | custom-call | tf_op jit(solution)/shard_map/pallas_call | solution.py:599
  58.3 0.2 collective-permute-start.23
  58.5 1.2 %collective-permute-done.23.refs_3_ = bf16[128,384]{1,0:T(8,128)(2,1)S(1)} collective-permute-done((bf16[128,384]{1,0:T(8,128)(2,1)S(1)}, bf16[128,384]{1,0:T(8,128)(2,1)S(1)}, u32[]{:S(2)}, u32[]{:S(2)}) %collective-permute-start.23) | collective-permute-done | bytes 98336 | tf_op jit(solution)/shard_map/ppermute | solution.py:416
  59.7 2.8 %collective-permute-start.24 = (bf16[128,384]{1,0:T(8,128)(2,1)S(1)}, bf16[128,384]{1,0:T(8,128)(2,1)S(1)}, u32[]{:S(2)}, u32[]{:S(2)}) collective-permute-start(bf16[128,384]{1,0:T(8,128)(2,1)S(1)} %get-tuple-element.184), channel_id=1, source_target_pairs={{0,16},{1,21},{2,18},{3,23},{4,20},{5,17},{6,22},{7,19},{8,24},{9,... | collective-permute-start | bytes 294920 | tf_op jit(solution)/shard_map/ppermute | solution.py:465
  62.5 1.8 %collective-permute-start.25 = (bf16[128,384]{1,0:T(8,128)(2,1)S(1)}, bf16[128,384]{1,0:T(8,128)(2,1)S(1)}, u32[]{:S(2)}, u32[]{:S(2)}) collective-permute-start(bf16[128,384]{1,0:T(8,128)(2,1)S(1)} %get-tuple-element.185), channel_id=1, source_target_pairs={{0,28},{1,13},{2,30},{3,15},{4,24},{5,9},{6,26},{7,11},{8,20},{9,5... | collective-permute-start | bytes 294920 | tf_op jit(solution)/shard_map/ppermute | solution.py:465
  64.3 0.7 collective-permute-start.27
  64.9 5.6 %collective-permute-done.24.refs_0_ = bf16[128,384]{1,0:T(8,128)(2,1)S(1)} collective-permute-done((bf16[128,384]{1,0:T(8,128)(2,1)S(1)}, bf16[128,384]{1,0:T(8,128)(2,1)S(1)}, u32[]{:S(2)}, u32[]{:S(2)}) %collective-permute-start.24) | collective-permute-done | bytes 98336 | tf_op jit(solution)/shard_map/ppermute | solution.py:465
  70.5 0.3 collective-permute-done.25.refs_1_
  70.8 0.5 collective-permute-done.26.refs_2_
  71.3 0.1 collective-permute-start.28
  71.4 1.4 %collective-permute-done.28.refs_4_ = bf16[256,384]{1,0:T(8,128)(2,1)S(1)} collective-permute-done((bf16[256,384]{1,0:T(8,128)(2,1)S(1)}, bf16[256,384]{1,0:T(8,128)(2,1)S(1)}, u32[]{:S(2)}, u32[]{:S(2)}) %collective-permute-start.28) | collective-permute-done | bytes 196640 | tf_op jit(solution)/shard_map/ppermute | solution.py:416
  72.8 0.8 %shard_map.119 = bf16[512,384]{1,0:T(8,128)(2,1)} custom-call(bf16[128,384]{1,0:T(8,128)(2,1)S(1)} %collective-permute-done.24.refs_0_, bf16[128,384]{1,0:T(8,128)(2,1)S(1)} %collective-permute-done.25.refs_1_, bf16[128,384]{1,0:T(8,128)(2,1)S(1)} %collective-permute-done.26.refs_2_, bf16[128,384]{1,0:T(8,128)(2,1)S(1)} %collective-permute-done.27.refs_3_, ...), custom_call_target="tpu_custom_call" | custom-call | tf_op jit(solution)/shard_map/pallas_call | solution.py:630
  (40 shorter events, 0.3 us)
Async XLA Ops:
  3.2 1.9 %collective-permute-start.11 = (bf16[128,1536]{1,0:T(8,128)(2,1)S(1)}, bf16[128,1536]{1,0:T(8,128)(2,1)S(1)}, u32[]{:S(2)}, u32[]{:S(2)}) collective-permute-start(bf16[128,1536]{1,0:T(8,128)(2,1)S(1)} %get-tuple-element.142), channel_id=1, source_target_pairs={{0,1},{1,0},{2,3},{3,2},{4,5},{5,4},{6,7},{7,6},{8,9},{9,8},{10,11... | collective-permute-start | bytes 1179656 | tf_op jit(solution)/shard_map/ppermute | solution.py:416
  5.2 12.3 %collective-permute-start.12 = (bf16[128,1536]{1,0:T(8,128)(2,1)S(1)}, bf16[128,1536]{1,0:T(8,128)(2,1)S(1)}, u32[]{:S(2)}, u32[]{:S(2)}) collective-permute-start(bf16[128,1536]{1,0:T(8,128)(2,1)S(1)} %shard_map.108), channel_id=1, source_target_pairs={{0,2},{1,3},{2,0},{3,1},{4,6},{5,7},{6,4},{7,5},{8,10},{9,11},{10,... | collective-permute-start | bytes 1179656 | tf_op jit(solution)/shard_map/ppermute | solution.py:416
  11.9 1.8 %collective-permute-start.2 = (bf16[128,1536]{1,0:T(8,128)(2,1)S(1)}, bf16[128,1536]{1,0:T(8,128)(2,1)S(1)}, u32[]{:S(2)}, u32[]{:S(2)}) collective-permute-start(bf16[128,1536]{1,0:T(8,128)(2,1)S(1)} %get-tuple-element.66), channel_id=1, source_target_pairs={{0,1},{1,0},{2,3},{3,2},{4,5},{5,4},{6,7},{7,6},{8,9},{9,8},{10,11... | collective-permute-start | bytes 1179656 | tf_op jit(solution)/shard_map/cond/branch_1_fun/ppermute | solution.py:416
  12.0 2.3 %collective-permute-start.1 = (bf16[128,1536]{1,0:T(8,128)(2,1)S(1)}, bf16[128,1536]{1,0:T(8,128)(2,1)S(1)}, u32[]{:S(2)}, u32[]{:S(2)}) collective-permute-start(bf16[128,1536]{1,0:T(8,128)(2,1)S(1)} %get-tuple-element.64), channel_id=1, source_target_pairs={{0,1},{1,0},{2,3},{3,2},{4,5},{5,4},{6,7},{7,6},{8,9},{9,8},{10,11... | collective-permute-start | bytes 1179656 | tf_op jit(solution)/shard_map/cond/branch_1_fun/ppermute | solution.py:416
  12.5 2.3 %collective-permute-start = (bf16[128,1536]{1,0:T(8,128)(2,1)S(1)}, bf16[128,1536]{1,0:T(8,128)(2,1)S(1)}, u32[]{:S(2)}, u32[]{:S(2)}) collective-permute-start(bf16[128,1536]{1,0:T(8,128)(2,1)S(1)} %get-tuple-element.62), channel_id=1, source_target_pairs={{0,1},{1,0},{2,3},{3,2},{4,5},{5,4},{6,7},{7,6},{8,9},{9,8},{10,11... | collective-permute-start | bytes 1179656 | tf_op jit(solution)/shard_map/cond/branch_1_fun/ppermute | solution.py:416
  15.7 15.8 %collective-permute-start.14 = (bf16[128,1536]{1,0:T(8,128)(2,1)}, bf16[128,1536]{1,0:T(8,128)(2,1)S(1)}, u32[]{:S(2)}, u32[]{:S(2)}) collective-permute-start(bf16[128,1536]{1,0:T(8,128)(2,1)} %get-tuple-element.146), channel_id=1, source_target_pairs={{0,2},{1,3},{2,0},{3,1},{4,6},{5,7},{6,4},{7,5},{8,10},{9,11},{10,... | collective-permute-start | bytes 1179656 | tf_op jit(solution)/shard_map/ppermute | solution.py:416
  17.7 10.9 %collective-permute-start.7 = (bf16[32,1536]{1,0:T(8,128)(2,1)S(1)}, bf16[32,1536]{1,0:T(8,128)(2,1)S(1)}, u32[]{:S(2)}, u32[]{:S(2)}) collective-permute-start(bf16[32,1536]{1,0:T(8,128)(2,1)S(1)} %get-tuple-element.256), channel_id=1, source_target_pairs={{0,16},{1,21},{2,18},{3,23},{4,20},{5,17},{6,22},{7,19},{8,24},{9,... | collective-permute-start | bytes 294920 | tf_op jit(solution)/shard_map/while/body/ppermute | solution.py:465
  20.6 8.2 %collective-permute-start.8 = (bf16[32,1536]{1,0:T(8,128)(2,1)S(1)}, bf16[32,1536]{1,0:T(8,128)(2,1)S(1)}, u32[]{:S(2)}, u32[]{:S(2)}) collective-permute-start(bf16[32,1536]{1,0:T(8,128)(2,1)S(1)} %get-tuple-element.257), channel_id=1, source_target_pairs={{0,28},{1,13},{2,30},{3,15},{4,24},{5,9},{6,26},{7,11},{8,20},{9,5... | collective-permute-start | bytes 294920 | tf_op jit(solution)/shard_map/while/body/ppermute | solution.py:465
  22.9 6.6 %collective-permute-start.9 = (bf16[32,1536]{1,0:T(8,128)(2,1)S(1)}, bf16[32,1536]{1,0:T(8,128)(2,1)S(1)}, u32[]{:S(2)}, u32[]{:S(2)}) collective-permute-start(bf16[32,1536]{1,0:T(8,128)(2,1)S(1)} %get-tuple-element.258), channel_id=1, source_target_pairs={{0,8},{1,25},{2,10},{3,27},{4,12},{5,29},{6,14},{7,31},{8,0},{9,17... | collective-permute-start | bytes 294920 | tf_op jit(solution)/shard_map/while/body/ppermute | solution.py:465
  22.9 6.6 %collective-permute-start.10 = (bf16[32,1536]{1,0:T(8,128)(2,1)S(1)}, bf16[32,1536]{1,0:T(8,128)(2,1)S(1)}, u32[]{:S(2)}, u32[]{:S(2)}) collective-permute-start(bf16[32,1536]{1,0:T(8,128)(2,1)S(1)} %get-tuple-element.259), channel_id=1, source_target_pairs={{0,0},{1,5},{2,2},{3,7},{4,4},{5,1},{6,6},{7,3},{8,8},{9,13},{10,1... | collective-permute-start | bytes 294920 | tf_op jit(solution)/shard_map/while/body/ppermute | solution.py:465
  29.6 13.5 %collective-permute-start.16 = (bf16[128,1536]{1,0:T(8,128)(2,1)S(1)}, bf16[128,1536]{1,0:T(8,128)(2,1)S(1)}, u32[]{:S(2)}, u32[]{:S(2)}) collective-permute-start(bf16[128,1536]{1,0:T(8,128)(2,1)S(1)} %constant_dynamic-update-slice_fusion.near), channel_id=1, source_target_pairs={{0,2},{1,3},{2,0},{3,1},{4,6},{5,7},{6,4},{7,5},{8,10},{9,11},{10,... | collective-permute-start | bytes 1179656 | tf_op jit(solution)/shard_map/ppermute | solution.py:416
  31.6 13.4 %copy-start = (f32[3072]{0:T(1024)S(1)}, f32[3072]{0:T(1024)}, u32[]{:S(2)}) copy-start(f32[3072]{0:T(1024)} %param.20) | copy-start | bytes 36868
  31.6 13.4 %copy-start.1 = (f32[3072]{0:T(1024)S(1)}, f32[3072]{0:T(1024)}, u32[]{:S(2)}) copy-start(f32[3072]{0:T(1024)} %param.19) | copy-start | bytes 36868
  31.6 13.4 %copy-start.2 = (f32[8,128]{1,0:T(8,128)S(1)}, f32[8,128]{1,0:T(8,128)}, u32[]{:S(2)}) copy-start(f32[8,128]{1,0:T(8,128)} %constant.22.clone.cos_ref.refs_7_) | copy-start | bytes 12292
  31.6 13.4 %copy-start.3 = (f32[8,128]{1,0:T(8,128)S(1)}, f32[8,128]{1,0:T(8,128)}, u32[]{:S(2)}) copy-start(f32[8,128]{1,0:T(8,128)} %constant.23.clone.sin_ref.refs_8_) | copy-start | bytes 12292
  31.6 8.9 %collective-permute-start.3 = (bf16[32,1536]{1,0:T(8,128)(2,1)S(1)}, bf16[32,1536]{1,0:T(8,128)(2,1)S(1)}, u32[]{:S(2)}, u32[]{:S(2)}) collective-permute-start(bf16[32,1536]{1,0:T(8,128)(2,1)S(1)} %get-tuple-element.79), channel_id=1, source_target_pairs={{0,16},{1,21},{2,18},{3,23},{4,20},{5,17},{6,22},{7,19},{8,24},{9,... | collective-permute-start | bytes 294920 | tf_op jit(solution)/shard_map/cond/branch_1_fun/ppermute | solution.py:465
  34.6 7.4 %collective-permute-start.4 = (bf16[32,1536]{1,0:T(8,128)(2,1)S(1)}, bf16[32,1536]{1,0:T(8,128)(2,1)S(1)}, u32[]{:S(2)}, u32[]{:S(2)}) collective-permute-start(bf16[32,1536]{1,0:T(8,128)(2,1)S(1)} %get-tuple-element.80), channel_id=1, source_target_pairs={{0,28},{1,13},{2,30},{3,15},{4,24},{5,9},{6,26},{7,11},{8,20},{9,5... | collective-permute-start | bytes 294920 | tf_op jit(solution)/shard_map/cond/branch_1_fun/ppermute | solution.py:465
  36.0 6.9 %collective-permute-start.5 = (bf16[32,1536]{1,0:T(8,128)(2,1)S(1)}, bf16[32,1536]{1,0:T(8,128)(2,1)S(1)}, u32[]{:S(2)}, u32[]{:S(2)}) collective-permute-start(bf16[32,1536]{1,0:T(8,128)(2,1)S(1)} %get-tuple-element.81), channel_id=1, source_target_pairs={{0,8},{1,25},{2,10},{3,27},{4,12},{5,29},{6,14},{7,31},{8,0},{9,17... | collective-permute-start | bytes 294920 | tf_op jit(solution)/shard_map/cond/branch_1_fun/ppermute | solution.py:465
  36.3 6.6 %collective-permute-start.6 = (bf16[32,1536]{1,0:T(8,128)(2,1)S(1)}, bf16[32,1536]{1,0:T(8,128)(2,1)S(1)}, u32[]{:S(2)}, u32[]{:S(2)}) collective-permute-start(bf16[32,1536]{1,0:T(8,128)(2,1)S(1)} %get-tuple-element.82), channel_id=1, source_target_pairs={{0,0},{1,5},{2,2},{3,7},{4,4},{5,1},{6,6},{7,3},{8,8},{9,13},{10,1... | collective-permute-start | bytes 294920 | tf_op jit(solution)/shard_map/cond/branch_1_fun/ppermute | solution.py:465
  42.9 1.8 %collective-permute-start.17 = (bf16[128,1536]{1,0:T(8,128)(2,1)S(1)}, bf16[128,1536]{1,0:T(8,128)(2,1)S(1)}, u32[]{:S(2)}, u32[]{:S(2)}) collective-permute-start(bf16[128,1536]{1,0:T(8,128)(2,1)S(1)} %constant_dynamic-update-slice_fusion.near), channel_id=1, source_target_pairs={{0,1},{1,0},{2,3},{3,2},{4,5},{5,4},{6,7},{7,6},{8,9},{9,8},{10,11... | collective-permute-start | bytes 1179656 | tf_op jit(solution)/shard_map/ppermute | solution.py:416
  43.1 3.8 %collective-permute-start.18 = (bf16[128,1536]{1,0:T(8,128)(2,1)S(1)}, bf16[128,1536]{1,0:T(8,128)(2,1)S(1)}, u32[]{:S(2)}, u32[]{:S(2)}) collective-permute-start(bf16[128,1536]{1,0:T(8,128)(2,1)S(1)} %collective-permute-done.16.far), channel_id=1, source_target_pairs={{0,1},{1,0},{2,3},{3,2},{4,5},{5,4},{6,7},{7,6},{8,9},{9,8},{10,11... | collective-permute-start | bytes 1179656 | tf_op jit(solution)/shard_map/ppermute | solution.py:416
  43.6 6.8 %collective-permute-start.21 = (bf16[128,1536]{1,0:T(8,128)(2,1)S(1)}, bf16[128,1536]{1,0:T(8,128)(2,1)S(1)}, u32[]{:S(2)}, u32[]{:S(2)}) collective-permute-start(bf16[128,1536]{1,0:T(8,128)(2,1)S(1)} %constant_dynamic-update-slice_fusion.4.own_ref), channel_id=1, source_target_pairs={{0,1},{1,0},{2,3},{3,2},{4,5},{5,4},{6,7},{7,6},{8,9},{9,8},{10,11... | collective-permute-start | bytes 1179656 | tf_op jit(solution)/shard_map/ppermute | solution.py:416
  43.7 11.5 %collective-permute-start.19 = (bf16[128,1536]{1,0:T(8,128)(2,1)S(1)}, bf16[128,1536]{1,0:T(8,128)(2,1)S(1)}, u32[]{:S(2)}, u32[]{:S(2)}) collective-permute-start(bf16[128,1536]{1,0:T(8,128)(2,1)S(1)} %constant_dynamic-update-slice_fusion.4.own_ref), channel_id=1, source_target_pairs={{0,2},{1,3},{2,0},{3,1},{4,6},{5,7},{6,4},{7,5},{8,10},{9,11},{10,... | collective-permute-start | bytes 1179656 | tf_op jit(solution)/shard_map/ppermute | solution.py:416
  44.5 5.0 %collective-permute-start.15 = (bf16[128,768]{1,0:T(8,128)(2,1)S(1)}, bf16[128,768]{1,0:T(8,128)(2,1)S(1)}, u32[]{:S(2)}, u32[]{:S(2)}) collective-permute-start(bf16[128,768]{1,0:T(8,128)(2,1)S(1)} %get-tuple-element.161), channel_id=1, source_target_pairs={{0,1},{1,0},{2,3},{3,2},{4,5},{5,4},{6,7},{7,6},{8,9},{9,8},{10,11... | collective-permute-start | bytes 589832 | tf_op jit(solution)/shard_map/ppermute | solution.py:416
  44.7 4.7 %collective-permute-start.13 = (bf16[128,768]{1,0:T(8,128)(2,1)S(1)}, bf16[128,768]{1,0:T(8,128)(2,1)S(1)}, u32[]{:S(2)}, u32[]{:S(2)}) collective-permute-start(bf16[128,768]{1,0:T(8,128)(2,1)S(1)} %get-tuple-element.149), channel_id=1, source_target_pairs={{0,1},{1,0},{2,3},{3,2},{4,5},{5,4},{6,7},{7,6},{8,9},{9,8},{10,11... | collective-permute-start | bytes 589832 | tf_op jit(solution)/shard_map/ppermute | solution.py:416
  49.1 6.0 %collective-permute-start.20 = (bf16[128,384]{1,0:T(8,128)(2,1)S(1)}, bf16[128,384]{1,0:T(8,128)(2,1)S(1)}, u32[]{:S(2)}, u32[]{:S(2)}) collective-permute-start(bf16[128,384]{1,0:T(8,128)(2,1)S(1)} %get-tuple-element.173), channel_id=1, source_target_pairs={{0,1},{1,0},{2,3},{3,2},{4,5},{5,4},{6,7},{7,6},{8,9},{9,8},{10,11... | collective-permute-start | bytes 294920 | tf_op jit(solution)/shard_map/ppermute | solution.py:416
  55.2 1.7 %collective-permute-start.22 = (bf16[128,1536]{1,0:T(8,128)(2,1)S(1)}, bf16[128,1536]{1,0:T(8,128)(2,1)S(1)}, u32[]{:S(2)}, u32[]{:S(2)}) collective-permute-start(bf16[128,1536]{1,0:T(8,128)(2,1)S(1)} %collective-permute-done.19.refs_0_), channel_id=1, source_target_pairs={{0,1},{1,0},{2,3},{3,2},{4,5},{5,4},{6,7},{7,6},{8,9},{9,8},{10,11... | collective-permute-start | bytes 1179656 | tf_op jit(solution)/shard_map/ppermute | solution.py:416
  58.3 1.4 %collective-permute-start.23 = (bf16[128,384]{1,0:T(8,128)(2,1)S(1)}, bf16[128,384]{1,0:T(8,128)(2,1)S(1)}, u32[]{:S(2)}, u32[]{:S(2)}) collective-permute-start(bf16[128,384]{1,0:T(8,128)(2,1)S(1)} %get-tuple-element.183), channel_id=1, source_target_pairs={{0,1},{1,0},{2,3},{3,2},{4,5},{5,4},{6,7},{7,6},{8,9},{9,8},{10,11... | collective-permute-start | bytes 294920 | tf_op jit(solution)/shard_map/ppermute | solution.py:416
  59.7 10.8 %collective-permute-start.24 = (bf16[128,384]{1,0:T(8,128)(2,1)S(1)}, bf16[128,384]{1,0:T(8,128)(2,1)S(1)}, u32[]{:S(2)}, u32[]{:S(2)}) collective-permute-start(bf16[128,384]{1,0:T(8,128)(2,1)S(1)} %get-tuple-element.184), channel_id=1, source_target_pairs={{0,16},{1,21},{2,18},{3,23},{4,20},{5,17},{6,22},{7,19},{8,24},{9,... | collective-permute-start | bytes 294920 | tf_op jit(solution)/shard_map/ppermute | solution.py:465
  62.5 8.3 %collective-permute-start.25 = (bf16[128,384]{1,0:T(8,128)(2,1)S(1)}, bf16[128,384]{1,0:T(8,128)(2,1)S(1)}, u32[]{:S(2)}, u32[]{:S(2)}) collective-permute-start(bf16[128,384]{1,0:T(8,128)(2,1)S(1)} %get-tuple-element.185), channel_id=1, source_target_pairs={{0,28},{1,13},{2,30},{3,15},{4,24},{5,9},{6,26},{7,11},{8,20},{9,5... | collective-permute-start | bytes 294920 | tf_op jit(solution)/shard_map/ppermute | solution.py:465
  64.3 7.0 %collective-permute-start.26 = (bf16[128,384]{1,0:T(8,128)(2,1)S(1)}, bf16[128,384]{1,0:T(8,128)(2,1)S(1)}, u32[]{:S(2)}, u32[]{:S(2)}) collective-permute-start(bf16[128,384]{1,0:T(8,128)(2,1)S(1)} %get-tuple-element.186), channel_id=1, source_target_pairs={{0,8},{1,25},{2,10},{3,27},{4,12},{5,29},{6,14},{7,31},{8,0},{9,17... | collective-permute-start | bytes 294920 | tf_op jit(solution)/shard_map/ppermute | solution.py:465
  64.3 7.0 %collective-permute-start.27 = (bf16[128,384]{1,0:T(8,128)(2,1)S(1)}, bf16[128,384]{1,0:T(8,128)(2,1)S(1)}, u32[]{:S(2)}, u32[]{:S(2)}) collective-permute-start(bf16[128,384]{1,0:T(8,128)(2,1)S(1)} %get-tuple-element.187), channel_id=1, source_target_pairs={{0,0},{1,5},{2,2},{3,7},{4,4},{5,1},{6,6},{7,3},{8,8},{9,13},{10,1... | collective-permute-start | bytes 294920 | tf_op jit(solution)/shard_map/ppermute | solution.py:465
  71.3 1.5 %collective-permute-start.28 = (bf16[256,384]{1,0:T(8,128)(2,1)S(1)}, bf16[256,384]{1,0:T(8,128)(2,1)S(1)}, u32[]{:S(2)}, u32[]{:S(2)}) collective-permute-start(bf16[256,384]{1,0:T(8,128)(2,1)S(1)} %shard_map.118), channel_id=1, source_target_pairs={{0,1},{1,0},{2,3},{3,2},{4,5},{5,4},{6,7},{7,6},{8,9},{9,8},{10,11... | collective-permute-start | bytes 589832 | tf_op jit(solution)/shard_map/ppermute | solution.py:416

commit v9 on v8

--- a/solution.py
+++ b/solution.py
@@ -560,20 +560,23 @@
     near0 = jnp.concatenate(pieces, axis=0)
     blocks1, pieces = update(rows1, base1, after(arrived1, near0))
 
-    def last_exchange(temporal_qkv, *pieces):
-        return (*send_pieces(pieces), hold_weights(temporal_qkv))
-
-    def no_exchange(temporal_qkv, *pieces):
-        return (*pieces, jnp.zeros((features, 3 * width), bf16))
-
-    *pieces, weights = lax.cond(once > 0, last_exchange, no_exchange, temporal_qkv, *pieces)
+    def last_exchange(temporal_qkv, near, *pieces):
+        far = swap(near, "mlp", n_mlp, 2)
+        return (*send_pieces(pieces), far, hold_weights(temporal_qkv))
+
+    def no_exchange(temporal_qkv, near, *pieces):
+        return (*pieces, near, jnp.zeros((features, 3 * width), bf16))
+
+    *pieces, far0, weights = lax.cond(
+        once > 0, last_exchange, no_exchange, temporal_qkv, near0, *pieces
+    )
     nears = [near0, jnp.concatenate(pieces, axis=0)]
     blocks = blocks0 + blocks1
 
     own_mixed, other_mixed = [], []
     for (first, rows), near in zip(chunks, nears):
         half = rows // 2
-        far = swap(near, "mlp", n_mlp, 2)
+        far = swap(near, "mlp", n_mlp, 2) if own_mixed else far0
         other_near = swap(near, "mlp", n_mlp, 1)
         if not own_mixed:
             far = after(far, *nears)

time: 73.8 us -> 73.6 us (level)
  waiting for transfers between devices: 25 us -> 23.7 us
  starting transfers between devices: 25.1 us -> 25.9 us
    pallas_call x1, Pallas kernels: 1.9 us -> 2.89 us  [split_on_device(): call(half_kernel, shape(half, 3 * width), inputs=7, scratch=(pltpu.VMEM((...]
    ppermute x17, waiting for transfers between devices: 10.1 us -> 9.18 us  [swap(): return lax.ppermute(value, axis, [(i, i ^ k) for i in range(size)])]
    pallas_call x1, Pallas kernels: 0.81 us -> 0.07 us  [rest(): sent = call(add_kernel, shape(half1, both), inputs=2)(far_term, message)]
  transfers between devices with their start and end apart: 29 -> 29, of which waited for: 19 -> 18; matrix products, arithmetic and copies ran while one was open for 0% -> 0% of each run, Pallas kernels for 24% -> 24%
where the time goes in v9:
time: 73.6 us; the launch traced here: 73.4 us
  starting transfers between devices  25.9 us (35%)
  waiting for transfers between devices  23.7 us (32%)
  Pallas kernels  22.6 us (31%)
  between operations  0.87 us (1%)
    ppermute x12, starting transfers between devices, send_pieces(): lax.ppermute(piece, ('seq', 'mlp'), piece_pairs(n_seq, n_mlp, i))  16.9 us
    ppermute x12, waiting for transfers between devices, send_pieces(): lax.ppermute(piece, ('seq', 'mlp'), piece_pairs(n_seq, n_mlp, i))  14.5 us
    ppermute x17, waiting for transfers between devices, swap(): return lax.ppermute(value, axis, [(i, i ^ k) for i in range(size)])  9.18 us
    ppermute x17, starting transfers between devices, swap(): return lax.ppermute(value, axis, [(i, i ^ k) for i in range(size)])  8.97 us
    pallas_call x1, Pallas kernels, rest(): call(functools.partial(rest_kernel, firsts=(first0, first1)), [shape(half...  3.81 us
    pallas_call x1, Pallas kernels, hold_weights(): pl.pallas_call(hold_kernel, out_shape=pltpu.VMEM((features, parts * width...  3.12 us
    pallas_call x1, Pallas kernels, split_on_device(): call(half_kernel, shape(half, 3 * width), inputs=7, scratch=(pltpu.VMEM((...  2.89 us
    pallas_call x1, Pallas kernels, split_on_device(): call(functools.partial(first_spatial_kernel, first=first0), [shape(half0,...  2.59 us
  transfers between devices with their start and end apart: 29, of which 18 were waited for; matrix products, arithmetic and copies ran while one was open for 0% of the time, Pallas kernels for 24%

profile of v9, /device:TPU:0, one launch (start us, length us, event | category | flops | bytes accessed | tf_op | source)
XLA Modules:
  0.0 73.4 jit_solution(6200506211466438488)
XLA Ops:
  0.6 2.6 %shard_map.106 = (bf16[128,384]{1,0:T(8,128)(2,1)S(1)}, bf16[128,1536]{1,0:T(8,128)(2,1)S(1)}, bf16[384,1536]{1,0:T(8,128)(2,1)S(1)}, f32[1,1536]{1,0:T(1,128)S(1)}, bf16[3,512,384]{2,1,0:T(8,128)(2,1)S(1)}) custom-call(bf16[3,512,384]{2,1,0:T(8,128)(2,1)} %bitcast.19, bf16[384,3072]{1,0:T(8,128)(2,1)} %w_far.1, f32[1,3072]{1,0:T(1,128)} %bitcast.24), custom_call_target="tpu_custom_call" | custom-call | tf_op jit(solution)/shard_map/pallas_call | solution.py:479
  3.2 0.5 collective-permute-start.12
  3.7 1.2 %shard_map.107 = (bf16[128,384]{1,0:T(8,128)(2,1)S(1)}, f32[128,1536]{1,0:T(8,128)S(1)}) custom-call(bf16[384,1536]{1,0:T(8,128)(2,1)S(1)} %get-tuple-element.144.w_ref, f32[1,1536]{1,0:T(1,128)S(1)} %get-tuple-element.145.gate_ref, bf16[3,512,384]{2,1,0:T(8,128)(2,1)S(1)} %get-tuple-element.146.qkv_ref), custom_call_target="tpu_custom_call" | custom-call | tf_op jit(solution)/shard_map/pallas_call | solution.py:493
  5.0 0.1 collective-permute-done.12.b_ref
  5.1 0.1 shard_map.108
  5.2 2.9 %collective-permute-start.13 = (bf16[128,1536]{1,0:T(8,128)(2,1)S(1)}, bf16[128,1536]{1,0:T(8,128)(2,1)S(1)}, u32[]{:S(2)}, u32[]{:S(2)}) collective-permute-start(bf16[128,1536]{1,0:T(8,128)(2,1)S(1)} %shard_map.108), channel_id=1, source_target_pairs={{0,2},{1,3},{2,0},{3,1},{4,6},{5,7},{6,4},{7,5},{8,10},{9,11},{10,... | collective-permute-start | bytes 1179656 | tf_op jit(solution)/shard_map/ppermute | solution.py:416
  8.1 6.8 %conditional.2 = (bf16[128,1536]{1,0:T(8,128)(2,1)S(1)}, f32[128,1536]{1,0:T(8,128)S(1)}, f32[128,1536]{1,0:T(8,128)S(1)}) conditional(s32[]{:T(128)} %convert_element_type.4, () %tuple.33, (bf16[1,512,768]{2,1,0:T(8,128)(2,1)}, bf16[128,384]{1,0:T(8,128)(2,1)S(1)}, bf16[128,384]{1,0:T(8,128)(2,1)S(1)}, bf16[3,512,384]{2,1,0:T(8,128)(2,1)}, ...), branch_computations={%region_0.0_spmd, %region_1.0_spmd} | conditional | bytes 4718736 | solution.py:535
  8.1 3.8 %branch_1_fun.5 = (bf16[128,1536]{1,0:T(8,128)(2,1)S(1)}, f32[128,1536]{1,0:T(8,128)S(1)}, f32[128,1536]{1,0:T(8,128)S(1)}, bf16[128,1536]{1,0:T(8,128)(2,1)S(1)...) custom-call(bf16[128,384]{1,0:T(8,128)(2,1)S(1)} %get-tuple-element.59.own0_ref, ...), custom_call_target="tpu_custom_call" | custom-call | tf_op jit(solution)/shard_map/cond/branch_1_fun/pallas_call | solution.py:502
  11.9 0.1 collective-permute-start
  12.0 0.5 collective-permute-start.1
  12.5 0.1 collective-permute-start.2
  12.6 1.1 %collective-permute-done.b_ref = bf16[128,1536]{1,0:T(8,128)(2,1)S(1)} collective-permute-done((bf16[128,1536]{1,0:T(8,128)(2,1)S(1)}, bf16[128,1536]{1,0:T(8,128)(2,1)S(1)}, u32[]{:S(2)}, u32[]{:S(2)}) %collective-permute-start) | collective-permute-done | bytes 393248 | tf_op jit(solution)/shard_map/cond/branch_1_fun/ppermute | solution.py:416
  13.7 0.1 branch_1_fun.6
  13.8 0.5 collective-permute-done.1.b_ref
  14.3 0.1 branch_1_fun.7
  14.3 0.5 collective-permute-done.2.b_ref
  14.8 0.1 branch_1_fun.8
  14.9 0.1 collective-permute-start.15
  15.0 2.6 %collective-permute-done.13.arrived_ref = bf16[128,1536]{1,0:T(8,128)(2,1)S(1)} collective-permute-done((bf16[128,1536]{1,0:T(8,128)(2,1)S(1)}, bf16[128,1536]{1,0:T(8,128)(2,1)S(1)}, u32[]{:S(2)}, u32[]{:S(2)}) %collective-permute-start.13) | collective-permute-done | bytes 393248 | tf_op jit(solution)/shard_map/ppermute | solution.py:416
  17.6 0.1 shard_map.109
  17.7 11.8 %while.16 = (s32[]{:T(128)}, bf16[32,1536]{1,0:T(8,128)(2,1)S(1)}, bf16[32,1536]{1,0:T(8,128)(2,1)S(1)}, bf16[32,1536]{1,0:T(8,128)(2,1)S(1)}, bf16[32,1536]{1,0:T(8,128)(2,1)S(1)}, /*index=5*/s32[]{:T(128)}, s32[]{:T(128)}) while((s32[]{:T(128)}, bf16[32,1536]{1,0:T(8,128)(2,1)S(1)}, bf16[32,1536]{1,0:T(8,128)(2,1)S(1)}, ...), condition=%wide.region_3.0_spmd, body=%wide.region_2.0_spmd.sunk | while | flops 2 | bytes 2359533 | solution.py:559
  17.7 2.9 %collective-permute-start.8 = (bf16[32,1536]{1,0:T(8,128)(2,1)S(1)}, bf16[32,1536]{1,0:T(8,128)(2,1)S(1)}, u32[]{:S(2)}, u32[]{:S(2)}) collective-permute-start(bf16[32,1536]{1,0:T(8,128)(2,1)S(1)} %get-tuple-element.264), channel_id=1, source_target_pairs={{0,16},{1,21},{2,18},{3,23},{4,20},{5,17},{6,22},{7,19},{8,24},{9,... | collective-permute-start | bytes 294920 | tf_op jit(solution)/shard_map/while/body/ppermute | solution.py:465
  20.6 2.3 %collective-permute-start.9 = (bf16[32,1536]{1,0:T(8,128)(2,1)S(1)}, bf16[32,1536]{1,0:T(8,128)(2,1)S(1)}, u32[]{:S(2)}, u32[]{:S(2)}) collective-permute-start(bf16[32,1536]{1,0:T(8,128)(2,1)S(1)} %get-tuple-element.265), channel_id=1, source_target_pairs={{0,28},{1,13},{2,30},{3,15},{4,24},{5,9},{6,26},{7,11},{8,20},{9,5... | collective-permute-start | bytes 294920 | tf_op jit(solution)/shard_map/while/body/ppermute | solution.py:465
  22.9 0.7 collective-permute-start.11
  23.5 5.0 %collective-permute-done.8 = bf16[32,1536]{1,0:T(8,128)(2,1)S(1)} collective-permute-done((bf16[32,1536]{1,0:T(8,128)(2,1)S(1)}, bf16[32,1536]{1,0:T(8,128)(2,1)S(1)}, u32[]{:S(2)}, u32[]{:S(2)}) %collective-permute-start.8) | collective-permute-done | bytes 98336 | tf_op jit(solution)/shard_map/while/body/ppermute | solution.py:465
  28.6 0.3 collective-permute-done.9
  28.8 0.7 collective-permute-done.10
  29.6 0.1 shard_map.110
  29.8 12.4 %conditional.3 = (bf16[32,1536]{1,0:T(8,128)(2,1)S(1)}, bf16[32,1536]{1,0:T(8,128)(2,1)S(1)}, bf16[32,1536]{1,0:T(8,128)(2,1)S(1)}, bf16[32,1536]{1,0:T(8,128)(2...) conditional(s32[]{:T(128)} %convert_element_type.4, (bf16[32,1536]{1,0:T(8,128)(2,1)S(1)}, ...), branch_computations={%region_4.0_spmd, %region_5.0_spmd} | conditional | bytes 7864370 | solution.py:570
  29.8 1.6 %collective-permute-start.7 = (bf16[128,1536]{1,0:T(8,128)(2,1)S(1)}, bf16[128,1536]{1,0:T(8,128)(2,1)}, u32[]{:S(2)}, u32[]{:S(2)}) collective-permute-start(bf16[128,1536]{1,0:T(8,128)(2,1)S(1)} %get-tuple-element.88), channel_id=1, source_target_pairs={{0,2},{1,3},{2,0},{3,1},{4,6},{5,7},{6,4},{7,5},{8,10},{9,11},{10,... | collective-permute-start | bytes 1179656 | tf_op jit(solution)/shard_map/cond/branch_1_fun/ppermute | solution.py:416
  31.4 3.2 %collective-permute-start.3 = (bf16[32,1536]{1,0:T(8,128)(2,1)S(1)}, bf16[32,1536]{1,0:T(8,128)(2,1)S(1)}, u32[]{:S(2)}, u32[]{:S(2)}) collective-permute-start(bf16[32,1536]{1,0:T(8,128)(2,1)S(1)} %get-tuple-element.84), channel_id=1, source_target_pairs={{0,16},{1,21},{2,18},{3,23},{4,20},{5,17},{6,22},{7,19},{8,24},{9,... | collective-permute-start | bytes 294920 | tf_op jit(solution)/shard_map/cond/branch_1_fun/ppermute | solution.py:465
  34.6 1.3 %collective-permute-start.4 = (bf16[32,1536]{1,0:T(8,128)(2,1)S(1)}, bf16[32,1536]{1,0:T(8,128)(2,1)S(1)}, u32[]{:S(2)}, u32[]{:S(2)}) collective-permute-start(bf16[32,1536]{1,0:T(8,128)(2,1)S(1)} %get-tuple-element.85), channel_id=1, source_target_pairs={{0,28},{1,13},{2,30},{3,15},{4,24},{5,9},{6,26},{7,11},{8,20},{9,5... | collective-permute-start | bytes 294920 | tf_op jit(solution)/shard_map/cond/branch_1_fun/ppermute | solution.py:465
  35.9 0.2 collective-permute-start.5
  36.1 0.8 %collective-permute-start.6 = (bf16[32,1536]{1,0:T(8,128)(2,1)S(1)}, bf16[32,1536]{1,0:T(8,128)(2,1)S(1)}, u32[]{:S(2)}, u32[]{:S(2)}) collective-permute-start(bf16[32,1536]{1,0:T(8,128)(2,1)S(1)} %get-tuple-element.87), channel_id=1, source_target_pairs={{0,0},{1,5},{2,2},{3,7},{4,4},{5,1},{6,6},{7,3},{8,8},{9,13},{10,1... | collective-permute-start | bytes 294920 | tf_op jit(solution)/shard_map/cond/branch_1_fun/ppermute | solution.py:465
  36.9 3.1 %branch_1_fun.9 = bf16[3072,1152]{1,0:T(8,128)(2,1)S(1)} custom-call(bf16[3,3072,384]{2,1,0:T(8,128)(2,1)} %bitcast.18), custom_call_target="tpu_custom_call" | custom-call | tf_op jit(solution)/shard_map/cond/branch_1_fun/pallas_call | solution.py:136
  40.1 0.3 collective-permute-done.3
  40.4 1.6 %collective-permute-done.4 = bf16[32,1536]{1,0:T(8,128)(2,1)S(1)} collective-permute-done((bf16[32,1536]{1,0:T(8,128)(2,1)S(1)}, bf16[32,1536]{1,0:T(8,128)(2,1)S(1)}, u32[]{:S(2)}, u32[]{:S(2)}) %collective-permute-start.4) | collective-permute-done | bytes 98336 | tf_op jit(solution)/shard_map/cond/branch_1_fun/ppermute | solution.py:465
  42.0 0.1 collective-permute-done.5
  42.2 0.1 collective-permute-start.17
  42.3 0.5 collective-permute-start.18
  42.9 0.1 collective-permute-start.21
  42.9 1.5 %collective-permute-start.19 = (bf16[128,1536]{1,0:T(8,128)(2,1)S(1)}, bf16[128,1536]{1,0:T(8,128)(2,1)S(1)}, u32[]{:S(2)}, u32[]{:S(2)}) collective-permute-start(bf16[128,1536]{1,0:T(8,128)(2,1)S(1)} %constant_dynamic-update-slice_fusion.4.own_ref), channel_id=1, source_target_pairs={{0,2},{1,3},{2,0},{3,1},{4,6},{5,7},{6,4},{7,5},{8,10},{9,11},{10,... | collective-permute-start | bytes 1179656 | tf_op jit(solution)/shard_map/ppermute | solution.py:416
  44.4 0.2 collective-permute-start.14
  44.6 0.3 collective-permute-start.16
  44.9 2.9 %shard_map.112.own_proj_ref = bf16[128,1152]{1,0:T(8,128)(2,1)S(1)} custom-call(bf16[128,1536]{1,0:T(8,128)(2,1)S(1)} %constant_dynamic-update-slice_fusion.near, bf16[128,1536]{1,0:T(8,128)(2,1)} %get-tuple-element.178.far, f32[1,3072]{1,0:T(1,128)S(1)} %bitcast.10, f32[1,3072]{1,0:T(1,128)S(1)} %bitcast.15, ...), custom_call_target="tpu_custom_call" | custom-call | tf_op jit(solution)/shard_map/pallas_call | solution.py:610
  47.8 2.2 %shard_map.113 = (bf16[128,384]{1,0:T(8,128)(2,1)S(1)}, bf16[128,384]{1,0:T(8,128)(2,1)S(1)}) custom-call(bf16[128,1152]{1,0:T(8,128)(2,1)S(1)} %shard_map.112.own_proj_ref, bf16[128,1536]{1,0:T(8,128)(2,1)S(1)} %collective-permute-done.17.near, bf16[128,1536]{1,0:T(8,128)(2,1)S(1)} %collective-permute-done.18.far, f32[1,3072]{1,0:T(1,128)S(1)} %bitcast.11, ...), custom_call_target="tpu_custom_call" | custom-call | tf_op jit(solution)/shard_map/pallas_call | solution.py:616
  50.1 0.2 collective-permute-start.20
  50.3 1.0 %shard_map.111 = bf16[512,768]{1,0:T(8,128)(2,1)} custom-call(bf16[128,768]{1,0:T(8,128)(2,1)S(1)} %get-tuple-element.155.refs_0_, bf16[128,768]{1,0:T(8,128)(2,1)S(1)} %collective-permute-done.14.refs_1_, bf16[128,768]{1,0:T(8,128)(2,1)S(1)} %get-tuple-element.167.refs_2_, bf16[128,768]{1,0:T(8,128)(2,1)S(1)} %collective-permute-done.16.refs_3_), custom_call_target="tpu_custom_call" | custom-call | tf_op jit(solution)/shard_map/pallas_call | solution.py:584
  51.3 2.2 %shard_map.114 = (f32[128,1152]{1,0:T(8,128)S(1)}, f32[128,1152]{1,0:T(8,128)S(1)}, f32[128,1]{1,0:T(8,128)S(1)}, f32[128,1]{1,0:T(8,128)S(1)}, f32[128,1]{1,0:T...) custom-call(bf16[128,1536]{1,0:T(8,128)(2,1)S(1)} %constant_dynamic-update-slice_fusion.4.own_ref, ...), custom_call_target="tpu_custom_call" | custom-call | tf_op jit(solution)/shard_map/pallas_call | solution.py:590
  53.5 0.9 %collective-permute-done.19.refs_0_ = bf16[128,1536]{1,0:T(8,128)(2,1)S(1)} collective-permute-done((bf16[128,1536]{1,0:T(8,128)(2,1)S(1)}, bf16[128,1536]{1,0:T(8,128)(2,1)S(1)}, u32[]{:S(2)}, u32[]{:S(2)}) %collective-permute-start.19) | collective-permute-done | bytes 393248 | tf_op jit(solution)/shard_map/ppermute | solution.py:416
  54.4 0.9 %shard_map.115.own_proj_ref = bf16[128,1152]{1,0:T(8,128)(2,1)S(1)} custom-call(bf16[128,1536]{1,0:T(8,128)(2,1)S(1)} %collective-permute-done.19.refs_0_, f32[128,1152]{1,0:T(8,128)S(1)} %get-tuple-element.184.refs_1_, f32[128,1]{1,0:T(8,128)S(1)} %get-tuple-element.185.refs_2_, f32[128,1]{1,0:T(8,128)S(1)} %get-tuple-element.186.refs_3_, ...), custom_call_target="tpu_custom_call" | custom-call | tf_op jit(solution)/shard_map/pallas_call | solution.py:599
  55.3 0.8 %collective-permute-done.22.refs_0_ = bf16[128,1536]{1,0:T(8,128)(2,1)S(1)} collective-permute-done((bf16[128,1536]{1,0:T(8,128)(2,1)S(1)}, bf16[128,1536]{1,0:T(8,128)(2,1)S(1)}, u32[]{:S(2)}, u32[]{:S(2)}) %collective-permute-start.22) | collective-permute-done | bytes 393248 | tf_op jit(solution)/shard_map/ppermute | solution.py:416
  56.1 1.4 %shard_map.116 = (bf16[128,384]{1,0:T(8,128)(2,1)S(1)}, bf16[128,384]{1,0:T(8,128)(2,1)S(1)}) custom-call(bf16[128,1152]{1,0:T(8,128)(2,1)S(1)} %shard_map.115.own_proj_ref, bf16[128,1536]{1,0:T(8,128)(2,1)S(1)} %collective-permute-done.22.refs_0_, f32[128,1152]{1,0:T(8,128)S(1)} %get-tuple-element.187.refs_1_, f32[128,1]{1,0:T(8,128)S(1)} %get-tuple-element.188.refs_2_, ...), custom_call_target="tpu_custom_call" | custom-call | tf_op jit(solution)/shard_map/pallas_call | solution.py:602
  57.5 0.2 collective-permute-start.23
  57.7 1.2 %collective-permute-done.23.refs_3_ = bf16[128,384]{1,0:T(8,128)(2,1)S(1)} collective-permute-done((bf16[128,384]{1,0:T(8,128)(2,1)S(1)}, bf16[128,384]{1,0:T(8,128)(2,1)S(1)}, u32[]{:S(2)}, u32[]{:S(2)}) %collective-permute-start.23) | collective-permute-done | bytes 98336 | tf_op jit(solution)/shard_map/ppermute | solution.py:416
  58.9 3.5 %collective-permute-start.24 = (bf16[128,384]{1,0:T(8,128)(2,1)S(1)}, bf16[128,384]{1,0:T(8,128)(2,1)S(1)}, u32[]{:S(2)}, u32[]{:S(2)}) collective-permute-start(bf16[128,384]{1,0:T(8,128)(2,1)S(1)} %get-tuple-element.192), channel_id=1, source_target_pairs={{0,16},{1,21},{2,18},{3,23},{4,20},{5,17},{6,22},{7,19},{8,24},{9,... | collective-permute-start | bytes 294920 | tf_op jit(solution)/shard_map/ppermute | solution.py:465
  62.4 1.4 %collective-permute-start.25 = (bf16[128,384]{1,0:T(8,128)(2,1)S(1)}, bf16[128,384]{1,0:T(8,128)(2,1)S(1)}, u32[]{:S(2)}, u32[]{:S(2)}) collective-permute-start(bf16[128,384]{1,0:T(8,128)(2,1)S(1)} %get-tuple-element.193), channel_id=1, source_target_pairs={{0,28},{1,13},{2,30},{3,15},{4,24},{5,9},{6,26},{7,11},{8,20},{9,5... | collective-permute-start | bytes 294920 | tf_op jit(solution)/shard_map/ppermute | solution.py:465
  63.9 0.7 collective-permute-start.27
  64.5 5.8 %collective-permute-done.24.refs_0_ = bf16[128,384]{1,0:T(8,128)(2,1)S(1)} collective-permute-done((bf16[128,384]{1,0:T(8,128)(2,1)S(1)}, bf16[128,384]{1,0:T(8,128)(2,1)S(1)}, u32[]{:S(2)}, u32[]{:S(2)}) %collective-permute-start.24) | collective-permute-done | bytes 98336 | tf_op jit(solution)/shard_map/ppermute | solution.py:465
  70.3 0.3 collective-permute-done.25.refs_1_
  70.6 0.5 collective-permute-done.26.refs_2_
  71.1 0.1 collective-permute-start.28
  71.2 1.4 %collective-permute-done.28.refs_4_ = bf16[256,384]{1,0:T(8,128)(2,1)S(1)} collective-permute-done((bf16[256,384]{1,0:T(8,128)(2,1)S(1)}, bf16[256,384]{1,0:T(8,128)(2,1)S(1)}, u32[]{:S(2)}, u32[]{:S(2)}) %collective-permute-start.28) | collective-permute-done | bytes 196640 | tf_op jit(solution)/shard_map/ppermute | solution.py:416
  72.6 0.8 %shard_map.119 = bf16[512,384]{1,0:T(8,128)(2,1)} custom-call(bf16[128,384]{1,0:T(8,128)(2,1)S(1)} %collective-permute-done.24.refs_0_, bf16[128,384]{1,0:T(8,128)(2,1)S(1)} %collective-permute-done.25.refs_1_, bf16[128,384]{1,0:T(8,128)(2,1)S(1)} %collective-permute-done.26.refs_2_, bf16[128,384]{1,0:T(8,128)(2,1)S(1)} %collective-permute-done.27.refs_3_, ...), custom_call_target="tpu_custom_call" | custom-call | tf_op jit(solution)/shard_map/pallas_call | solution.py:633
  (40 shorter events, 0.2 us)
Async XLA Ops:
  3.2 1.9 %collective-permute-start.12 = (bf16[128,1536]{1,0:T(8,128)(2,1)S(1)}, bf16[128,1536]{1,0:T(8,128)(2,1)S(1)}, u32[]{:S(2)}, u32[]{:S(2)}) collective-permute-start(bf16[128,1536]{1,0:T(8,128)(2,1)S(1)} %get-tuple-element.149), channel_id=1, source_target_pairs={{0,1},{1,0},{2,3},{3,2},{4,5},{5,4},{6,7},{7,6},{8,9},{9,8},{10,11... | collective-permute-start | bytes 1179656 | tf_op jit(solution)/shard_map/ppermute | solution.py:416
  5.2 12.4 %collective-permute-start.13 = (bf16[128,1536]{1,0:T(8,128)(2,1)S(1)}, bf16[128,1536]{1,0:T(8,128)(2,1)S(1)}, u32[]{:S(2)}, u32[]{:S(2)}) collective-permute-start(bf16[128,1536]{1,0:T(8,128)(2,1)S(1)} %shard_map.108), channel_id=1, source_target_pairs={{0,2},{1,3},{2,0},{3,1},{4,6},{5,7},{6,4},{7,5},{8,10},{9,11},{10,... | collective-permute-start | bytes 1179656 | tf_op jit(solution)/shard_map/ppermute | solution.py:416
  11.9 1.8 %collective-permute-start = (bf16[128,1536]{1,0:T(8,128)(2,1)S(1)}, bf16[128,1536]{1,0:T(8,128)(2,1)S(1)}, u32[]{:S(2)}, u32[]{:S(2)}) collective-permute-start(bf16[128,1536]{1,0:T(8,128)(2,1)S(1)} %get-tuple-element.66), channel_id=1, source_target_pairs={{0,1},{1,0},{2,3},{3,2},{4,5},{5,4},{6,7},{7,6},{8,9},{9,8},{10,11... | collective-permute-start | bytes 1179656 | tf_op jit(solution)/shard_map/cond/branch_1_fun/ppermute | solution.py:416
  12.0 2.3 %collective-permute-start.1 = (bf16[128,1536]{1,0:T(8,128)(2,1)S(1)}, bf16[128,1536]{1,0:T(8,128)(2,1)S(1)}, u32[]{:S(2)}, u32[]{:S(2)}) collective-permute-start(bf16[128,1536]{1,0:T(8,128)(2,1)S(1)} %get-tuple-element.68), channel_id=1, source_target_pairs={{0,1},{1,0},{2,3},{3,2},{4,5},{5,4},{6,7},{7,6},{8,9},{9,8},{10,11... | collective-permute-start | bytes 1179656 | tf_op jit(solution)/shard_map/cond/branch_1_fun/ppermute | solution.py:416
  12.5 2.3 %collective-permute-start.2 = (bf16[128,1536]{1,0:T(8,128)(2,1)S(1)}, bf16[128,1536]{1,0:T(8,128)(2,1)S(1)}, u32[]{:S(2)}, u32[]{:S(2)}) collective-permute-start(bf16[128,1536]{1,0:T(8,128)(2,1)S(1)} %get-tuple-element.70), channel_id=1, source_target_pairs={{0,1},{1,0},{2,3},{3,2},{4,5},{5,4},{6,7},{7,6},{8,9},{9,8},{10,11... | collective-permute-start | bytes 1179656 | tf_op jit(solution)/shard_map/cond/branch_1_fun/ppermute | solution.py:416
  14.9 14.7 %collective-permute-start.15 = (bf16[128,1536]{1,0:T(8,128)(2,1)S(1)}, bf16[128,1536]{1,0:T(8,128)(2,1)S(1)}, u32[]{:S(2)}, u32[]{:S(2)}) collective-permute-start(bf16[128,1536]{1,0:T(8,128)(2,1)S(1)} %get-tuple-element.153), channel_id=1, source_target_pairs={{0,2},{1,3},{2,0},{3,1},{4,6},{5,7},{6,4},{7,5},{8,10},{9,11},{10,... | collective-permute-start | bytes 1179656 | tf_op jit(solution)/shard_map/ppermute | solution.py:416
  17.7 10.8 %collective-permute-start.8 = (bf16[32,1536]{1,0:T(8,128)(2,1)S(1)}, bf16[32,1536]{1,0:T(8,128)(2,1)S(1)}, u32[]{:S(2)}, u32[]{:S(2)}) collective-permute-start(bf16[32,1536]{1,0:T(8,128)(2,1)S(1)} %get-tuple-element.264), channel_id=1, source_target_pairs={{0,16},{1,21},{2,18},{3,23},{4,20},{5,17},{6,22},{7,19},{8,24},{9,... | collective-permute-start | bytes 294920 | tf_op jit(solution)/shard_map/while/body/ppermute | solution.py:465
  20.6 8.2 %collective-permute-start.9 = (bf16[32,1536]{1,0:T(8,128)(2,1)S(1)}, bf16[32,1536]{1,0:T(8,128)(2,1)S(1)}, u32[]{:S(2)}, u32[]{:S(2)}) collective-permute-start(bf16[32,1536]{1,0:T(8,128)(2,1)S(1)} %get-tuple-element.265), channel_id=1, source_target_pairs={{0,28},{1,13},{2,30},{3,15},{4,24},{5,9},{6,26},{7,11},{8,20},{9,5... | collective-permute-start | bytes 294920 | tf_op jit(solution)/shard_map/while/body/ppermute | solution.py:465
  22.9 6.6 %collective-permute-start.10 = (bf16[32,1536]{1,0:T(8,128)(2,1)S(1)}, bf16[32,1536]{1,0:T(8,128)(2,1)S(1)}, u32[]{:S(2)}, u32[]{:S(2)}) collective-permute-start(bf16[32,1536]{1,0:T(8,128)(2,1)S(1)} %get-tuple-element.266), channel_id=1, source_target_pairs={{0,8},{1,25},{2,10},{3,27},{4,12},{5,29},{6,14},{7,31},{8,0},{9,17... | collective-permute-start | bytes 294920 | tf_op jit(solution)/shard_map/while/body/ppermute | solution.py:465
  22.9 6.6 %collective-permute-start.11 = (bf16[32,1536]{1,0:T(8,128)(2,1)S(1)}, bf16[32,1536]{1,0:T(8,128)(2,1)S(1)}, u32[]{:S(2)}, u32[]{:S(2)}) collective-permute-start(bf16[32,1536]{1,0:T(8,128)(2,1)S(1)} %get-tuple-element.267), channel_id=1, source_target_pairs={{0,0},{1,5},{2,2},{3,7},{4,4},{5,1},{6,6},{7,3},{8,8},{9,13},{10,1... | collective-permute-start | bytes 294920 | tf_op jit(solution)/shard_map/while/body/ppermute | solution.py:465
  29.7 15.2 %copy-start = (f32[3072]{0:T(1024)S(1)}, f32[3072]{0:T(1024)}, u32[]{:S(2)}) copy-start(f32[3072]{0:T(1024)} %param.20) | copy-start | bytes 36868
  29.8 15.2 %copy-start.1 = (f32[3072]{0:T(1024)S(1)}, f32[3072]{0:T(1024)}, u32[]{:S(2)}) copy-start(f32[3072]{0:T(1024)} %param.19) | copy-start | bytes 36868
  29.8 15.2 %copy-start.2 = (f32[8,128]{1,0:T(8,128)S(1)}, f32[8,128]{1,0:T(8,128)}, u32[]{:S(2)}) copy-start(f32[8,128]{1,0:T(8,128)} %constant.22.clone.cos_ref.refs_7_) | copy-start | bytes 12292
  29.8 15.2 %copy-start.3 = (f32[8,128]{1,0:T(8,128)S(1)}, f32[8,128]{1,0:T(8,128)}, u32[]{:S(2)}) copy-start(f32[8,128]{1,0:T(8,128)} %constant.23.clone.sin_ref.refs_8_) | copy-start | bytes 12292
  29.8 12.4 %collective-permute-start.7 = (bf16[128,1536]{1,0:T(8,128)(2,1)S(1)}, bf16[128,1536]{1,0:T(8,128)(2,1)}, u32[]{:S(2)}, u32[]{:S(2)}) collective-permute-start(bf16[128,1536]{1,0:T(8,128)(2,1)S(1)} %get-tuple-element.88), channel_id=1, source_target_pairs={{0,2},{1,3},{2,0},{3,1},{4,6},{5,7},{6,4},{7,5},{8,10},{9,11},{10,... | collective-permute-start | bytes 1179656 | tf_op jit(solution)/shard_map/cond/branch_1_fun/ppermute | solution.py:416
  31.4 9.0 %collective-permute-start.3 = (bf16[32,1536]{1,0:T(8,128)(2,1)S(1)}, bf16[32,1536]{1,0:T(8,128)(2,1)S(1)}, u32[]{:S(2)}, u32[]{:S(2)}) collective-permute-start(bf16[32,1536]{1,0:T(8,128)(2,1)S(1)} %get-tuple-element.84), channel_id=1, source_target_pairs={{0,16},{1,21},{2,18},{3,23},{4,20},{5,17},{6,22},{7,19},{8,24},{9,... | collective-permute-start | bytes 294920 | tf_op jit(solution)/shard_map/cond/branch_1_fun/ppermute | solution.py:465
  34.6 7.4 %collective-permute-start.4 = (bf16[32,1536]{1,0:T(8,128)(2,1)S(1)}, bf16[32,1536]{1,0:T(8,128)(2,1)S(1)}, u32[]{:S(2)}, u32[]{:S(2)}) collective-permute-start(bf16[32,1536]{1,0:T(8,128)(2,1)S(1)} %get-tuple-element.85), channel_id=1, source_target_pairs={{0,28},{1,13},{2,30},{3,15},{4,24},{5,9},{6,26},{7,11},{8,20},{9,5... | collective-permute-start | bytes 294920 | tf_op jit(solution)/shard_map/cond/branch_1_fun/ppermute | solution.py:465
  35.9 6.3 %collective-permute-start.5 = (bf16[32,1536]{1,0:T(8,128)(2,1)S(1)}, bf16[32,1536]{1,0:T(8,128)(2,1)S(1)}, u32[]{:S(2)}, u32[]{:S(2)}) collective-permute-start(bf16[32,1536]{1,0:T(8,128)(2,1)S(1)} %get-tuple-element.86), channel_id=1, source_target_pairs={{0,8},{1,25},{2,10},{3,27},{4,12},{5,29},{6,14},{7,31},{8,0},{9,17... | collective-permute-start | bytes 294920 | tf_op jit(solution)/shard_map/cond/branch_1_fun/ppermute | solution.py:465
  36.1 6.0 %collective-permute-start.6 = (bf16[32,1536]{1,0:T(8,128)(2,1)S(1)}, bf16[32,1536]{1,0:T(8,128)(2,1)S(1)}, u32[]{:S(2)}, u32[]{:S(2)}) collective-permute-start(bf16[32,1536]{1,0:T(8,128)(2,1)S(1)} %get-tuple-element.87), channel_id=1, source_target_pairs={{0,0},{1,5},{2,2},{3,7},{4,4},{5,1},{6,6},{7,3},{8,8},{9,13},{10,1... | collective-permute-start | bytes 294920 | tf_op jit(solution)/shard_map/cond/branch_1_fun/ppermute | solution.py:465
  42.2 2.4 %collective-permute-start.17 = (bf16[128,1536]{1,0:T(8,128)(2,1)S(1)}, bf16[128,1536]{1,0:T(8,128)(2,1)S(1)}, u32[]{:S(2)}, u32[]{:S(2)}) collective-permute-start(bf16[128,1536]{1,0:T(8,128)(2,1)S(1)} %constant_dynamic-update-slice_fusion.near), channel_id=1, source_target_pairs={{0,1},{1,0},{2,3},{3,2},{4,5},{5,4},{6,7},{7,6},{8,9},{9,8},{10,11... | collective-permute-start | bytes 1179656 | tf_op jit(solution)/shard_map/ppermute | solution.py:416
  42.3 5.5 %collective-permute-start.18 = (bf16[128,1536]{1,0:T(8,128)(2,1)}, bf16[128,1536]{1,0:T(8,128)(2,1)S(1)}, u32[]{:S(2)}, u32[]{:S(2)}) collective-permute-start(bf16[128,1536]{1,0:T(8,128)(2,1)} %get-tuple-element.178.far), channel_id=1, source_target_pairs={{0,1},{1,0},{2,3},{3,2},{4,5},{5,4},{6,7},{7,6},{8,9},{9,8},{10,11... | collective-permute-start | bytes 1179656 | tf_op jit(solution)/shard_map/ppermute | solution.py:416
  42.9 8.4 %collective-permute-start.21 = (bf16[128,1536]{1,0:T(8,128)(2,1)S(1)}, bf16[128,1536]{1,0:T(8,128)(2,1)S(1)}, u32[]{:S(2)}, u32[]{:S(2)}) collective-permute-start(bf16[128,1536]{1,0:T(8,128)(2,1)S(1)} %constant_dynamic-update-slice_fusion.4.own_ref), channel_id=1, source_target_pairs={{0,1},{1,0},{2,3},{3,2},{4,5},{5,4},{6,7},{7,6},{8,9},{9,8},{10,11... | collective-permute-start | bytes 1179656 | tf_op jit(solution)/shard_map/ppermute | solution.py:416
  42.9 11.5 %collective-permute-start.19 = (bf16[128,1536]{1,0:T(8,128)(2,1)S(1)}, bf16[128,1536]{1,0:T(8,128)(2,1)S(1)}, u32[]{:S(2)}, u32[]{:S(2)}) collective-permute-start(bf16[128,1536]{1,0:T(8,128)(2,1)S(1)} %constant_dynamic-update-slice_fusion.4.own_ref), channel_id=1, source_target_pairs={{0,2},{1,3},{2,0},{3,1},{4,6},{5,7},{6,4},{7,5},{8,10},{9,11},{10,... | collective-permute-start | bytes 1179656 | tf_op jit(solution)/shard_map/ppermute | solution.py:416
  44.4 5.9 %collective-permute-start.14 = (bf16[128,768]{1,0:T(8,128)(2,1)S(1)}, bf16[128,768]{1,0:T(8,128)(2,1)S(1)}, u32[]{:S(2)}, u32[]{:S(2)}) collective-permute-start(bf16[128,768]{1,0:T(8,128)(2,1)S(1)} %get-tuple-element.156), channel_id=1, source_target_pairs={{0,1},{1,0},{2,3},{3,2},{4,5},{5,4},{6,7},{7,6},{8,9},{9,8},{10,11... | collective-permute-start | bytes 589832 | tf_op jit(solution)/shard_map/ppermute | solution.py:416
  44.6 5.7 %collective-permute-start.16 = (bf16[128,768]{1,0:T(8,128)(2,1)S(1)}, bf16[128,768]{1,0:T(8,128)(2,1)S(1)}, u32[]{:S(2)}, u32[]{:S(2)}) collective-permute-start(bf16[128,768]{1,0:T(8,128)(2,1)S(1)} %get-tuple-element.168), channel_id=1, source_target_pairs={{0,1},{1,0},{2,3},{3,2},{4,5},{5,4},{6,7},{7,6},{8,9},{9,8},{10,11... | collective-permute-start | bytes 589832 | tf_op jit(solution)/shard_map/ppermute | solution.py:416
  50.1 4.3 %collective-permute-start.20 = (bf16[128,384]{1,0:T(8,128)(2,1)S(1)}, bf16[128,384]{1,0:T(8,128)(2,1)S(1)}, u32[]{:S(2)}, u32[]{:S(2)}) collective-permute-start(bf16[128,384]{1,0:T(8,128)(2,1)S(1)} %get-tuple-element.181), channel_id=1, source_target_pairs={{0,1},{1,0},{2,3},{3,2},{4,5},{5,4},{6,7},{7,6},{8,9},{9,8},{10,11... | collective-permute-start | bytes 294920 | tf_op jit(solution)/shard_map/ppermute | solution.py:416
  54.4 1.7 %collective-permute-start.22 = (bf16[128,1536]{1,0:T(8,128)(2,1)S(1)}, bf16[128,1536]{1,0:T(8,128)(2,1)S(1)}, u32[]{:S(2)}, u32[]{:S(2)}) collective-permute-start(bf16[128,1536]{1,0:T(8,128)(2,1)S(1)} %collective-permute-done.19.refs_0_), channel_id=1, source_target_pairs={{0,1},{1,0},{2,3},{3,2},{4,5},{5,4},{6,7},{7,6},{8,9},{9,8},{10,11... | collective-permute-start | bytes 1179656 | tf_op jit(solution)/shard_map/ppermute | solution.py:416
  57.5 1.4 %collective-permute-start.23 = (bf16[128,384]{1,0:T(8,128)(2,1)S(1)}, bf16[128,384]{1,0:T(8,128)(2,1)S(1)}, u32[]{:S(2)}, u32[]{:S(2)}) collective-permute-start(bf16[128,384]{1,0:T(8,128)(2,1)S(1)} %get-tuple-element.191), channel_id=1, source_target_pairs={{0,1},{1,0},{2,3},{3,2},{4,5},{5,4},{6,7},{7,6},{8,9},{9,8},{10,11... | collective-permute-start | bytes 294920 | tf_op jit(solution)/shard_map/ppermute | solution.py:416
  58.9 11.4 %collective-permute-start.24 = (bf16[128,384]{1,0:T(8,128)(2,1)S(1)}, bf16[128,384]{1,0:T(8,128)(2,1)S(1)}, u32[]{:S(2)}, u32[]{:S(2)}) collective-permute-start(bf16[128,384]{1,0:T(8,128)(2,1)S(1)} %get-tuple-element.192), channel_id=1, source_target_pairs={{0,16},{1,21},{2,18},{3,23},{4,20},{5,17},{6,22},{7,19},{8,24},{9,... | collective-permute-start | bytes 294920 | tf_op jit(solution)/shard_map/ppermute | solution.py:465
  62.4 8.1 %collective-permute-start.25 = (bf16[128,384]{1,0:T(8,128)(2,1)S(1)}, bf16[128,384]{1,0:T(8,128)(2,1)S(1)}, u32[]{:S(2)}, u32[]{:S(2)}) collective-permute-start(bf16[128,384]{1,0:T(8,128)(2,1)S(1)} %get-tuple-element.193), channel_id=1, source_target_pairs={{0,28},{1,13},{2,30},{3,15},{4,24},{5,9},{6,26},{7,11},{8,20},{9,5... | collective-permute-start | bytes 294920 | tf_op jit(solution)/shard_map/ppermute | solution.py:465
  63.9 7.2 %collective-permute-start.26 = (bf16[128,384]{1,0:T(8,128)(2,1)S(1)}, bf16[128,384]{1,0:T(8,128)(2,1)S(1)}, u32[]{:S(2)}, u32[]{:S(2)}) collective-permute-start(bf16[128,384]{1,0:T(8,128)(2,1)S(1)} %get-tuple-element.194), channel_id=1, source_target_pairs={{0,8},{1,25},{2,10},{3,27},{4,12},{5,29},{6,14},{7,31},{8,0},{9,17... | collective-permute-start | bytes 294920 | tf_op jit(solution)/shard_map/ppermute | solution.py:465
  63.9 7.2 %collective-permute-start.27 = (bf16[128,384]{1,0:T(8,128)(2,1)S(1)}, bf16[128,384]{1,0:T(8,128)(2,1)S(1)}, u32[]{:S(2)}, u32[]{:S(2)}) collective-permute-start(bf16[128,384]{1,0:T(8,128)(2,1)S(1)} %get-tuple-element.195), channel_id=1, source_target_pairs={{0,0},{1,5},{2,2},{3,7},{4,4},{5,1},{6,6},{7,3},{8,8},{9,13},{10,1... | collective-permute-start | bytes 294920 | tf_op jit(solution)/shard_map/ppermute | solution.py:465
  71.1 1.5 %collective-permute-start.28 = (bf16[256,384]{1,0:T(8,128)(2,1)S(1)}, bf16[256,384]{1,0:T(8,128)(2,1)S(1)}, u32[]{:S(2)}, u32[]{:S(2)}) collective-permute-start(bf16[256,384]{1,0:T(8,128)(2,1)S(1)} %shard_map.118), channel_id=1, source_target_pairs={{0,1},{1,0},{2,3},{3,2},{4,5},{5,4},{6,7},{7,6},{8,9},{9,8},{10,11... | collective-permute-start | bytes 589832 | tf_op jit(solution)/shard_map/ppermute | solution.py:416

commit v10 on v9

--- a/solution.py
+++ b/solution.py
@@ -194,8 +194,8 @@
         (gate_far.at[:, far], gate_ref),
     ]
     copies = [pltpu.make_async_copy(*move, semaphores.at[i]) for i, move in enumerate(moves)]
-    for copy in copies:
-        copy.start()
+    for i in (2, 0, 1, 3):
+        copies[i].start()
     for copy in copies[:2]:
         copy.wait()
     spatial_heads(qkv_ref, heads_ref, first, OTHER)

time: 73.6 us -> 73.9 us (level)
  no operation moved by 1% of the time
where the time goes in v10:
time: 73.9 us; the launch traced here: 73.7 us
  starting transfers between devices  25.9 us (35%)
  waiting for transfers between devices  23.7 us (32%)
  Pallas kernels  23 us (31%)
  between operations  0.87 us (1%)
    ppermute x12, starting transfers between devices, send_pieces(): lax.ppermute(piece, ('seq', 'mlp'), piece_pairs(n_seq, n_mlp, i))  16.9 us
    ppermute x12, waiting for transfers between devices, send_pieces(): lax.ppermute(piece, ('seq', 'mlp'), piece_pairs(n_seq, n_mlp, i))  14.5 us
    ppermute x17, waiting for transfers between devices, swap(): return lax.ppermute(value, axis, [(i, i ^ k) for i in range(size)])  9.18 us
    ppermute x17, starting transfers between devices, swap(): return lax.ppermute(value, axis, [(i, i ^ k) for i in range(size)])  8.96 us
    pallas_call x1, Pallas kernels, rest(): call(functools.partial(rest_kernel, firsts=(first0, first1)), [shape(half...  3.81 us
    pallas_call x1, Pallas kernels, hold_weights(): pl.pallas_call(hold_kernel, out_shape=pltpu.VMEM((features, parts * width...  3.12 us
    pallas_call x1, Pallas kernels, split_on_device(): call(functools.partial(first_spatial_kernel, first=first0), [shape(half0,...  2.9 us
    pallas_call x1, Pallas kernels, split_on_device(): call(half_kernel, shape(half, 3 * width), inputs=7, scratch=(pltpu.VMEM((...  2.88 us
  transfers between devices with their start and end apart: 29, of which 18 were waited for; matrix products, arithmetic and copies ran while one was open for 0% of the time, Pallas kernels for 24%

profile of v10, /device:TPU:0, one launch (start us, length us, event | category | flops | bytes accessed | tf_op | source)
XLA Modules:
  0.0 73.7 jit_solution(5373602969040157583)
XLA Ops:
  0.6 2.9 %shard_map.106 = (bf16[128,384]{1,0:T(8,128)(2,1)S(1)}, bf16[128,1536]{1,0:T(8,128)(2,1)S(1)}, bf16[384,1536]{1,0:T(8,128)(2,1)S(1)}, f32[1,1536]{1,0:T(1,128)S(1)}, bf16[3,512,384]{2,1,0:T(8,128)(2,1)S(1)}) custom-call(bf16[3,512,384]{2,1,0:T(8,128)(2,1)} %bitcast.19, bf16[384,3072]{1,0:T(8,128)(2,1)} %w_far.1, f32[1,3072]{1,0:T(1,128)} %bitcast.24), custom_call_target="tpu_custom_call" | custom-call | tf_op jit(solution)/shard_map/pallas_call | solution.py:479
  3.5 0.5 collective-permute-start.12
  4.1 1.2 %shard_map.107 = (bf16[128,384]{1,0:T(8,128)(2,1)S(1)}, f32[128,1536]{1,0:T(8,128)S(1)}) custom-call(bf16[384,1536]{1,0:T(8,128)(2,1)S(1)} %get-tuple-element.144.w_ref, f32[1,1536]{1,0:T(1,128)S(1)} %get-tuple-element.145.gate_ref, bf16[3,512,384]{2,1,0:T(8,128)(2,1)S(1)} %get-tuple-element.146.qkv_ref), custom_call_target="tpu_custom_call" | custom-call | tf_op jit(solution)/shard_map/pallas_call | solution.py:493
  5.3 0.1 collective-permute-done.12.b_ref
  5.4 0.1 shard_map.108
  5.5 2.9 %collective-permute-start.13 = (bf16[128,1536]{1,0:T(8,128)(2,1)S(1)}, bf16[128,1536]{1,0:T(8,128)(2,1)S(1)}, u32[]{:S(2)}, u32[]{:S(2)}) collective-permute-start(bf16[128,1536]{1,0:T(8,128)(2,1)S(1)} %shard_map.108), channel_id=1, source_target_pairs={{0,2},{1,3},{2,0},{3,1},{4,6},{5,7},{6,4},{7,5},{8,10},{9,11},{10,... | collective-permute-start | bytes 1179656 | tf_op jit(solution)/shard_map/ppermute | solution.py:416
  8.4 6.8 %conditional.2 = (bf16[128,1536]{1,0:T(8,128)(2,1)S(1)}, f32[128,1536]{1,0:T(8,128)S(1)}, f32[128,1536]{1,0:T(8,128)S(1)}) conditional(s32[]{:T(128)} %convert_element_type.4, () %tuple.33, (bf16[1,512,768]{2,1,0:T(8,128)(2,1)}, bf16[128,384]{1,0:T(8,128)(2,1)S(1)}, bf16[128,384]{1,0:T(8,128)(2,1)S(1)}, bf16[3,512,384]{2,1,0:T(8,128)(2,1)}, ...), branch_computations={%region_0.0_spmd, %region_1.0_spmd} | conditional | bytes 4718736 | solution.py:535
  8.4 3.8 %branch_1_fun.5 = (bf16[128,1536]{1,0:T(8,128)(2,1)S(1)}, f32[128,1536]{1,0:T(8,128)S(1)}, f32[128,1536]{1,0:T(8,128)S(1)}, bf16[128,1536]{1,0:T(8,128)(2,1)S(1)...) custom-call(bf16[128,384]{1,0:T(8,128)(2,1)S(1)} %get-tuple-element.59.own0_ref, ...), custom_call_target="tpu_custom_call" | custom-call | tf_op jit(solution)/shard_map/cond/branch_1_fun/pallas_call | solution.py:502
  12.2 0.1 collective-permute-start
  12.3 0.5 collective-permute-start.1
  12.8 0.1 collective-permute-start.2
  12.9 1.1 %collective-permute-done.b_ref = bf16[128,1536]{1,0:T(8,128)(2,1)S(1)} collective-permute-done((bf16[128,1536]{1,0:T(8,128)(2,1)S(1)}, bf16[128,1536]{1,0:T(8,128)(2,1)S(1)}, u32[]{:S(2)}, u32[]{:S(2)}) %collective-permute-start) | collective-permute-done | bytes 393248 | tf_op jit(solution)/shard_map/cond/branch_1_fun/ppermute | solution.py:416
  14.0 0.1 branch_1_fun.6
  14.1 0.5 collective-permute-done.1.b_ref
  14.6 0.1 branch_1_fun.7
  14.7 0.5 collective-permute-done.2.b_ref
  15.2 0.1 branch_1_fun.8
  15.2 0.1 collective-permute-start.15
  15.3 2.6 %collective-permute-done.13.arrived_ref = bf16[128,1536]{1,0:T(8,128)(2,1)S(1)} collective-permute-done((bf16[128,1536]{1,0:T(8,128)(2,1)S(1)}, bf16[128,1536]{1,0:T(8,128)(2,1)S(1)}, u32[]{:S(2)}, u32[]{:S(2)}) %collective-permute-start.13) | collective-permute-done | bytes 393248 | tf_op jit(solution)/shard_map/ppermute | solution.py:416
  17.9 0.1 shard_map.109
  18.0 11.8 %while.16 = (s32[]{:T(128)}, bf16[32,1536]{1,0:T(8,128)(2,1)S(1)}, bf16[32,1536]{1,0:T(8,128)(2,1)S(1)}, bf16[32,1536]{1,0:T(8,128)(2,1)S(1)}, bf16[32,1536]{1,0:T(8,128)(2,1)S(1)}, /*index=5*/s32[]{:T(128)}, s32[]{:T(128)}) while((s32[]{:T(128)}, bf16[32,1536]{1,0:T(8,128)(2,1)S(1)}, bf16[32,1536]{1,0:T(8,128)(2,1)S(1)}, ...), condition=%wide.region_3.0_spmd, body=%wide.region_2.0_spmd.sunk | while | flops 2 | bytes 2359533 | solution.py:559
  18.0 2.9 %collective-permute-start.8 = (bf16[32,1536]{1,0:T(8,128)(2,1)S(1)}, bf16[32,1536]{1,0:T(8,128)(2,1)S(1)}, u32[]{:S(2)}, u32[]{:S(2)}) collective-permute-start(bf16[32,1536]{1,0:T(8,128)(2,1)S(1)} %get-tuple-element.264), channel_id=1, source_target_pairs={{0,16},{1,21},{2,18},{3,23},{4,20},{5,17},{6,22},{7,19},{8,24},{9,... | collective-permute-start | bytes 294920 | tf_op jit(solution)/shard_map/while/body/ppermute | solution.py:465
  20.9 2.3 %collective-permute-start.9 = (bf16[32,1536]{1,0:T(8,128)(2,1)S(1)}, bf16[32,1536]{1,0:T(8,128)(2,1)S(1)}, u32[]{:S(2)}, u32[]{:S(2)}) collective-permute-start(bf16[32,1536]{1,0:T(8,128)(2,1)S(1)} %get-tuple-element.265), channel_id=1, source_target_pairs={{0,28},{1,13},{2,30},{3,15},{4,24},{5,9},{6,26},{7,11},{8,20},{9,5... | collective-permute-start | bytes 294920 | tf_op jit(solution)/shard_map/while/body/ppermute | solution.py:465
  23.2 0.7 collective-permute-start.11
  23.9 5.0 %collective-permute-done.8 = bf16[32,1536]{1,0:T(8,128)(2,1)S(1)} collective-permute-done((bf16[32,1536]{1,0:T(8,128)(2,1)S(1)}, bf16[32,1536]{1,0:T(8,128)(2,1)S(1)}, u32[]{:S(2)}, u32[]{:S(2)}) %collective-permute-start.8) | collective-permute-done | bytes 98336 | tf_op jit(solution)/shard_map/while/body/ppermute | solution.py:465
  28.9 0.2 collective-permute-done.9
  29.1 0.7 collective-permute-done.10
  29.9 0.1 shard_map.110
  30.1 12.4 %conditional.3 = (bf16[32,1536]{1,0:T(8,128)(2,1)S(1)}, bf16[32,1536]{1,0:T(8,128)(2,1)S(1)}, bf16[32,1536]{1,0:T(8,128)(2,1)S(1)}, bf16[32,1536]{1,0:T(8,128)(2...) conditional(s32[]{:T(128)} %convert_element_type.4, (bf16[32,1536]{1,0:T(8,128)(2,1)S(1)}, ...), branch_computations={%region_4.0_spmd, %region_5.0_spmd} | conditional | bytes 7864370 | solution.py:570
  30.1 1.6 %collective-permute-start.7 = (bf16[128,1536]{1,0:T(8,128)(2,1)S(1)}, bf16[128,1536]{1,0:T(8,128)(2,1)}, u32[]{:S(2)}, u32[]{:S(2)}) collective-permute-start(bf16[128,1536]{1,0:T(8,128)(2,1)S(1)} %get-tuple-element.88), channel_id=1, source_target_pairs={{0,2},{1,3},{2,0},{3,1},{4,6},{5,7},{6,4},{7,5},{8,10},{9,11},{10,... | collective-permute-start | bytes 1179656 | tf_op jit(solution)/shard_map/cond/branch_1_fun/ppermute | solution.py:416
  31.7 3.2 %collective-permute-start.3 = (bf16[32,1536]{1,0:T(8,128)(2,1)S(1)}, bf16[32,1536]{1,0:T(8,128)(2,1)S(1)}, u32[]{:S(2)}, u32[]{:S(2)}) collective-permute-start(bf16[32,1536]{1,0:T(8,128)(2,1)S(1)} %get-tuple-element.84), channel_id=1, source_target_pairs={{0,16},{1,21},{2,18},{3,23},{4,20},{5,17},{6,22},{7,19},{8,24},{9,... | collective-permute-start | bytes 294920 | tf_op jit(solution)/shard_map/cond/branch_1_fun/ppermute | solution.py:465
  34.9 1.2 %collective-permute-start.4 = (bf16[32,1536]{1,0:T(8,128)(2,1)S(1)}, bf16[32,1536]{1,0:T(8,128)(2,1)S(1)}, u32[]{:S(2)}, u32[]{:S(2)}) collective-permute-start(bf16[32,1536]{1,0:T(8,128)(2,1)S(1)} %get-tuple-element.85), channel_id=1, source_target_pairs={{0,28},{1,13},{2,30},{3,15},{4,24},{5,9},{6,26},{7,11},{8,20},{9,5... | collective-permute-start | bytes 294920 | tf_op jit(solution)/shard_map/cond/branch_1_fun/ppermute | solution.py:465
  36.2 0.2 collective-permute-start.5
  36.4 0.8 %collective-permute-start.6 = (bf16[32,1536]{1,0:T(8,128)(2,1)S(1)}, bf16[32,1536]{1,0:T(8,128)(2,1)S(1)}, u32[]{:S(2)}, u32[]{:S(2)}) collective-permute-start(bf16[32,1536]{1,0:T(8,128)(2,1)S(1)} %get-tuple-element.87), channel_id=1, source_target_pairs={{0,0},{1,5},{2,2},{3,7},{4,4},{5,1},{6,6},{7,3},{8,8},{9,13},{10,1... | collective-permute-start | bytes 294920 | tf_op jit(solution)/shard_map/cond/branch_1_fun/ppermute | solution.py:465
  37.3 3.1 %branch_1_fun.9 = bf16[3072,1152]{1,0:T(8,128)(2,1)S(1)} custom-call(bf16[3,3072,384]{2,1,0:T(8,128)(2,1)} %bitcast.18), custom_call_target="tpu_custom_call" | custom-call | tf_op jit(solution)/shard_map/cond/branch_1_fun/pallas_call | solution.py:136
  40.4 0.3 collective-permute-done.3
  40.7 1.6 %collective-permute-done.4 = bf16[32,1536]{1,0:T(8,128)(2,1)S(1)} collective-permute-done((bf16[32,1536]{1,0:T(8,128)(2,1)S(1)}, bf16[32,1536]{1,0:T(8,128)(2,1)S(1)}, u32[]{:S(2)}, u32[]{:S(2)}) %collective-permute-start.4) | collective-permute-done | bytes 98336 | tf_op jit(solution)/shard_map/cond/branch_1_fun/ppermute | solution.py:465
  42.3 0.1 collective-permute-done.5
  42.5 0.1 collective-permute-start.17
  42.6 0.5 collective-permute-start.18
  43.2 0.1 collective-permute-start.21
  43.3 1.5 %collective-permute-start.19 = (bf16[128,1536]{1,0:T(8,128)(2,1)S(1)}, bf16[128,1536]{1,0:T(8,128)(2,1)S(1)}, u32[]{:S(2)}, u32[]{:S(2)}) collective-permute-start(bf16[128,1536]{1,0:T(8,128)(2,1)S(1)} %constant_dynamic-update-slice_fusion.4.own_ref), channel_id=1, source_target_pairs={{0,2},{1,3},{2,0},{3,1},{4,6},{5,7},{6,4},{7,5},{8,10},{9,11},{10,... | collective-permute-start | bytes 1179656 | tf_op jit(solution)/shard_map/ppermute | solution.py:416
  44.7 0.2 collective-permute-start.14
  44.9 0.3 collective-permute-start.16
  45.2 2.9 %shard_map.112.own_proj_ref = bf16[128,1152]{1,0:T(8,128)(2,1)S(1)} custom-call(bf16[128,1536]{1,0:T(8,128)(2,1)S(1)} %constant_dynamic-update-slice_fusion.near, bf16[128,1536]{1,0:T(8,128)(2,1)} %get-tuple-element.178.far, f32[1,3072]{1,0:T(1,128)S(1)} %bitcast.10, f32[1,3072]{1,0:T(1,128)S(1)} %bitcast.15, ...), custom_call_target="tpu_custom_call" | custom-call | tf_op jit(solution)/shard_map/pallas_call | solution.py:610
  48.1 2.2 %shard_map.113 = (bf16[128,384]{1,0:T(8,128)(2,1)S(1)}, bf16[128,384]{1,0:T(8,128)(2,1)S(1)}) custom-call(bf16[128,1152]{1,0:T(8,128)(2,1)S(1)} %shard_map.112.own_proj_ref, bf16[128,1536]{1,0:T(8,128)(2,1)S(1)} %collective-permute-done.17.near, bf16[128,1536]{1,0:T(8,128)(2,1)S(1)} %collective-permute-done.18.far, f32[1,3072]{1,0:T(1,128)S(1)} %bitcast.11, ...), custom_call_target="tpu_custom_call" | custom-call | tf_op jit(solution)/shard_map/pallas_call | solution.py:616
  50.4 0.2 collective-permute-start.20
  50.6 1.0 %shard_map.111 = bf16[512,768]{1,0:T(8,128)(2,1)} custom-call(bf16[128,768]{1,0:T(8,128)(2,1)S(1)} %get-tuple-element.155.refs_0_, bf16[128,768]{1,0:T(8,128)(2,1)S(1)} %collective-permute-done.14.refs_1_, bf16[128,768]{1,0:T(8,128)(2,1)S(1)} %get-tuple-element.167.refs_2_, bf16[128,768]{1,0:T(8,128)(2,1)S(1)} %collective-permute-done.16.refs_3_), custom_call_target="tpu_custom_call" | custom-call | tf_op jit(solution)/shard_map/pallas_call | solution.py:584
  51.6 2.2 %shard_map.114 = (f32[128,1152]{1,0:T(8,128)S(1)}, f32[128,1152]{1,0:T(8,128)S(1)}, f32[128,1]{1,0:T(8,128)S(1)}, f32[128,1]{1,0:T(8,128)S(1)}, f32[128,1]{1,0:T...) custom-call(bf16[128,1536]{1,0:T(8,128)(2,1)S(1)} %constant_dynamic-update-slice_fusion.4.own_ref, ...), custom_call_target="tpu_custom_call" | custom-call | tf_op jit(solution)/shard_map/pallas_call | solution.py:590
  53.8 0.9 %collective-permute-done.19.refs_0_ = bf16[128,1536]{1,0:T(8,128)(2,1)S(1)} collective-permute-done((bf16[128,1536]{1,0:T(8,128)(2,1)S(1)}, bf16[128,1536]{1,0:T(8,128)(2,1)S(1)}, u32[]{:S(2)}, u32[]{:S(2)}) %collective-permute-start.19) | collective-permute-done | bytes 393248 | tf_op jit(solution)/shard_map/ppermute | solution.py:416
  54.7 0.9 %shard_map.115.own_proj_ref = bf16[128,1152]{1,0:T(8,128)(2,1)S(1)} custom-call(bf16[128,1536]{1,0:T(8,128)(2,1)S(1)} %collective-permute-done.19.refs_0_, f32[128,1152]{1,0:T(8,128)S(1)} %get-tuple-element.184.refs_1_, f32[128,1]{1,0:T(8,128)S(1)} %get-tuple-element.185.refs_2_, f32[128,1]{1,0:T(8,128)S(1)} %get-tuple-element.186.refs_3_, ...), custom_call_target="tpu_custom_call" | custom-call | tf_op jit(solution)/shard_map/pallas_call | solution.py:599
  55.6 0.8 %collective-permute-done.22.refs_0_ = bf16[128,1536]{1,0:T(8,128)(2,1)S(1)} collective-permute-done((bf16[128,1536]{1,0:T(8,128)(2,1)S(1)}, bf16[128,1536]{1,0:T(8,128)(2,1)S(1)}, u32[]{:S(2)}, u32[]{:S(2)}) %collective-permute-start.22) | collective-permute-done | bytes 393248 | tf_op jit(solution)/shard_map/ppermute | solution.py:416
  56.5 1.4 %shard_map.116 = (bf16[128,384]{1,0:T(8,128)(2,1)S(1)}, bf16[128,384]{1,0:T(8,128)(2,1)S(1)}) custom-call(bf16[128,1152]{1,0:T(8,128)(2,1)S(1)} %shard_map.115.own_proj_ref, bf16[128,1536]{1,0:T(8,128)(2,1)S(1)} %collective-permute-done.22.refs_0_, f32[128,1152]{1,0:T(8,128)S(1)} %get-tuple-element.187.refs_1_, f32[128,1]{1,0:T(8,128)S(1)} %get-tuple-element.188.refs_2_, ...), custom_call_target="tpu_custom_call" | custom-call | tf_op jit(solution)/shard_map/pallas_call | solution.py:602
  57.8 0.2 collective-permute-start.23
  58.0 1.2 %collective-permute-done.23.refs_3_ = bf16[128,384]{1,0:T(8,128)(2,1)S(1)} collective-permute-done((bf16[128,384]{1,0:T(8,128)(2,1)S(1)}, bf16[128,384]{1,0:T(8,128)(2,1)S(1)}, u32[]{:S(2)}, u32[]{:S(2)}) %collective-permute-start.23) | collective-permute-done | bytes 98336 | tf_op jit(solution)/shard_map/ppermute | solution.py:416
  59.3 3.5 %collective-permute-start.24 = (bf16[128,384]{1,0:T(8,128)(2,1)S(1)}, bf16[128,384]{1,0:T(8,128)(2,1)S(1)}, u32[]{:S(2)}, u32[]{:S(2)}) collective-permute-start(bf16[128,384]{1,0:T(8,128)(2,1)S(1)} %get-tuple-element.192), channel_id=1, source_target_pairs={{0,16},{1,21},{2,18},{3,23},{4,20},{5,17},{6,22},{7,19},{8,24},{9,... | collective-permute-start | bytes 294920 | tf_op jit(solution)/shard_map/ppermute | solution.py:465
  62.7 1.4 %collective-permute-start.25 = (bf16[128,384]{1,0:T(8,128)(2,1)S(1)}, bf16[128,384]{1,0:T(8,128)(2,1)S(1)}, u32[]{:S(2)}, u32[]{:S(2)}) collective-permute-start(bf16[128,384]{1,0:T(8,128)(2,1)S(1)} %get-tuple-element.193), channel_id=1, source_target_pairs={{0,28},{1,13},{2,30},{3,15},{4,24},{5,9},{6,26},{7,11},{8,20},{9,5... | collective-permute-start | bytes 294920 | tf_op jit(solution)/shard_map/ppermute | solution.py:465
  64.2 0.7 collective-permute-start.27
  64.8 5.8 %collective-permute-done.24.refs_0_ = bf16[128,384]{1,0:T(8,128)(2,1)S(1)} collective-permute-done((bf16[128,384]{1,0:T(8,128)(2,1)S(1)}, bf16[128,384]{1,0:T(8,128)(2,1)S(1)}, u32[]{:S(2)}, u32[]{:S(2)}) %collective-permute-start.24) | collective-permute-done | bytes 98336 | tf_op jit(solution)/shard_map/ppermute | solution.py:465
  70.6 0.3 collective-permute-done.25.refs_1_
  70.9 0.5 collective-permute-done.26.refs_2_
  71.4 0.1 collective-permute-start.28
  71.5 1.4 %collective-permute-done.28.refs_4_ = bf16[256,384]{1,0:T(8,128)(2,1)S(1)} collective-permute-done((bf16[256,384]{1,0:T(8,128)(2,1)S(1)}, bf16[256,384]{1,0:T(8,128)(2,1)S(1)}, u32[]{:S(2)}, u32[]{:S(2)}) %collective-permute-start.28) | collective-permute-done | bytes 196640 | tf_op jit(solution)/shard_map/ppermute | solution.py:416
  72.9 0.8 %shard_map.119 = bf16[512,384]{1,0:T(8,128)(2,1)} custom-call(bf16[128,384]{1,0:T(8,128)(2,1)S(1)} %collective-permute-done.24.refs_0_, bf16[128,384]{1,0:T(8,128)(2,1)S(1)} %collective-permute-done.25.refs_1_, bf16[128,384]{1,0:T(8,128)(2,1)S(1)} %collective-permute-done.26.refs_2_, bf16[128,384]{1,0:T(8,128)(2,1)S(1)} %collective-permute-done.27.refs_3_, ...), custom_call_target="tpu_custom_call" | custom-call | tf_op jit(solution)/shard_map/pallas_call | solution.py:633
  (40 shorter events, 0.2 us)
Async XLA Ops:
  3.5 1.9 %collective-permute-start.12 = (bf16[128,1536]{1,0:T(8,128)(2,1)S(1)}, bf16[128,1536]{1,0:T(8,128)(2,1)S(1)}, u32[]{:S(2)}, u32[]{:S(2)}) collective-permute-start(bf16[128,1536]{1,0:T(8,128)(2,1)S(1)} %get-tuple-element.149), channel_id=1, source_target_pairs={{0,1},{1,0},{2,3},{3,2},{4,5},{5,4},{6,7},{7,6},{8,9},{9,8},{10,11... | collective-permute-start | bytes 1179656 | tf_op jit(solution)/shard_map/ppermute | solution.py:416
  5.5 12.4 %collective-permute-start.13 = (bf16[128,1536]{1,0:T(8,128)(2,1)S(1)}, bf16[128,1536]{1,0:T(8,128)(2,1)S(1)}, u32[]{:S(2)}, u32[]{:S(2)}) collective-permute-start(bf16[128,1536]{1,0:T(8,128)(2,1)S(1)} %shard_map.108), channel_id=1, source_target_pairs={{0,2},{1,3},{2,0},{3,1},{4,6},{5,7},{6,4},{7,5},{8,10},{9,11},{10,... | collective-permute-start | bytes 1179656 | tf_op jit(solution)/shard_map/ppermute | solution.py:416
  12.2 1.8 %collective-permute-start = (bf16[128,1536]{1,0:T(8,128)(2,1)S(1)}, bf16[128,1536]{1,0:T(8,128)(2,1)S(1)}, u32[]{:S(2)}, u32[]{:S(2)}) collective-permute-start(bf16[128,1536]{1,0:T(8,128)(2,1)S(1)} %get-tuple-element.66), channel_id=1, source_target_pairs={{0,1},{1,0},{2,3},{3,2},{4,5},{5,4},{6,7},{7,6},{8,9},{9,8},{10,11... | collective-permute-start | bytes 1179656 | tf_op jit(solution)/shard_map/cond/branch_1_fun/ppermute | solution.py:416
  12.3 2.3 %collective-permute-start.1 = (bf16[128,1536]{1,0:T(8,128)(2,1)S(1)}, bf16[128,1536]{1,0:T(8,128)(2,1)S(1)}, u32[]{:S(2)}, u32[]{:S(2)}) collective-permute-start(bf16[128,1536]{1,0:T(8,128)(2,1)S(1)} %get-tuple-element.68), channel_id=1, source_target_pairs={{0,1},{1,0},{2,3},{3,2},{4,5},{5,4},{6,7},{7,6},{8,9},{9,8},{10,11... | collective-permute-start | bytes 1179656 | tf_op jit(solution)/shard_map/cond/branch_1_fun/ppermute | solution.py:416
  12.8 2.3 %collective-permute-start.2 = (bf16[128,1536]{1,0:T(8,128)(2,1)S(1)}, bf16[128,1536]{1,0:T(8,128)(2,1)S(1)}, u32[]{:S(2)}, u32[]{:S(2)}) collective-permute-start(bf16[128,1536]{1,0:T(8,128)(2,1)S(1)} %get-tuple-element.70), channel_id=1, source_target_pairs={{0,1},{1,0},{2,3},{3,2},{4,5},{5,4},{6,7},{7,6},{8,9},{9,8},{10,11... | collective-permute-start | bytes 1179656 | tf_op jit(solution)/shard_map/cond/branch_1_fun/ppermute | solution.py:416
  15.2 14.7 %collective-permute-start.15 = (bf16[128,1536]{1,0:T(8,128)(2,1)S(1)}, bf16[128,1536]{1,0:T(8,128)(2,1)S(1)}, u32[]{:S(2)}, u32[]{:S(2)}) collective-permute-start(bf16[128,1536]{1,0:T(8,128)(2,1)S(1)} %get-tuple-element.153), channel_id=1, source_target_pairs={{0,2},{1,3},{2,0},{3,1},{4,6},{5,7},{6,4},{7,5},{8,10},{9,11},{10,... | collective-permute-start | bytes 1179656 | tf_op jit(solution)/shard_map/ppermute | solution.py:416
  18.0 10.8 %collective-permute-start.8 = (bf16[32,1536]{1,0:T(8,128)(2,1)S(1)}, bf16[32,1536]{1,0:T(8,128)(2,1)S(1)}, u32[]{:S(2)}, u32[]{:S(2)}) collective-permute-start(bf16[32,1536]{1,0:T(8,128)(2,1)S(1)} %get-tuple-element.264), channel_id=1, source_target_pairs={{0,16},{1,21},{2,18},{3,23},{4,20},{5,17},{6,22},{7,19},{8,24},{9,... | collective-permute-start | bytes 294920 | tf_op jit(solution)/shard_map/while/body/ppermute | solution.py:465
  20.9 8.2 %collective-permute-start.9 = (bf16[32,1536]{1,0:T(8,128)(2,1)S(1)}, bf16[32,1536]{1,0:T(8,128)(2,1)S(1)}, u32[]{:S(2)}, u32[]{:S(2)}) collective-permute-start(bf16[32,1536]{1,0:T(8,128)(2,1)S(1)} %get-tuple-element.265), channel_id=1, source_target_pairs={{0,28},{1,13},{2,30},{3,15},{4,24},{5,9},{6,26},{7,11},{8,20},{9,5... | collective-permute-start | bytes 294920 | tf_op jit(solution)/shard_map/while/body/ppermute | solution.py:465
  23.2 6.6 %collective-permute-start.10 = (bf16[32,1536]{1,0:T(8,128)(2,1)S(1)}, bf16[32,1536]{1,0:T(8,128)(2,1)S(1)}, u32[]{:S(2)}, u32[]{:S(2)}) collective-permute-start(bf16[32,1536]{1,0:T(8,128)(2,1)S(1)} %get-tuple-element.266), channel_id=1, source_target_pairs={{0,8},{1,25},{2,10},{3,27},{4,12},{5,29},{6,14},{7,31},{8,0},{9,17... | collective-permute-start | bytes 294920 | tf_op jit(solution)/shard_map/while/body/ppermute | solution.py:465
  23.2 6.6 %collective-permute-start.11 = (bf16[32,1536]{1,0:T(8,128)(2,1)S(1)}, bf16[32,1536]{1,0:T(8,128)(2,1)S(1)}, u32[]{:S(2)}, u32[]{:S(2)}) collective-permute-start(bf16[32,1536]{1,0:T(8,128)(2,1)S(1)} %get-tuple-element.267), channel_id=1, source_target_pairs={{0,0},{1,5},{2,2},{3,7},{4,4},{5,1},{6,6},{7,3},{8,8},{9,13},{10,1... | collective-permute-start | bytes 294920 | tf_op jit(solution)/shard_map/while/body/ppermute | solution.py:465
  30.1 15.2 %copy-start = (f32[3072]{0:T(1024)S(1)}, f32[3072]{0:T(1024)}, u32[]{:S(2)}) copy-start(f32[3072]{0:T(1024)} %param.20) | copy-start | bytes 36868
  30.1 15.2 %copy-start.1 = (f32[3072]{0:T(1024)S(1)}, f32[3072]{0:T(1024)}, u32[]{:S(2)}) copy-start(f32[3072]{0:T(1024)} %param.19) | copy-start | bytes 36868
  30.1 15.2 %copy-start.2 = (f32[8,128]{1,0:T(8,128)S(1)}, f32[8,128]{1,0:T(8,128)}, u32[]{:S(2)}) copy-start(f32[8,128]{1,0:T(8,128)} %constant.22.clone.cos_ref.refs_7_) | copy-start | bytes 12292
  30.1 15.2 %copy-start.3 = (f32[8,128]{1,0:T(8,128)S(1)}, f32[8,128]{1,0:T(8,128)}, u32[]{:S(2)}) copy-start(f32[8,128]{1,0:T(8,128)} %constant.23.clone.sin_ref.refs_8_) | copy-start | bytes 12292
  30.1 12.4 %collective-permute-start.7 = (bf16[128,1536]{1,0:T(8,128)(2,1)S(1)}, bf16[128,1536]{1,0:T(8,128)(2,1)}, u32[]{:S(2)}, u32[]{:S(2)}) collective-permute-start(bf16[128,1536]{1,0:T(8,128)(2,1)S(1)} %get-tuple-element.88), channel_id=1, source_target_pairs={{0,2},{1,3},{2,0},{3,1},{4,6},{5,7},{6,4},{7,5},{8,10},{9,11},{10,... | collective-permute-start | bytes 1179656 | tf_op jit(solution)/shard_map/cond/branch_1_fun/ppermute | solution.py:416
  31.7 9.0 %collective-permute-start.3 = (bf16[32,1536]{1,0:T(8,128)(2,1)S(1)}, bf16[32,1536]{1,0:T(8,128)(2,1)S(1)}, u32[]{:S(2)}, u32[]{:S(2)}) collective-permute-start(bf16[32,1536]{1,0:T(8,128)(2,1)S(1)} %get-tuple-element.84), channel_id=1, source_target_pairs={{0,16},{1,21},{2,18},{3,23},{4,20},{5,17},{6,22},{7,19},{8,24},{9,... | collective-permute-start | bytes 294920 | tf_op jit(solution)/shard_map/cond/branch_1_fun/ppermute | solution.py:465
  34.9 7.4 %collective-permute-start.4 = (bf16[32,1536]{1,0:T(8,128)(2,1)S(1)}, bf16[32,1536]{1,0:T(8,128)(2,1)S(1)}, u32[]{:S(2)}, u32[]{:S(2)}) collective-permute-start(bf16[32,1536]{1,0:T(8,128)(2,1)S(1)} %get-tuple-element.85), channel_id=1, source_target_pairs={{0,28},{1,13},{2,30},{3,15},{4,24},{5,9},{6,26},{7,11},{8,20},{9,5... | collective-permute-start | bytes 294920 | tf_op jit(solution)/shard_map/cond/branch_1_fun/ppermute | solution.py:465
  36.2 6.3 %collective-permute-start.5 = (bf16[32,1536]{1,0:T(8,128)(2,1)S(1)}, bf16[32,1536]{1,0:T(8,128)(2,1)S(1)}, u32[]{:S(2)}, u32[]{:S(2)}) collective-permute-start(bf16[32,1536]{1,0:T(8,128)(2,1)S(1)} %get-tuple-element.86), channel_id=1, source_target_pairs={{0,8},{1,25},{2,10},{3,27},{4,12},{5,29},{6,14},{7,31},{8,0},{9,17... | collective-permute-start | bytes 294920 | tf_op jit(solution)/shard_map/cond/branch_1_fun/ppermute | solution.py:465
  36.4 6.0 %collective-permute-start.6 = (bf16[32,1536]{1,0:T(8,128)(2,1)S(1)}, bf16[32,1536]{1,0:T(8,128)(2,1)S(1)}, u32[]{:S(2)}, u32[]{:S(2)}) collective-permute-start(bf16[32,1536]{1,0:T(8,128)(2,1)S(1)} %get-tuple-element.87), channel_id=1, source_target_pairs={{0,0},{1,5},{2,2},{3,7},{4,4},{5,1},{6,6},{7,3},{8,8},{9,13},{10,1... | collective-permute-start | bytes 294920 | tf_op jit(solution)/shard_map/cond/branch_1_fun/ppermute | solution.py:465
  42.5 2.4 %collective-permute-start.17 = (bf16[128,1536]{1,0:T(8,128)(2,1)S(1)}, bf16[128,1536]{1,0:T(8,128)(2,1)S(1)}, u32[]{:S(2)}, u32[]{:S(2)}) collective-permute-start(bf16[128,1536]{1,0:T(8,128)(2,1)S(1)} %constant_dynamic-update-slice_fusion.near), channel_id=1, source_target_pairs={{0,1},{1,0},{2,3},{3,2},{4,5},{5,4},{6,7},{7,6},{8,9},{9,8},{10,11... | collective-permute-start | bytes 1179656 | tf_op jit(solution)/shard_map/ppermute | solution.py:416
  42.6 5.5 %collective-permute-start.18 = (bf16[128,1536]{1,0:T(8,128)(2,1)}, bf16[128,1536]{1,0:T(8,128)(2,1)S(1)}, u32[]{:S(2)}, u32[]{:S(2)}) collective-permute-start(bf16[128,1536]{1,0:T(8,128)(2,1)} %get-tuple-element.178.far), channel_id=1, source_target_pairs={{0,1},{1,0},{2,3},{3,2},{4,5},{5,4},{6,7},{7,6},{8,9},{9,8},{10,11... | collective-permute-start | bytes 1179656 | tf_op jit(solution)/shard_map/ppermute | solution.py:416
  43.2 8.4 %collective-permute-start.21 = (bf16[128,1536]{1,0:T(8,128)(2,1)S(1)}, bf16[128,1536]{1,0:T(8,128)(2,1)S(1)}, u32[]{:S(2)}, u32[]{:S(2)}) collective-permute-start(bf16[128,1536]{1,0:T(8,128)(2,1)S(1)} %constant_dynamic-update-slice_fusion.4.own_ref), channel_id=1, source_target_pairs={{0,1},{1,0},{2,3},{3,2},{4,5},{5,4},{6,7},{7,6},{8,9},{9,8},{10,11... | collective-permute-start | bytes 1179656 | tf_op jit(solution)/shard_map/ppermute | solution.py:416
  43.3 11.5 %collective-permute-start.19 = (bf16[128,1536]{1,0:T(8,128)(2,1)S(1)}, bf16[128,1536]{1,0:T(8,128)(2,1)S(1)}, u32[]{:S(2)}, u32[]{:S(2)}) collective-permute-start(bf16[128,1536]{1,0:T(8,128)(2,1)S(1)} %constant_dynamic-update-slice_fusion.4.own_ref), channel_id=1, source_target_pairs={{0,2},{1,3},{2,0},{3,1},{4,6},{5,7},{6,4},{7,5},{8,10},{9,11},{10,... | collective-permute-start | bytes 1179656 | tf_op jit(solution)/shard_map/ppermute | solution.py:416
  44.7 5.9 %collective-permute-start.14 = (bf16[128,768]{1,0:T(8,128)(2,1)S(1)}, bf16[128,768]{1,0:T(8,128)(2,1)S(1)}, u32[]{:S(2)}, u32[]{:S(2)}) collective-permute-start(bf16[128,768]{1,0:T(8,128)(2,1)S(1)} %get-tuple-element.156), channel_id=1, source_target_pairs={{0,1},{1,0},{2,3},{3,2},{4,5},{5,4},{6,7},{7,6},{8,9},{9,8},{10,11... | collective-permute-start | bytes 589832 | tf_op jit(solution)/shard_map/ppermute | solution.py:416
  44.9 5.7 %collective-permute-start.16 = (bf16[128,768]{1,0:T(8,128)(2,1)S(1)}, bf16[128,768]{1,0:T(8,128)(2,1)S(1)}, u32[]{:S(2)}, u32[]{:S(2)}) collective-permute-start(bf16[128,768]{1,0:T(8,128)(2,1)S(1)} %get-tuple-element.168), channel_id=1, source_target_pairs={{0,1},{1,0},{2,3},{3,2},{4,5},{5,4},{6,7},{7,6},{8,9},{9,8},{10,11... | collective-permute-start | bytes 589832 | tf_op jit(solution)/shard_map/ppermute | solution.py:416
  50.4 4.4 %collective-permute-start.20 = (bf16[128,384]{1,0:T(8,128)(2,1)S(1)}, bf16[128,384]{1,0:T(8,128)(2,1)S(1)}, u32[]{:S(2)}, u32[]{:S(2)}) collective-permute-start(bf16[128,384]{1,0:T(8,128)(2,1)S(1)} %get-tuple-element.181), channel_id=1, source_target_pairs={{0,1},{1,0},{2,3},{3,2},{4,5},{5,4},{6,7},{7,6},{8,9},{9,8},{10,11... | collective-permute-start | bytes 294920 | tf_op jit(solution)/shard_map/ppermute | solution.py:416
  54.7 1.7 %collective-permute-start.22 = (bf16[128,1536]{1,0:T(8,128)(2,1)S(1)}, bf16[128,1536]{1,0:T(8,128)(2,1)S(1)}, u32[]{:S(2)}, u32[]{:S(2)}) collective-permute-start(bf16[128,1536]{1,0:T(8,128)(2,1)S(1)} %collective-permute-done.19.refs_0_), channel_id=1, source_target_pairs={{0,1},{1,0},{2,3},{3,2},{4,5},{5,4},{6,7},{7,6},{8,9},{9,8},{10,11... | collective-permute-start | bytes 1179656 | tf_op jit(solution)/shard_map/ppermute | solution.py:416
  57.8 1.4 %collective-permute-start.23 = (bf16[128,384]{1,0:T(8,128)(2,1)S(1)}, bf16[128,384]{1,0:T(8,128)(2,1)S(1)}, u32[]{:S(2)}, u32[]{:S(2)}) collective-permute-start(bf16[128,384]{1,0:T(8,128)(2,1)S(1)} %get-tuple-element.191), channel_id=1, source_target_pairs={{0,1},{1,0},{2,3},{3,2},{4,5},{5,4},{6,7},{7,6},{8,9},{9,8},{10,11... | collective-permute-start | bytes 294920 | tf_op jit(solution)/shard_map/ppermute | solution.py:416
  59.3 11.3 %collective-permute-start.24 = (bf16[128,384]{1,0:T(8,128)(2,1)S(1)}, bf16[128,384]{1,0:T(8,128)(2,1)S(1)}, u32[]{:S(2)}, u32[]{:S(2)}) collective-permute-start(bf16[128,384]{1,0:T(8,128)(2,1)S(1)} %get-tuple-element.192), channel_id=1, source_target_pairs={{0,16},{1,21},{2,18},{3,23},{4,20},{5,17},{6,22},{7,19},{8,24},{9,... | collective-permute-start | bytes 294920 | tf_op jit(solution)/shard_map/ppermute | solution.py:465
  62.7 8.2 %collective-permute-start.25 = (bf16[128,384]{1,0:T(8,128)(2,1)S(1)}, bf16[128,384]{1,0:T(8,128)(2,1)S(1)}, u32[]{:S(2)}, u32[]{:S(2)}) collective-permute-start(bf16[128,384]{1,0:T(8,128)(2,1)S(1)} %get-tuple-element.193), channel_id=1, source_target_pairs={{0,28},{1,13},{2,30},{3,15},{4,24},{5,9},{6,26},{7,11},{8,20},{9,5... | collective-permute-start | bytes 294920 | tf_op jit(solution)/shard_map/ppermute | solution.py:465
  64.2 7.2 %collective-permute-start.26 = (bf16[128,384]{1,0:T(8,128)(2,1)S(1)}, bf16[128,384]{1,0:T(8,128)(2,1)S(1)}, u32[]{:S(2)}, u32[]{:S(2)}) collective-permute-start(bf16[128,384]{1,0:T(8,128)(2,1)S(1)} %get-tuple-element.194), channel_id=1, source_target_pairs={{0,8},{1,25},{2,10},{3,27},{4,12},{5,29},{6,14},{7,31},{8,0},{9,17... | collective-permute-start | bytes 294920 | tf_op jit(solution)/shard_map/ppermute | solution.py:465
  64.2 7.2 %collective-permute-start.27 = (bf16[128,384]{1,0:T(8,128)(2,1)S(1)}, bf16[128,384]{1,0:T(8,128)(2,1)S(1)}, u32[]{:S(2)}, u32[]{:S(2)}) collective-permute-start(bf16[128,384]{1,0:T(8,128)(2,1)S(1)} %get-tuple-element.195), channel_id=1, source_target_pairs={{0,0},{1,5},{2,2},{3,7},{4,4},{5,1},{6,6},{7,3},{8,8},{9,13},{10,1... | collective-permute-start | bytes 294920 | tf_op jit(solution)/shard_map/ppermute | solution.py:465
  71.4 1.5 %collective-permute-start.28 = (bf16[256,384]{1,0:T(8,128)(2,1)S(1)}, bf16[256,384]{1,0:T(8,128)(2,1)S(1)}, u32[]{:S(2)}, u32[]{:S(2)}) collective-permute-start(bf16[256,384]{1,0:T(8,128)(2,1)S(1)} %shard_map.118), channel_id=1, source_target_pairs={{0,1},{1,0},{2,3},{3,2},{4,5},{5,4},{6,7},{7,6},{8,9},{9,8},{10,11... | collective-permute-start | bytes 589832 | tf_op jit(solution)/shard_map/ppermute | solution.py:416
